TPU v7x, 32 devices: a whole 2x2x4 slice. The times are simulated.
32 devices in a mesh: gx: 4 (over z), gy: 4 (over x, core), gz: 2 (over y).
Axes of the slice: x: 2, y: 2, z: 4, core: 2. Of those that a mesh axis runs over, the one named last changes fastest.
Arguments:
- adjoint_efield: float32 [3, 48, 32, 2048], P(None, 'gz', 'gx', 'gy'), may hold values from -6 to 6
- adjoint_hfield: float32 [3, 48, 32, 2048], P(None, 'gz', 'gx', 'gy'), may hold values from -6 to 6
- forward_efield: float32 [3, 48, 32, 2048], P(None, 'gz', 'gx', 'gy'), may hold values from -6 to 6
- material: int32 [48, 32, 2048], P('gz', 'gx', 'gy'), may hold values from 0 to 3
- permittivity: float32 [4], replicated, may hold values from 1 to 12
- design_mask: int32 [4, 256], P('gx', 'gy'), may hold values 0 or 1
- grad_sum: float32 [32, 32, 2048], P('gz', 'gx', 'gy'), may hold values from -6 to 6
Outputs:
- efield_next: float32 [3, 48, 32, 2048], P(None, 'gz', 'gx', 'gy')
- hfield_next: float32 [3, 48, 32, 2048], P(None, 'gz', 'gx', 'gy')
- grad_total: float32 [32, 32, 2048], P('gz', 'gx', 'gy')
- grad_filtered: float32 [32, 32, 2048], P('gz', 'gx', 'gy')
Inputs may be any that keep to these rules, and one draw needn't show every extreme that they name: material indices name rows of permittivity.
All inputs are finite; a program needn't handle non-finite values. No bound on the sum of `design_mask` on one device may be relied on, other than what follows from the above.
Results may differ from a plain program's by a relative error of at most 0.0003.
Values sent between devices are 32-bit elements; how exact they have to be, the bound alone decides.
No kernel may reach another device: no remote copies, remote signals or barrier semaphores. Data moves between devices by JAX's collectives and lax.ppermute only.
A program may use at most 128 MiB of HBM per device.

v0:
```python
import functools
import math

import jax
import jax.numpy as jnp
import numpy as np
from jax import lax
from jax.experimental import pallas as pl
from jax.experimental.pallas import tpu as pltpu
from jax.sharding import PartitionSpec as P

RADIUS = 6
BLOCK = 8
HALF = 0.5

ROWS = 8
LANES = 128
STRIP = 8
SLOTS = LANES // STRIP
VMEM_LIMIT = 24 * 1024 * 1024

VMEM = pl.BlockSpec(memory_space=pltpu.VMEM)
SMEM = pl.BlockSpec(memory_space=pltpu.SMEM)


def params():
    return pltpu.CompilerParams(vmem_limit_bytes=VMEM_LIMIT)


def f32(*shape):
    return jax.ShapeDtypeStruct(shape, jnp.float32)


def exchange(to_lower, to_upper, axis):
    count = lax.axis_size(axis)
    zero = jnp.zeros_like(to_lower)
    if count == 1:
        return zero, zero
    odd = lax.axis_index(axis) % 2 == 1
    even_pairs = [(i, i + 1) for i in range(0, count - 1, 2)]
    odd_pairs = [(i, i + 1) for i in range(1, count - 1, 2)]

    def swap(value, pairs):
        return lax.ppermute(value, axis, pairs + [(b, a) for a, b in pairs])

    first = swap(jnp.where(odd, to_lower, to_upper), even_pairs)
    second = swap(jnp.where(odd, to_upper, to_lower), odd_pairs) if odd_pairs else zero
    return jnp.where(odd, first, second), jnp.where(odd, second, first)


def z_faces_kernel(e_low, e_high, h_high, low_ref, high_ref):
    low_ref[0] = e_low[0, 0]
    low_ref[1] = e_low[1, 0]
    low_ref[2] = jnp.zeros_like(e_low[0, 0])
    ez = e_high[2, 0]
    high_ref[0] = h_high[0, 0] + HALF * ez - HALF * e_high[1, 0]
    high_ref[1] = h_high[1, 0] + HALF * e_high[0, 0] - HALF * ez
    high_ref[2] = ez


def z_faces(efield, hfield):
    _, cells_z, cells_x, cells_y = efield.shape
    block = (3, 1, cells_x, cells_y)
    face = f32(3, cells_x, cells_y)
    whole = pl.BlockSpec((3, cells_x, cells_y), lambda i: (0, 0, 0))
    return pl.pallas_call(
        z_faces_kernel,
        grid=(1,),
        in_specs=[
            pl.BlockSpec(block, lambda i: (0, 0, 0, 0)),
            pl.BlockSpec(block, lambda i: (0, cells_z - 1, 0, 0)),
            pl.BlockSpec(block, lambda i: (0, cells_z - 1, 0, 0)),
        ],
        out_specs=[whole, whole],
        out_shape=[face, face],
        compiler_params=params(),
    )(efield, efield, hfield)


def x_faces_kernel(e_ref, h_ref, below_ref, above_ref, low_ref, high_ref, rows_ref):
    cells_z = e_ref.shape[1]
    last = ROWS - 1
    low_ref[...] = jnp.zeros_like(low_ref)
    for z in range(cells_z):
        low_ref[z : z + 1, :] = e_ref[1, z, 0:1, :]
        low_ref[cells_z + z : cells_z + z + 1, :] = e_ref[2, z, 0:1, :]
        for c in range(3):
            rows_ref[c, z : z + 1, :] = e_ref[c, z, last : last + 1, :]
        for c in range(2):
            rows_ref[3 + c, z : z + 1, :] = h_ref[1 + c, z, last : last + 1, :]
        if z > 0:
            rows_ref[5, z - 1 : z, :] = e_ref[0, z, last : last + 1, :]
    rows_ref[5, cells_z - 1 : cells_z, :] = above_ref[0, last : last + 1, :]
    low_ref[2 * cells_z : 2 * cells_z + 1, :] = below_ref[2, 0:1, :]
    ex = rows_ref[0]
    high_ref[0:cells_z, :] = rows_ref[3] - HALF * (rows_ref[5] - ex + rows_ref[2])
    high_ref[cells_z : 2 * cells_z, :] = rows_ref[4] + HALF * rows_ref[1] - HALF * ex
    high_ref[2 * cells_z : 3 * cells_z, :] = ex


def x_faces(efield, hfield, below, above):
    cells_z, cells_y = efield.shape[1], efield.shape[3]
    face = f32(3 * cells_z, cells_y)
    return pl.pallas_call(
        x_faces_kernel,
        in_specs=[VMEM] * 4,
        out_specs=[VMEM] * 2,
        out_shape=[face, face],
        scratch_shapes=[pltpu.VMEM((6, cells_z, cells_y), jnp.float32)],
        compiler_params=params(),
    )(efield, hfield, below, above)


def lane_group():
    return lax.broadcasted_iota(jnp.int32, (ROWS, LANES), 1) // STRIP


def pack_strips(tiles, low_ref, high_ref, first):
    group = lane_group()
    width = tiles[0][1]
    for start in range(0, len(tiles), SLOTS):
        low = jnp.zeros((ROWS, LANES), jnp.float32)
        high = jnp.zeros((ROWS, LANES), jnp.float32)
        for k, (load, _) in enumerate(tiles[start : start + SLOTS]):
            if load is None:
                continue
            here = group == k
            shift = (STRIP * k) % LANES
            left = load(slice(0, LANES))
            right = load(slice(width - LANES, width))
            low = jnp.where(here, pltpu.roll(left, shift, 1) if shift else left, low)
            shift = (STRIP * k + STRIP) % LANES
            high = jnp.where(here, pltpu.roll(right, shift, 1) if shift else right, high)
        low_ref[first + start // SLOTS] = low
        high_ref[first + start // SLOTS] = high


def y_own_kernel(e_ref, h_ref, f_ref, mat_ref, grad_ref, mask_ref, place_ref, low_ref, high_ref, wide_ref):
    cells_z, width = e_ref.shape[1], e_ref.shape[3]
    layers = grad_ref.shape[0]
    blocks = mask_ref.shape[1]
    spread = (
        lax.broadcasted_iota(jnp.int32, (blocks, width), 0)
        == lax.broadcasted_iota(jnp.int32, (blocks, width), 1) // BLOCK
    ).astype(jnp.float32)
    mask = jnp.broadcast_to(mask_ref[...].astype(jnp.float32), (ROWS, blocks))
    wide_ref[...] = jnp.dot(mask, spread, preferred_element_type=jnp.float32)
    first = place_ref[1]
    tiles = []
    for z in range(cells_z):
        for ref in (e_ref, h_ref):
            for c in range(3):
                tiles.append((lambda s, r=ref, c=c, z=z: r[c, z, :, s], width))
    for layer in range(layers):
        for c in range(3):
            tiles.append((lambda s, c=c, l=layer: f_ref[c, first + l, :, s], width))
        tiles.append((lambda s, l=layer: mat_ref[first + l, :, s].astype(jnp.float32), width))
        tiles.append((lambda s, l=layer: grad_ref[l, :, s], width))
        tiles.append((lambda s: wide_ref[:, s], width) if layer % ROWS == 0 else (None, width))
    pack_strips(tiles, low_ref, high_ref, 0)


def y_halo_kernel(own_low, own_high, below_ref, above_ref, left_ref, right_ref, low_ref, high_ref):
    count = own_low.shape[0]
    width = below_ref.shape[2]
    low_ref[0:count] = own_low[...]
    high_ref[0:count] = own_high[...]
    pack_strips(halo_tiles(below_ref, above_ref, left_ref, right_ref, width), low_ref, high_ref, count)


def halo_tiles(below_ref, above_ref, left_ref, right_ref, width):
    tiles = []
    for c in range(3):
        tiles.append((lambda s, c=c: below_ref[c, :, s], width))
    for c in range(2):
        tiles.append((lambda s, c=c: above_ref[c, :, s], width))
    for ref in (left_ref, right_ref):
        for start in range(0, ref.shape[0], ROWS):
            tiles.append((lambda s, r=ref, t=start: r[t : t + ROWS, s], width))
    return tiles


def y_own(efield, hfield, forward, material, grad_sum, mask, place):
    cells_z, width = efield.shape[1], efield.shape[3]
    count = (cells_z * 6 + grad_sum.shape[0] * 6) // SLOTS
    packed = f32(count, ROWS, LANES)
    return pl.pallas_call(
        y_own_kernel,
        in_specs=[VMEM] * 6 + [SMEM],
        out_specs=[VMEM] * 3,
        out_shape=[packed, packed, f32(ROWS, width)],
        compiler_params=params(),
    )(efield, hfield, forward, material, grad_sum, mask, place)


def y_halo(own_low, own_high, below, above, left, right):
    extra = 5 + (left.shape[0] + right.shape[0]) // ROWS
    packed = f32(own_low.shape[0] + math.ceil(extra / SLOTS), ROWS, LANES)
    return pl.pallas_call(
        y_halo_kernel,
        in_specs=[VMEM] * 6,
        out_specs=[VMEM] * 2,
        out_shape=[packed, packed],
        compiler_params=params(),
    )(own_low, own_high, below, above, left, right)


def step_kernel(
    per_device,
    e_ref,
    h_ref,
    f_ref,
    mat_ref,
    grad_ref,
    mask_ref,
    below_ref,
    above_ref,
    left_ref,
    right_ref,
    ylow_ref,
    yhigh_ref,
    permit_ref,
    place_ref,
    e_out,
    h_out,
    grad_out,
    send_ref,
    left_wide,
    right_wide,
    grad_halo,
):
    _, cells_z, _, width = e_ref.shape
    layers = grad_ref.shape[0]
    mats = permit_ref.shape[0]
    wide = width + LANES
    lane = lax.broadcasted_iota(jnp.int32, (ROWS, LANES), 1)
    row = lax.broadcasted_iota(jnp.int32, (ROWS, wide), 0)
    per_group = 6 * ROWS // SLOTS
    groups = cells_z // ROWS
    grad_base = per_group * groups
    halo_base = grad_base + per_group * (layers // ROWS)
    me = place_ref[0]
    first_group = place_ref[1] // ROWS

    def halo(tile, k):
        right = yhigh_ref[tile]
        left = ylow_ref[tile]
        back = (LANES - STRIP * k) % LANES
        over = (LANES - STRIP - STRIP * k) % LANES
        return jnp.where(
            lane < STRIP,
            pltpu.roll(right, back, 1) if back else right,
            pltpu.roll(left, over, 1) if over else left,
        )

    def with_halo(own, tile, k):
        return jnp.concatenate([own, halo(tile, k)], axis=1)

    def static_slot(index):
        return halo_base + index // SLOTS, index % SLOTS

    def y_up(v):
        return pltpu.roll(v, wide - 1, 1)

    def y_down(v):
        return pltpu.roll(v, 1, 1)

    def x_up(v, line):
        return jnp.where(row == ROWS - 1, line, pltpu.roll(v, ROWS - 1, 0))

    def x_down(v, line):
        return jnp.where(row == 0, line, pltpu.roll(v, 1, 0))

    below = [with_halo(below_ref[c], *static_slot(c)) for c in range(3)]
    above = [with_halo(above_ref[c], *static_slot(3 + c)) for c in range(2)]
    slot = 5
    for source, target in ((left_ref, left_wide), (right_ref, right_wide)):
        for start in range(0, source.shape[0], ROWS):
            target[start : start + ROWS, :] = with_halo(source[start : start + ROWS, :], *static_slot(slot))
            slot += 1
    left_wide[cells_z : 2 * cells_z, :] += HALF * y_up(left_wide[2 * cells_z : 3 * cells_z, :])

    def field(ref, which, c, a, b):
        slot = 6 * b + 3 * which + c
        return with_halo(ref[c, ROWS * a + b], per_group * a + slot // SLOTS, slot % SLOTS)

    inverse = [1.0 / permit_ref[m] for m in range(mats)]

    ex0 = field(e_ref, 0, 0, 0, 0)
    ey0 = field(e_ref, 0, 1, 0, 0)
    low_line = jnp.broadcast_to(right_wide[2 * cells_z : 2 * cells_z + 1, :], (ROWS, wide))
    hx_z = below[0] - HALF * y_up(below[2]) + HALF * ey0
    hy_z = below[1] - HALF * ex0 + HALF * x_up(below[2], low_line)

    def group(a, carry):
        ex, ey, hx_z, hy_z = carry
        layer_group = a - first_group
        design = jnp.logical_and(layer_group >= 0, layer_group < layers // ROWS)
        safe_group = jnp.clip(layer_group, 0, layers // ROWS - 1)
        for b in range(ROWS):
            z = ROWS * a + b

            def line(ref, base):
                return jnp.broadcast_to(ref[pl.ds(base + z, 1), :], (ROWS, wide))

            ez = field(e_ref, 0, 2, a, b)
            if b < ROWS - 1:
                ex_next = field(e_ref, 0, 0, a, b + 1)
                ey_next = field(e_ref, 0, 1, a, b + 1)
            else:
                end = a == groups - 1
                after = jnp.minimum(a + 1, groups - 1)
                ex_next = jnp.where(end, above[0], field(e_ref, 0, 0, after, 0))
                ey_next = jnp.where(end, above[1], field(e_ref, 0, 1, after, 0))
            hx = field(h_ref, 1, 0, a, b) - HALF * (y_up(ez) - ez - ey_next + ey)
            hy = field(h_ref, 1, 1, a, b) - HALF * (
                ex_next - ex - x_up(ez, line(right_wide, cells_z)) + ez
            )
            hz = field(h_ref, 1, 2, a, b) - HALF * (x_up(ey, line(right_wide, 0)) - ey - y_up(ex) + ex)
            hy_x = x_down(hy, line(left_wide, 0) + HALF * ez)
            hz_x = x_down(hz, line(left_wide, cells_z) - HALF * ey)
            curl_x = (hz - y_down(hz)) - (hy - hy_z)
            curl_y = (hx - hx_z) - (hz - hz_x)
            curl_z = (hy - hy_x) - (hx - y_down(hx))

            grad_tile = grad_base + per_group * safe_group
            mat_halo = halo(grad_tile + (6 * b + 3) // SLOTS, (6 * b + 3) % SLOTS)
            mat = jnp.concatenate([mat_ref[z], mat_halo.astype(jnp.int32)], axis=1)
            inv = jnp.full((ROWS, wide), inverse[0])
            for m in range(1, mats):
                inv = jnp.where(mat == m, inverse[m], inv)
            half_inv = HALF * inv
            e_new = [
                ex + half_inv * curl_x,
                ey + half_inv * curl_y,
                ez + half_inv * curl_z,
            ]
            for c, (new_e, new_h) in enumerate(zip(e_new, (hx, hy, hz))):
                e_out[c, z] = new_e[:, :width]
                h_out[c, z] = new_h[:, :width]

            @pl.when(design)
            def _():
                layer = ROWS * safe_group + b
                total = None
                for c in range(3):
                    slot = 6 * b + c
                    fwd = with_halo(f_ref[c, z], grad_tile + slot // SLOTS, slot % SLOTS)
                    total = fwd * e_new[c] if total is None else total + fwd * e_new[c]
                slot = 6 * b + 4
                grad = with_halo(grad_ref[layer], grad_tile + slot // SLOTS, slot % SLOTS)
                mask = with_halo(mask_ref[...], grad_base, 5)
                grad = grad + mask * total
                grad_out[layer] = grad[:, :width]
                grad_halo[layer] = grad[:, width:]

            ex, ey, hx_z, hy_z = ex_next, ey_next, hx, hy
        return ex, ey, hx_z, hy_z

    lax.fori_loop(0, groups, group, (ex0, ey0, hx_z, hy_z))

    def pack(k, carry):
        chunk = lax.bitwise_xor(me, k)
        edge = jnp.zeros((ROWS, LANES), jnp.float32)
        for i in range(per_device):
            layer = chunk * per_device + i
            send_ref[k, :, i * width : (i + 1) * width] = grad_out[layer]
            side = grad_halo[layer]
            at = 2 * STRIP * i
            upper = pltpu.roll(side, at, 1) if at else side
            lower = pltpu.roll(side, (at + 2 * STRIP) % LANES, 1)
            edge = jnp.where(lane // STRIP == 2 * i, upper, edge)
            edge = jnp.where(lane // STRIP == 2 * i + 1, lower, edge)
        send_ref[k, :, per_device * width :] = edge
        return carry

    lax.fori_loop(0, send_ref.shape[0], pack, 0)


def step(efield, hfield, forward, material, grad_sum, mask, below, above, left, right, ylow, yhigh, permit, place, count):
    _, cells_z, _, width = efield.shape
    layers = grad_sum.shape[0]
    per_device = layers // count
    wide = width + LANES
    return pl.pallas_call(
        functools.partial(step_kernel, per_device),
        in_specs=[VMEM] * 12 + [SMEM] * 2,
        out_specs=[VMEM] * 4,
        out_shape=[
            f32(*efield.shape),
            f32(*efield.shape),
            f32(*grad_sum.shape),
            f32(count, ROWS, per_device * width + LANES),
        ],
        scratch_shapes=[
            pltpu.VMEM((left.shape[0], wide), jnp.float32),
            pltpu.VMEM((right.shape[0], wide), jnp.float32),
            pltpu.VMEM((layers, ROWS, LANES), jnp.float32),
        ],
        compiler_params=params(),
    )(efield, hfield, forward, material, grad_sum, mask, below, above, left, right, ylow, yhigh, permit, place)


def cone_matrix(rows):
    span = np.arange(-RADIUS, RADIUS + 1, dtype=np.float64)
    cone = np.maximum(RADIUS - np.sqrt(span[:, None] ** 2 + span[None, :] ** 2), 0.0)
    weight = cone / cone.sum()
    x = np.arange(rows)
    out = np.zeros((RADIUS + 1, rows, rows))
    for b in range(RADIUS + 1):
        for apart in (x[:, None] - x[None, :], 2 * rows - 1 - x[:, None] - x[None, :]):
            near = np.abs(apart) <= RADIUS
            out[b] += np.where(near, weight[np.clip(apart, -RADIUS, RADIUS) + RADIUS, RADIUS + b], 0.0)
    out = out.reshape((RADIUS + 1) * rows, rows).astype(np.float32)
    high = out.astype(jnp.bfloat16)
    low = (out - high.astype(np.float32)).astype(jnp.bfloat16)
    return np.concatenate([high, low, high], axis=1)


def flip_rows(v):
    row = lax.broadcasted_iota(jnp.int32, v.shape, 0)
    v = pltpu.roll(v, 4, 0)
    v = jnp.where(row % 4 < 2, pltpu.roll(v, ROWS - 2, 0), pltpu.roll(v, 2, 0))
    return jnp.where(row % 2 < 1, pltpu.roll(v, ROWS - 1, 0), pltpu.roll(v, 1, 0))


def filter_kernel(count, per_device, width, *refs):
    taps_ref, place_ref = refs[0], refs[1]
    got = refs[2 : 2 + count]
    outs = refs[2 + count : 2 + 2 * count]
    slabs, parts, done = refs[2 + 2 * count :]
    me = place_ref[0]
    wide = width + LANES
    half = count // 2
    rows = half * ROWS
    lane = lax.broadcasted_iota(jnp.int32, (ROWS, LANES), 1)
    for k in range(count):
        slabs[lax.bitwise_xor(me, k)] = got[k][...]

    def layer_of(slab, i):
        edge = slabs[slab, :, per_device * width :]
        at = 2 * STRIP * i
        upper = pltpu.roll(edge, (LANES - at) % LANES, 1) if at else edge
        lower = pltpu.roll(edge, (LANES - 2 * STRIP - at) % LANES, 1)
        side = jnp.where(lane < STRIP, upper, lower)
        return jnp.concatenate([slabs[slab, :, i * width : (i + 1) * width], side], axis=1)

    for i in range(per_device):
        halves = [layer_of(s, i) + flip_rows(layer_of(count - 1 - s, i)) for s in range(half)]
        symmetric = jnp.concatenate(halves, axis=0)
        high = symmetric.astype(jnp.bfloat16)
        low = (symmetric - high.astype(jnp.float32)).astype(jnp.bfloat16)
        parts[0:rows, :] = high
        parts[rows : 2 * rows, :] = high
        parts[2 * rows : 3 * rows, :] = low
        mixed = jnp.dot(taps_ref[...], parts[...], preferred_element_type=jnp.float32)
        total = mixed[0:rows]
        for b in range(1, RADIUS + 1):
            part = mixed[b * rows : (b + 1) * rows]
            total = total + (pltpu.roll(part, b, 1) + pltpu.roll(part, wide - b, 1))
        for s in range(half):
            own = total[s * ROWS : (s + 1) * ROWS, :width]
            done[s, i] = own
            done[count - 1 - s, i] = flip_rows(own)
    for k in range(count):
        outs[k][...] = done[lax.bitwise_xor(me, k)]


def cone_filter(got, place, per_device, width):
    count = len(got)
    rows = count // 2 * ROWS
    taps = jnp.asarray(cone_matrix(rows))
    return pl.pallas_call(
        functools.partial(filter_kernel, count, per_device, width),
        in_specs=[VMEM, SMEM] + [VMEM] * count,
        out_specs=[VMEM] * count,
        out_shape=[f32(per_device, ROWS, width)] * count,
        scratch_shapes=[
            pltpu.VMEM((count, ROWS, per_device * width + LANES), jnp.float32),
            pltpu.VMEM((3 * rows, width + LANES), jnp.bfloat16),
            pltpu.VMEM((count, per_device, ROWS, width), jnp.float32),
        ],
        compiler_params=params(),
    )(taps, place, *got)


def place_kernel(count, per_device, place_ref, *refs):
    out = refs[count]
    me = place_ref[0]
    for k in range(count):
        out[pl.ds(lax.bitwise_xor(me, k) * per_device, per_device)] = refs[k][...]


def place_layers(parts, place):
    count = len(parts)
    per_device, rows, width = parts[0].shape
    return pl.pallas_call(
        functools.partial(place_kernel, count, per_device),
        in_specs=[SMEM] + [VMEM] * count,
        out_specs=VMEM,
        out_shape=f32(count * per_device, rows, width),
        compiler_params=params(),
    )(place, *parts)


def spread(parts):
    count = len(parts)
    return [parts[0]] + [
        lax.ppermute(parts[k], "gx", [(i, i ^ k) for i in range(count)]) for k in range(1, count)
    ]


def on_device(efield, hfield, forward, material, permittivity, design_mask, grad_sum):
    count = lax.axis_size("gx")
    cells_z, width = efield.shape[1], efield.shape[3]
    layers = grad_sum.shape[0]
    per_device = layers // count
    first = (cells_z - layers) * (1 - lax.axis_index("gz"))
    place = jnp.stack([lax.axis_index("gx"), first]).astype(jnp.int32)

    below, above = exchange(*z_faces(efield, hfield), "gz")
    left, right = exchange(*x_faces(efield, hfield, below, above), "gx")
    own_low, own_high, mask = y_own(efield, hfield, forward, material, grad_sum, design_mask, place)
    strips = y_halo(own_low, own_high, below, above, left, right)
    ylow, yhigh = exchange(*strips, "gy")
    e_next, h_next, grad_total, send = step(
        efield, hfield, forward, material, grad_sum, mask, below, above, left, right, ylow, yhigh, permittivity, place, count
    )
    got = spread([send[k] for k in range(count)])
    filtered = spread(cone_filter(got, place, per_device, width))
    return e_next, h_next, grad_total, place_layers(filtered, place)


def solution(mesh):
    field = P(None, "gz", "gx", "gy")
    cells = P("gz", "gx", "gy")
    return jax.shard_map(
        on_device,
        mesh=mesh,
        in_specs=(field, field, field, cells, P(), P("gx", "gy"), cells),
        out_specs=(field, field, cells, cells),
        check_vma=False,
    )
```

profile of v0, /device:TPU:0, one launch (start us, length us, event | category | flops | bytes accessed | tf_op | source)
XLA Modules:
  0.0 56.1 jit_solution(8105628911909371721)
XLA Ops:
  0.7 1.3 %copy-done = f32[3,24,8,512]{3,2,1,0:T(8,128)S(1)} copy-done((f32[3,24,8,512]{3,2,1,0:T(8,128)S(1)}, f32[3,24,8,512]{3,2,1,0:T(8,128)}, u32[]{:S(2)}) %copy-start) | copy-done | bytes 1179672
  1.9 1.3 %copy-done.2 = f32[3,24,8,512]{3,2,1,0:T(8,128)S(1)} copy-done((f32[3,24,8,512]{3,2,1,0:T(8,128)S(1)}, f32[3,24,8,512]{3,2,1,0:T(8,128)}, u32[]{:S(2)}) %copy-start.2) | copy-done | bytes 1179672
  3.2 3.0 %collective-permute-start = (f32[3,8,512]{2,1,0:T(8,128)S(1)}, f32[3,8,512]{2,1,0:T(8,128)S(1)}, u32[]{:S(2)}, u32[]{:S(2)}) collective-permute-start(f32[3,8,512]{2,1,0:T(8,128)S(1)} %broadcast_select_fusion.10), channel_id=1, source_target_pairs={{0,1},{1,0},{2,3},{3,2},{4,5},{5,4},{6,7},{7,6},{8,9},{9,8},{10,11... | collective-permute-start | bytes 147464 | tf_op jit(solution)/shard_map/ppermute | solution.py:44
  6.3 2.1 %collective-permute-done = f32[3,8,512]{2,1,0:T(8,128)S(1)} collective-permute-done((f32[3,8,512]{2,1,0:T(8,128)S(1)}, f32[3,8,512]{2,1,0:T(8,128)S(1)}, u32[]{:S(2)}, u32[]{:S(2)}) %collective-permute-start) | collective-permute-done | bytes 49184 | tf_op jit(solution)/shard_map/ppermute | solution.py:44
  8.3 0.0 copy-start.9
  8.3 0.0 copy-start.11
  8.4 0.0 copy-start.4
  8.4 0.0 copy-start.14
  8.4 0.1 shard_map.113
  8.5 0.4 copy-done.9
  9.0 0.0 copy-done.11
  9.0 0.7 %broadcast_select_fusion.2 = (f32[72,512]{1,0:T(8,128)}, f32[72,512]{1,0:T(8,128)}) fusion(f32[72,512]{1,0:T(8,128)S(1)} %get-tuple-element.25, f32[72,512]{1,0:T(8,128)S(1)} %get-tuple-element.24, pred[]{:T(512)S(6)} %eq.14), kind=kLoop, calls=%fused_computation.2 | loop fusion | flops 73728 | bytes 589825 | tf_op jit(solution)/shard_map/jit(_where)/select_n | solution.py:47
  9.7 1.3 %collective-permute-start.2 = (f32[72,512]{1,0:T(8,128)}, f32[72,512]{1,0:T(8,128)}, u32[]{:S(2)}, u32[]{:S(2)}) collective-permute-start(f32[72,512]{1,0:T(8,128)} %get-tuple-element.40), channel_id=1, source_target_pairs={{8,16},{16,8},{9,17},{17,9},{10,18},{18,10},{11,19},{19,11},{12,20... | collective-permute-start | bytes 442376 | tf_op jit(solution)/shard_map/ppermute | solution.py:44
  11.0 4.3 %collective-permute-start.1 = (f32[72,512]{1,0:T(8,128)}, f32[72,512]{1,0:T(8,128)}, u32[]{:S(2)}, u32[]{:S(2)}) collective-permute-start(f32[72,512]{1,0:T(8,128)} %get-tuple-element.41), channel_id=1, source_target_pairs={{0,8},{16,24},{8,0},{24,16},{1,9},{17,25},{9,1},{25,17},{2,10},{18... | collective-permute-start | bytes 442376 | tf_op jit(solution)/shard_map/ppermute | solution.py:44
  15.3 0.1 pad_add_fusion.place_ref.refs_1_
  15.4 0.0 copy-done.14
  15.4 1.0 %copy-done.5 = s32[24,8,512]{2,1,0:T(8,128)S(1)} copy-done((s32[24,8,512]{2,1,0:T(8,128)S(1)}, s32[24,8,512]{2,1,0:T(8,128)}, u32[]{:S(2)}) %copy-start.5) | copy-done | bytes 393240
  16.4 0.9 %copy-done.7 = f32[16,8,512]{2,1,0:T(8,128)S(1)} copy-done((f32[16,8,512]{2,1,0:T(8,128)S(1)}, f32[16,8,512]{2,1,0:T(8,128)}, u32[]{:S(2)}) %copy-start.7) | copy-done | bytes 262168
  17.4 1.0 %shard_map.111 = (f32[15,8,128]{2,1,0:T(8,128)S(1)}, f32[15,8,128]{2,1,0:T(8,128)S(1)}, f32[8,512]{1,0:T(8,128)S(1)}) custom-call(f32[3,24,8,512]{3,2,1,0:T(8,128)S(1)} %copy-done.1, f32[3,24,8,512]{3,2,1,0:T(8,128)S(1)} %copy-done.3, f32[3,24,8,512]{3,2,1,0:T(8,128)S(1)} %copy-done.4, s32[24,8,512]{2,1,0:T(8,128)S(1)} %copy-done.5, ...), custom_call_target="tpu_custom_call" | custom-call | tf_op jit(solution)/shard_map/pallas_call | solution.py:187
  18.4 0.0 copy-start.6
  18.4 0.0 copy-start.8
  18.4 0.0 copy-start.15
  18.5 0.0 collective-permute-done.2
  18.5 0.3 collective-permute-done.1
  18.8 1.0 %broadcast_select_fusion = (f32[72,512]{1,0:T(8,128)S(1)}, f32[72,512]{1,0:T(8,128)S(1)}) fusion(f32[72,512]{1,0:T(8,128)} %collective-permute-done.2, f32[72,512]{1,0:T(8,128)} %collective-permute-done.1, pred[]{:T(512)S(6)} %eq.14), kind=kLoop, calls=%fused_computation | loop fusion | flops 73728 | bytes 589825 | tf_op jit(solution)/shard_map/jit(_where)/select_n | solution.py:48
  19.8 0.0 copy-done.10
  19.8 0.0 copy-done.12
  19.8 0.1 shard_map.114
  19.9 0.7 %collective-permute-start.4 = (f32[17,8,128]{2,1,0:T(8,128)S(1)}, f32[17,8,128]{2,1,0:T(8,128)S(1)}, u32[]{:S(2)}, u32[]{:S(2)}) collective-permute-start(f32[17,8,128]{2,1,0:T(8,128)S(1)} %get-tuple-element.48), channel_id=1, source_target_pairs={{2,4},{4,2},{3,5},{5,3},{10,12},{12,10},{11,13},{13,11},{18,20},{2... | collective-permute-start | bytes 208904 | tf_op jit(solution)/shard_map/ppermute | solution.py:44
  20.6 2.9 %collective-permute-start.3 = (f32[17,8,128]{2,1,0:T(8,128)S(1)}, f32[17,8,128]{2,1,0:T(8,128)S(1)}, u32[]{:S(2)}, u32[]{:S(2)}) collective-permute-start(f32[17,8,128]{2,1,0:T(8,128)S(1)} %get-tuple-element.49), channel_id=1, source_target_pairs={{0,2},{4,6},{2,0},{6,4},{1,3},{5,7},{3,1},{7,5},{8,10},{12,14},{10... | collective-permute-start | bytes 208904 | tf_op jit(solution)/shard_map/ppermute | solution.py:44
  23.5 0.0 collective-permute-done.4
  23.5 0.9 %collective-permute-done.3 = f32[17,8,128]{2,1,0:T(8,128)S(1)} collective-permute-done((f32[17,8,128]{2,1,0:T(8,128)S(1)}, f32[17,8,128]{2,1,0:T(8,128)S(1)}, u32[]{:S(2)}, u32[]{:S(2)}) %collective-permute-start.3) | collective-permute-done | bytes 69664 | tf_op jit(solution)/shard_map/ppermute | solution.py:44
  24.5 0.0 copy-start.13
  24.5 9.0 %shard_map.115 = (f32[3,24,8,512]{3,2,1,0:T(8,128)}, f32[3,24,8,512]{3,2,1,0:T(8,128)}, f32[16,8,512]{2,1,0:T(8,128)}, f32[4,8,2176]{2,1,0:T(8,128)S(1)}) custom-call(f32[3,24,8,512]{3,2,1,0:T(8,128)S(1)} %copy-done.1, f32[3,24,8,512]{3,2,1,0:T(8,128)S(1)} %copy-done.3, f32[3,24,8,512]{3,2,1,0:T(8,128)S(1)} %copy-done.4, s32[24,8,512]{2,1,0:T(8,128)S(1)} %copy-done.6, ...), custom_call_target="tpu_custom_call" | custom-call | tf_op jit(solution)/shard_map/pallas_call | solution.py:385
  33.5 1.9 %collective-permute-start.7 = (f32[8,2176]{1,0:T(8,128)S(1)}, f32[8,2176]{1,0:T(8,128)S(1)}, u32[]{:S(2)}, u32[]{:S(2)}) collective-permute-start(f32[8,2176]{1,0:T(8,128)S(1)} %get-tuple-element.42), channel_id=1, source_target_pairs={{0,24},{8,16},{16,8},{24,0},{1,25},{9,17},{17,9},{25,1},{2,26},{10... | collective-permute-start | bytes 208904 | tf_op jit(solution)/shard_map/ppermute | solution.py:509
  35.4 1.7 %collective-permute-start.6 = (f32[8,2176]{1,0:T(8,128)S(1)}, f32[8,2176]{1,0:T(8,128)S(1)}, u32[]{:S(2)}, u32[]{:S(2)}) collective-permute-start(f32[8,2176]{1,0:T(8,128)S(1)} %get-tuple-element.43), channel_id=1, source_target_pairs={{0,16},{8,24},{16,0},{24,8},{1,17},{9,25},{17,1},{25,9},{2,18},{10... | collective-permute-start | bytes 208904 | tf_op jit(solution)/shard_map/ppermute | solution.py:509
  37.1 0.9 %collective-permute-start.5 = (f32[8,2176]{1,0:T(8,128)S(1)}, f32[8,2176]{1,0:T(8,128)S(1)}, u32[]{:S(2)}, u32[]{:S(2)}) collective-permute-start(f32[8,2176]{1,0:T(8,128)S(1)} %get-tuple-element.44), channel_id=1, source_target_pairs={{0,8},{8,0},{16,24},{24,16},{1,9},{9,1},{17,25},{25,17},{2,10},{10... | collective-permute-start | bytes 208904 | tf_op jit(solution)/shard_map/ppermute | solution.py:509
  38.0 2.6 %collective-permute-done.7.refs_5_ = f32[8,2176]{1,0:T(8,128)S(1)} collective-permute-done((f32[8,2176]{1,0:T(8,128)S(1)}, f32[8,2176]{1,0:T(8,128)S(1)}, u32[]{:S(2)}, u32[]{:S(2)}) %collective-permute-start.7) | collective-permute-done | bytes 69664 | tf_op jit(solution)/shard_map/ppermute | solution.py:509
  40.6 4.0 %collective-permute-done.6.refs_4_ = f32[8,2176]{1,0:T(8,128)S(1)} collective-permute-done((f32[8,2176]{1,0:T(8,128)S(1)}, f32[8,2176]{1,0:T(8,128)S(1)}, u32[]{:S(2)}, u32[]{:S(2)}) %collective-permute-start.6) | collective-permute-done | bytes 69664 | tf_op jit(solution)/shard_map/ppermute | solution.py:509
  44.5 0.0 collective-permute-done.5.refs_3_
  44.6 1.6 %shard_map.116 = (f32[4,8,512]{2,1,0:T(8,128)S(1)}, f32[4,8,512]{2,1,0:T(8,128)S(1)}, f32[4,8,512]{2,1,0:T(8,128)S(1)}, f32[4,8,512]{2,1,0:T(8,128)S(1)}) custom-call(bf16[112,48]{1,0:T(8,128)(2,1)S(1)} %copy-done.13, s32[2]{0:T(128)S(1)} %pad_add_fusion.place_ref.refs_1_, f32[8,2176]{1,0:T(8,128)S(1)} %get-tuple-element.45.refs_2_, ...), custom_call_target="tpu_custom_call" | custom-call | tf_op jit(solution)/shard_map/pallas_call | solution.py:473
  46.2 0.1 collective-permute-start.8
  46.3 1.9 %collective-permute-start.9 = (f32[4,8,512]{2,1,0:T(8,128)S(1)}, f32[4,8,512]{2,1,0:T(8,128)S(1)}, u32[]{:S(2)}, u32[]{:S(2)}) collective-permute-start(f32[4,8,512]{2,1,0:T(8,128)S(1)} %get-tuple-element.36), channel_id=1, source_target_pairs={{0,16},{8,24},{16,0},{24,8},{1,17},{9,25},{17,1},{25,9},{2,18},{10... | collective-permute-start | bytes 196616 | tf_op jit(solution)/shard_map/ppermute | solution.py:509
  48.2 2.5 %collective-permute-start.10 = (f32[4,8,512]{2,1,0:T(8,128)S(1)}, f32[4,8,512]{2,1,0:T(8,128)S(1)}, u32[]{:S(2)}, u32[]{:S(2)}) collective-permute-start(f32[4,8,512]{2,1,0:T(8,128)S(1)} %get-tuple-element.37), channel_id=1, source_target_pairs={{0,24},{8,16},{16,8},{24,0},{1,25},{9,17},{17,9},{25,1},{2,26},{10... | collective-permute-start | bytes 196616 | tf_op jit(solution)/shard_map/ppermute | solution.py:509
  50.6 0.8 %collective-permute-done.8.refs_1_ = f32[4,8,512]{2,1,0:T(8,128)S(1)} collective-permute-done((f32[4,8,512]{2,1,0:T(8,128)S(1)}, f32[4,8,512]{2,1,0:T(8,128)S(1)}, u32[]{:S(2)}, u32[]{:S(2)}) %collective-permute-start.8) | collective-permute-done | bytes 65568 | tf_op jit(solution)/shard_map/ppermute | solution.py:509
  51.4 3.4 %collective-permute-done.9.refs_2_ = f32[4,8,512]{2,1,0:T(8,128)S(1)} collective-permute-done((f32[4,8,512]{2,1,0:T(8,128)S(1)}, f32[4,8,512]{2,1,0:T(8,128)S(1)}, u32[]{:S(2)}, u32[]{:S(2)}) %collective-permute-start.9) | collective-permute-done | bytes 65568 | tf_op jit(solution)/shard_map/ppermute | solution.py:509
  54.9 0.0 collective-permute-done.10.refs_3_
  54.9 1.3 %shard_map.117 = f32[16,8,512]{2,1,0:T(8,128)} custom-call(s32[2]{0:T(128)S(1)} %pad_add_fusion.place_ref.refs_1_, f32[4,8,512]{2,1,0:T(8,128)S(1)} %get-tuple-element.34.refs_0_, f32[4,8,512]{2,1,0:T(8,128)S(1)} %collective-permute-done.8.refs_1_, f32[4,8,512]{2,1,0:T(8,128)S(1)} %collective-permute-done.9.refs_2_, ...), custom_call_target="tpu_custom_call" | custom-call | tf_op jit(solution)/shard_map/pallas_call | solution.py:497
  (21 shorter events, 0.1 us)
Async XLA Ops:
  0.6 1.3 %copy-start = (f32[3,24,8,512]{3,2,1,0:T(8,128)S(1)}, f32[3,24,8,512]{3,2,1,0:T(8,128)}, u32[]{:S(2)}) copy-start(f32[3,24,8,512]{3,2,1,0:T(8,128)} %e_ref.5) | copy-start | bytes 3538948
  1.9 1.3 %copy-start.2 = (f32[3,24,8,512]{3,2,1,0:T(8,128)S(1)}, f32[3,24,8,512]{3,2,1,0:T(8,128)}, u32[]{:S(2)}) copy-start(f32[3,24,8,512]{3,2,1,0:T(8,128)} %h_ref.5) | copy-start | bytes 3538948
  3.2 5.2 %copy-start.1 = (f32[3,24,8,512]{3,2,1,0:T(8,128)S(1)}, f32[3,24,8,512]{3,2,1,0:T(8,128)}, u32[]{:S(2)}) copy-start(f32[3,24,8,512]{3,2,1,0:T(8,128)} %e_ref.5) | copy-start | bytes 3538948
  3.2 5.2 %copy-start.3 = (f32[3,24,8,512]{3,2,1,0:T(8,128)S(1)}, f32[3,24,8,512]{3,2,1,0:T(8,128)}, u32[]{:S(2)}) copy-start(f32[3,24,8,512]{3,2,1,0:T(8,128)} %h_ref.5) | copy-start | bytes 3538948
  3.2 5.1 %collective-permute-start = (f32[3,8,512]{2,1,0:T(8,128)S(1)}, f32[3,8,512]{2,1,0:T(8,128)S(1)}, u32[]{:S(2)}, u32[]{:S(2)}) collective-permute-start(f32[3,8,512]{2,1,0:T(8,128)S(1)} %broadcast_select_fusion.10), channel_id=1, source_target_pairs={{0,1},{1,0},{2,3},{3,2},{4,5},{5,4},{6,7},{7,6},{8,9},{9,8},{10,11... | collective-permute-start | bytes 147464 | tf_op jit(solution)/shard_map/ppermute | solution.py:44
  8.3 0.6 %copy-start.9 = (f32[3,8,512]{2,1,0:T(8,128)}, f32[3,8,512]{2,1,0:T(8,128)S(1)}, u32[]{:S(2)}) copy-start(f32[3,8,512]{2,1,0:T(8,128)S(1)} %get-tuple-element.50.above_ref) | copy-start | bytes 147460
  8.3 0.6 %copy-start.11 = (f32[3,8,512]{2,1,0:T(8,128)}, f32[3,8,512]{2,1,0:T(8,128)S(1)}, u32[]{:S(2)}) copy-start(f32[3,8,512]{2,1,0:T(8,128)S(1)} %get-tuple-element.51.below_ref) | copy-start | bytes 147460
  8.4 7.0 %copy-start.4 = (f32[3,24,8,512]{3,2,1,0:T(8,128)S(1)}, f32[3,24,8,512]{3,2,1,0:T(8,128)}, u32[]{:S(2)}) copy-start(f32[3,24,8,512]{3,2,1,0:T(8,128)} %f_ref.3) | copy-start | bytes 3538948
  8.4 7.0 %copy-start.14 = (s32[1,64]{1,0:T(1,128)S(1)}, s32[1,64]{1,0:T(1,128)}, u32[]{:S(2)}) copy-start(s32[1,64]{1,0:T(1,128)} %mask_ref.1) | copy-start | bytes 772
  9.7 8.8 %collective-permute-start.2 = (f32[72,512]{1,0:T(8,128)}, f32[72,512]{1,0:T(8,128)}, u32[]{:S(2)}, u32[]{:S(2)}) collective-permute-start(f32[72,512]{1,0:T(8,128)} %get-tuple-element.40), channel_id=1, source_target_pairs={{8,16},{16,8},{9,17},{17,9},{10,18},{18,10},{11,19},{19,11},{12,20... | collective-permute-start | bytes 442376 | tf_op jit(solution)/shard_map/ppermute | solution.py:44
  11.0 7.8 %collective-permute-start.1 = (f32[72,512]{1,0:T(8,128)}, f32[72,512]{1,0:T(8,128)}, u32[]{:S(2)}, u32[]{:S(2)}) collective-permute-start(f32[72,512]{1,0:T(8,128)} %get-tuple-element.41), channel_id=1, source_target_pairs={{0,8},{16,24},{8,0},{24,16},{1,9},{17,25},{9,1},{25,17},{2,10},{18... | collective-permute-start | bytes 442376 | tf_op jit(solution)/shard_map/ppermute | solution.py:44
  15.4 1.0 %copy-start.5 = (s32[24,8,512]{2,1,0:T(8,128)S(1)}, s32[24,8,512]{2,1,0:T(8,128)}, u32[]{:S(2)}) copy-start(s32[24,8,512]{2,1,0:T(8,128)} %mat_ref.3) | copy-start | bytes 1179652
  16.4 0.9 %copy-start.7 = (f32[16,8,512]{2,1,0:T(8,128)S(1)}, f32[16,8,512]{2,1,0:T(8,128)}, u32[]{:S(2)}) copy-start(f32[16,8,512]{2,1,0:T(8,128)} %grad_ref.3) | copy-start | bytes 786436
  17.4 2.4 %copy-start.10 = (f32[3,8,512]{2,1,0:T(8,128)S(1)}, f32[3,8,512]{2,1,0:T(8,128)}, u32[]{:S(2)}) copy-start(f32[3,8,512]{2,1,0:T(8,128)} %copy-done.9) | copy-start | bytes 147460
  17.4 2.4 %copy-start.12 = (f32[3,8,512]{2,1,0:T(8,128)S(1)}, f32[3,8,512]{2,1,0:T(8,128)}, u32[]{:S(2)}) copy-start(f32[3,8,512]{2,1,0:T(8,128)} %copy-done.11) | copy-start | bytes 147460
  18.4 6.0 %copy-start.6 = (s32[24,8,512]{2,1,0:T(8,128)S(1)}, s32[24,8,512]{2,1,0:T(8,128)}, u32[]{:S(2)}) copy-start(s32[24,8,512]{2,1,0:T(8,128)} %mat_ref.3) | copy-start | bytes 1179652
  18.4 6.0 %copy-start.8 = (f32[16,8,512]{2,1,0:T(8,128)S(1)}, f32[16,8,512]{2,1,0:T(8,128)}, u32[]{:S(2)}) copy-start(f32[16,8,512]{2,1,0:T(8,128)} %grad_ref.3) | copy-start | bytes 786436
  18.4 6.0 %copy-start.15 = (f32[4]{0:T(128)S(1)}, f32[4]{0:T(128)}, u32[]{:S(2)}) copy-start(f32[4]{0:T(128)} %permit_ref.1) | copy-start | bytes 52
  19.9 3.6 %collective-permute-start.4 = (f32[17,8,128]{2,1,0:T(8,128)S(1)}, f32[17,8,128]{2,1,0:T(8,128)S(1)}, u32[]{:S(2)}, u32[]{:S(2)}) collective-permute-start(f32[17,8,128]{2,1,0:T(8,128)S(1)} %get-tuple-element.48), channel_id=1, source_target_pairs={{2,4},{4,2},{3,5},{5,3},{10,12},{12,10},{11,13},{13,11},{18,20},{2... | collective-permute-start | bytes 208904 | tf_op jit(solution)/shard_map/ppermute | solution.py:44
  20.6 3.8 %collective-permute-start.3 = (f32[17,8,128]{2,1,0:T(8,128)S(1)}, f32[17,8,128]{2,1,0:T(8,128)S(1)}, u32[]{:S(2)}, u32[]{:S(2)}) collective-permute-start(f32[17,8,128]{2,1,0:T(8,128)S(1)} %get-tuple-element.49), channel_id=1, source_target_pairs={{0,2},{4,6},{2,0},{6,4},{1,3},{5,7},{3,1},{7,5},{8,10},{12,14},{10... | collective-permute-start | bytes 208904 | tf_op jit(solution)/shard_map/ppermute | solution.py:44
  24.5 20.1 %copy-start.13 = (bf16[112,48]{1,0:T(8,128)(2,1)S(1)}, bf16[112,48]{1,0:T(8,128)(2,1)}, u32[]{:S(2)}) copy-start(bf16[112,48]{1,0:T(8,128)(2,1)} %constant.39.clone.refs_0_) | copy-start | bytes 32260
  33.5 7.0 %collective-permute-start.7 = (f32[8,2176]{1,0:T(8,128)S(1)}, f32[8,2176]{1,0:T(8,128)S(1)}, u32[]{:S(2)}, u32[]{:S(2)}) collective-permute-start(f32[8,2176]{1,0:T(8,128)S(1)} %get-tuple-element.42), channel_id=1, source_target_pairs={{0,24},{8,16},{16,8},{24,0},{1,25},{9,17},{17,9},{25,1},{2,26},{10... | collective-permute-start | bytes 208904 | tf_op jit(solution)/shard_map/ppermute | solution.py:509
  35.4 9.1 %collective-permute-start.6 = (f32[8,2176]{1,0:T(8,128)S(1)}, f32[8,2176]{1,0:T(8,128)S(1)}, u32[]{:S(2)}, u32[]{:S(2)}) collective-permute-start(f32[8,2176]{1,0:T(8,128)S(1)} %get-tuple-element.43), channel_id=1, source_target_pairs={{0,16},{8,24},{16,0},{24,8},{1,17},{9,25},{17,1},{25,9},{2,18},{10... | collective-permute-start | bytes 208904 | tf_op jit(solution)/shard_map/ppermute | solution.py:509
  37.1 7.5 %collective-permute-start.5 = (f32[8,2176]{1,0:T(8,128)S(1)}, f32[8,2176]{1,0:T(8,128)S(1)}, u32[]{:S(2)}, u32[]{:S(2)}) collective-permute-start(f32[8,2176]{1,0:T(8,128)S(1)} %get-tuple-element.44), channel_id=1, source_target_pairs={{0,8},{8,0},{16,24},{24,16},{1,9},{9,1},{17,25},{25,17},{2,10},{10... | collective-permute-start | bytes 208904 | tf_op jit(solution)/shard_map/ppermute | solution.py:509
  46.2 5.2 %collective-permute-start.8 = (f32[4,8,512]{2,1,0:T(8,128)S(1)}, f32[4,8,512]{2,1,0:T(8,128)S(1)}, u32[]{:S(2)}, u32[]{:S(2)}) collective-permute-start(f32[4,8,512]{2,1,0:T(8,128)S(1)} %get-tuple-element.35), channel_id=1, source_target_pairs={{0,8},{8,0},{16,24},{24,16},{1,9},{9,1},{17,25},{25,17},{2,10},{10... | collective-permute-start | bytes 196616 | tf_op jit(solution)/shard_map/ppermute | solution.py:509
  46.3 8.6 %collective-permute-start.9 = (f32[4,8,512]{2,1,0:T(8,128)S(1)}, f32[4,8,512]{2,1,0:T(8,128)S(1)}, u32[]{:S(2)}, u32[]{:S(2)}) collective-permute-start(f32[4,8,512]{2,1,0:T(8,128)S(1)} %get-tuple-element.36), channel_id=1, source_target_pairs={{0,16},{8,24},{16,0},{24,8},{1,17},{9,25},{17,1},{25,9},{2,18},{10... | collective-permute-start | bytes 196616 | tf_op jit(solution)/shard_map/ppermute | solution.py:509
  48.2 6.7 %collective-permute-start.10 = (f32[4,8,512]{2,1,0:T(8,128)S(1)}, f32[4,8,512]{2,1,0:T(8,128)S(1)}, u32[]{:S(2)}, u32[]{:S(2)}) collective-permute-start(f32[4,8,512]{2,1,0:T(8,128)S(1)} %get-tuple-element.37), channel_id=1, source_target_pairs={{0,24},{8,16},{16,8},{24,0},{1,25},{9,17},{17,9},{25,1},{2,26},{10... | collective-permute-start | bytes 196616 | tf_op jit(solution)/shard_map/ppermute | solution.py:509
where the time goes:
time: 56.4 us; the launch traced here: 56.1 us
  starting transfers between devices  21.1 us (37%)
  waiting for transfers between devices  14.1 us (25%)
  Pallas kernels  13.2 us (23%)
  local copies, waits for them, and re-layouts  5 us (9%)
  other arithmetic  1.86 us (3%)
  between operations  0.87 us (2%)
    ppermute x5, starting transfers between devices, swap(): return lax.ppermute(value, axis, pairs + [(b, a) for a, b in pairs])  12.2 us
    ppermute x6, waiting for transfers between devices, spread(): lax.ppermute(parts[k], 'gx', [(i, i ^ k) for i in range(count)])  10.8 us
    pallas_call x1, Pallas kernels, step(): pl.pallas_call(functools.partial(step_kernel, per_device), in_specs=[VMEM...  9.01 us
    ppermute x6, starting transfers between devices, spread(): lax.ppermute(parts[k], 'gx', [(i, i ^ k) for i in range(count)])  8.9 us
    unnamed x32, local copies, waits for them, and re-layouts  4.98 us
    ppermute x5, waiting for transfers between devices, swap(): return lax.ppermute(value, axis, pairs + [(b, a) for a, b in pairs])  3.28 us
    pallas_call x1, Pallas kernels, cone_filter(): pl.pallas_call(functools.partial(filter_kernel, count, per_device, width)...  1.63 us
    pallas_call x1, Pallas kernels, place_layers(): pl.pallas_call(functools.partial(place_kernel, count, per_device), in_spe...  1.26 us
  transfers between devices with their start and end apart: 11, of which 7 were waited for; matrix products, arithmetic and copies ran while one was open for 0% of the time, Pallas kernels for 2%

commit v1 on v0

v1 whole, which is shorter than its diff:
```python
import functools
import math

import jax
import jax.numpy as jnp
import numpy as np
from jax import lax
from jax.experimental import pallas as pl
from jax.experimental.pallas import tpu as pltpu
from jax.sharding import PartitionSpec as P

RADIUS = 6
BLOCK = 8
HALF = 0.5

ROWS = 8
LANES = 128
STRIP = 8
SLOTS = LANES // STRIP
VMEM_LIMIT = 24 * 1024 * 1024

VMEM = pl.BlockSpec(memory_space=pltpu.VMEM)
SMEM = pl.BlockSpec(memory_space=pltpu.SMEM)
HBM = pl.BlockSpec(memory_space=pltpu.HBM)
ANY = pl.BlockSpec(memory_space=pl.ANY)


def params():
    return pltpu.CompilerParams(vmem_limit_bytes=VMEM_LIMIT)


def f32(*shape):
    return jax.ShapeDtypeStruct(shape, jnp.float32)


GX, GY, GZ, FIRST = range(4)


def swap_pairs(value, axis, pairs):
    return lax.ppermute(value, axis, pairs + [(b, a) for a, b in pairs])


def exchange(first, second, axis, wrap=False):
    count = lax.axis_size(axis)
    if count == 1:
        return first, second
    got_first = swap_pairs(first, axis, [(i, i + 1) for i in range(0, count - 1, 2)])
    odd_pairs = [(i, i + 1) for i in range(1, count - 1, 2)]
    if not odd_pairs:
        return got_first, got_first
    if wrap and count % 2 == 0:
        odd_pairs.append((0, count - 1))
    return got_first, swap_pairs(second, axis, odd_pairs)


class Side:
    def __init__(self, index, count):
        self.odd = index % 2 == 1
        self.bottom = index == 0
        self.top = index == count - 1

    def sends(self, low, high):
        return jnp.where(self.odd, low, high), jnp.where(self.odd, high, low)

    def lower(self, first, second):
        return jnp.where(self.bottom, 0.0, jnp.where(self.odd, first, second))

    def upper(self, first, second):
        return jnp.where(self.top, 0.0, jnp.where(self.odd, second, first))


def z_faces_kernel(count, place_ref, e_ref, h_ref, first_ref, second_ref, e_low, e_high, h_high, sems):
    last = e_ref.shape[1] - 1
    copies = [
        pltpu.make_async_copy(e_ref.at[:, 0], e_low, sems.at[0]),
        pltpu.make_async_copy(e_ref.at[:, last], e_high, sems.at[1]),
        pltpu.make_async_copy(h_ref.at[:, last], h_high, sems.at[2]),
    ]
    for copy in copies:
        copy.start()
    for copy in copies:
        copy.wait()
    side = Side(place_ref[GZ], count)
    ez = e_high[2]
    lows = (e_low[0], e_low[1], jnp.zeros_like(ez))
    highs = (
        h_high[0] + HALF * ez - HALF * e_high[1],
        h_high[1] + HALF * e_high[0] - HALF * ez,
        ez,
    )
    for c in range(3):
        first_ref[c], second_ref[c] = side.sends(lows[c], highs[c])


def z_faces(efield, hfield, place):
    _, _, cells_x, cells_y = efield.shape
    face = f32(3, cells_x, cells_y)
    scratch = pltpu.VMEM(face.shape, jnp.float32)
    return pl.pallas_call(
        functools.partial(z_faces_kernel, lax.axis_size("gz")),
        in_specs=[SMEM, HBM, HBM],
        out_specs=[VMEM] * 2,
        out_shape=[face, face],
        scratch_shapes=[scratch] * 3 + [pltpu.SemaphoreType.DMA((3,))],
        compiler_params=params(),
    )(place, efield, hfield)


def x_faces_kernel(counts, place_ref, e_ref, h_ref, zfirst_ref, zsecond_ref, first_ref, second_ref, low_ref, rows_ref):
    cells_z = e_ref.shape[1]
    last = ROWS - 1
    z_side = Side(place_ref[GZ], counts[1])
    low_ref[...] = jnp.zeros_like(low_ref)
    for z in range(cells_z):
        low_ref[z : z + 1, :] = e_ref[1, z, 0:1, :]
        low_ref[cells_z + z : cells_z + z + 1, :] = e_ref[2, z, 0:1, :]
        for c in range(3):
            rows_ref[c, z : z + 1, :] = e_ref[c, z, last : last + 1, :]
        for c in range(2):
            rows_ref[3 + c, z : z + 1, :] = h_ref[1 + c, z, last : last + 1, :]
        if z > 0:
            rows_ref[5, z - 1 : z, :] = e_ref[0, z, last : last + 1, :]
    rows_ref[5, cells_z - 1 : cells_z, :] = z_side.upper(
        zfirst_ref[0, last : last + 1, :], zsecond_ref[0, last : last + 1, :]
    )
    low_ref[2 * cells_z : 2 * cells_z + 1, :] = z_side.lower(zfirst_ref[2, 0:1, :], zsecond_ref[2, 0:1, :])
    ex = rows_ref[0]
    high = (
        rows_ref[3] - HALF * (rows_ref[5] - ex + rows_ref[2]),
        rows_ref[4] + HALF * rows_ref[1] - HALF * ex,
        ex,
    )
    side = Side(place_ref[GX], counts[0])
    for c in range(3):
        here = slice(c * cells_z, (c + 1) * cells_z)
        first_ref[here, :], second_ref[here, :] = side.sends(low_ref[here, :], high[c])


def x_faces(efield, hfield, zfaces, place):
    cells_z, cells_y = efield.shape[1], efield.shape[3]
    face = f32(3 * cells_z, cells_y)
    return pl.pallas_call(
        functools.partial(x_faces_kernel, (lax.axis_size("gx"), lax.axis_size("gz"))),
        in_specs=[SMEM] + [VMEM] * 4,
        out_specs=[VMEM] * 2,
        out_shape=[face, face],
        scratch_shapes=[
            pltpu.VMEM(face.shape, jnp.float32),
            pltpu.VMEM((6, cells_z, cells_y), jnp.float32),
        ],
        compiler_params=params(),
    )(place, efield, hfield, *zfaces)


def lane_group():
    return lax.broadcasted_iota(jnp.int32, (ROWS, LANES), 1) // STRIP


def pack_strips(tiles, low_ref, high_ref, first):
    group = lane_group()
    width = tiles[0][1]
    for start in range(0, len(tiles), SLOTS):
        low = jnp.zeros((ROWS, LANES), jnp.float32)
        high = jnp.zeros((ROWS, LANES), jnp.float32)
        for k, (load, _) in enumerate(tiles[start : start + SLOTS]):
            if load is None:
                continue
            here = group == k
            shift = (STRIP * k) % LANES
            left = load(slice(0, LANES))
            right = load(slice(width - LANES, width))
            low = jnp.where(here, pltpu.roll(left, shift, 1) if shift else left, low)
            shift = (STRIP * k + STRIP) % LANES
            high = jnp.where(here, pltpu.roll(right, shift, 1) if shift else right, high)
        low_ref[first + start // SLOTS] = low
        high_ref[first + start // SLOTS] = high


def y_own_kernel(place_ref, e_ref, h_ref, f_ref, mat_ref, grad_ref, mask_ref, low_ref, high_ref, wide_ref):
    cells_z, width = e_ref.shape[1], e_ref.shape[3]
    layers = grad_ref.shape[0]
    blocks = mask_ref.shape[1]
    spread = (
        lax.broadcasted_iota(jnp.int32, (blocks, width), 0)
        == lax.broadcasted_iota(jnp.int32, (blocks, width), 1) // BLOCK
    ).astype(jnp.float32)
    mask = jnp.broadcast_to(mask_ref[...].astype(jnp.float32), (ROWS, blocks))
    wide_ref[...] = jnp.dot(mask, spread, preferred_element_type=jnp.float32)
    first = place_ref[FIRST]
    tiles = []
    for z in range(cells_z):
        for ref in (e_ref, h_ref):
            for c in range(3):
                tiles.append((lambda s, r=ref, c=c, z=z: r[c, z, :, s], width))
    for layer in range(layers):
        for c in range(3):
            tiles.append((lambda s, c=c, l=layer: f_ref[c, first + l, :, s], width))
        tiles.append((lambda s, l=layer: mat_ref[first + l, :, s].astype(jnp.float32), width))
        tiles.append((lambda s, l=layer: grad_ref[l, :, s], width))
        tiles.append((lambda s: wide_ref[:, s], width) if layer % ROWS == 0 else (None, width))
    pack_strips(tiles, low_ref, high_ref, 0)


def y_own(efield, hfield, forward, material, grad_sum, mask, place):
    cells_z, width = efield.shape[1], efield.shape[3]
    count = (cells_z * 6 + grad_sum.shape[0] * 6) // SLOTS
    packed = f32(count, ROWS, LANES)
    return pl.pallas_call(
        y_own_kernel,
        in_specs=[SMEM] + [VMEM] * 6,
        out_specs=[VMEM] * 3,
        out_shape=[packed, packed, f32(ROWS, width)],
        compiler_params=params(),
    )(place, efield, hfield, forward, material, grad_sum, mask)


def face_tiles(place_ref, counts, zfirst, zsecond, xfirst, xsecond):
    width = xfirst.shape[1]
    z_side = Side(place_ref[GZ], counts[2])
    x_side = Side(place_ref[GX], counts[0])
    tiles = []
    for c in range(3):
        tiles.append((lambda s, c=c: z_side.lower(zfirst[c, :, s], zsecond[c, :, s]), width))
    for c in range(2):
        tiles.append((lambda s, c=c: z_side.upper(zfirst[c, :, s], zsecond[c, :, s]), width))
    for pick in (x_side.lower, x_side.upper):
        for t in range(0, xfirst.shape[0], ROWS):
            tiles.append((lambda s, p=pick, t=t: p(xfirst[t : t + ROWS, s], xsecond[t : t + ROWS, s]), width))
    return tiles


def face_count(xface):
    return 5 + 2 * (xface.shape[0] // ROWS)


def y_faces_kernel(
    counts, place_ref, own_low, own_high, zfirst, zsecond, xfirst, xsecond, first_ref, second_ref, low_ref, high_ref
):
    count = own_low.shape[0]
    pack_strips(face_tiles(place_ref, counts, zfirst, zsecond, xfirst, xsecond), low_ref, high_ref, 0)
    side = Side(place_ref[GY], counts[1])
    first_ref[0:count], second_ref[0:count] = side.sends(own_low[...], own_high[...])
    first_ref[count:], second_ref[count:] = side.sends(low_ref[...], high_ref[...])


def y_faces(own_low, own_high, zfaces, xfaces, place):
    extra = math.ceil(face_count(xfaces[0]) / SLOTS)
    packed = f32(own_low.shape[0] + extra, ROWS, LANES)
    return pl.pallas_call(
        functools.partial(y_faces_kernel, axis_sizes()),
        in_specs=[SMEM] + [VMEM] * 6,
        out_specs=[VMEM] * 2,
        out_shape=[packed, packed],
        scratch_shapes=[pltpu.VMEM((extra, ROWS, LANES), jnp.float32)] * 2,
        compiler_params=params(),
    )(place, own_low, own_high, *zfaces, *xfaces)


def axis_sizes():
    return lax.axis_size("gx"), lax.axis_size("gy"), lax.axis_size("gz")


class Fields:
    def __init__(self, counts, layers, place_ref, e_ref, h_ref, faces, ybuf, left_wide, right_wide):
        self.e_ref, self.h_ref = e_ref, h_ref
        self.cells_z, self.width = e_ref.shape[1], e_ref.shape[3]
        self.wide = self.width + LANES
        self.lane = lax.broadcasted_iota(jnp.int32, (ROWS, LANES), 1)
        self.row = lax.broadcasted_iota(jnp.int32, (ROWS, self.wide), 0)
        self.per_group = 6 * ROWS // SLOTS
        self.groups = self.cells_z // ROWS
        self.grad_base = self.per_group * self.groups
        halo_base = self.grad_base + self.per_group * (layers // ROWS)
        zfirst, zsecond, xfirst, xsecond, yfirst, ysecond = faces
        y_side = Side(place_ref[GY], counts[1])
        ybuf[0] = y_side.lower(yfirst[...], ysecond[...])
        ybuf[1] = y_side.upper(yfirst[...], ysecond[...])
        self.ybuf = ybuf
        self.left_wide, self.right_wide = left_wide, right_wide

        tiles = face_tiles(place_ref, counts, zfirst, zsecond, xfirst, xsecond)
        whole = slice(0, self.width)
        full = [
            self.with_halo(load(whole), halo_base + t // SLOTS, t % SLOTS)
            for t, (load, _) in enumerate(tiles)
        ]
        self.below, self.above = full[:3], full[3:5]
        per_face = xfirst.shape[0] // ROWS
        for t in range(per_face):
            left_wide[t * ROWS : (t + 1) * ROWS, :] = full[5 + t]
            right_wide[t * ROWS : (t + 1) * ROWS, :] = full[5 + per_face + t]
        cells_z = self.cells_z
        left_wide[cells_z : 2 * cells_z, :] += HALF * self.y_up(left_wide[2 * cells_z : 3 * cells_z, :])

    def halo(self, tile, k):
        right = self.ybuf[1, tile]
        left = self.ybuf[0, tile]
        back = (LANES - STRIP * k) % LANES
        over = (LANES - STRIP - STRIP * k) % LANES
        return jnp.where(
            self.lane < STRIP,
            pltpu.roll(right, back, 1) if back else right,
            pltpu.roll(left, over, 1) if over else left,
        )

    def with_halo(self, own, tile, k):
        return jnp.concatenate([own, self.halo(tile, k)], axis=1)

    def y_up(self, v):
        return pltpu.roll(v, self.wide - 1, 1)

    def y_down(self, v):
        return pltpu.roll(v, 1, 1)

    def x_up(self, v, line):
        return jnp.where(self.row == ROWS - 1, line, pltpu.roll(v, ROWS - 1, 0))

    def x_down(self, v, line):
        return jnp.where(self.row == 0, line, pltpu.roll(v, 1, 0))

    def line(self, ref, at):
        return jnp.broadcast_to(ref[pl.ds(at, 1), :], (ROWS, self.wide))

    def field(self, which, c, a, b):
        slot = 6 * b + 3 * which + c
        ref = self.h_ref if which else self.e_ref
        return self.with_halo(ref[c, ROWS * a + b], self.per_group * a + slot // SLOTS, slot % SLOTS)

    def hx(self, a, b, ey, ez, ey_next):
        return self.field(1, 0, a, b) - HALF * (self.y_up(ez) - ez - ey_next + ey)

    def hy(self, a, b, ex, ez, ex_next):
        up = self.x_up(ez, self.line(self.right_wide, self.cells_z + ROWS * a + b))
        return self.field(1, 1, a, b) - HALF * (ex_next - ex - up + ez)

    def hz(self, a, b, ex, ey):
        up = self.x_up(ey, self.line(self.right_wide, ROWS * a + b))
        return self.field(1, 2, a, b) - HALF * (up - ey - self.y_up(ex) + ex)

    def start(self, a):
        ex, ey = self.field(0, 0, a, 0), self.field(0, 1, a, 0)
        below = self.below
        at_bottom = (
            below[0] - HALF * self.y_up(below[2]) + HALF * ey,
            below[1] - HALF * ex + HALF * self.x_up(below[2], self.line(self.right_wide, 2 * self.cells_z)),
        )
        before, b = jnp.maximum(a - 1, 0), ROWS - 1
        ex_before, ey_before, ez_before = (self.field(0, c, before, b) for c in range(3))
        inside = (
            self.hx(before, b, ey_before, ez_before, ey),
            self.hy(before, b, ex_before, ez_before, ex),
        )
        bottom = a == 0
        return (ex, ey) + tuple(jnp.where(bottom, one, two) for one, two in zip(at_bottom, inside))

    def group(self, a, carry, emit):
        ex, ey, hx_z, hy_z = carry
        for b in range(ROWS):
            z = ROWS * a + b
            ez = self.field(0, 2, a, b)
            if b < ROWS - 1:
                ex_next, ey_next = (self.field(0, c, a, b + 1) for c in range(2))
            else:
                end = a == self.groups - 1
                after = jnp.minimum(a + 1, self.groups - 1)
                ex_next, ey_next = (
                    jnp.where(end, self.above[c], self.field(0, c, after, 0)) for c in range(2)
                )
            hx = self.hx(a, b, ey, ez, ey_next)
            hy = self.hy(a, b, ex, ez, ex_next)
            hz = self.hz(a, b, ex, ey)
            hy_x = self.x_down(hy, self.line(self.left_wide, z) + HALF * ez)
            hz_x = self.x_down(hz, self.line(self.left_wide, self.cells_z + z) - HALF * ey)
            curl = (
                (hz - self.y_down(hz)) - (hy - hy_z),
                (hx - hx_z) - (hz - hz_x),
                (hy - hy_x) - (hx - self.y_down(hx)),
            )
            emit(a, b, (ex, ey, ez), (hx, hy, hz), curl)
            ex, ey, hx_z, hy_z = ex_next, ey_next, hx, hy
        return ex, ey, hx_z, hy_z


def half_inverse(permit_ref, mat):
    inverse = [HALF * (1.0 / permit_ref[m]) for m in range(permit_ref.shape[0])]
    out = jnp.full(mat.shape, inverse[0])
    for m in range(1, len(inverse)):
        out = jnp.where(mat == m, inverse[m], out)
    return out


def gradient_kernel(counts, per_device, *refs):
    place_ref, permit_ref, e_ref, h_ref, f_ref, mat_ref, grad_ref, mask_ref = refs[:8]
    faces, (grad_out, send_ref), (ybuf, left_wide, right_wide, grad_halo) = refs[8:14], refs[14:16], refs[16:]
    layers, _, width = grad_ref.shape
    lane = lax.broadcasted_iota(jnp.int32, (ROWS, LANES), 1)
    me = place_ref[GX]
    first_group = place_ref[FIRST] // ROWS
    fields = Fields(counts, layers, place_ref, e_ref, h_ref, faces, ybuf, left_wide, right_wide)
    mask = fields.with_halo(mask_ref[...], fields.grad_base, 5)

    def emit(a, b, efield, hfield, curl):
        z = ROWS * a + b
        layer = z - place_ref[FIRST]
        tile = fields.grad_base + fields.per_group * (a - first_group)

        def spot(which):
            return tile + (6 * b + which) // SLOTS, (6 * b + which) % SLOTS

        mat_halo = fields.halo(*spot(3)).astype(jnp.int32)
        half_inv = half_inverse(permit_ref, jnp.concatenate([mat_ref[z], mat_halo], axis=1))
        total = None
        for c in range(3):
            term = fields.with_halo(f_ref[c, z], *spot(c)) * (efield[c] + half_inv * curl[c])
            total = term if total is None else total + term
        grad = fields.with_halo(grad_ref[layer], *spot(4)) + mask * total
        grad_out[layer] = grad[:, :width]
        grad_halo[layer] = grad[:, width:]

    carry = fields.start(first_group)
    lax.fori_loop(0, layers // ROWS, lambda i, c: fields.group(first_group + i, c, emit), carry)

    def pack(k, carry):
        chunk = lax.bitwise_xor(me, k)
        edge = jnp.zeros((ROWS, LANES), jnp.float32)
        for i in range(per_device):
            layer = chunk * per_device + i
            send_ref[k, :, i * width : (i + 1) * width] = grad_out[layer]
            side = grad_halo[layer]
            at = 2 * STRIP * i
            upper = pltpu.roll(side, at, 1) if at else side
            lower = pltpu.roll(side, (at + 2 * STRIP) % LANES, 1)
            edge = jnp.where(lane // STRIP == 2 * i, upper, edge)
            edge = jnp.where(lane // STRIP == 2 * i + 1, lower, edge)
        send_ref[k, :, per_device * width :] = edge
        return carry

    lax.fori_loop(0, send_ref.shape[0], pack, 0)


def wide_scratch(xface, yface, width):
    rows = xface.shape[0]
    return [
        pltpu.VMEM((2,) + yface.shape, jnp.float32),
        pltpu.VMEM((rows, width + LANES), jnp.float32),
        pltpu.VMEM((rows, width + LANES), jnp.float32),
    ]


def gradient(place, permit, efield, hfield, forward, material, grad_sum, mask, faces):
    layers, _, width = grad_sum.shape
    count = lax.axis_size("gx")
    per_device = layers // count
    return pl.pallas_call(
        functools.partial(gradient_kernel, axis_sizes(), per_device),
        in_specs=[SMEM] * 2 + [VMEM] * 12,
        out_specs=[VMEM] * 2,
        out_shape=[f32(*grad_sum.shape), f32(count, ROWS, per_device * width + LANES)],
        scratch_shapes=wide_scratch(faces[2], faces[4], width)
        + [pltpu.VMEM((layers, ROWS, LANES), jnp.float32)],
        compiler_params=params(),
    )(place, permit, efield, hfield, forward, material, grad_sum, mask, *faces)


def step_kernel(counts, layers, *refs):
    place_ref, permit_ref, e_ref, h_ref, mat_ref = refs[:5]
    faces, (e_out, h_out), (ybuf, left_wide, right_wide, carry_ref) = refs[5:11], refs[11:13], refs[13:]
    width = e_ref.shape[3]
    fields = Fields(counts, layers, place_ref, e_ref, h_ref, faces, ybuf, left_wide, right_wide)
    a = pl.program_id(0)

    def emit(a, b, efield, hfield, curl):
        half_inv = half_inverse(permit_ref, mat_ref[ROWS * a + b])
        for c in range(3):
            e_out[c, b] = efield[c][:, :width] + half_inv * curl[c][:, :width]
            h_out[c, b] = hfield[c][:, :width]

    @pl.when(a == 0)
    def _():
        for i, v in enumerate(fields.start(0)):
            carry_ref[i] = v

    carry = tuple(carry_ref[i] for i in range(4))
    for i, v in enumerate(fields.group(a, carry, emit)):
        carry_ref[i] = v


def step(place, permit, efield, hfield, material, faces, layers):
    _, cells_z, _, width = efield.shape
    block = pl.BlockSpec((3, ROWS, ROWS, width), lambda a: (0, a, 0, 0))
    return pl.pallas_call(
        functools.partial(step_kernel, axis_sizes(), layers),
        grid=(cells_z // ROWS,),
        in_specs=[SMEM] * 2 + [VMEM] * 9,
        out_specs=[block] * 2,
        out_shape=[f32(*efield.shape)] * 2,
        scratch_shapes=wide_scratch(faces[2], faces[4], width)
        + [pltpu.VMEM((4, ROWS, width + LANES), jnp.float32)],
        compiler_params=params(),
    )(place, permit, efield, hfield, material, *faces)


def cone_matrix(rows):
    span = np.arange(-RADIUS, RADIUS + 1, dtype=np.float64)
    cone = np.maximum(RADIUS - np.sqrt(span[:, None] ** 2 + span[None, :] ** 2), 0.0)
    weight = cone / cone.sum()
    x = np.arange(rows)
    out = np.zeros((RADIUS + 1, rows, rows))
    for b in range(RADIUS + 1):
        for apart in (x[:, None] - x[None, :], 2 * rows - 1 - x[:, None] - x[None, :]):
            near = np.abs(apart) <= RADIUS
            out[b] += np.where(near, weight[np.clip(apart, -RADIUS, RADIUS) + RADIUS, RADIUS + b], 0.0)
    out = out.reshape((RADIUS + 1) * rows, rows).astype(np.float32)
    high = out.astype(jnp.bfloat16)
    low = (out - high.astype(np.float32)).astype(jnp.bfloat16)
    return np.concatenate([high, low, high], axis=1)


def flip_rows(v):
    row = lax.broadcasted_iota(jnp.int32, v.shape, 0)
    v = pltpu.roll(v, 4, 0)
    v = jnp.where(row % 4 < 2, pltpu.roll(v, ROWS - 2, 0), pltpu.roll(v, 2, 0))
    return jnp.where(row % 2 < 1, pltpu.roll(v, ROWS - 1, 0), pltpu.roll(v, 1, 0))


def filter_kernel(count, per_device, width, *refs):
    taps_ref, place_ref = refs[0], refs[1]
    got = refs[2 : 2 + count]
    outs = refs[2 + count : 2 + 2 * count]
    slabs, parts, done = refs[2 + 2 * count :]
    me = place_ref[GX]
    wide = width + LANES
    half = count // 2
    rows = half * ROWS
    lane = lax.broadcasted_iota(jnp.int32, (ROWS, LANES), 1)
    for k in range(count):
        slabs[lax.bitwise_xor(me, k)] = got[k][...]

    def layer_of(slab, i):
        edge = slabs[slab, :, per_device * width :]
        at = 2 * STRIP * i
        upper = pltpu.roll(edge, (LANES - at) % LANES, 1) if at else edge
        lower = pltpu.roll(edge, (LANES - 2 * STRIP - at) % LANES, 1)
        side = jnp.where(lane < STRIP, upper, lower)
        return jnp.concatenate([slabs[slab, :, i * width : (i + 1) * width], side], axis=1)

    for i in range(per_device):
        halves = [layer_of(s, i) + flip_rows(layer_of(count - 1 - s, i)) for s in range(half)]
        symmetric = jnp.concatenate(halves, axis=0)
        high = symmetric.astype(jnp.bfloat16)
        low = (symmetric - high.astype(jnp.float32)).astype(jnp.bfloat16)
        parts[0:rows, :] = high
        parts[rows : 2 * rows, :] = high
        parts[2 * rows : 3 * rows, :] = low
        mixed = jnp.dot(taps_ref[...], parts[...], preferred_element_type=jnp.float32)
        total = mixed[0:rows]
        for b in range(1, RADIUS + 1):
            part = mixed[b * rows : (b + 1) * rows]
            total = total + (pltpu.roll(part, b, 1) + pltpu.roll(part, wide - b, 1))
        for s in range(half):
            own = total[s * ROWS : (s + 1) * ROWS, :width]
            done[s, i] = own
            done[count - 1 - s, i] = flip_rows(own)
    for k in range(count):
        outs[k][...] = done[lax.bitwise_xor(me, k)]


def cone_filter(got, place, per_device, width):
    count = len(got)
    rows = count // 2 * ROWS
    taps = jnp.asarray(cone_matrix(rows))
    return pl.pallas_call(
        functools.partial(filter_kernel, count, per_device, width),
        in_specs=[VMEM, SMEM] + [VMEM] * count,
        out_specs=[VMEM] * count,
        out_shape=[f32(per_device, ROWS, width)] * count,
        scratch_shapes=[
            pltpu.VMEM((count, ROWS, per_device * width + LANES), jnp.float32),
            pltpu.VMEM((3 * rows, width + LANES), jnp.bfloat16),
            pltpu.VMEM((count, per_device, ROWS, width), jnp.float32),
        ],
        compiler_params=params(),
    )(taps, place, *got)


def place_kernel(count, per_device, place_ref, *refs):
    out, sems = refs[count], refs[count + 1]
    copies = []
    for k in range(count):
        at = lax.bitwise_xor(place_ref[GX], k) * per_device
        copies.append(pltpu.make_async_copy(refs[k], out.at[pl.ds(at, per_device)], sems.at[k]))
    for copy in copies:
        copy.start()
    for copy in copies:
        copy.wait()


def place_layers(parts, place):
    count = len(parts)
    per_device, rows, width = parts[0].shape
    return pl.pallas_call(
        functools.partial(place_kernel, count, per_device),
        in_specs=[SMEM] + [ANY] * count,
        out_specs=ANY,
        out_shape=f32(count * per_device, rows, width),
        scratch_shapes=[pltpu.SemaphoreType.DMA((count,))],
        compiler_params=params(),
    )(place, *parts)


def spread(parts):
    count = len(parts)
    return [parts[0]] + [
        lax.ppermute(parts[k], "gx", [(i, i ^ k) for i in range(count)]) for k in range(1, count)
    ]


def on_device(efield, hfield, forward, material, permit, design_mask, grad_sum):
    cells_z, width = efield.shape[1], efield.shape[3]
    layers = grad_sum.shape[0]
    first = (cells_z - layers) * (1 - lax.axis_index("gz"))
    indices = [lax.axis_index(axis) for axis in ("gx", "gy", "gz")]
    place = jnp.stack(indices + [first]).astype(jnp.int32)

    zfaces = exchange(*z_faces(efield, hfield, place), "gz")
    xfaces = exchange(*x_faces(efield, hfield, zfaces, place), "gx")
    own_low, own_high, mask = y_own(efield, hfield, forward, material, grad_sum, design_mask, place)
    yfaces = exchange(*y_faces(own_low, own_high, zfaces, xfaces, place), "gy", wrap=True)
    faces = zfaces + xfaces + yfaces
    grad_total, send = gradient(place, permit, efield, hfield, forward, material, grad_sum, mask, faces)
    got = spread([send[k] for k in range(send.shape[0])])
    e_next, h_next = step(place, permit, efield, hfield, material, faces, layers)
    filtered = spread(cone_filter(got, place, layers // len(got), width))
    return e_next, h_next, grad_total, place_layers(filtered, place)


def solution(mesh):
    field = P(None, "gz", "gx", "gy")
    cells = P("gz", "gx", "gy")
    return jax.shard_map(
        on_device,
        mesh=mesh,
        in_specs=(field, field, field, cells, P(), P("gx", "gy"), cells),
        out_specs=(field, field, cells, cells),
        check_vma=False,
    )
```

time: 56.4 us -> 49.2 us (0.87)
  local copies, waits for them, and re-layouts: 5 us -> 2.6 us
  waiting for transfers between devices: 14.1 us -> 11.8 us
  starting transfers between devices: 21.1 us -> 19.3 us
  other arithmetic: 1.86 us -> 0.08 us
  Pallas kernels: 13.2 us -> 14.3 us
    ppermute x6, waiting for transfers between devices: 10.8 us -> 6.14 us  [spread(): lax.ppermute(parts[k], 'gx', [(i, i ^ k) for i in range(count)])]
    ppermute x5, starting transfers between devices: 12.2 us -> 8.09 us  [swap_pairs(): return lax.ppermute(value, axis, pairs + [(b, a) for a, b in pairs])]
    ppermute x5, waiting for transfers between devices: 3.28 us -> 5.69 us  [swap_pairs(): return lax.ppermute(value, axis, pairs + [(b, a) for a, b in pairs])]
    unnamed x32 -> x18, local copies, waits for them, and re-layouts: 4.98 us -> 2.58 us
    ppermute x6, starting transfers between devices: 8.9 us -> 11.2 us  [spread(): lax.ppermute(parts[k], 'gx', [(i, i ^ k) for i in range(count)])]
    select_n x6 -> x0, other arithmetic: 1.79 us -> none  [the longest x3 1.03 us: exchange(): return (jnp.where(odd, first, second), jnp.where(odd, second, first))]
    pallas_call x5 -> x6, Pallas kernels: 10.3 us -> 11.5 us  [the longest x1 4.05 us: step(): pl.pallas_call(functools.partial(step_kernel, axis_sizes(), layers), grid...]
  transfers between devices with their start and end apart: 11 -> 11, of which waited for: 7 -> 6; matrix products, arithmetic and copies ran while one was open for 0% -> 0% of each run, Pallas kernels for 2% -> 10%
where the time goes in v1:
time: 49.2 us; the launch traced here: 49 us
  starting transfers between devices  19.3 us (39%)
  Pallas kernels  14.3 us (29%)
  waiting for transfers between devices  11.8 us (24%)
  local copies, waits for them, and re-layouts  2.6 us (5%)
  between operations  0.78 us (2%)
    ppermute x6, starting transfers between devices, spread(): lax.ppermute(parts[k], 'gx', [(i, i ^ k) for i in range(count)])  11.2 us
    ppermute x5, starting transfers between devices, swap_pairs(): return lax.ppermute(value, axis, pairs + [(b, a) for a, b in pairs])  8.09 us
    ppermute x6, waiting for transfers between devices, spread(): lax.ppermute(parts[k], 'gx', [(i, i ^ k) for i in range(count)])  6.14 us
    ppermute x5, waiting for transfers between devices, swap_pairs(): return lax.ppermute(value, axis, pairs + [(b, a) for a, b in pairs])  5.69 us
    pallas_call x1, Pallas kernels, step(): pl.pallas_call(functools.partial(step_kernel, axis_sizes(), layers), grid...  4.05 us
    pallas_call x1, Pallas kernels, gradient(): pl.pallas_call(functools.partial(gradient_kernel, axis_sizes(), per_devic...  3.73 us
    unnamed x18, local copies, waits for them, and re-layouts  2.58 us
    pallas_call x1, Pallas kernels, cone_filter(): pl.pallas_call(functools.partial(filter_kernel, count, per_device, width)...  1.63 us
  transfers between devices with their start and end apart: 11, of which 6 were waited for; matrix products, arithmetic and copies ran while one was open for 0% of the time, Pallas kernels for 10%

profile of v1, /device:TPU:0, one launch (start us, length us, event | category | flops | bytes accessed | tf_op | source)
XLA Modules:
  0.0 49.0 jit_solution(16147337121937305941)
XLA Ops:
  0.6 0.1 pad_add_fusion.place_ref.refs_0_.refs_1_
  0.7 0.0 copy-start
  0.7 1.3 %copy-done = f32[3,24,8,512]{3,2,1,0:T(8,128)S(1)} copy-done((f32[3,24,8,512]{3,2,1,0:T(8,128)S(1)}, f32[3,24,8,512]{3,2,1,0:T(8,128)}, u32[]{:S(2)}) %copy-start) | copy-done | bytes 1179672
  2.0 0.0 copy-start.2
  2.0 1.3 %copy-done.2 = f32[3,24,8,512]{3,2,1,0:T(8,128)S(1)} copy-done((f32[3,24,8,512]{3,2,1,0:T(8,128)S(1)}, f32[3,24,8,512]{3,2,1,0:T(8,128)}, u32[]{:S(2)}) %copy-start.2) | copy-done | bytes 1179672
  3.3 1.3 %shard_map.111 = (f32[3,8,512]{2,1,0:T(8,128)S(1)}, f32[3,8,512]{2,1,0:T(8,128)}) custom-call(s32[4]{0:T(128)S(1)} %pad_add_fusion.place_ref.refs_0_.refs_1_, f32[3,24,8,512]{3,2,1,0:T(8,128)S(1)} %copy-done, f32[3,24,8,512]{3,2,1,0:T(8,128)S(1)} %copy-done.2), custom_call_target="tpu_custom_call" | custom-call | tf_op jit(solution)/shard_map/pallas_call | solution.py:99
  4.5 0.0 copy-start.3
  4.5 0.0 copy-start.4
  4.6 0.0 copy-start.5
  4.6 0.0 copy-start.8
  4.6 3.0 %collective-permute-start = (f32[3,8,512]{2,1,0:T(8,128)S(1)}, f32[3,8,512]{2,1,0:T(8,128)S(1)}, u32[]{:S(2)}, u32[]{:S(2)}) collective-permute-start(f32[3,8,512]{2,1,0:T(8,128)S(1)} %get-tuple-element.20), channel_id=1, source_target_pairs={{0,1},{1,0},{2,3},{3,2},{4,5},{5,4},{6,7},{7,6},{8,9},{9,8},{10,11... | collective-permute-start | bytes 147464 | tf_op jit(solution)/shard_map/ppermute | solution.py:40
  7.6 2.1 %collective-permute-done.zfirst_ref.zsecond_ref.zfirst.zsecond.refs_5_.refs_6_.refs_8_.refs_9_ = f32[3,8,512]{2,1,0:T(8,128)S(1)} collective-permute-done((f32[3,8,512]{2,1,0:T(8,128)S(1)}, f32[3,8,512]{2,1,0:T(8,128)S(1)}, u32[]{:S(2)}, u32[]{:S(2)}) %collective-permute-start) | collective-permute-done | bytes 49184 | tf_op jit(solution)/shard_map/ppermute | solution.py:40
  9.7 0.7 %shard_map.112 = (f32[72,512]{1,0:T(8,128)S(1)}, f32[72,512]{1,0:T(8,128)S(1)}) custom-call(s32[4]{0:T(128)S(1)} %pad_add_fusion.place_ref.refs_0_.refs_1_, f32[3,24,8,512]{3,2,1,0:T(8,128)S(1)} %copy-done, f32[3,24,8,512]{3,2,1,0:T(8,128)S(1)} %copy-done.2, ...), custom_call_target="tpu_custom_call" | custom-call | tf_op jit(solution)/shard_map/pallas_call | solution.py:142
  10.4 2.1 %collective-permute-start.1 = (f32[72,512]{1,0:T(8,128)S(1)}, f32[72,512]{1,0:T(8,128)S(1)}, u32[]{:S(2)}, u32[]{:S(2)}) collective-permute-start(f32[72,512]{1,0:T(8,128)S(1)} %get-tuple-element.21), channel_id=1, source_target_pairs={{0,8},{16,24},{8,0},{24,16},{1,9},{17,25},{9,1},{25,17},{2,10},{18... | collective-permute-start | bytes 442376 | tf_op jit(solution)/shard_map/ppermute | solution.py:40
  12.5 0.0 copy-start.7
  12.5 0.8 %collective-permute-start.2 = (f32[72,512]{1,0:T(8,128)S(1)}, f32[72,512]{1,0:T(8,128)S(1)}, u32[]{:S(2)}, u32[]{:S(2)}) collective-permute-start(f32[72,512]{1,0:T(8,128)S(1)} %get-tuple-element.22), channel_id=1, source_target_pairs={{8,16},{16,8},{9,17},{17,9},{10,18},{18,10},{11,19},{19,11},{12,20... | collective-permute-start | bytes 442376 | tf_op jit(solution)/shard_map/ppermute | solution.py:40
  13.3 0.0 copy-done.3
  13.3 0.0 copy-done.4
  13.3 0.0 copy-done.5
  13.3 0.0 copy-done.8
  13.4 0.0 copy-start.1
  13.4 1.1 %shard_map.113 = (f32[15,8,128]{2,1,0:T(8,128)S(1)}, f32[15,8,128]{2,1,0:T(8,128)S(1)}, f32[8,512]{1,0:T(8,128)S(1)}) custom-call(s32[4]{0:T(128)S(1)} %pad_add_fusion.place_ref.refs_0_.refs_1_, f32[3,24,8,512]{3,2,1,0:T(8,128)S(1)} %copy-done, f32[3,24,8,512]{3,2,1,0:T(8,128)S(1)} %copy-done.2, f32[3,24,8,512]{3,2,1,0:T(8,128)S(1)} %copy-done.3, ...), custom_call_target="tpu_custom_call" | custom-call | tf_op jit(solution)/shard_map/pallas_call | solution.py:208
  14.4 1.2 %collective-permute-done.1.xfirst.refs_7_.refs_10_ = f32[72,512]{1,0:T(8,128)S(1)} collective-permute-done((f32[72,512]{1,0:T(8,128)S(1)}, f32[72,512]{1,0:T(8,128)S(1)}, u32[]{:S(2)}, u32[]{:S(2)}) %collective-permute-start.1) | collective-permute-done | bytes 147488 | tf_op jit(solution)/shard_map/ppermute | solution.py:40
  15.6 0.0 collective-permute-done.2.xsecond.refs_8_.refs_11_
  15.6 0.7 %shard_map.114 = (f32[17,8,128]{2,1,0:T(8,128)S(1)}, f32[17,8,128]{2,1,0:T(8,128)S(1)}) custom-call(s32[4]{0:T(128)S(1)} %pad_add_fusion.place_ref.refs_0_.refs_1_, f32[15,8,128]{2,1,0:T(8,128)S(1)} %get-tuple-element.23.own_low, f32[15,8,128]{2,1,0:T(8,128)S(1)} %get-tuple-element.24.own_high, ...), custom_call_target="tpu_custom_call" | custom-call | tf_op jit(solution)/shard_map/pallas_call | solution.py:249
  16.3 0.1 collective-permute-start.3
  16.4 2.1 %collective-permute-start.4 = (f32[17,8,128]{2,1,0:T(8,128)S(1)}, f32[17,8,128]{2,1,0:T(8,128)S(1)}, u32[]{:S(2)}, u32[]{:S(2)}) collective-permute-start(f32[17,8,128]{2,1,0:T(8,128)S(1)} %get-tuple-element.26), channel_id=1, source_target_pairs={{2,4},{0,6},{4,2},{6,0},{3,5},{1,7},{5,3},{7,1},{10,12},{8,14},{12... | collective-permute-start | bytes 208904 | tf_op jit(solution)/shard_map/ppermute | solution.py:40
  18.4 0.0 collective-permute-done.3.refs_9_.refs_12_
  18.4 2.4 %collective-permute-done.4.refs_10_.refs_13_ = f32[17,8,128]{2,1,0:T(8,128)S(1)} collective-permute-done((f32[17,8,128]{2,1,0:T(8,128)S(1)}, f32[17,8,128]{2,1,0:T(8,128)S(1)}, u32[]{:S(2)}, u32[]{:S(2)}) %collective-permute-start.4) | collective-permute-done | bytes 69664 | tf_op jit(solution)/shard_map/ppermute | solution.py:40
  20.8 0.0 copy-done.7
  20.8 0.0 copy-done.1
  20.9 3.7 %shard_map.116 = (f32[16,8,512]{2,1,0:T(8,128)}, f32[4,8,2176]{2,1,0:T(8,128)S(1)}) custom-call(s32[4]{0:T(128)S(1)} %pad_add_fusion.place_ref.refs_0_.refs_1_, f32[4]{0:T(128)S(1)} %copy-done.7, f32[3,24,8,512]{3,2,1,0:T(8,128)S(1)} %copy-done.1, f32[3,24,8,512]{3,2,1,0:T(8,128)S(1)} %copy-done.2, f32[3,24,8,512]{3,2,1,0:T(8,128)S(1)} %copy-done.3, ...), custom_call_target="tpu_custom_call" | custom-call | tf_op jit(solution)/shard_map/pallas_call | solution.py:454
  24.6 3.7 %collective-permute-start.7 = (f32[8,2176]{1,0:T(8,128)S(1)}, f32[8,2176]{1,0:T(8,128)S(1)}, u32[]{:S(2)}, u32[]{:S(2)}) collective-permute-start(f32[8,2176]{1,0:T(8,128)S(1)} %get-tuple-element.36), channel_id=1, source_target_pairs={{0,24},{8,16},{16,8},{24,0},{1,25},{9,17},{17,9},{25,1},{2,26},{10... | collective-permute-start | bytes 208904 | tf_op jit(solution)/shard_map/ppermute | solution.py:614
  28.3 2.7 %collective-permute-start.6 = (f32[8,2176]{1,0:T(8,128)S(1)}, f32[8,2176]{1,0:T(8,128)S(1)}, u32[]{:S(2)}, u32[]{:S(2)}) collective-permute-start(f32[8,2176]{1,0:T(8,128)S(1)} %get-tuple-element.37), channel_id=1, source_target_pairs={{0,16},{8,24},{16,0},{24,8},{1,17},{9,25},{17,1},{25,9},{2,18},{10... | collective-permute-start | bytes 208904 | tf_op jit(solution)/shard_map/ppermute | solution.py:614
  30.9 0.5 collective-permute-start.5
  31.4 0.0 collective-permute-done.7.refs_5_
  31.4 4.9 %collective-permute-done.6.refs_4_ = f32[8,2176]{1,0:T(8,128)S(1)} collective-permute-done((f32[8,2176]{1,0:T(8,128)S(1)}, f32[8,2176]{1,0:T(8,128)S(1)}, u32[]{:S(2)}, u32[]{:S(2)}) %collective-permute-start.6) | collective-permute-done | bytes 69664 | tf_op jit(solution)/shard_map/ppermute | solution.py:614
  36.3 0.1 collective-permute-done.5.refs_3_
  36.4 0.0 copy-done.6
  36.4 1.6 %shard_map.117 = (f32[4,8,512]{2,1,0:T(8,128)S(1)}, f32[4,8,512]{2,1,0:T(8,128)S(1)}, f32[4,8,512]{2,1,0:T(8,128)S(1)}, f32[4,8,512]{2,1,0:T(8,128)S(1)}) custom-call(bf16[112,48]{1,0:T(8,128)(2,1)S(1)} %copy-done.6, s32[4]{0:T(128)S(1)} %pad_add_fusion.place_ref.refs_0_.refs_1_, f32[8,2176]{1,0:T(8,128)S(1)} %get-tuple-element.39.refs_2_, ...), custom_call_target="tpu_custom_call" | custom-call | tf_op jit(solution)/shard_map/pallas_call | solution.py:572
  38.0 0.9 %collective-permute-start.8 = (f32[4,8,512]{2,1,0:T(8,128)S(1)}, f32[4,8,512]{2,1,0:T(8,128)S(1)}, u32[]{:S(2)}, u32[]{:S(2)}) collective-permute-start(f32[4,8,512]{2,1,0:T(8,128)S(1)} %get-tuple-element.33), channel_id=1, source_target_pairs={{0,8},{8,0},{16,24},{24,16},{1,9},{9,1},{17,25},{25,17},{2,10},{10... | collective-permute-start | bytes 196616 | tf_op jit(solution)/shard_map/ppermute | solution.py:614
  38.9 2.7 %collective-permute-start.9 = (f32[4,8,512]{2,1,0:T(8,128)S(1)}, f32[4,8,512]{2,1,0:T(8,128)S(1)}, u32[]{:S(2)}, u32[]{:S(2)}) collective-permute-start(f32[4,8,512]{2,1,0:T(8,128)S(1)} %get-tuple-element.34), channel_id=1, source_target_pairs={{0,16},{8,24},{16,0},{24,8},{1,17},{9,25},{17,1},{25,9},{2,18},{10... | collective-permute-start | bytes 196616 | tf_op jit(solution)/shard_map/ppermute | solution.py:614
  41.6 0.8 %collective-permute-start.10 = (f32[4,8,512]{2,1,0:T(8,128)S(1)}, f32[4,8,512]{2,1,0:T(8,128)S(1)}, u32[]{:S(2)}, u32[]{:S(2)}) collective-permute-start(f32[4,8,512]{2,1,0:T(8,128)S(1)} %get-tuple-element.35), channel_id=1, source_target_pairs={{0,24},{8,16},{16,8},{24,0},{1,25},{9,17},{17,9},{25,1},{2,26},{10... | collective-permute-start | bytes 196616 | tf_op jit(solution)/shard_map/ppermute | solution.py:614
  42.5 4.1 %shard_map.115 = (f32[3,24,8,512]{3,2,1,0:T(8,128)}, f32[3,24,8,512]{3,2,1,0:T(8,128)}) custom-call(s32[4]{0:T(128)S(1)} %pad_add_fusion.place_ref.refs_0_.refs_1_, f32[4]{0:T(128)S(1)} %copy-done.7, f32[3,24,8,512]{3,2,1,0:T(8,128)S(1)} %copy-done.1, f32[3,24,8,512]{3,2,1,0:T(8,128)S(1)} %copy-done.2, s32[24,8,512]{2,1,0:T(8,128)S(1)} %copy-done.4, ...), custom_call_target="tpu_custom_call" | custom-call | tf_op jit(solution)/shard_map/pallas_call | solution.py:491
  46.5 0.0 collective-permute-done.8.refs_1_
  46.5 0.0 collective-permute-done.9.refs_2_
  46.5 1.2 %collective-permute-done.10.refs_3_ = f32[4,8,512]{2,1,0:T(8,128)S(1)} collective-permute-done((f32[4,8,512]{2,1,0:T(8,128)S(1)}, f32[4,8,512]{2,1,0:T(8,128)S(1)}, u32[]{:S(2)}, u32[]{:S(2)}) %collective-permute-start.10) | collective-permute-done | bytes 65568 | tf_op jit(solution)/shard_map/ppermute | solution.py:614
  47.7 1.3 %shard_map.118 = f32[16,8,512]{2,1,0:T(8,128)} custom-call(s32[4]{0:T(128)S(1)} %pad_add_fusion.place_ref.refs_0_.refs_1_, f32[4,8,512]{2,1,0:T(8,128)S(1)} %get-tuple-element.32.refs_0_, f32[4,8,512]{2,1,0:T(8,128)S(1)} %collective-permute-done.8.refs_1_, f32[4,8,512]{2,1,0:T(8,128)S(1)} %collective-permute-done.9.refs_2_, ...), custom_call_target="tpu_custom_call" | custom-call | tf_op jit(solution)/shard_map/pallas_call | solution.py:601
  (2 shorter events, 0.0 us)
Async XLA Ops:
  0.7 1.3 %copy-start = (f32[3,24,8,512]{3,2,1,0:T(8,128)S(1)}, f32[3,24,8,512]{3,2,1,0:T(8,128)}, u32[]{:S(2)}) copy-start(f32[3,24,8,512]{3,2,1,0:T(8,128)} %refs_2_.3) | copy-start | bytes 3538948
  2.0 1.3 %copy-start.2 = (f32[3,24,8,512]{3,2,1,0:T(8,128)S(1)}, f32[3,24,8,512]{3,2,1,0:T(8,128)}, u32[]{:S(2)}) copy-start(f32[3,24,8,512]{3,2,1,0:T(8,128)} %refs_3_.3) | copy-start | bytes 3538948
  4.5 8.8 %copy-start.3 = (f32[3,24,8,512]{3,2,1,0:T(8,128)S(1)}, f32[3,24,8,512]{3,2,1,0:T(8,128)}, u32[]{:S(2)}) copy-start(f32[3,24,8,512]{3,2,1,0:T(8,128)} %refs_4_.3) | copy-start | bytes 3538948
  4.5 8.8 %copy-start.4 = (s32[24,8,512]{2,1,0:T(8,128)S(1)}, s32[24,8,512]{2,1,0:T(8,128)}, u32[]{:S(2)}) copy-start(s32[24,8,512]{2,1,0:T(8,128)} %refs_5_.1) | copy-start | bytes 1179652
  4.6 8.8 %copy-start.5 = (f32[16,8,512]{2,1,0:T(8,128)S(1)}, f32[16,8,512]{2,1,0:T(8,128)}, u32[]{:S(2)}) copy-start(f32[16,8,512]{2,1,0:T(8,128)} %refs_6_.1) | copy-start | bytes 786436
  4.6 8.8 %copy-start.8 = (s32[1,64]{1,0:T(1,128)S(1)}, s32[1,64]{1,0:T(1,128)}, u32[]{:S(2)}) copy-start(s32[1,64]{1,0:T(1,128)} %mask_ref.1) | copy-start | bytes 772
  4.6 5.1 %collective-permute-start = (f32[3,8,512]{2,1,0:T(8,128)S(1)}, f32[3,8,512]{2,1,0:T(8,128)S(1)}, u32[]{:S(2)}, u32[]{:S(2)}) collective-permute-start(f32[3,8,512]{2,1,0:T(8,128)S(1)} %get-tuple-element.20), channel_id=1, source_target_pairs={{0,1},{1,0},{2,3},{3,2},{4,5},{5,4},{6,7},{7,6},{8,9},{9,8},{10,11... | collective-permute-start | bytes 147464 | tf_op jit(solution)/shard_map/ppermute | solution.py:40
  10.4 5.3 %collective-permute-start.1 = (f32[72,512]{1,0:T(8,128)S(1)}, f32[72,512]{1,0:T(8,128)S(1)}, u32[]{:S(2)}, u32[]{:S(2)}) collective-permute-start(f32[72,512]{1,0:T(8,128)S(1)} %get-tuple-element.21), channel_id=1, source_target_pairs={{0,8},{16,24},{8,0},{24,16},{1,9},{17,25},{9,1},{25,17},{2,10},{18... | collective-permute-start | bytes 442376 | tf_op jit(solution)/shard_map/ppermute | solution.py:40
  12.5 8.3 %copy-start.7 = (f32[4]{0:T(128)S(1)}, f32[4]{0:T(128)}, u32[]{:S(2)}) copy-start(f32[4]{0:T(128)} %refs_1_.3) | copy-start | bytes 52
  12.5 3.1 %collective-permute-start.2 = (f32[72,512]{1,0:T(8,128)S(1)}, f32[72,512]{1,0:T(8,128)S(1)}, u32[]{:S(2)}, u32[]{:S(2)}) collective-permute-start(f32[72,512]{1,0:T(8,128)S(1)} %get-tuple-element.22), channel_id=1, source_target_pairs={{8,16},{16,8},{9,17},{17,9},{10,18},{18,10},{11,19},{19,11},{12,20... | collective-permute-start | bytes 442376 | tf_op jit(solution)/shard_map/ppermute | solution.py:40
  13.4 7.5 %copy-start.1 = (f32[3,24,8,512]{3,2,1,0:T(8,128)S(1)}, f32[3,24,8,512]{3,2,1,0:T(8,128)}, u32[]{:S(2)}) copy-start(f32[3,24,8,512]{3,2,1,0:T(8,128)} %refs_2_.3) | copy-start | bytes 3538948
  16.3 2.1 %collective-permute-start.3 = (f32[17,8,128]{2,1,0:T(8,128)S(1)}, f32[17,8,128]{2,1,0:T(8,128)S(1)}, u32[]{:S(2)}, u32[]{:S(2)}) collective-permute-start(f32[17,8,128]{2,1,0:T(8,128)S(1)} %get-tuple-element.25), channel_id=1, source_target_pairs={{0,2},{4,6},{2,0},{6,4},{1,3},{5,7},{3,1},{7,5},{8,10},{12,14},{10... | collective-permute-start | bytes 208904 | tf_op jit(solution)/shard_map/ppermute | solution.py:40
  16.4 4.5 %collective-permute-start.4 = (f32[17,8,128]{2,1,0:T(8,128)S(1)}, f32[17,8,128]{2,1,0:T(8,128)S(1)}, u32[]{:S(2)}, u32[]{:S(2)}) collective-permute-start(f32[17,8,128]{2,1,0:T(8,128)S(1)} %get-tuple-element.26), channel_id=1, source_target_pairs={{2,4},{0,6},{4,2},{6,0},{3,5},{1,7},{5,3},{7,1},{10,12},{8,14},{12... | collective-permute-start | bytes 208904 | tf_op jit(solution)/shard_map/ppermute | solution.py:40
  20.9 15.5 %copy-start.6 = (bf16[112,48]{1,0:T(8,128)(2,1)S(1)}, bf16[112,48]{1,0:T(8,128)(2,1)}, u32[]{:S(2)}) copy-start(bf16[112,48]{1,0:T(8,128)(2,1)} %constant.17.clone.refs_0_) | copy-start | bytes 32260
  24.6 6.8 %collective-permute-start.7 = (f32[8,2176]{1,0:T(8,128)S(1)}, f32[8,2176]{1,0:T(8,128)S(1)}, u32[]{:S(2)}, u32[]{:S(2)}) collective-permute-start(f32[8,2176]{1,0:T(8,128)S(1)} %get-tuple-element.36), channel_id=1, source_target_pairs={{0,24},{8,16},{16,8},{24,0},{1,25},{9,17},{17,9},{25,1},{2,26},{10... | collective-permute-start | bytes 208904 | tf_op jit(solution)/shard_map/ppermute | solution.py:614
  28.3 8.0 %collective-permute-start.6 = (f32[8,2176]{1,0:T(8,128)S(1)}, f32[8,2176]{1,0:T(8,128)S(1)}, u32[]{:S(2)}, u32[]{:S(2)}) collective-permute-start(f32[8,2176]{1,0:T(8,128)S(1)} %get-tuple-element.37), channel_id=1, source_target_pairs={{0,16},{8,24},{16,0},{24,8},{1,17},{9,25},{17,1},{25,9},{2,18},{10... | collective-permute-start | bytes 208904 | tf_op jit(solution)/shard_map/ppermute | solution.py:614
  30.9 5.5 %collective-permute-start.5 = (f32[8,2176]{1,0:T(8,128)S(1)}, f32[8,2176]{1,0:T(8,128)S(1)}, u32[]{:S(2)}, u32[]{:S(2)}) collective-permute-start(f32[8,2176]{1,0:T(8,128)S(1)} %get-tuple-element.38), channel_id=1, source_target_pairs={{0,8},{8,0},{16,24},{24,16},{1,9},{9,1},{17,25},{25,17},{2,10},{10... | collective-permute-start | bytes 208904 | tf_op jit(solution)/shard_map/ppermute | solution.py:614
  38.0 8.5 %collective-permute-start.8 = (f32[4,8,512]{2,1,0:T(8,128)S(1)}, f32[4,8,512]{2,1,0:T(8,128)S(1)}, u32[]{:S(2)}, u32[]{:S(2)}) collective-permute-start(f32[4,8,512]{2,1,0:T(8,128)S(1)} %get-tuple-element.33), channel_id=1, source_target_pairs={{0,8},{8,0},{16,24},{24,16},{1,9},{9,1},{17,25},{25,17},{2,10},{10... | collective-permute-start | bytes 196616 | tf_op jit(solution)/shard_map/ppermute | solution.py:614
  38.9 7.6 %collective-permute-start.9 = (f32[4,8,512]{2,1,0:T(8,128)S(1)}, f32[4,8,512]{2,1,0:T(8,128)S(1)}, u32[]{:S(2)}, u32[]{:S(2)}) collective-permute-start(f32[4,8,512]{2,1,0:T(8,128)S(1)} %get-tuple-element.34), channel_id=1, source_target_pairs={{0,16},{8,24},{16,0},{24,8},{1,17},{9,25},{17,1},{25,9},{2,18},{10... | collective-permute-start | bytes 196616 | tf_op jit(solution)/shard_map/ppermute | solution.py:614
  41.6 6.1 %collective-permute-start.10 = (f32[4,8,512]{2,1,0:T(8,128)S(1)}, f32[4,8,512]{2,1,0:T(8,128)S(1)}, u32[]{:S(2)}, u32[]{:S(2)}) collective-permute-start(f32[4,8,512]{2,1,0:T(8,128)S(1)} %get-tuple-element.35), channel_id=1, source_target_pairs={{0,24},{8,16},{16,8},{24,0},{1,25},{9,17},{17,9},{25,1},{2,26},{10... | collective-permute-start | bytes 196616 | tf_op jit(solution)/shard_map/ppermute | solution.py:614

commit v2 on v1

v2 whole, which is shorter than its diff:
```python
import functools
import math

import jax
import jax.numpy as jnp
import numpy as np
from jax import lax
from jax.experimental import pallas as pl
from jax.experimental.pallas import tpu as pltpu
from jax.sharding import PartitionSpec as P

RADIUS = 6
BLOCK = 8
HALF = 0.5

ROWS = 8
LANES = 128
STRIP = 8
SLOTS = LANES // STRIP
VMEM_LIMIT = 24 * 1024 * 1024

VMEM = pl.BlockSpec(memory_space=pltpu.VMEM)
SMEM = pl.BlockSpec(memory_space=pltpu.SMEM)
ANY = pl.BlockSpec(memory_space=pl.ANY)


def params():
    return pltpu.CompilerParams(vmem_limit_bytes=VMEM_LIMIT)


def f32(*shape):
    return jax.ShapeDtypeStruct(shape, jnp.float32)


def swap_pairs(value, axis, pairs):
    return lax.ppermute(value, axis, pairs + [(b, a) for a, b in pairs])


def rounds(axis):
    return 2 if lax.axis_size(axis) > 2 else 1


def exchange(sends, axis, wrap=False):
    count = lax.axis_size(axis)
    if count == 1:
        return sends
    got = [swap_pairs(sends[0], axis, [(i, i + 1) for i in range(0, count - 1, 2)])]
    if len(sends) > 1:
        odd_pairs = [(i, i + 1) for i in range(1, count - 1, 2)]
        if wrap and count % 2 == 0:
            odd_pairs.append((0, count - 1))
        got.append(swap_pairs(sends[1], axis, odd_pairs))
    return got


class Side:
    def __init__(self, axis):
        index = lax.axis_index(axis)
        self.rounds = rounds(axis)
        self.odd = index % 2 == 1
        self.bottom = index == 0
        self.top = index == lax.axis_size(axis) - 1

    def sends(self, low, high):
        both = [jnp.where(self.odd, low, high)]
        if self.rounds > 1:
            both.append(jnp.where(self.odd, high, low))
        return both

    def lower(self, got):
        return jnp.where(self.bottom, 0.0, jnp.where(self.odd, got[0], got[-1]))

    def upper(self, got):
        return jnp.where(self.top, 0.0, jnp.where(self.odd, got[-1], got[0]))


def first_layer(cells_z, layers):
    return (cells_z - layers) * (1 - lax.axis_index("gz"))


def z_faces(efield, hfield):
    top = efield.shape[1] - 1
    ex, ey, ez = (efield[c, top] for c in range(3))
    high = jnp.stack(
        [
            hfield[0, top] + HALF * ez - HALF * ey,
            hfield[1, top] + HALF * ex - HALF * ez,
            ez,
        ]
    )
    return Side("gz").sends(efield[:, 0], high)


def x_faces_kernel(z_rounds, *refs):
    e_ref, h_ref = refs[:2]
    zfaces = refs[2 : 2 + z_rounds]
    sends, (low_ref, rows_ref) = refs[2 + z_rounds : -2], refs[-2:]
    cells_z = e_ref.shape[1]
    last = ROWS - 1
    z_side = Side("gz")
    low_ref[...] = jnp.zeros_like(low_ref)
    for z in range(cells_z):
        low_ref[z : z + 1, :] = e_ref[1, z, 0:1, :]
        low_ref[cells_z + z : cells_z + z + 1, :] = e_ref[2, z, 0:1, :]
        for c in range(3):
            rows_ref[c, z : z + 1, :] = e_ref[c, z, last : last + 1, :]
        for c in range(2):
            rows_ref[3 + c, z : z + 1, :] = h_ref[1 + c, z, last : last + 1, :]
        if z > 0:
            rows_ref[5, z - 1 : z, :] = e_ref[0, z, last : last + 1, :]
    rows_ref[5, cells_z - 1 : cells_z, :] = z_side.upper([f[0, last : last + 1, :] for f in zfaces])
    low_ref[2 * cells_z : 2 * cells_z + 1, :] = z_side.lower([f[2, 0:1, :] for f in zfaces])
    ex = rows_ref[0]
    high = (
        rows_ref[3] - HALF * (rows_ref[5] - ex + rows_ref[2]),
        rows_ref[4] + HALF * rows_ref[1] - HALF * ex,
        ex,
    )
    side = Side("gx")
    for c in range(3):
        here = slice(c * cells_z, (c + 1) * cells_z)
        for ref, value in zip(sends, side.sends(low_ref[here, :], high[c])):
            ref[here, :] = value


def x_faces(efield, hfield, zfaces):
    cells_z, cells_y = efield.shape[1], efield.shape[3]
    face = f32(3 * cells_z, cells_y)
    return pl.pallas_call(
        functools.partial(x_faces_kernel, len(zfaces)),
        in_specs=[VMEM] * (2 + len(zfaces)),
        out_specs=[VMEM] * rounds("gx"),
        out_shape=[face] * rounds("gx"),
        scratch_shapes=[
            pltpu.VMEM(face.shape, jnp.float32),
            pltpu.VMEM((6, cells_z, cells_y), jnp.float32),
        ],
        compiler_params=params(),
    )(efield, hfield, *zfaces)


def lane_group():
    return lax.broadcasted_iota(jnp.int32, (ROWS, LANES), 1) // STRIP


def pack_strips(tiles, low_ref, high_ref, first):
    group = lane_group()
    width = tiles[0][1]
    for start in range(0, len(tiles), SLOTS):
        low = jnp.zeros((ROWS, LANES), jnp.float32)
        high = jnp.zeros((ROWS, LANES), jnp.float32)
        for k, (load, _) in enumerate(tiles[start : start + SLOTS]):
            if load is None:
                continue
            here = group == k
            shift = (STRIP * k) % LANES
            left = load(slice(0, LANES))
            right = load(slice(width - LANES, width))
            low = jnp.where(here, pltpu.roll(left, shift, 1) if shift else left, low)
            shift = (STRIP * k + STRIP) % LANES
            high = jnp.where(here, pltpu.roll(right, shift, 1) if shift else right, high)
        low_ref[first + start // SLOTS] = low
        high_ref[first + start // SLOTS] = high


def y_own_kernel(
    permit_ref, e_ref, h_ref, f_ref, mat_ref, grad_ref, mask_ref, low_ref, high_ref, wide_ref, inv_ref
):
    cells_z, width = e_ref.shape[1], e_ref.shape[3]
    layers = grad_ref.shape[0]
    blocks = mask_ref.shape[1]
    inverse = [HALF * (1.0 / permit_ref[m]) for m in range(permit_ref.shape[0])]
    for z in range(cells_z):
        inv = jnp.full((ROWS, width), inverse[0])
        for m in range(1, len(inverse)):
            inv = jnp.where(mat_ref[z] == m, inverse[m], inv)
        inv_ref[z] = inv
    spread = (
        lax.broadcasted_iota(jnp.int32, (blocks, width), 0)
        == lax.broadcasted_iota(jnp.int32, (blocks, width), 1) // BLOCK
    ).astype(jnp.float32)
    mask = jnp.broadcast_to(mask_ref[...].astype(jnp.float32), (ROWS, blocks))
    wide_ref[...] = jnp.dot(mask, spread, preferred_element_type=jnp.float32)
    first = first_layer(cells_z, layers)
    tiles = []
    for z in range(cells_z):
        for ref in (e_ref, h_ref):
            for c in range(3):
                tiles.append((lambda s, r=ref, c=c, z=z: r[c, z, :, s], width))
    for layer in range(layers):
        for c in range(3):
            tiles.append((lambda s, c=c, l=layer: f_ref[c, first + l, :, s], width))
        tiles.append((lambda s, l=layer: inv_ref[first + l, :, s], width))
        tiles.append((lambda s, l=layer: grad_ref[l, :, s], width))
        tiles.append((lambda s: wide_ref[:, s], width) if layer % ROWS == 0 else (None, width))
    pack_strips(tiles, low_ref, high_ref, 0)


def y_own(permit, efield, hfield, forward, material, grad_sum, mask):
    cells_z, width = efield.shape[1], efield.shape[3]
    count = (cells_z * 6 + grad_sum.shape[0] * 6) // SLOTS
    packed = f32(count, ROWS, LANES)
    return pl.pallas_call(
        y_own_kernel,
        in_specs=[SMEM] + [VMEM] * 6,
        out_specs=[VMEM] * 4,
        out_shape=[packed, packed, f32(ROWS, width), f32(*material.shape)],
        compiler_params=params(),
    )(permit, efield, hfield, forward, material, grad_sum, mask)


def face_tiles(zfaces, xfaces):
    width = xfaces[0].shape[1]
    z_side, x_side = Side("gz"), Side("gx")
    tiles = []
    for c in range(3):
        tiles.append((lambda s, c=c: z_side.lower([f[c, :, s] for f in zfaces]), width))
    for c in range(2):
        tiles.append((lambda s, c=c: z_side.upper([f[c, :, s] for f in zfaces]), width))
    for pick in (x_side.lower, x_side.upper):
        for t in range(0, xfaces[0].shape[0], ROWS):
            tiles.append((lambda s, p=pick, t=t: p([f[t : t + ROWS, s] for f in xfaces]), width))
    return tiles


def face_count(xface):
    return 5 + 2 * (xface.shape[0] // ROWS)


def y_faces_kernel(counts, *refs):
    own_low, own_high = refs[:2]
    zfaces, xfaces = refs[2 : 2 + counts[0]], refs[2 + counts[0] : 2 + sum(counts)]
    sends, (low_ref, high_ref) = refs[2 + sum(counts) : -2], refs[-2:]
    own = own_low.shape[0]
    pack_strips(face_tiles(zfaces, xfaces), low_ref, high_ref, 0)
    side = Side("gy")
    for ref, value in zip(sends, side.sends(own_low[...], own_high[...])):
        ref[0:own] = value
    for ref, value in zip(sends, side.sends(low_ref[...], high_ref[...])):
        ref[own:] = value


def y_faces(own_low, own_high, zfaces, xfaces):
    extra = math.ceil(face_count(xfaces[0]) / SLOTS)
    packed = f32(own_low.shape[0] + extra, ROWS, LANES)
    return pl.pallas_call(
        functools.partial(y_faces_kernel, (len(zfaces), len(xfaces))),
        in_specs=[VMEM] * (2 + len(zfaces) + len(xfaces)),
        out_specs=[VMEM] * rounds("gy"),
        out_shape=[packed] * rounds("gy"),
        scratch_shapes=[pltpu.VMEM((extra, ROWS, LANES), jnp.float32)] * 2,
        compiler_params=params(),
    )(own_low, own_high, *zfaces, *xfaces)


OWN, CIRCLE, EDGE = range(3)


def faces_wide(mode, width):
    return {OWN: width, CIRCLE: width + LANES, EDGE: LANES}[mode]


class Fields:
    def __init__(self, mode, layers, e_ref, h_ref, zfaces, xfaces, yfaces, scratch):
        self.mode = mode
        self.e_ref, self.h_ref = e_ref, h_ref
        self.cells_z, self.width = e_ref.shape[1], e_ref.shape[3]
        self.wide = faces_wide(mode, self.width)
        self.lane = lax.broadcasted_iota(jnp.int32, (ROWS, LANES), 1)
        self.row = lax.broadcasted_iota(jnp.int32, (ROWS, self.wide), 0)
        self.per_group = 6 * ROWS // SLOTS
        self.groups = self.cells_z // ROWS
        self.grad_base = self.per_group * self.groups
        halo_base = self.grad_base + self.per_group * (layers // ROWS)
        self.left_wide, self.right_wide = left_wide, right_wide = scratch[:2]
        if mode != OWN:
            self.ybuf = scratch[2]
            y_side = Side("gy")
            self.ybuf[0] = y_side.lower([f[...] for f in yfaces])
            self.ybuf[1] = y_side.upper([f[...] for f in yfaces])

        full = [
            self.wider(load, halo_base + t // SLOTS, t % SLOTS)
            for t, (load, _) in enumerate(face_tiles(zfaces, xfaces))
        ]
        self.below, self.above = full[:3], full[3:5]
        per_face = xfaces[0].shape[0] // ROWS
        for t in range(per_face):
            left_wide[t * ROWS : (t + 1) * ROWS, :] = full[5 + t]
            right_wide[t * ROWS : (t + 1) * ROWS, :] = full[5 + per_face + t]
        cells_z = self.cells_z
        left_wide[cells_z : 2 * cells_z, :] += HALF * self.y_up(left_wide[2 * cells_z : 3 * cells_z, :])

    def wider(self, load, tile, k):
        if self.mode == OWN:
            return load(slice(0, self.width))

        def moved(v, to):
            shift = (to - STRIP * k) % LANES
            return pltpu.roll(v, shift, 1) if shift else v

        lower, upper = self.ybuf[0, tile], self.ybuf[1, tile]
        if self.mode == CIRCLE:
            halo = jnp.where(self.lane < STRIP, moved(upper, 0), moved(lower, LANES - STRIP))
            return jnp.concatenate([load(slice(0, self.width)), halo], axis=1)
        head = pltpu.roll(load(slice(0, LANES)), STRIP, 1)
        tail = pltpu.roll(load(slice(self.width - LANES, self.width)), LANES - STRIP, 1)
        own = jnp.where(self.lane < LANES // 2, head, tail)
        own = jnp.where(self.lane < STRIP, moved(lower, 0), own)
        return jnp.where(self.lane >= LANES - STRIP, moved(upper, LANES - STRIP), own)

    def y_up(self, v):
        return pltpu.roll(v, self.wide - 1, 1)

    def y_down(self, v):
        return pltpu.roll(v, 1, 1)

    def x_up(self, v, line):
        return jnp.where(self.row == ROWS - 1, line, pltpu.roll(v, ROWS - 1, 0))

    def x_down(self, v, line):
        return jnp.where(self.row == 0, line, pltpu.roll(v, 1, 0))

    def line(self, ref, at):
        return jnp.broadcast_to(ref[pl.ds(at, 1), :], (ROWS, self.wide))

    def field(self, which, c, a, b):
        slot = 6 * b + 3 * which + c
        ref = self.h_ref if which else self.e_ref
        tile = self.per_group * a + slot // SLOTS
        return self.wider(lambda s: ref[c, ROWS * a + b, :, s], tile, slot % SLOTS)

    def hx(self, a, b, ey, ez, ey_next):
        return self.field(1, 0, a, b) - HALF * (self.y_up(ez) - ez - ey_next + ey)

    def hy(self, a, b, ex, ez, ex_next):
        up = self.x_up(ez, self.line(self.right_wide, self.cells_z + ROWS * a + b))
        return self.field(1, 1, a, b) - HALF * (ex_next - ex - up + ez)

    def hz(self, a, b, ex, ey):
        up = self.x_up(ey, self.line(self.right_wide, ROWS * a + b))
        return self.field(1, 2, a, b) - HALF * (up - ey - self.y_up(ex) + ex)

    def start(self, a):
        ex, ey = self.field(0, 0, a, 0), self.field(0, 1, a, 0)
        below = self.below
        at_bottom = (
            below[0] - HALF * self.y_up(below[2]) + HALF * ey,
            below[1] - HALF * ex + HALF * self.x_up(below[2], self.line(self.right_wide, 2 * self.cells_z)),
        )
        before, b = jnp.maximum(a - 1, 0), ROWS - 1
        ex_before, ey_before, ez_before = (self.field(0, c, before, b) for c in range(3))
        inside = (
            self.hx(before, b, ey_before, ez_before, ey),
            self.hy(before, b, ex_before, ez_before, ex),
        )
        bottom = a == 0
        return (ex, ey) + tuple(jnp.where(bottom, one, two) for one, two in zip(at_bottom, inside))

    def group(self, a, carry, emit):
        ex, ey, hx_z, hy_z = carry
        for b in range(ROWS):
            z = ROWS * a + b
            ez = self.field(0, 2, a, b)
            if b < ROWS - 1:
                ex_next, ey_next = (self.field(0, c, a, b + 1) for c in range(2))
            else:
                end = a == self.groups - 1
                after = jnp.minimum(a + 1, self.groups - 1)
                ex_next, ey_next = (
                    jnp.where(end, self.above[c], self.field(0, c, after, 0)) for c in range(2)
                )
            hx = self.hx(a, b, ey, ez, ey_next)
            hy = self.hy(a, b, ex, ez, ex_next)
            hz = self.hz(a, b, ex, ey)
            hy_x = self.x_down(hy, self.line(self.left_wide, z) + HALF * ez)
            hz_x = self.x_down(hz, self.line(self.left_wide, self.cells_z + z) - HALF * ey)
            curl = (
                (hz - self.y_down(hz)) - (hy - hy_z),
                (hx - hx_z) - (hz - hz_x),
                (hy - hy_x) - (hx - self.y_down(hx)),
            )
            emit(a, b, (ex, ey, ez), (hx, hy, hz), curl)
            ex, ey, hx_z, hy_z = ex_next, ey_next, hx, hy
        return ex, ey, hx_z, hy_z

    def gradient(self, f_ref, inv_ref, grad_ref, mask_ref, store):
        layers = grad_ref.shape[0]
        first = first_layer(self.cells_z, layers)
        first_group = first // ROWS
        mask = self.wider(lambda s: mask_ref[:, s], self.grad_base, 5)

        def emit(a, b, efield, hfield, curl):
            z = ROWS * a + b
            tile = self.grad_base + self.per_group * (a - first_group)

            def wider(load, which):
                slot = 6 * b + which
                return self.wider(load, tile + slot // SLOTS, slot % SLOTS)

            half_inv = wider(lambda s: inv_ref[z, :, s], 3)
            total = None
            for c in range(3):
                term = wider(lambda s: f_ref[c, z, :, s], c) * (efield[c] + half_inv * curl[c])
                total = term if total is None else total + term
            store(z - first, wider(lambda s: grad_ref[z - first, :, s], 4) + mask * total)

        def body(i, carry):
            return self.group(first_group + i, carry, emit)

        lax.fori_loop(0, layers // ROWS, body, self.start(first_group))


def fields_scratch(mode, xface, yface, width):
    rows, wide = xface.shape[0], faces_wide(mode, width)
    out = [pltpu.VMEM((rows, wide), jnp.float32)] * 2
    if mode != OWN:
        out.append(pltpu.VMEM((2,) + yface.shape, jnp.float32))
    return out


def own_gradient_kernel(counts, *refs):
    e_ref, h_ref, f_ref, inv_ref, grad_ref, mask_ref = refs[:6]
    zfaces, xfaces = refs[6 : 6 + counts[0]], refs[6 + counts[0] : 6 + sum(counts)]
    grad_out, scratch = refs[6 + sum(counts)], refs[7 + sum(counts) :]
    fields = Fields(OWN, grad_ref.shape[0], e_ref, h_ref, zfaces, xfaces, None, scratch)

    def store(layer, value):
        grad_out[layer] = value

    fields.gradient(f_ref, inv_ref, grad_ref, mask_ref, store)


def own_gradient(arrays, zfaces, xfaces):
    grad_sum = arrays[4]
    return pl.pallas_call(
        functools.partial(own_gradient_kernel, (len(zfaces), len(xfaces))),
        in_specs=[VMEM] * (6 + len(zfaces) + len(xfaces)),
        out_specs=VMEM,
        out_shape=f32(*grad_sum.shape),
        scratch_shapes=fields_scratch(OWN, xfaces[0], None, grad_sum.shape[2]),
        compiler_params=params(),
    )(*arrays, *zfaces, *xfaces)


def edge_gradient_kernel(counts, per_device, *refs):
    own_ref, e_ref, h_ref, f_ref, inv_ref, grad_ref, mask_ref = refs[:7]
    ends = np.cumsum((7,) + counts)
    zfaces, xfaces, yfaces = (refs[i:j] for i, j in zip(ends[:-1], ends[1:]))
    sends, scratch, edge_ref = refs[ends[-1] : -4], refs[-4:-1], refs[-1]
    layers, _, width = grad_ref.shape
    lane = lax.broadcasted_iota(jnp.int32, (ROWS, LANES), 1)
    me = lax.axis_index("gx")
    fields = Fields(EDGE, layers, e_ref, h_ref, zfaces, xfaces, yfaces, scratch)

    def store(layer, value):
        edge_ref[layer] = value

    fields.gradient(f_ref, inv_ref, grad_ref, mask_ref, store)

    for k, send_ref in enumerate(sends):
        chunk = lax.bitwise_xor(me, k)
        packed = jnp.zeros((ROWS, LANES), jnp.float32)
        for i in range(per_device):
            layer = chunk * per_device + i
            edge = edge_ref[layer]
            at = i * width
            head, tail = own_ref[layer, :, 0:LANES], own_ref[layer, :, width - LANES :]
            send_ref[:, at : at + LANES] = jnp.where(lane == 0, pltpu.roll(edge, LANES - STRIP, 1), head)
            send_ref[:, at + LANES : at + width - LANES] = own_ref[layer, :, LANES : width - LANES]
            send_ref[:, at + width - LANES : at + width] = jnp.where(
                lane == LANES - 1, pltpu.roll(edge, STRIP, 1), tail
            )
            side = pltpu.roll(edge, (2 * STRIP * i + STRIP) % LANES, 1)
            packed = jnp.where(lane // (2 * STRIP) == i, side, packed)
        send_ref[:, per_device * width :] = packed


def edge_gradient(own, arrays, zfaces, xfaces, yfaces):
    layers, _, width = own.shape
    count = lax.axis_size("gx")
    per_device = layers // count
    faces = (*zfaces, *xfaces, *yfaces)
    return pl.pallas_call(
        functools.partial(edge_gradient_kernel, (len(zfaces), len(xfaces), len(yfaces)), per_device),
        in_specs=[VMEM] * (7 + len(faces)),
        out_specs=[VMEM] * count,
        out_shape=[f32(ROWS, per_device * width + LANES)] * count,
        scratch_shapes=fields_scratch(EDGE, xfaces[0], yfaces[0], width)
        + [pltpu.VMEM((layers, ROWS, LANES), jnp.float32)],
        compiler_params=params(),
    )(own, *arrays, *faces)


def step_kernel(counts, layers, *refs):
    e_ref, h_ref, inv_ref = refs[:3]
    ends = np.cumsum((3,) + counts)
    zfaces, xfaces, yfaces, shares = (refs[i:j] for i, j in zip(ends[:-1], ends[1:]))
    (e_out, h_out, grad_out), scratch, carry_ref = refs[ends[-1] : -4], refs[-4:-1], refs[-1]
    width = e_ref.shape[3]
    fields = Fields(CIRCLE, layers, e_ref, h_ref, zfaces, xfaces, yfaces, scratch)
    a = pl.program_id(0)

    def emit(a, b, efield, hfield, curl):
        half_inv = inv_ref[ROWS * a + b]
        for c in range(3):
            e_out[c, b] = efield[c][:, :width] + half_inv * curl[c][:, :width]
            h_out[c, b] = hfield[c][:, :width]

    @pl.when(a == 0)
    def _():
        for i, v in enumerate(fields.start(0)):
            carry_ref[i] = v
        per_device = layers // len(shares)
        me = lax.axis_index("gx")
        for k, share in enumerate(shares):
            chunk = lax.bitwise_xor(me, k)
            for i in range(per_device):
                grad_out[chunk * per_device + i] = share[:, i * width : (i + 1) * width]

    carry = tuple(carry_ref[i] for i in range(4))
    for i, v in enumerate(fields.group(a, carry, emit)):
        carry_ref[i] = v


def step(efield, hfield, inv, zfaces, xfaces, yfaces, shares, layers):
    _, cells_z, _, width = efield.shape
    block = pl.BlockSpec((3, ROWS, ROWS, width), lambda a: (0, a, 0, 0))
    groups = (zfaces, xfaces, yfaces, shares)
    counts = tuple(len(group) for group in groups)
    return pl.pallas_call(
        functools.partial(step_kernel, counts, layers),
        grid=(cells_z // ROWS,),
        in_specs=[VMEM] * (3 + sum(counts)),
        out_specs=[block, block, VMEM],
        out_shape=[f32(*efield.shape)] * 2 + [f32(layers, ROWS, width)],
        scratch_shapes=fields_scratch(CIRCLE, xfaces[0], yfaces[0], width)
        + [pltpu.VMEM((4, ROWS, width + LANES), jnp.float32)],
        compiler_params=params(),
    )(efield, hfield, inv, *(one for group in groups for one in group))


def cone_matrix(rows):
    span = np.arange(-RADIUS, RADIUS + 1, dtype=np.float64)
    cone = np.maximum(RADIUS - np.sqrt(span[:, None] ** 2 + span[None, :] ** 2), 0.0)
    weight = cone / cone.sum()
    x = np.arange(rows)
    out = np.zeros((RADIUS + 1, rows, rows))
    for b in range(RADIUS + 1):
        for apart in (x[:, None] - x[None, :], 2 * rows - 1 - x[:, None] - x[None, :]):
            near = np.abs(apart) <= RADIUS
            out[b] += np.where(near, weight[np.clip(apart, -RADIUS, RADIUS) + RADIUS, RADIUS + b], 0.0)
    out = out.reshape((RADIUS + 1) * rows, rows).astype(np.float32)
    high = out.astype(jnp.bfloat16)
    low = (out - high.astype(np.float32)).astype(jnp.bfloat16)
    return np.concatenate([high, low, high], axis=1)


def flip_rows(v):
    row = lax.broadcasted_iota(jnp.int32, v.shape, 0)
    v = pltpu.roll(v, 4, 0)
    v = jnp.where(row % 4 < 2, pltpu.roll(v, ROWS - 2, 0), pltpu.roll(v, 2, 0))
    return jnp.where(row % 2 < 1, pltpu.roll(v, ROWS - 1, 0), pltpu.roll(v, 1, 0))


def filter_kernel(count, per_device, width, *refs):
    taps_ref = refs[0]
    got = refs[1 : 1 + count]
    outs = refs[1 + count : 1 + 2 * count]
    slabs, parts, done = refs[1 + 2 * count :]
    me = lax.axis_index("gx")
    wide = width + LANES
    half = count // 2
    rows = half * ROWS
    lane = lax.broadcasted_iota(jnp.int32, (ROWS, LANES), 1)
    for k in range(count):
        slabs[lax.bitwise_xor(me, k)] = got[k][...]

    def layer_of(slab, i):
        edge = slabs[slab, :, per_device * width :]
        at = 2 * STRIP * i
        upper = pltpu.roll(edge, (LANES - at) % LANES, 1) if at else edge
        lower = pltpu.roll(edge, (LANES - 2 * STRIP - at) % LANES, 1)
        side = jnp.where(lane < STRIP, upper, lower)
        return jnp.concatenate([slabs[slab, :, i * width : (i + 1) * width], side], axis=1)

    for i in range(per_device):
        halves = [layer_of(s, i) + flip_rows(layer_of(count - 1 - s, i)) for s in range(half)]
        symmetric = jnp.concatenate(halves, axis=0)
        high = symmetric.astype(jnp.bfloat16)
        low = (symmetric - high.astype(jnp.float32)).astype(jnp.bfloat16)
        parts[0:rows, :] = high
        parts[rows : 2 * rows, :] = high
        parts[2 * rows : 3 * rows, :] = low
        mixed = jnp.dot(taps_ref[...], parts[...], preferred_element_type=jnp.float32)
        total = mixed[0:rows]
        for b in range(1, RADIUS + 1):
            part = mixed[b * rows : (b + 1) * rows]
            total = total + (pltpu.roll(part, b, 1) + pltpu.roll(part, wide - b, 1))
        for s in range(half):
            own = total[s * ROWS : (s + 1) * ROWS, :width]
            done[s, i] = own
            done[count - 1 - s, i] = flip_rows(own)
    for k in range(count):
        outs[k][...] = done[lax.bitwise_xor(me, k)]


def cone_filter(got, per_device, width):
    count = len(got)
    rows = count // 2 * ROWS
    taps = jnp.asarray(cone_matrix(rows))
    return pl.pallas_call(
        functools.partial(filter_kernel, count, per_device, width),
        in_specs=[VMEM] * (1 + count),
        out_specs=[VMEM] * count,
        out_shape=[f32(per_device, ROWS, width)] * count,
        scratch_shapes=[
            pltpu.VMEM((count, ROWS, per_device * width + LANES), jnp.float32),
            pltpu.VMEM((3 * rows, width + LANES), jnp.bfloat16),
            pltpu.VMEM((count, per_device, ROWS, width), jnp.float32),
        ],
        compiler_params=params(),
    )(taps, *got)


def place_kernel(count, per_device, *refs):
    out, sems = refs[count], refs[count + 1]
    copies = []
    for k in range(count):
        at = lax.bitwise_xor(lax.axis_index("gx"), k) * per_device
        copies.append(pltpu.make_async_copy(refs[k], out.at[pl.ds(at, per_device)], sems.at[k]))
    for copy in copies:
        copy.start()
    for copy in copies:
        copy.wait()


def place_layers(parts):
    count = len(parts)
    per_device, rows, width = parts[0].shape
    return pl.pallas_call(
        functools.partial(place_kernel, count, per_device),
        in_specs=[ANY] * count,
        out_specs=ANY,
        out_shape=f32(count * per_device, rows, width),
        scratch_shapes=[pltpu.SemaphoreType.DMA((count,))],
        compiler_params=params(),
    )(*parts)


def spread(parts):
    count = len(parts)
    return [parts[0]] + [
        lax.ppermute(parts[k], "gx", [(i, i ^ k) for i in range(count)]) for k in range(1, count)
    ]


def on_device(efield, hfield, forward, material, permit, design_mask, grad_sum):
    layers, _, width = grad_sum.shape
    zfaces = exchange(z_faces(efield, hfield), "gz")
    xfaces = exchange(x_faces(efield, hfield, zfaces), "gx")
    own_low, own_high, mask, inv = y_own(permit, efield, hfield, forward, material, grad_sum, design_mask)
    arrays = (efield, hfield, forward, inv, grad_sum, mask)
    yfaces = exchange(y_faces(own_low, own_high, zfaces, xfaces), "gy", wrap=True)
    own = own_gradient(arrays, zfaces, xfaces)
    shares = edge_gradient(own, arrays, zfaces, xfaces, yfaces)
    got = spread(shares)
    e_next, h_next, grad_total = step(efield, hfield, inv, zfaces, xfaces, yfaces, shares, layers)
    filtered = spread(cone_filter(got, layers // len(got), width))
    return e_next, h_next, grad_total, place_layers(filtered)


def solution(mesh):
    field = P(None, "gz", "gx", "gy")
    cells = P("gz", "gx", "gy")
    return jax.shard_map(
        on_device,
        mesh=mesh,
        in_specs=(field, field, field, cells, P(), P("gx", "gy"), cells),
        out_specs=(field, field, cells, cells),
        check_vma=False,
    )
```

time: 49.2 us -> 48.4 us (0.984)
  Pallas kernels: 14.3 us -> 9.97 us
  local copies, waits for them, and re-layouts: 2.6 us -> 4.28 us
  other arithmetic: 0.08 us -> 1.65 us
  starting transfers between devices: 19.3 us -> 19.9 us
    pallas_call x5, Pallas kernels: 10.4 us -> 7.17 us  [the longest x1 3.6 us: step(): pl.pallas_call(functools.partial(step_kernel, counts, layers), grid=(cell...]
    ppermute x5, waiting for transfers between devices: 5.69 us -> 3.95 us  [swap_pairs(): return lax.ppermute(value, axis, pairs + [(b, a) for a, b in pairs])]
    ppermute x6, waiting for transfers between devices: 6.14 us -> 7.5 us  [spread(): lax.ppermute(parts[k], 'gx', [(i, i ^ k) for i in range(count)])]
    unnamed x18, local copies, waits for them, and re-layouts: 2.58 us -> 3.56 us
    sub x0 -> x1, other arithmetic: none -> 0.84 us  [z_faces(): hfield[0, top] + HALF * ez - HALF * ey]
    select_n x0 -> x1, other arithmetic: none -> 0.82 us  [sends(): both = [jnp.where(self.odd, low, high)]]
    ppermute x6, starting transfers between devices: 11.2 us -> 12 us  [spread(): lax.ppermute(parts[k], 'gx', [(i, i ^ k) for i in range(count)])]
    squeeze x1, local copies, waits for them, and re-layouts: 0.02 us -> 0.72 us  [z_faces(): ex, ey, ez = (efield[c, top] for c in range(3))]
  transfers between devices with their start and end apart: 11 -> 11, of which waited for: 6 -> 6; matrix products, arithmetic and copies ran while one was open for 0% -> 0% of each run, Pallas kernels for 10% -> 11%
where the time goes in v2:
time: 48.4 us; the launch traced here: 48.1 us
  starting transfers between devices  19.9 us (41%)
  waiting for transfers between devices  11.5 us (24%)
  Pallas kernels  9.97 us (21%)
  local copies, waits for them, and re-layouts  4.28 us (9%)
  other arithmetic  1.65 us (3%)
  between operations  0.8 us (2%)
    ppermute x6, starting transfers between devices, spread(): lax.ppermute(parts[k], 'gx', [(i, i ^ k) for i in range(count)])  12 us
    ppermute x5, starting transfers between devices, swap_pairs(): return lax.ppermute(value, axis, pairs + [(b, a) for a, b in pairs])  7.89 us
    ppermute x6, waiting for transfers between devices, spread(): lax.ppermute(parts[k], 'gx', [(i, i ^ k) for i in range(count)])  7.5 us
    ppermute x5, waiting for transfers between devices, swap_pairs(): return lax.ppermute(value, axis, pairs + [(b, a) for a, b in pairs])  3.95 us
    pallas_call x1, Pallas kernels, step(): pl.pallas_call(functools.partial(step_kernel, counts, layers), grid=(cell...  3.6 us
    unnamed x18, local copies, waits for them, and re-layouts  3.56 us
    pallas_call x1, Pallas kernels, edge_gradient(): pl.pallas_call(functools.partial(edge_gradient_kernel, (len(zfaces), len(...  2.49 us
    pallas_call x1, Pallas kernels, y_own(): pl.pallas_call(y_own_kernel, in_specs=[SMEM] + [VMEM] * 6, out_specs=[VME...  1.08 us
  transfers between devices with their start and end apart: 11, of which 6 were waited for; matrix products, arithmetic and copies ran while one was open for 0% of the time, Pallas kernels for 11%

profile of v2, /device:TPU:0, one launch (start us, length us, event | category | flops | bytes accessed | tf_op | source)
XLA Modules:
  0.0 48.1 jit_solution(7636613340998507196)
XLA Ops:
  0.6 0.7 %slice_bitcast_fusion = f32[1,8,512]{2,1,0:T(8,128)S(1)} fusion(f32[3,24,8,512]{3,2,1,0:T(8,128)} %refs_0_.6), kind=kLoop, calls=%fused_computation.4 | loop fusion | bytes 32768 | tf_op jit(solution)/shard_map/squeeze | solution.py:83
  1.4 0.0 copy-start.4
  1.4 0.8 %bitcast_subtract_fusion.1 = (f32[1,8,512]{2,1,0:T(8,128)S(1)}, f32[1,8,512]{2,1,0:T(8,128)S(1)}) fusion(f32[3,24,8,512]{3,2,1,0:T(8,128)} %refs_0_.6, f32[3,24,8,512]{3,2,1,0:T(8,128)} %refs_1_.7), kind=kLoop, calls=%fused_computation.2 | loop fusion | flops 28672 | bytes 114688 | tf_op jit(solution)/shard_map/sub | solution.py:86
  2.2 0.0 copy-start.7
  2.2 0.0 copy-start.8
  2.2 0.8 %maximum_select_fusion = f32[3,8,512]{2,1,0:T(8,128)S(1)} fusion(f32[1,8,512]{2,1,0:T(8,128)S(1)} %slice_bitcast_fusion, f32[1,8,512]{2,1,0:T(8,128)S(1)} %get-tuple-element.43, f32[1,8,512]{2,1,0:T(8,128)S(1)} %get-tuple-element.42, f32[3,24,8,512]{3,2,1,0:T(8,128)} %refs_0_.6, pred[]{:T(512)S(6)} %eq.5), kind=kLoop, calls=%fused_computation | loop fusion | flops 36864 | bytes 147457 | tf_op jit(solution)/shard_map/jit(_where)/select_n | solution.py:65
  3.1 3.0 %collective-permute-start = (f32[3,8,512]{2,1,0:T(8,128)S(1)}, f32[3,8,512]{2,1,0:T(8,128)S(1)}, u32[]{:S(2)}, u32[]{:S(2)}) collective-permute-start(f32[3,8,512]{2,1,0:T(8,128)S(1)} %maximum_select_fusion), channel_id=1, source_target_pairs={{0,1},{1,0},{2,3},{3,2},{4,5},{5,4},{6,7},{7,6},{8,9},{9,8},{10,11... | collective-permute-start | bytes 147464 | tf_op jit(solution)/shard_map/ppermute | solution.py:36
  6.0 2.1 %collective-permute-done.refs_2_.refs_6_.refs_7_.refs_3_ = f32[3,8,512]{2,1,0:T(8,128)S(1)} collective-permute-done((f32[3,8,512]{2,1,0:T(8,128)S(1)}, f32[3,8,512]{2,1,0:T(8,128)S(1)}, u32[]{:S(2)}, u32[]{:S(2)}) %collective-permute-start) | collective-permute-done | bytes 49184 | tf_op jit(solution)/shard_map/ppermute | solution.py:36
  8.1 0.0 copy-start
  8.1 1.3 %copy-done = f32[3,24,8,512]{3,2,1,0:T(8,128)S(1)} copy-done((f32[3,24,8,512]{3,2,1,0:T(8,128)S(1)}, f32[3,24,8,512]{3,2,1,0:T(8,128)}, u32[]{:S(2)}) %copy-start) | copy-done | bytes 1179672
  9.4 1.3 %copy-done.2 = f32[3,24,8,512]{3,2,1,0:T(8,128)S(1)} copy-done((f32[3,24,8,512]{3,2,1,0:T(8,128)S(1)}, f32[3,24,8,512]{3,2,1,0:T(8,128)}, u32[]{:S(2)}) %copy-start.2) | copy-done | bytes 1179672
  10.6 0.1 shard_map.112
  10.8 2.1 %collective-permute-start.1 = (f32[72,512]{1,0:T(8,128)S(1)}, f32[72,512]{1,0:T(8,128)S(1)}, u32[]{:S(2)}, u32[]{:S(2)}) collective-permute-start(f32[72,512]{1,0:T(8,128)S(1)} %get-tuple-element.24), channel_id=1, source_target_pairs={{0,8},{16,24},{8,0},{24,16},{1,9},{17,25},{9,1},{25,17},{2,10},{18... | collective-permute-start | bytes 442376 | tf_op jit(solution)/shard_map/ppermute | solution.py:36
  12.9 0.7 %collective-permute-start.2 = (f32[72,512]{1,0:T(8,128)S(1)}, f32[72,512]{1,0:T(8,128)S(1)}, u32[]{:S(2)}, u32[]{:S(2)}) collective-permute-start(f32[72,512]{1,0:T(8,128)S(1)} %get-tuple-element.25), channel_id=1, source_target_pairs={{8,16},{16,8},{9,17},{17,9},{10,18},{18,10},{11,19},{19,11},{12,20... | collective-permute-start | bytes 442376 | tf_op jit(solution)/shard_map/ppermute | solution.py:36
  13.6 0.0 copy-done.4
  13.6 0.0 copy-done.7
  13.6 0.0 copy-done.8
  13.6 0.0 copy-done.1
  13.6 0.0 copy-done.3
  13.6 0.0 copy-start.5
  13.6 1.0 %copy-done.5 = s32[24,8,512]{2,1,0:T(8,128)S(1)} copy-done((s32[24,8,512]{2,1,0:T(8,128)S(1)}, s32[24,8,512]{2,1,0:T(8,128)}, u32[]{:S(2)}) %copy-start.5) | copy-done | bytes 393240
  14.6 1.1 %shard_map.111 = (f32[15,8,128]{2,1,0:T(8,128)S(1)}, f32[15,8,128]{2,1,0:T(8,128)S(1)}, f32[8,512]{1,0:T(8,128)S(1)}, f32[24,8,512]{2,1,0:T(8,128)S(1)}) custom-call(f32[4]{0:T(128)S(1)} %copy-done.7, f32[3,24,8,512]{3,2,1,0:T(8,128)S(1)} %copy-done.1, f32[3,24,8,512]{3,2,1,0:T(8,128)S(1)} %copy-done.2, f32[3,24,8,512]{3,2,1,0:T(8,128)S(1)} %copy-done.3, ...), custom_call_target="tpu_custom_call" | custom-call | tf_op jit(solution)/shard_map/pallas_call | solution.py:203
  15.7 0.3 collective-permute-done.1.refs_3_.refs_7_.refs_8_.refs_4_
  16.0 0.0 collective-permute-done.2.refs_4_.refs_8_.refs_9_.refs_5_
  16.0 0.1 shard_map.113
  16.2 0.1 collective-permute-start.3
  16.2 2.1 %collective-permute-start.4 = (f32[17,8,128]{2,1,0:T(8,128)S(1)}, f32[17,8,128]{2,1,0:T(8,128)S(1)}, u32[]{:S(2)}, u32[]{:S(2)}) collective-permute-start(f32[17,8,128]{2,1,0:T(8,128)S(1)} %get-tuple-element.29), channel_id=1, source_target_pairs={{2,4},{0,6},{4,2},{6,0},{3,5},{1,7},{5,3},{7,1},{10,12},{8,14},{12... | collective-permute-start | bytes 208904 | tf_op jit(solution)/shard_map/ppermute | solution.py:36
  18.3 0.8 %shard_map.114.refs_0_ = f32[16,8,512]{2,1,0:T(8,128)S(1)} custom-call(f32[3,24,8,512]{3,2,1,0:T(8,128)S(1)} %copy-done.1, f32[3,24,8,512]{3,2,1,0:T(8,128)S(1)} %copy-done.2, f32[3,24,8,512]{3,2,1,0:T(8,128)S(1)} %copy-done.3, f32[24,8,512]{2,1,0:T(8,128)S(1)} %get-tuple-element.23.refs_3_.refs_4_.refs_2_, f32[16,8,512]{2,1,0:T(8,128)S(1)} %copy-done.4, ...), custom_call_target="tpu_custom_call" | custom-call | tf_op jit(solution)/shard_map/pallas_call | solution.py:436
  19.1 0.0 copy-start.6
  19.1 0.0 collective-permute-done.3.refs_10_.refs_6_
  19.2 1.6 %collective-permute-done.4.refs_11_.refs_7_ = f32[17,8,128]{2,1,0:T(8,128)S(1)} collective-permute-done((f32[17,8,128]{2,1,0:T(8,128)S(1)}, f32[17,8,128]{2,1,0:T(8,128)S(1)}, u32[]{:S(2)}, u32[]{:S(2)}) %collective-permute-start.4) | collective-permute-done | bytes 69664 | tf_op jit(solution)/shard_map/ppermute | solution.py:36
  20.7 2.5 %shard_map.115 = (f32[8,2176]{1,0:T(8,128)S(1)}, f32[8,2176]{1,0:T(8,128)S(1)}, f32[8,2176]{1,0:T(8,128)S(1)}, f32[8,2176]{1,0:T(8,128)S(1)}) custom-call(f32[16,8,512]{2,1,0:T(8,128)S(1)} %shard_map.114.refs_0_, f32[3,24,8,512]{3,2,1,0:T(8,128)S(1)} %copy-done.1, f32[3,24,8,512]{3,2,1,0:T(8,128)S(1)} %copy-done.2, f32[3,24,8,512]{3,2,1,0:T(8,128)S(1)} %copy-done.3, ...), custom_call_target="tpu_custom_call" | custom-call | tf_op jit(solution)/shard_map/pallas_call | solution.py:484
  23.2 4.6 %collective-permute-start.5 = (f32[8,2176]{1,0:T(8,128)S(1)}, f32[8,2176]{1,0:T(8,128)S(1)}, u32[]{:S(2)}, u32[]{:S(2)}) collective-permute-start(f32[8,2176]{1,0:T(8,128)S(1)} %get-tuple-element.32.refs_9_), channel_id=1, source_target_pairs={{0,8},{8,0},{16,24},{24,16},{1,9},{9,1},{17,25},{25,17},{2,10},{10... | collective-permute-start | bytes 208904 | tf_op jit(solution)/shard_map/ppermute | solution.py:654
  27.9 1.5 %collective-permute-start.6 = (f32[8,2176]{1,0:T(8,128)S(1)}, f32[8,2176]{1,0:T(8,128)S(1)}, u32[]{:S(2)}, u32[]{:S(2)}) collective-permute-start(f32[8,2176]{1,0:T(8,128)S(1)} %get-tuple-element.33.refs_10_), channel_id=1, source_target_pairs={{0,16},{8,24},{16,0},{24,8},{1,17},{9,25},{17,1},{25,9},{2,18},{10... | collective-permute-start | bytes 208904 | tf_op jit(solution)/shard_map/ppermute | solution.py:654
  29.4 1.4 %collective-permute-start.7 = (f32[8,2176]{1,0:T(8,128)S(1)}, f32[8,2176]{1,0:T(8,128)S(1)}, u32[]{:S(2)}, u32[]{:S(2)}) collective-permute-start(f32[8,2176]{1,0:T(8,128)S(1)} %get-tuple-element.34.refs_11_), channel_id=1, source_target_pairs={{0,24},{8,16},{16,8},{24,0},{1,25},{9,17},{17,9},{25,1},{2,26},{10... | collective-permute-start | bytes 208904 | tf_op jit(solution)/shard_map/ppermute | solution.py:654
  30.8 0.0 collective-permute-done.5.refs_2_
  30.8 3.0 %collective-permute-done.6.refs_3_ = f32[8,2176]{1,0:T(8,128)S(1)} collective-permute-done((f32[8,2176]{1,0:T(8,128)S(1)}, f32[8,2176]{1,0:T(8,128)S(1)}, u32[]{:S(2)}, u32[]{:S(2)}) %collective-permute-start.6) | collective-permute-done | bytes 69664 | tf_op jit(solution)/shard_map/ppermute | solution.py:654
  33.8 2.5 %collective-permute-done.7.refs_4_ = f32[8,2176]{1,0:T(8,128)S(1)} collective-permute-done((f32[8,2176]{1,0:T(8,128)S(1)}, f32[8,2176]{1,0:T(8,128)S(1)}, u32[]{:S(2)}, u32[]{:S(2)}) %collective-permute-start.7) | collective-permute-done | bytes 69664 | tf_op jit(solution)/shard_map/ppermute | solution.py:654
  36.3 0.0 copy-done.6
  36.3 1.0 %shard_map.117 = (f32[4,8,512]{2,1,0:T(8,128)S(1)}, f32[4,8,512]{2,1,0:T(8,128)S(1)}, f32[4,8,512]{2,1,0:T(8,128)S(1)}, f32[4,8,512]{2,1,0:T(8,128)S(1)}) custom-call(bf16[112,48]{1,0:T(8,128)(2,1)S(1)} %copy-done.6, f32[8,2176]{1,0:T(8,128)S(1)} %get-tuple-element.31.refs_8_.refs_1_, f32[8,2176]{1,0:T(8,128)S(1)} %collective-permute-done.5.refs_2_, ...), custom_call_target="tpu_custom_call" | custom-call | tf_op jit(solution)/shard_map/pallas_call | solution.py:612
  37.3 1.9 %collective-permute-start.8 = (f32[4,8,512]{2,1,0:T(8,128)S(1)}, f32[4,8,512]{2,1,0:T(8,128)S(1)}, u32[]{:S(2)}, u32[]{:S(2)}) collective-permute-start(f32[4,8,512]{2,1,0:T(8,128)S(1)} %get-tuple-element.39), channel_id=1, source_target_pairs={{0,8},{8,0},{16,24},{24,16},{1,9},{9,1},{17,25},{25,17},{2,10},{10... | collective-permute-start | bytes 196616 | tf_op jit(solution)/shard_map/ppermute | solution.py:654
  39.2 1.2 %collective-permute-start.9 = (f32[4,8,512]{2,1,0:T(8,128)S(1)}, f32[4,8,512]{2,1,0:T(8,128)S(1)}, u32[]{:S(2)}, u32[]{:S(2)}) collective-permute-start(f32[4,8,512]{2,1,0:T(8,128)S(1)} %get-tuple-element.40), channel_id=1, source_target_pairs={{0,16},{8,24},{16,0},{24,8},{1,17},{9,25},{17,1},{25,9},{2,18},{10... | collective-permute-start | bytes 196616 | tf_op jit(solution)/shard_map/ppermute | solution.py:654
  40.4 1.4 %collective-permute-start.10 = (f32[4,8,512]{2,1,0:T(8,128)S(1)}, f32[4,8,512]{2,1,0:T(8,128)S(1)}, u32[]{:S(2)}, u32[]{:S(2)}) collective-permute-start(f32[4,8,512]{2,1,0:T(8,128)S(1)} %get-tuple-element.41), channel_id=1, source_target_pairs={{0,24},{8,16},{16,8},{24,0},{1,25},{9,17},{17,9},{25,1},{2,26},{10... | collective-permute-start | bytes 196616 | tf_op jit(solution)/shard_map/ppermute | solution.py:654
  41.8 3.6 %shard_map.116 = (f32[3,24,8,512]{3,2,1,0:T(8,128)}, f32[3,24,8,512]{3,2,1,0:T(8,128)}, f32[16,8,512]{2,1,0:T(8,128)}) custom-call(f32[3,24,8,512]{3,2,1,0:T(8,128)S(1)} %copy-done.1, f32[3,24,8,512]{3,2,1,0:T(8,128)S(1)} %copy-done.2, f32[24,8,512]{2,1,0:T(8,128)S(1)} %get-tuple-element.23.refs_3_.refs_4_.refs_2_, ...), custom_call_target="tpu_custom_call" | custom-call | tf_op jit(solution)/shard_map/pallas_call | solution.py:531
  45.4 0.0 collective-permute-done.8.refs_1_
  45.4 2.0 %collective-permute-done.9.refs_2_ = f32[4,8,512]{2,1,0:T(8,128)S(1)} collective-permute-done((f32[4,8,512]{2,1,0:T(8,128)S(1)}, f32[4,8,512]{2,1,0:T(8,128)S(1)}, u32[]{:S(2)}, u32[]{:S(2)}) %collective-permute-start.9) | collective-permute-done | bytes 65568 | tf_op jit(solution)/shard_map/ppermute | solution.py:654
  47.4 0.0 collective-permute-done.10.refs_3_
  47.4 0.7 %shard_map.118 = f32[16,8,512]{2,1,0:T(8,128)} custom-call(f32[4,8,512]{2,1,0:T(8,128)S(1)} %get-tuple-element.38.refs_0_, f32[4,8,512]{2,1,0:T(8,128)S(1)} %collective-permute-done.8.refs_1_, f32[4,8,512]{2,1,0:T(8,128)S(1)} %collective-permute-done.9.refs_2_, f32[4,8,512]{2,1,0:T(8,128)S(1)} %collective-permute-done.10.refs_3_), custom_call_target="tpu_custom_call" | custom-call | tf_op jit(solution)/shard_map/pallas_call | solution.py:641
  (3 shorter events, 0.0 us)
Async XLA Ops:
  1.4 12.2 %copy-start.4 = (f32[16,8,512]{2,1,0:T(8,128)S(1)}, f32[16,8,512]{2,1,0:T(8,128)}, u32[]{:S(2)}) copy-start(f32[16,8,512]{2,1,0:T(8,128)} %refs_5_.1) | copy-start | bytes 786436
  2.2 11.4 %copy-start.7 = (f32[4]{0:T(128)S(1)}, f32[4]{0:T(128)}, u32[]{:S(2)}) copy-start(f32[4]{0:T(128)} %permit_ref.1) | copy-start | bytes 52
  2.2 11.4 %copy-start.8 = (s32[1,64]{1,0:T(1,128)S(1)}, s32[1,64]{1,0:T(1,128)}, u32[]{:S(2)}) copy-start(s32[1,64]{1,0:T(1,128)} %mask_ref.1) | copy-start | bytes 772
  3.1 5.0 %collective-permute-start = (f32[3,8,512]{2,1,0:T(8,128)S(1)}, f32[3,8,512]{2,1,0:T(8,128)S(1)}, u32[]{:S(2)}, u32[]{:S(2)}) collective-permute-start(f32[3,8,512]{2,1,0:T(8,128)S(1)} %maximum_select_fusion), channel_id=1, source_target_pairs={{0,1},{1,0},{2,3},{3,2},{4,5},{5,4},{6,7},{7,6},{8,9},{9,8},{10,11... | collective-permute-start | bytes 147464 | tf_op jit(solution)/shard_map/ppermute | solution.py:36
  8.1 1.3 %copy-start = (f32[3,24,8,512]{3,2,1,0:T(8,128)S(1)}, f32[3,24,8,512]{3,2,1,0:T(8,128)}, u32[]{:S(2)}) copy-start(f32[3,24,8,512]{3,2,1,0:T(8,128)} %refs_0_.6) | copy-start | bytes 3538948
  9.4 1.3 %copy-start.2 = (f32[3,24,8,512]{3,2,1,0:T(8,128)S(1)}, f32[3,24,8,512]{3,2,1,0:T(8,128)}, u32[]{:S(2)}) copy-start(f32[3,24,8,512]{3,2,1,0:T(8,128)} %refs_1_.7) | copy-start | bytes 3538948
  10.6 3.0 %copy-start.1 = (f32[3,24,8,512]{3,2,1,0:T(8,128)S(1)}, f32[3,24,8,512]{3,2,1,0:T(8,128)}, u32[]{:S(2)}) copy-start(f32[3,24,8,512]{3,2,1,0:T(8,128)} %refs_0_.6) | copy-start | bytes 3538948
  10.6 3.0 %copy-start.3 = (f32[3,24,8,512]{3,2,1,0:T(8,128)S(1)}, f32[3,24,8,512]{3,2,1,0:T(8,128)}, u32[]{:S(2)}) copy-start(f32[3,24,8,512]{3,2,1,0:T(8,128)} %refs_3_.1) | copy-start | bytes 3538948
  10.8 5.3 %collective-permute-start.1 = (f32[72,512]{1,0:T(8,128)S(1)}, f32[72,512]{1,0:T(8,128)S(1)}, u32[]{:S(2)}, u32[]{:S(2)}) collective-permute-start(f32[72,512]{1,0:T(8,128)S(1)} %get-tuple-element.24), channel_id=1, source_target_pairs={{0,8},{16,24},{8,0},{24,16},{1,9},{17,25},{9,1},{25,17},{2,10},{18... | collective-permute-start | bytes 442376 | tf_op jit(solution)/shard_map/ppermute | solution.py:36
  12.9 3.1 %collective-permute-start.2 = (f32[72,512]{1,0:T(8,128)S(1)}, f32[72,512]{1,0:T(8,128)S(1)}, u32[]{:S(2)}, u32[]{:S(2)}) collective-permute-start(f32[72,512]{1,0:T(8,128)S(1)} %get-tuple-element.25), channel_id=1, source_target_pairs={{8,16},{16,8},{9,17},{17,9},{10,18},{18,10},{11,19},{19,11},{12,20... | collective-permute-start | bytes 442376 | tf_op jit(solution)/shard_map/ppermute | solution.py:36
  13.6 1.0 %copy-start.5 = (s32[24,8,512]{2,1,0:T(8,128)S(1)}, s32[24,8,512]{2,1,0:T(8,128)}, u32[]{:S(2)}) copy-start(s32[24,8,512]{2,1,0:T(8,128)} %mat_ref.1) | copy-start | bytes 1179652
  16.2 3.0 %collective-permute-start.3 = (f32[17,8,128]{2,1,0:T(8,128)S(1)}, f32[17,8,128]{2,1,0:T(8,128)S(1)}, u32[]{:S(2)}, u32[]{:S(2)}) collective-permute-start(f32[17,8,128]{2,1,0:T(8,128)S(1)} %get-tuple-element.28), channel_id=1, source_target_pairs={{0,2},{4,6},{2,0},{6,4},{1,3},{5,7},{3,1},{7,5},{8,10},{12,14},{10... | collective-permute-start | bytes 208904 | tf_op jit(solution)/shard_map/ppermute | solution.py:36
  16.2 4.5 %collective-permute-start.4 = (f32[17,8,128]{2,1,0:T(8,128)S(1)}, f32[17,8,128]{2,1,0:T(8,128)S(1)}, u32[]{:S(2)}, u32[]{:S(2)}) collective-permute-start(f32[17,8,128]{2,1,0:T(8,128)S(1)} %get-tuple-element.29), channel_id=1, source_target_pairs={{2,4},{0,6},{4,2},{6,0},{3,5},{1,7},{5,3},{7,1},{10,12},{8,14},{12... | collective-permute-start | bytes 208904 | tf_op jit(solution)/shard_map/ppermute | solution.py:36
  19.1 17.1 %copy-start.6 = (bf16[112,48]{1,0:T(8,128)(2,1)S(1)}, bf16[112,48]{1,0:T(8,128)(2,1)}, u32[]{:S(2)}) copy-start(bf16[112,48]{1,0:T(8,128)(2,1)} %constant.22.clone.refs_0_) | copy-start | bytes 32260
  23.2 7.6 %collective-permute-start.5 = (f32[8,2176]{1,0:T(8,128)S(1)}, f32[8,2176]{1,0:T(8,128)S(1)}, u32[]{:S(2)}, u32[]{:S(2)}) collective-permute-start(f32[8,2176]{1,0:T(8,128)S(1)} %get-tuple-element.32.refs_9_), channel_id=1, source_target_pairs={{0,8},{8,0},{16,24},{24,16},{1,9},{9,1},{17,25},{25,17},{2,10},{10... | collective-permute-start | bytes 208904 | tf_op jit(solution)/shard_map/ppermute | solution.py:654
  27.9 5.9 %collective-permute-start.6 = (f32[8,2176]{1,0:T(8,128)S(1)}, f32[8,2176]{1,0:T(8,128)S(1)}, u32[]{:S(2)}, u32[]{:S(2)}) collective-permute-start(f32[8,2176]{1,0:T(8,128)S(1)} %get-tuple-element.33.refs_10_), channel_id=1, source_target_pairs={{0,16},{8,24},{16,0},{24,8},{1,17},{9,25},{17,1},{25,9},{2,18},{10... | collective-permute-start | bytes 208904 | tf_op jit(solution)/shard_map/ppermute | solution.py:654
  29.4 6.9 %collective-permute-start.7 = (f32[8,2176]{1,0:T(8,128)S(1)}, f32[8,2176]{1,0:T(8,128)S(1)}, u32[]{:S(2)}, u32[]{:S(2)}) collective-permute-start(f32[8,2176]{1,0:T(8,128)S(1)} %get-tuple-element.34.refs_11_), channel_id=1, source_target_pairs={{0,24},{8,16},{16,8},{24,0},{1,25},{9,17},{17,9},{25,1},{2,26},{10... | collective-permute-start | bytes 208904 | tf_op jit(solution)/shard_map/ppermute | solution.py:654
  37.3 8.1 %collective-permute-start.8 = (f32[4,8,512]{2,1,0:T(8,128)S(1)}, f32[4,8,512]{2,1,0:T(8,128)S(1)}, u32[]{:S(2)}, u32[]{:S(2)}) collective-permute-start(f32[4,8,512]{2,1,0:T(8,128)S(1)} %get-tuple-element.39), channel_id=1, source_target_pairs={{0,8},{8,0},{16,24},{24,16},{1,9},{9,1},{17,25},{25,17},{2,10},{10... | collective-permute-start | bytes 196616 | tf_op jit(solution)/shard_map/ppermute | solution.py:654
  39.2 8.2 %collective-permute-start.9 = (f32[4,8,512]{2,1,0:T(8,128)S(1)}, f32[4,8,512]{2,1,0:T(8,128)S(1)}, u32[]{:S(2)}, u32[]{:S(2)}) collective-permute-start(f32[4,8,512]{2,1,0:T(8,128)S(1)} %get-tuple-element.40), channel_id=1, source_target_pairs={{0,16},{8,24},{16,0},{24,8},{1,17},{9,25},{17,1},{25,9},{2,18},{10... | collective-permute-start | bytes 196616 | tf_op jit(solution)/shard_map/ppermute | solution.py:654
  40.4 7.0 %collective-permute-start.10 = (f32[4,8,512]{2,1,0:T(8,128)S(1)}, f32[4,8,512]{2,1,0:T(8,128)S(1)}, u32[]{:S(2)}, u32[]{:S(2)}) collective-permute-start(f32[4,8,512]{2,1,0:T(8,128)S(1)} %get-tuple-element.41), channel_id=1, source_target_pairs={{0,24},{8,16},{16,8},{24,0},{1,25},{9,17},{17,9},{25,1},{2,26},{10... | collective-permute-start | bytes 196616 | tf_op jit(solution)/shard_map/ppermute | solution.py:654

commit v3 on v2

--- a/solution.py
+++ b/solution.py
@@ -17,15 +17,15 @@
 LANES = 128
 STRIP = 8
 SLOTS = LANES // STRIP
-VMEM_LIMIT = 24 * 1024 * 1024
+MIB = 1024 * 1024
 
 VMEM = pl.BlockSpec(memory_space=pltpu.VMEM)
 SMEM = pl.BlockSpec(memory_space=pltpu.SMEM)
 ANY = pl.BlockSpec(memory_space=pl.ANY)
 
 
-def params():
-    return pltpu.CompilerParams(vmem_limit_bytes=VMEM_LIMIT)
+def params(mib=24):
+    return pltpu.CompilerParams(vmem_limit_bytes=mib * MIB)
 
 
 def f32(*shape):
@@ -78,17 +78,37 @@
     return (cells_z - layers) * (1 - lax.axis_index("gz"))
 
 
+def z_faces_kernel(*refs):
+    e_ref, h_ref = refs[:2]
+    sends, (e_low, e_high, h_high, sems) = refs[2:-4], refs[-4:]
+    top = e_ref.shape[1] - 1
+    copies = [
+        pltpu.make_async_copy(e_ref.at[:, 0], e_low, sems.at[0]),
+        pltpu.make_async_copy(e_ref.at[:, top], e_high, sems.at[1]),
+        pltpu.make_async_copy(h_ref.at[:, top], h_high, sems.at[2]),
+    ]
+    for copy in copies:
+        copy.start()
+    for copy in copies:
+        copy.wait()
+    side = Side("gz")
+    ex, ey, ez = (e_high[c] for c in range(3))
+    high = (h_high[0] + HALF * ez - HALF * ey, h_high[1] + HALF * ex - HALF * ez, ez)
+    for c in range(3):
+        for ref, value in zip(sends, side.sends(e_low[c], high[c])):
+            ref[c] = value
+
+
 def z_faces(efield, hfield):
-    top = efield.shape[1] - 1
-    ex, ey, ez = (efield[c, top] for c in range(3))
-    high = jnp.stack(
-        [
-            hfield[0, top] + HALF * ez - HALF * ey,
-            hfield[1, top] + HALF * ex - HALF * ez,
-            ez,
-        ]
-    )
-    return Side("gz").sends(efield[:, 0], high)
+    face = f32(*efield.shape[:1], *efield.shape[2:])
+    return pl.pallas_call(
+        z_faces_kernel,
+        in_specs=[ANY] * 2,
+        out_specs=[VMEM] * rounds("gz"),
+        out_shape=[face] * rounds("gz"),
+        scratch_shapes=[pltpu.VMEM(face.shape, jnp.float32)] * 3 + [pltpu.SemaphoreType.DMA((3,))],
+        compiler_params=params(60),
+    )(efield, hfield)
 
 
 def x_faces_kernel(z_rounds, *refs):
@@ -163,50 +183,121 @@
         high_ref[first + start // SLOTS] = high
 
 
-def y_own_kernel(
-    permit_ref, e_ref, h_ref, f_ref, mat_ref, grad_ref, mask_ref, low_ref, high_ref, wide_ref, inv_ref
+def load_kernel(
+    permit_ref, e_in, h_in, f_in, mat_in, grad_in, mask_ref,
+    e_ref, h_ref, f_ref, grad_ref, low_ref, high_ref, wide_ref, inv_ref, mat_ref, sems,
 ):
     cells_z, width = e_ref.shape[1], e_ref.shape[3]
     layers = grad_ref.shape[0]
     blocks = mask_ref.shape[1]
+    pairs = [(e_in, e_ref), (h_in, h_ref), (f_in, f_ref)]
+    copies = [[pltpu.make_async_copy(mat_in, mat_ref, sems.at[0])]]
+    copies.append([pltpu.make_async_copy(grad_in, grad_ref, sems.at[1])])
+    for n, (source, target) in enumerate(pairs):
+        copies.append(
+            [pltpu.make_async_copy(source.at[c], target.at[c], sems.at[2 + 3 * n + c]) for c in range(3)]
+        )
+    for group in copies:
+        for copy in group:
+            copy.start()
+
+    spread = (
+        lax.broadcasted_iota(jnp.int32, (blocks, width), 0)
+        == lax.broadcasted_iota(jnp.int32, (blocks, width), 1) // BLOCK
+    ).astype(jnp.float32)
+    mask = jnp.broadcast_to(mask_ref[...].astype(jnp.float32), (ROWS, blocks))
+    wide_ref[...] = jnp.dot(mask, spread, preferred_element_type=jnp.float32)
+
+    def arrived(*groups):
+        for n in groups:
+            for copy in copies[n]:
+                copy.wait()
+
+    arrived(0)
     inverse = [HALF * (1.0 / permit_ref[m]) for m in range(permit_ref.shape[0])]
     for z in range(cells_z):
         inv = jnp.full((ROWS, width), inverse[0])
         for m in range(1, len(inverse)):
             inv = jnp.where(mat_ref[z] == m, inverse[m], inv)
         inv_ref[z] = inv
-    spread = (
-        lax.broadcasted_iota(jnp.int32, (blocks, width), 0)
-        == lax.broadcasted_iota(jnp.int32, (blocks, width), 1) // BLOCK
-    ).astype(jnp.float32)
-    mask = jnp.broadcast_to(mask_ref[...].astype(jnp.float32), (ROWS, blocks))
-    wide_ref[...] = jnp.dot(mask, spread, preferred_element_type=jnp.float32)
+    arrived(1, 2, 3)
     first = first_layer(cells_z, layers)
     tiles = []
     for z in range(cells_z):
         for ref in (e_ref, h_ref):
             for c in range(3):
                 tiles.append((lambda s, r=ref, c=c, z=z: r[c, z, :, s], width))
+    pack_strips(tiles, low_ref, high_ref, 0)
+    arrived(4)
+    done = len(tiles) // SLOTS
+    tiles = []
     for layer in range(layers):
         for c in range(3):
             tiles.append((lambda s, c=c, l=layer: f_ref[c, first + l, :, s], width))
         tiles.append((lambda s, l=layer: inv_ref[first + l, :, s], width))
         tiles.append((lambda s, l=layer: grad_ref[l, :, s], width))
         tiles.append((lambda s: wide_ref[:, s], width) if layer % ROWS == 0 else (None, width))
-    pack_strips(tiles, low_ref, high_ref, 0)
-
-
-def y_own(permit, efield, hfield, forward, material, grad_sum, mask):
+    pack_strips(tiles, low_ref, high_ref, done)
+
+
+def load(permit, efield, hfield, forward, material, grad_sum, mask):
     cells_z, width = efield.shape[1], efield.shape[3]
     count = (cells_z * 6 + grad_sum.shape[0] * 6) // SLOTS
-    packed = f32(count, ROWS, LANES)
-    return pl.pallas_call(
-        y_own_kernel,
-        in_specs=[SMEM] + [VMEM] * 6,
-        out_specs=[VMEM] * 4,
-        out_shape=[packed, packed, f32(ROWS, width), f32(*material.shape)],
+    packed = (count, ROWS, LANES)
+    return pl.pallas_call(
+        load_kernel,
+        in_specs=[SMEM] + [ANY] * 5 + [VMEM],
+        out_specs=[VMEM] * 8,
+        out_shape=[
+            pltpu.VMEM(shape, jnp.float32)
+            for shape in (
+                efield.shape,
+                hfield.shape,
+                forward.shape,
+                grad_sum.shape,
+                packed,
+                packed,
+                (ROWS, width),
+                material.shape,
+            )
+        ],
+        scratch_shapes=[pltpu.VMEM(material.shape, jnp.int32), pltpu.SemaphoreType.DMA((11,))],
+        compiler_params=params(56),
+    )(permit, efield, hfield, forward, material, grad_sum, mask)
+
+
+def edge_tile(load, width):
+    lane = lax.broadcasted_iota(jnp.int32, (ROWS, LANES), 1)
+    head = pltpu.roll(load(slice(0, LANES)), STRIP, 1)
+    tail = pltpu.roll(load(slice(width - LANES, width)), LANES - STRIP, 1)
+    return jnp.where(lane < LANES // 2, head, tail)
+
+
+def edges_kernel(e_ref, h_ref, f_ref, inv_ref, grad_ref, mask_ref, eh_out, grad_out, mask_out):
+    cells_z, width = e_ref.shape[1], e_ref.shape[3]
+    layers = grad_ref.shape[0]
+    first = first_layer(cells_z, layers)
+    for z in range(cells_z):
+        for c in range(3):
+            eh_out[z, c] = edge_tile(lambda s: e_ref[c, z, :, s], width)
+            eh_out[z, 3 + c] = edge_tile(lambda s: h_ref[c, z, :, s], width)
+    for layer in range(layers):
+        for c in range(3):
+            grad_out[layer, c] = edge_tile(lambda s: f_ref[c, first + layer, :, s], width)
+        grad_out[layer, 3] = edge_tile(lambda s: inv_ref[first + layer, :, s], width)
+        grad_out[layer, 4] = edge_tile(lambda s: grad_ref[layer, :, s], width)
+    mask_out[...] = edge_tile(lambda s: mask_ref[:, s], width)
+
+
+def own_edges(arrays):
+    cells_z, layers = arrays[0].shape[1], arrays[4].shape[0]
+    return pl.pallas_call(
+        edges_kernel,
+        in_specs=[VMEM] * 6,
+        out_specs=[VMEM] * 3,
+        out_shape=[f32(cells_z, 6, ROWS, LANES), f32(layers, 5, ROWS, LANES), f32(ROWS, LANES)],
         compiler_params=params(),
-    )(permit, efield, hfield, forward, material, grad_sum, mask)
+    )(*arrays)
 
 
 def face_tiles(zfaces, xfaces):
@@ -261,10 +352,13 @@
 
 
 class Fields:
-    def __init__(self, mode, layers, e_ref, h_ref, zfaces, xfaces, yfaces, scratch):
+    def __init__(self, mode, layers, fields, zfaces, xfaces, yfaces, scratch):
         self.mode = mode
-        self.e_ref, self.h_ref = e_ref, h_ref
-        self.cells_z, self.width = e_ref.shape[1], e_ref.shape[3]
+        self.fields = fields
+        if mode == EDGE:
+            self.cells_z, self.width = fields.shape[0], xfaces[0].shape[1]
+        else:
+            self.cells_z, self.width = fields[0].shape[1], fields[0].shape[3]
         self.wide = faces_wide(mode, self.width)
         self.lane = lax.broadcasted_iota(jnp.int32, (ROWS, LANES), 1)
         self.row = lax.broadcasted_iota(jnp.int32, (ROWS, self.wide), 0)
@@ -276,13 +370,25 @@
         if mode != OWN:
             self.ybuf = scratch[2]
             y_side = Side("gy")
-            self.ybuf[0] = y_side.lower([f[...] for f in yfaces])
-            self.ybuf[1] = y_side.upper([f[...] for f in yfaces])
-
-        full = [
-            self.wider(load, halo_base + t // SLOTS, t % SLOTS)
-            for t, (load, _) in enumerate(face_tiles(zfaces, xfaces))
-        ]
+            for t in range(yfaces[0].shape[0]):
+                lower = y_side.lower([f[t] for f in yfaces])
+                upper = y_side.upper([f[t] for f in yfaces])
+                if mode == EDGE:
+                    even = self.lane // STRIP % 2 == 0
+                    lower, upper = (
+                        jnp.where(even, upper, pltpu.roll(lower, STRIP, 1)),
+                        jnp.where(even, pltpu.roll(upper, LANES - STRIP, 1), lower),
+                    )
+                self.ybuf[0, t] = lower
+                self.ybuf[1, t] = upper
+
+        def face(load, slot):
+            if mode == EDGE:
+                own = edge_tile(load, self.width)
+                return self.edge(own, halo_base + slot // SLOTS, slot % SLOTS)
+            return self.wider(load, halo_base + slot // SLOTS, slot % SLOTS)
+
+        full = [face(load, slot) for slot, (load, _) in enumerate(face_tiles(zfaces, xfaces))]
         self.below, self.above = full[:3], full[3:5]
         per_face = xfaces[0].shape[0] // ROWS
         for t in range(per_face):
@@ -300,14 +406,14 @@
             return pltpu.roll(v, shift, 1) if shift else v
 
         lower, upper = self.ybuf[0, tile], self.ybuf[1, tile]
-        if self.mode == CIRCLE:
-            halo = jnp.where(self.lane < STRIP, moved(upper, 0), moved(lower, LANES - STRIP))
-            return jnp.concatenate([load(slice(0, self.width)), halo], axis=1)
-        head = pltpu.roll(load(slice(0, LANES)), STRIP, 1)
-        tail = pltpu.roll(load(slice(self.width - LANES, self.width)), LANES - STRIP, 1)
-        own = jnp.where(self.lane < LANES // 2, head, tail)
-        own = jnp.where(self.lane < STRIP, moved(lower, 0), own)
-        return jnp.where(self.lane >= LANES - STRIP, moved(upper, LANES - STRIP), own)
+        halo = jnp.where(self.lane < STRIP, moved(upper, 0), moved(lower, LANES - STRIP))
+        return jnp.concatenate([load(slice(0, self.width)), halo], axis=1)
+
+    def edge(self, own, tile, k):
+        shift = (LANES - STRIP - 2 * STRIP * (k // 2)) % LANES
+        both = pltpu.roll(self.ybuf[k % 2, tile], shift, 1)
+        inside = jnp.logical_and(self.lane >= STRIP, self.lane < LANES - STRIP)
+        return jnp.where(inside, own, both)
 
     def y_up(self, v):
         return pltpu.roll(v, self.wide - 1, 1)
@@ -326,8 +432,10 @@
 
     def field(self, which, c, a, b):
         slot = 6 * b + 3 * which + c
-        ref = self.h_ref if which else self.e_ref
         tile = self.per_group * a + slot // SLOTS
+        if self.mode == EDGE:
+            return self.edge(self.fields[ROWS * a + b, 3 * which + c], tile, slot % SLOTS)
+        ref = self.fields[which]
         return self.wider(lambda s: ref[c, ROWS * a + b, :, s], tile, slot % SLOTS)
 
     def hx(self, a, b, ey, ez, ey_next):
@@ -384,26 +492,33 @@
             ex, ey, hx_z, hy_z = ex_next, ey_next, hx, hy
         return ex, ey, hx_z, hy_z
 
-    def gradient(self, f_ref, inv_ref, grad_ref, mask_ref, store):
-        layers = grad_ref.shape[0]
+    def gradient(self, layers, arrays, store):
         first = first_layer(self.cells_z, layers)
         first_group = first // ROWS
-        mask = self.wider(lambda s: mask_ref[:, s], self.grad_base, 5)
+        if self.mode == EDGE:
+            grad_edges, mask_ref = arrays
+            mask = self.edge(mask_ref[...], self.grad_base, 5)
+        else:
+            f_ref, inv_ref, grad_ref, mask_ref = arrays
+            mask = mask_ref[...]
 
         def emit(a, b, efield, hfield, curl):
             z = ROWS * a + b
-            tile = self.grad_base + self.per_group * (a - first_group)
-
-            def wider(load, which):
-                slot = 6 * b + which
-                return self.wider(load, tile + slot // SLOTS, slot % SLOTS)
-
-            half_inv = wider(lambda s: inv_ref[z, :, s], 3)
+            layer = z - first
+            if self.mode == EDGE:
+                tile = self.grad_base + self.per_group * (a - first_group)
+                slots = [6 * b + n for n in range(5)]
+                values = [
+                    self.edge(grad_edges[layer, n], tile + slot // SLOTS, slot % SLOTS)
+                    for n, slot in enumerate(slots)
+                ]
+            else:
+                values = [f_ref[c, z] for c in range(3)] + [inv_ref[z], grad_ref[layer]]
             total = None
             for c in range(3):
-                term = wider(lambda s: f_ref[c, z, :, s], c) * (efield[c] + half_inv * curl[c])
+                term = values[c] * (efield[c] + values[3] * curl[c])
                 total = term if total is None else total + term
-            store(z - first, wider(lambda s: grad_ref[z - first, :, s], 4) + mask * total)
+            store(layer, values[4] + mask * total)
 
         def body(i, carry):
             return self.group(first_group + i, carry, emit)
@@ -423,12 +538,13 @@
     e_ref, h_ref, f_ref, inv_ref, grad_ref, mask_ref = refs[:6]
     zfaces, xfaces = refs[6 : 6 + counts[0]], refs[6 + counts[0] : 6 + sum(counts)]
     grad_out, scratch = refs[6 + sum(counts)], refs[7 + sum(counts) :]
-    fields = Fields(OWN, grad_ref.shape[0], e_ref, h_ref, zfaces, xfaces, None, scratch)
+    layers = grad_ref.shape[0]
+    fields = Fields(OWN, layers, (e_ref, h_ref), zfaces, xfaces, None, scratch)
 
     def store(layer, value):
         grad_out[layer] = value
 
-    fields.gradient(f_ref, inv_ref, grad_ref, mask_ref, store)
+    fields.gradient(layers, (f_ref, inv_ref, grad_ref, mask_ref), store)
 
 
 def own_gradient(arrays, zfaces, xfaces):
@@ -444,19 +560,19 @@
 
 
 def edge_gradient_kernel(counts, per_device, *refs):
-    own_ref, e_ref, h_ref, f_ref, inv_ref, grad_ref, mask_ref = refs[:7]
-    ends = np.cumsum((7,) + counts)
+    own_ref, eh_ref, grad_ref, mask_ref = refs[:4]
+    ends = np.cumsum((4,) + counts)
     zfaces, xfaces, yfaces = (refs[i:j] for i, j in zip(ends[:-1], ends[1:]))
     sends, scratch, edge_ref = refs[ends[-1] : -4], refs[-4:-1], refs[-1]
-    layers, _, width = grad_ref.shape
+    layers, _, width = own_ref.shape
     lane = lax.broadcasted_iota(jnp.int32, (ROWS, LANES), 1)
     me = lax.axis_index("gx")
-    fields = Fields(EDGE, layers, e_ref, h_ref, zfaces, xfaces, yfaces, scratch)
+    fields = Fields(EDGE, layers, eh_ref, zfaces, xfaces, yfaces, scratch)
 
     def store(layer, value):
         edge_ref[layer] = value
 
-    fields.gradient(f_ref, inv_ref, grad_ref, mask_ref, store)
+    fields.gradient(layers, (grad_ref, mask_ref), store)
 
     for k, send_ref in enumerate(sends):
         chunk = lax.bitwise_xor(me, k)
@@ -476,20 +592,20 @@
         send_ref[:, per_device * width :] = packed
 
 
-def edge_gradient(own, arrays, zfaces, xfaces, yfaces):
+def edge_gradient(own, edges, zfaces, xfaces, yfaces):
     layers, _, width = own.shape
     count = lax.axis_size("gx")
     per_device = layers // count
     faces = (*zfaces, *xfaces, *yfaces)
     return pl.pallas_call(
         functools.partial(edge_gradient_kernel, (len(zfaces), len(xfaces), len(yfaces)), per_device),
-        in_specs=[VMEM] * (7 + len(faces)),
+        in_specs=[VMEM] * (4 + len(faces)),
         out_specs=[VMEM] * count,
         out_shape=[f32(ROWS, per_device * width + LANES)] * count,
         scratch_shapes=fields_scratch(EDGE, xfaces[0], yfaces[0], width)
         + [pltpu.VMEM((layers, ROWS, LANES), jnp.float32)],
         compiler_params=params(),
-    )(own, *arrays, *faces)
+    )(own, *edges, *faces)
 
 
 def step_kernel(counts, layers, *refs):
@@ -498,7 +614,7 @@
     zfaces, xfaces, yfaces, shares = (refs[i:j] for i, j in zip(ends[:-1], ends[1:]))
     (e_out, h_out, grad_out), scratch, carry_ref = refs[ends[-1] : -4], refs[-4:-1], refs[-1]
     width = e_ref.shape[3]
-    fields = Fields(CIRCLE, layers, e_ref, h_ref, zfaces, xfaces, yfaces, scratch)
+    fields = Fields(CIRCLE, layers, (e_ref, h_ref), zfaces, xfaces, yfaces, scratch)
     a = pl.program_id(0)
 
     def emit(a, b, efield, hfield, curl):
@@ -650,20 +766,24 @@
 
 def spread(parts):
     count = len(parts)
-    return [parts[0]] + [
-        lax.ppermute(parts[k], "gx", [(i, i ^ k) for i in range(count)]) for k in range(1, count)
-    ]
+    got = list(parts)
+    for k in range(count - 1, 0, -1):
+        got[k] = lax.ppermute(parts[k], "gx", [(i, i ^ k) for i in range(count)])
+    return got
 
 
 def on_device(efield, hfield, forward, material, permit, design_mask, grad_sum):
     layers, _, width = grad_sum.shape
     zfaces = exchange(z_faces(efield, hfield), "gz")
+    efield, hfield, forward, grad_sum, own_low, own_high, mask, inv = load(
+        permit, efield, hfield, forward, material, grad_sum, design_mask
+    )
+    arrays = (efield, hfield, forward, inv, grad_sum, mask)
     xfaces = exchange(x_faces(efield, hfield, zfaces), "gx")
-    own_low, own_high, mask, inv = y_own(permit, efield, hfield, forward, material, grad_sum, design_mask)
-    arrays = (efield, hfield, forward, inv, grad_sum, mask)
+    edges = own_edges(arrays)
     yfaces = exchange(y_faces(own_low, own_high, zfaces, xfaces), "gy", wrap=True)
     own = own_gradient(arrays, zfaces, xfaces)
-    shares = edge_gradient(own, arrays, zfaces, xfaces, yfaces)
+    shares = edge_gradient(own, edges, zfaces, xfaces, yfaces)
     got = spread(shares)
     e_next, h_next, grad_total = step(efield, hfield, inv, zfaces, xfaces, yfaces, shares, layers)
     filtered = spread(cone_filter(got, layers // len(got), width))

time: 48.4 us -> 44 us (0.909)
  local copies, waits for them, and re-layouts: 4.28 us -> 0.01 us
  Pallas kernels: 9.97 us -> 12.4 us
  other arithmetic: 1.65 us -> 0 us
  starting transfers between devices: 19.9 us -> 18.9 us
    pallas_call x1 -> x3, Pallas kernels: 1.08 us -> 5.17 us  [the longest x1 3.13 us: load(): pl.pallas_call(load_kernel, in_specs=[SMEM] + [ANY] * 5 + [VMEM], out_spe...]
    unnamed x18 -> x2, local copies, waits for them, and re-layouts: 3.56 us -> 0.01 us
    pallas_call x1, Pallas kernels: 2.49 us -> 0.87 us  [edge_gradient(): pl.pallas_call(functools.partial(edge_gradient_kernel, (len(zfaces), len(...]
    ppermute x5, starting transfers between devices: 7.89 us -> 7.01 us  [swap_pairs(): return lax.ppermute(value, axis, pairs + [(b, a) for a, b in pairs])]
    sub x1 -> x0, other arithmetic: 0.84 us -> none  [z_faces(): hfield[0, top] + HALF * ez - HALF * ey]
    select_n x1 -> x0, other arithmetic: 0.82 us -> none  [sends(): both = [jnp.where(self.odd, low, high)]]
    squeeze x1 -> x0, local copies, waits for them, and re-layouts: 0.72 us -> none  [z_faces(): ex, ey, ez = (efield[c, top] for c in range(3))]
  transfers between devices with their start and end apart: 11 -> 11, of which waited for: 6 -> 4; matrix products, arithmetic and copies ran while one was open for 0% -> 0% of each run, Pallas kernels for 11% -> 18%
where the time goes in v3:
time: 44 us; the launch traced here: 43.8 us
  starting transfers between devices  18.9 us (43%)
  Pallas kernels  12.4 us (28%)
  waiting for transfers between devices  11.7 us (27%)
  between operations  0.74 us (2%)
    ppermute x6, starting transfers between devices, spread(): got[k] = lax.ppermute(parts[k], 'gx', [(i, i ^ k) for i in range(count)])  11.9 us
    ppermute x6, waiting for transfers between devices, spread(): got[k] = lax.ppermute(parts[k], 'gx', [(i, i ^ k) for i in range(count)])  7.67 us
    ppermute x5, starting transfers between devices, swap_pairs(): return lax.ppermute(value, axis, pairs + [(b, a) for a, b in pairs])  7.01 us
    ppermute x5, waiting for transfers between devices, swap_pairs(): return lax.ppermute(value, axis, pairs + [(b, a) for a, b in pairs])  4.05 us
    pallas_call x1, Pallas kernels, step(): pl.pallas_call(functools.partial(step_kernel, counts, layers), grid=(cell...  3.59 us
    pallas_call x1, Pallas kernels, load(): pl.pallas_call(load_kernel, in_specs=[SMEM] + [ANY] * 5 + [VMEM], out_spe...  3.13 us
    pallas_call x1, Pallas kernels, z_faces(): pl.pallas_call(z_faces_kernel, in_specs=[ANY] * 2, out_specs=[VMEM] * rou...  1.5 us
    pallas_call x1, Pallas kernels, cone_filter(): pl.pallas_call(functools.partial(filter_kernel, count, per_device, width)...  0.99 us
  transfers between devices with their start and end apart: 11, of which 4 were waited for; matrix products, arithmetic and copies ran while one was open for 0% of the time, Pallas kernels for 18%

profile of v3, /device:TPU:0, one launch (start us, length us, event | category | flops | bytes accessed | tf_op | source)
XLA Modules:
  0.0 43.8 jit_solution(485841797715649104)
XLA Ops:
  0.6 1.5 %shard_map.112 = f32[3,8,512]{2,1,0:T(8,128)} custom-call(f32[3,24,8,512]{3,2,1,0:T(8,128)} %refs_0_.2, f32[3,24,8,512]{3,2,1,0:T(8,128)} %refs_1_.1), custom_call_target="tpu_custom_call" | custom-call | tf_op jit(solution)/shard_map/pallas_call | solution.py:104
  2.1 3.0 %collective-permute-start = (f32[3,8,512]{2,1,0:T(8,128)}, f32[3,8,512]{2,1,0:T(8,128)S(1)}, u32[]{:S(2)}, u32[]{:S(2)}) collective-permute-start(f32[3,8,512]{2,1,0:T(8,128)} %shard_map.112), channel_id=1, source_target_pairs={{0,1},{1,0},{2,3},{3,2},{4,5},{5,4},{6,7},{7,6},{8,9},{9,8},{10,11... | collective-permute-start | bytes 147464 | tf_op jit(solution)/shard_map/ppermute | solution.py:36
  5.2 3.1 %shard_map.111 = (f32[3,24,8,512]{3,2,1,0:T(8,128)S(1)}, f32[3,24,8,512]{3,2,1,0:T(8,128)S(1)}, f32[3,24,8,512]{3,2,1,0:T(8,128)S(1)}, f32[16,8,512]{2,1,0:T(8,1...) custom-call(f32[4]{0:T(128)} %permit_ref.1, ...), custom_call_target="tpu_custom_call" | custom-call | tf_op jit(solution)/shard_map/pallas_call | solution.py:247
  8.3 0.0 collective-permute-done.refs_2_.refs_6_.refs_4_.refs_3_
  8.3 0.1 shard_map.113
  8.5 1.6 %collective-permute-start.1 = (f32[72,512]{1,0:T(8,128)S(1)}, f32[72,512]{1,0:T(8,128)S(1)}, u32[]{:S(2)}, u32[]{:S(2)}) collective-permute-start(f32[72,512]{1,0:T(8,128)S(1)} %get-tuple-element.33), channel_id=1, source_target_pairs={{0,8},{16,24},{8,0},{24,16},{1,9},{17,25},{9,1},{25,17},{2,10},{18... | collective-permute-start | bytes 442376 | tf_op jit(solution)/shard_map/ppermute | solution.py:36
  10.1 0.7 %collective-permute-start.2 = (f32[72,512]{1,0:T(8,128)S(1)}, f32[72,512]{1,0:T(8,128)S(1)}, u32[]{:S(2)}, u32[]{:S(2)}) collective-permute-start(f32[72,512]{1,0:T(8,128)S(1)} %get-tuple-element.34), channel_id=1, source_target_pairs={{8,16},{16,8},{9,17},{17,9},{10,18},{18,10},{11,19},{19,11},{12,20... | collective-permute-start | bytes 442376 | tf_op jit(solution)/shard_map/ppermute | solution.py:36
  10.8 3.1 %collective-permute-done.1.refs_3_.refs_7_.refs_5_.refs_4_ = f32[72,512]{1,0:T(8,128)S(1)} collective-permute-done((f32[72,512]{1,0:T(8,128)S(1)}, f32[72,512]{1,0:T(8,128)S(1)}, u32[]{:S(2)}, u32[]{:S(2)}) %collective-permute-start.1) | collective-permute-done | bytes 147488 | tf_op jit(solution)/shard_map/ppermute | solution.py:36
  13.8 0.0 collective-permute-done.2.refs_4_.refs_8_.refs_6_.refs_5_
  13.8 0.1 shard_map.114
  14.0 0.1 collective-permute-start.3
  14.1 1.6 %collective-permute-start.4 = (f32[17,8,128]{2,1,0:T(8,128)S(1)}, f32[17,8,128]{2,1,0:T(8,128)S(1)}, u32[]{:S(2)}, u32[]{:S(2)}) collective-permute-start(f32[17,8,128]{2,1,0:T(8,128)S(1)} %get-tuple-element.38), channel_id=1, source_target_pairs={{2,4},{0,6},{4,2},{6,0},{3,5},{1,7},{5,3},{7,1},{10,12},{8,14},{12... | collective-permute-start | bytes 208904 | tf_op jit(solution)/shard_map/ppermute | solution.py:36
  15.7 0.5 %shard_map.116 = (f32[24,6,8,128]{3,2,1,0:T(8,128)S(1)}, f32[16,5,8,128]{3,2,1,0:T(8,128)S(1)}, f32[8,128]{1,0:T(8,128)S(1)}) custom-call(f32[3,24,8,512]{3,2,1,0:T(8,128)S(1)} %get-tuple-element.30.refs_0_.e_ref, f32[3,24,8,512]{3,2,1,0:T(8,128)S(1)} %get-tuple-element.31.refs_1_.h_ref, f32[3,24,8,512]{3,2,1,0:T(8,128)S(1)} %get-tuple-element.39.refs_2_.f_ref, ...), custom_call_target="tpu_custom_call" | custom-call | tf_op jit(solution)/shard_map/pallas_call | solution.py:294
  16.2 0.8 %shard_map.115.refs_0_ = f32[16,8,512]{2,1,0:T(8,128)S(1)} custom-call(f32[3,24,8,512]{3,2,1,0:T(8,128)S(1)} %get-tuple-element.30.refs_0_.e_ref, f32[3,24,8,512]{3,2,1,0:T(8,128)S(1)} %get-tuple-element.31.refs_1_.h_ref, f32[3,24,8,512]{3,2,1,0:T(8,128)S(1)} %get-tuple-element.39.refs_2_.f_ref, f32[24,8,512]{2,1,0:T(8,128)S(1)} %get-tuple-element.32.refs_3_.inv_ref.refs_2_, ...), custom_call_target="tpu_custom_call" | custom-call | tf_op jit(solution)/shard_map/pallas_call | solution.py:552
  17.0 0.0 copy-start
  17.0 0.0 collective-permute-done.3.refs_7_.refs_6_
  17.0 1.0 %collective-permute-done.4.refs_8_.refs_7_ = f32[17,8,128]{2,1,0:T(8,128)S(1)} collective-permute-done((f32[17,8,128]{2,1,0:T(8,128)S(1)}, f32[17,8,128]{2,1,0:T(8,128)S(1)}, u32[]{:S(2)}, u32[]{:S(2)}) %collective-permute-start.4) | collective-permute-done | bytes 69664 | tf_op jit(solution)/shard_map/ppermute | solution.py:36
  18.0 0.9 %shard_map.117 = (f32[8,2176]{1,0:T(8,128)S(1)}, f32[8,2176]{1,0:T(8,128)S(1)}, f32[8,2176]{1,0:T(8,128)S(1)}, f32[8,2176]{1,0:T(8,128)S(1)}) custom-call(f32[16,8,512]{2,1,0:T(8,128)S(1)} %shard_map.115.refs_0_, f32[24,6,8,128]{3,2,1,0:T(8,128)S(1)} %get-tuple-element.42.refs_1_, f32[16,5,8,128]{3,2,1,0:T(8,128)S(1)} %get-tuple-element.43.refs_2_, ...), custom_call_target="tpu_custom_call" | custom-call | tf_op jit(solution)/shard_map/pallas_call | solution.py:600
  18.9 4.7 %collective-permute-start.5 = (f32[8,2176]{1,0:T(8,128)S(1)}, f32[8,2176]{1,0:T(8,128)S(1)}, u32[]{:S(2)}, u32[]{:S(2)}) collective-permute-start(f32[8,2176]{1,0:T(8,128)S(1)} %get-tuple-element.46.refs_9_), channel_id=1, source_target_pairs={{0,8},{8,0},{16,24},{24,16},{1,9},{9,1},{17,25},{25,17},{2,10},{10... | collective-permute-start | bytes 208904 | tf_op jit(solution)/shard_map/ppermute | solution.py:771
  23.6 1.4 %collective-permute-start.6 = (f32[8,2176]{1,0:T(8,128)S(1)}, f32[8,2176]{1,0:T(8,128)S(1)}, u32[]{:S(2)}, u32[]{:S(2)}) collective-permute-start(f32[8,2176]{1,0:T(8,128)S(1)} %get-tuple-element.47.refs_10_), channel_id=1, source_target_pairs={{0,16},{8,24},{16,0},{24,8},{1,17},{9,25},{17,1},{25,9},{2,18},{10... | collective-permute-start | bytes 208904 | tf_op jit(solution)/shard_map/ppermute | solution.py:771
  25.0 1.4 %collective-permute-start.7 = (f32[8,2176]{1,0:T(8,128)S(1)}, f32[8,2176]{1,0:T(8,128)S(1)}, u32[]{:S(2)}, u32[]{:S(2)}) collective-permute-start(f32[8,2176]{1,0:T(8,128)S(1)} %get-tuple-element.48.refs_11_), channel_id=1, source_target_pairs={{0,24},{8,16},{16,8},{24,0},{1,25},{9,17},{17,9},{25,1},{2,26},{10... | collective-permute-start | bytes 208904 | tf_op jit(solution)/shard_map/ppermute | solution.py:771
  26.3 0.0 collective-permute-done.5.refs_2_
  26.4 5.8 %collective-permute-done.6.refs_3_ = f32[8,2176]{1,0:T(8,128)S(1)} collective-permute-done((f32[8,2176]{1,0:T(8,128)S(1)}, f32[8,2176]{1,0:T(8,128)S(1)}, u32[]{:S(2)}, u32[]{:S(2)}) %collective-permute-start.6) | collective-permute-done | bytes 69664 | tf_op jit(solution)/shard_map/ppermute | solution.py:771
  32.2 0.0 collective-permute-done.7.refs_4_
  32.2 0.0 copy-done
  32.2 1.0 %shard_map.119 = (f32[4,8,512]{2,1,0:T(8,128)S(1)}, f32[4,8,512]{2,1,0:T(8,128)S(1)}, f32[4,8,512]{2,1,0:T(8,128)S(1)}, f32[4,8,512]{2,1,0:T(8,128)S(1)}) custom-call(bf16[112,48]{1,0:T(8,128)(2,1)S(1)} %copy-done, f32[8,2176]{1,0:T(8,128)S(1)} %get-tuple-element.45.refs_8_.refs_1_, f32[8,2176]{1,0:T(8,128)S(1)} %collective-permute-done.5.refs_2_, ...), custom_call_target="tpu_custom_call" | custom-call | tf_op jit(solution)/shard_map/pallas_call | solution.py:728
  33.2 1.7 %collective-permute-start.8 = (f32[4,8,512]{2,1,0:T(8,128)S(1)}, f32[4,8,512]{2,1,0:T(8,128)S(1)}, u32[]{:S(2)}, u32[]{:S(2)}) collective-permute-start(f32[4,8,512]{2,1,0:T(8,128)S(1)} %get-tuple-element.53), channel_id=1, source_target_pairs={{0,8},{8,0},{16,24},{24,16},{1,9},{9,1},{17,25},{25,17},{2,10},{10... | collective-permute-start | bytes 196616 | tf_op jit(solution)/shard_map/ppermute | solution.py:771
  34.9 1.1 %collective-permute-start.9 = (f32[4,8,512]{2,1,0:T(8,128)S(1)}, f32[4,8,512]{2,1,0:T(8,128)S(1)}, u32[]{:S(2)}, u32[]{:S(2)}) collective-permute-start(f32[4,8,512]{2,1,0:T(8,128)S(1)} %get-tuple-element.54), channel_id=1, source_target_pairs={{0,16},{8,24},{16,0},{24,8},{1,17},{9,25},{17,1},{25,9},{2,18},{10... | collective-permute-start | bytes 196616 | tf_op jit(solution)/shard_map/ppermute | solution.py:771
  36.1 1.6 %collective-permute-start.10 = (f32[4,8,512]{2,1,0:T(8,128)S(1)}, f32[4,8,512]{2,1,0:T(8,128)S(1)}, u32[]{:S(2)}, u32[]{:S(2)}) collective-permute-start(f32[4,8,512]{2,1,0:T(8,128)S(1)} %get-tuple-element.55), channel_id=1, source_target_pairs={{0,24},{8,16},{16,8},{24,0},{1,25},{9,17},{17,9},{25,1},{2,26},{10... | collective-permute-start | bytes 196616 | tf_op jit(solution)/shard_map/ppermute | solution.py:771
  37.6 3.6 %shard_map.118 = (f32[3,24,8,512]{3,2,1,0:T(8,128)}, f32[3,24,8,512]{3,2,1,0:T(8,128)}, f32[16,8,512]{2,1,0:T(8,128)}) custom-call(f32[3,24,8,512]{3,2,1,0:T(8,128)S(1)} %get-tuple-element.30.refs_0_.e_ref, f32[3,24,8,512]{3,2,1,0:T(8,128)S(1)} %get-tuple-element.31.refs_1_.h_ref, f32[24,8,512]{2,1,0:T(8,128)S(1)} %get-tuple-element.32.refs_3_.inv_ref.refs_2_, ...), custom_call_target="tpu_custom_call" | custom-call | tf_op jit(solution)/shard_map/pallas_call | solution.py:647
  41.2 0.0 collective-permute-done.8.refs_1_
  41.2 1.8 %collective-permute-done.9.refs_2_ = f32[4,8,512]{2,1,0:T(8,128)S(1)} collective-permute-done((f32[4,8,512]{2,1,0:T(8,128)S(1)}, f32[4,8,512]{2,1,0:T(8,128)S(1)}, u32[]{:S(2)}, u32[]{:S(2)}) %collective-permute-start.9) | collective-permute-done | bytes 65568 | tf_op jit(solution)/shard_map/ppermute | solution.py:771
  43.1 0.0 collective-permute-done.10.refs_3_
  43.1 0.7 %shard_map.120 = f32[16,8,512]{2,1,0:T(8,128)} custom-call(f32[4,8,512]{2,1,0:T(8,128)S(1)} %get-tuple-element.52.refs_0_, f32[4,8,512]{2,1,0:T(8,128)S(1)} %collective-permute-done.8.refs_1_, f32[4,8,512]{2,1,0:T(8,128)S(1)} %collective-permute-done.9.refs_2_, f32[4,8,512]{2,1,0:T(8,128)S(1)} %collective-permute-done.10.refs_3_), custom_call_target="tpu_custom_call" | custom-call | tf_op jit(solution)/shard_map/pallas_call | solution.py:757
Async XLA Ops:
  2.1 6.2 %collective-permute-start = (f32[3,8,512]{2,1,0:T(8,128)}, f32[3,8,512]{2,1,0:T(8,128)S(1)}, u32[]{:S(2)}, u32[]{:S(2)}) collective-permute-start(f32[3,8,512]{2,1,0:T(8,128)} %shard_map.112), channel_id=1, source_target_pairs={{0,1},{1,0},{2,3},{3,2},{4,5},{5,4},{6,7},{7,6},{8,9},{9,8},{10,11... | collective-permute-start | bytes 147464 | tf_op jit(solution)/shard_map/ppermute | solution.py:36
  8.5 5.4 %collective-permute-start.1 = (f32[72,512]{1,0:T(8,128)S(1)}, f32[72,512]{1,0:T(8,128)S(1)}, u32[]{:S(2)}, u32[]{:S(2)}) collective-permute-start(f32[72,512]{1,0:T(8,128)S(1)} %get-tuple-element.33), channel_id=1, source_target_pairs={{0,8},{16,24},{8,0},{24,16},{1,9},{17,25},{9,1},{25,17},{2,10},{18... | collective-permute-start | bytes 442376 | tf_op jit(solution)/shard_map/ppermute | solution.py:36
  10.1 3.7 %collective-permute-start.2 = (f32[72,512]{1,0:T(8,128)S(1)}, f32[72,512]{1,0:T(8,128)S(1)}, u32[]{:S(2)}, u32[]{:S(2)}) collective-permute-start(f32[72,512]{1,0:T(8,128)S(1)} %get-tuple-element.34), channel_id=1, source_target_pairs={{8,16},{16,8},{9,17},{17,9},{10,18},{18,10},{11,19},{19,11},{12,20... | collective-permute-start | bytes 442376 | tf_op jit(solution)/shard_map/ppermute | solution.py:36
  14.0 3.1 %collective-permute-start.3 = (f32[17,8,128]{2,1,0:T(8,128)S(1)}, f32[17,8,128]{2,1,0:T(8,128)S(1)}, u32[]{:S(2)}, u32[]{:S(2)}) collective-permute-start(f32[17,8,128]{2,1,0:T(8,128)S(1)} %get-tuple-element.37), channel_id=1, source_target_pairs={{0,2},{4,6},{2,0},{6,4},{1,3},{5,7},{3,1},{7,5},{8,10},{12,14},{10... | collective-permute-start | bytes 208904 | tf_op jit(solution)/shard_map/ppermute | solution.py:36
  14.1 4.0 %collective-permute-start.4 = (f32[17,8,128]{2,1,0:T(8,128)S(1)}, f32[17,8,128]{2,1,0:T(8,128)S(1)}, u32[]{:S(2)}, u32[]{:S(2)}) collective-permute-start(f32[17,8,128]{2,1,0:T(8,128)S(1)} %get-tuple-element.38), channel_id=1, source_target_pairs={{2,4},{0,6},{4,2},{6,0},{3,5},{1,7},{5,3},{7,1},{10,12},{8,14},{12... | collective-permute-start | bytes 208904 | tf_op jit(solution)/shard_map/ppermute | solution.py:36
  17.0 15.1 %copy-start = (bf16[112,48]{1,0:T(8,128)(2,1)S(1)}, bf16[112,48]{1,0:T(8,128)(2,1)}, u32[]{:S(2)}) copy-start(bf16[112,48]{1,0:T(8,128)(2,1)} %constant.2.clone.refs_0_) | copy-start | bytes 32260
  18.9 7.4 %collective-permute-start.5 = (f32[8,2176]{1,0:T(8,128)S(1)}, f32[8,2176]{1,0:T(8,128)S(1)}, u32[]{:S(2)}, u32[]{:S(2)}) collective-permute-start(f32[8,2176]{1,0:T(8,128)S(1)} %get-tuple-element.46.refs_9_), channel_id=1, source_target_pairs={{0,8},{8,0},{16,24},{24,16},{1,9},{9,1},{17,25},{25,17},{2,10},{10... | collective-permute-start | bytes 208904 | tf_op jit(solution)/shard_map/ppermute | solution.py:771
  23.6 8.6 %collective-permute-start.6 = (f32[8,2176]{1,0:T(8,128)S(1)}, f32[8,2176]{1,0:T(8,128)S(1)}, u32[]{:S(2)}, u32[]{:S(2)}) collective-permute-start(f32[8,2176]{1,0:T(8,128)S(1)} %get-tuple-element.47.refs_10_), channel_id=1, source_target_pairs={{0,16},{8,24},{16,0},{24,8},{1,17},{9,25},{17,1},{25,9},{2,18},{10... | collective-permute-start | bytes 208904 | tf_op jit(solution)/shard_map/ppermute | solution.py:771
  25.0 7.2 %collective-permute-start.7 = (f32[8,2176]{1,0:T(8,128)S(1)}, f32[8,2176]{1,0:T(8,128)S(1)}, u32[]{:S(2)}, u32[]{:S(2)}) collective-permute-start(f32[8,2176]{1,0:T(8,128)S(1)} %get-tuple-element.48.refs_11_), channel_id=1, source_target_pairs={{0,24},{8,16},{16,8},{24,0},{1,25},{9,17},{17,9},{25,1},{2,26},{10... | collective-permute-start | bytes 208904 | tf_op jit(solution)/shard_map/ppermute | solution.py:771
  33.2 8.0 %collective-permute-start.8 = (f32[4,8,512]{2,1,0:T(8,128)S(1)}, f32[4,8,512]{2,1,0:T(8,128)S(1)}, u32[]{:S(2)}, u32[]{:S(2)}) collective-permute-start(f32[4,8,512]{2,1,0:T(8,128)S(1)} %get-tuple-element.53), channel_id=1, source_target_pairs={{0,8},{8,0},{16,24},{24,16},{1,9},{9,1},{17,25},{25,17},{2,10},{10... | collective-permute-start | bytes 196616 | tf_op jit(solution)/shard_map/ppermute | solution.py:771
  34.9 8.1 %collective-permute-start.9 = (f32[4,8,512]{2,1,0:T(8,128)S(1)}, f32[4,8,512]{2,1,0:T(8,128)S(1)}, u32[]{:S(2)}, u32[]{:S(2)}) collective-permute-start(f32[4,8,512]{2,1,0:T(8,128)S(1)} %get-tuple-element.54), channel_id=1, source_target_pairs={{0,16},{8,24},{16,0},{24,8},{1,17},{9,25},{17,1},{25,9},{2,18},{10... | collective-permute-start | bytes 196616 | tf_op jit(solution)/shard_map/ppermute | solution.py:771
  36.1 7.0 %collective-permute-start.10 = (f32[4,8,512]{2,1,0:T(8,128)S(1)}, f32[4,8,512]{2,1,0:T(8,128)S(1)}, u32[]{:S(2)}, u32[]{:S(2)}) collective-permute-start(f32[4,8,512]{2,1,0:T(8,128)S(1)} %get-tuple-element.55), channel_id=1, source_target_pairs={{0,24},{8,16},{16,8},{24,0},{1,25},{9,17},{17,9},{25,1},{2,26},{10... | collective-permute-start | bytes 196616 | tf_op jit(solution)/shard_map/ppermute | solution.py:771

commit v4 on v3

--- a/solution.py
+++ b/solution.py
@@ -574,7 +574,7 @@
 
     fields.gradient(layers, (grad_ref, mask_ref), store)
 
-    for k, send_ref in enumerate(sends):
+    for k, send_ref in enumerate(sends[::-1]):
         chunk = lax.bitwise_xor(me, k)
         packed = jnp.zeros((ROWS, LANES), jnp.float32)
         for i in range(per_device):
@@ -597,7 +597,7 @@
     count = lax.axis_size("gx")
     per_device = layers // count
     faces = (*zfaces, *xfaces, *yfaces)
-    return pl.pallas_call(
+    shares = pl.pallas_call(
         functools.partial(edge_gradient_kernel, (len(zfaces), len(xfaces), len(yfaces)), per_device),
         in_specs=[VMEM] * (4 + len(faces)),
         out_specs=[VMEM] * count,
@@ -606,12 +606,14 @@
         + [pltpu.VMEM((layers, ROWS, LANES), jnp.float32)],
         compiler_params=params(),
     )(own, *edges, *faces)
+    return shares[::-1]
 
 
 def step_kernel(counts, layers, *refs):
     e_ref, h_ref, inv_ref = refs[:3]
     ends = np.cumsum((3,) + counts)
     zfaces, xfaces, yfaces, shares = (refs[i:j] for i, j in zip(ends[:-1], ends[1:]))
+    shares = shares[::-1]
     (e_out, h_out, grad_out), scratch, carry_ref = refs[ends[-1] : -4], refs[-4:-1], refs[-1]
     width = e_ref.shape[3]
     fields = Fields(CIRCLE, layers, (e_ref, h_ref), zfaces, xfaces, yfaces, scratch)
@@ -642,7 +644,7 @@
 def step(efield, hfield, inv, zfaces, xfaces, yfaces, shares, layers):
     _, cells_z, _, width = efield.shape
     block = pl.BlockSpec((3, ROWS, ROWS, width), lambda a: (0, a, 0, 0))
-    groups = (zfaces, xfaces, yfaces, shares)
+    groups = (zfaces, xfaces, yfaces, shares[::-1])
     counts = tuple(len(group) for group in groups)
     return pl.pallas_call(
         functools.partial(step_kernel, counts, layers),
@@ -681,7 +683,7 @@
 
 def filter_kernel(count, per_device, width, *refs):
     taps_ref = refs[0]
-    got = refs[1 : 1 + count]
+    got = refs[count:0:-1]
     outs = refs[1 + count : 1 + 2 * count]
     slabs, parts, done = refs[1 + 2 * count :]
     me = lax.axis_index("gx")
@@ -736,15 +738,16 @@
             pltpu.VMEM((count, per_device, ROWS, width), jnp.float32),
         ],
         compiler_params=params(),
-    )(taps, *got)
+    )(taps, *got[::-1])
 
 
 def place_kernel(count, per_device, *refs):
     out, sems = refs[count], refs[count + 1]
+    parts = refs[count - 1 :: -1]
     copies = []
     for k in range(count):
         at = lax.bitwise_xor(lax.axis_index("gx"), k) * per_device
-        copies.append(pltpu.make_async_copy(refs[k], out.at[pl.ds(at, per_device)], sems.at[k]))
+        copies.append(pltpu.make_async_copy(parts[k], out.at[pl.ds(at, per_device)], sems.at[k]))
     for copy in copies:
         copy.start()
     for copy in copies:
@@ -761,7 +764,7 @@
         out_shape=f32(count * per_device, rows, width),
         scratch_shapes=[pltpu.SemaphoreType.DMA((count,))],
         compiler_params=params(),
-    )(*parts)
+    )(*parts[::-1])
 
 
 def spread(parts):

time: 44 us -> 41.2 us (0.936)
  waiting for transfers between devices: 11.7 us -> 9.81 us
  starting transfers between devices: 18.9 us -> 18 us
    ppermute x6, waiting for transfers between devices: 7.67 us -> 5.75 us  [spread(): got[k] = lax.ppermute(parts[k], 'gx', [(i, i ^ k) for i in range(count)])]
    ppermute x6, starting transfers between devices: 11.9 us -> 11 us  [spread(): got[k] = lax.ppermute(parts[k], 'gx', [(i, i ^ k) for i in range(count)])]
  transfers between devices with their start and end apart: 11 -> 11, of which waited for: 4 -> 5; matrix products, arithmetic and copies ran while one was open for 0% -> 0% of each run, Pallas kernels for 18% -> 20%
where the time goes in v4:
time: 41.2 us; the launch traced here: 41 us
  starting transfers between devices  18 us (44%)
  Pallas kernels  12.4 us (30%)
  waiting for transfers between devices  9.81 us (24%)
  between operations  0.74 us (2%)
    ppermute x6, starting transfers between devices, spread(): got[k] = lax.ppermute(parts[k], 'gx', [(i, i ^ k) for i in range(count)])  11 us
    ppermute x5, starting transfers between devices, swap_pairs(): return lax.ppermute(value, axis, pairs + [(b, a) for a, b in pairs])  7.01 us
    ppermute x6, waiting for transfers between devices, spread(): got[k] = lax.ppermute(parts[k], 'gx', [(i, i ^ k) for i in range(count)])  5.75 us
    ppermute x5, waiting for transfers between devices, swap_pairs(): return lax.ppermute(value, axis, pairs + [(b, a) for a, b in pairs])  4.05 us
    pallas_call x1, Pallas kernels, step(): pl.pallas_call(functools.partial(step_kernel, counts, layers), grid=(cell...  3.59 us
    pallas_call x1, Pallas kernels, load(): pl.pallas_call(load_kernel, in_specs=[SMEM] + [ANY] * 5 + [VMEM], out_spe...  3.13 us
    pallas_call x1, Pallas kernels, z_faces(): pl.pallas_call(z_faces_kernel, in_specs=[ANY] * 2, out_specs=[VMEM] * rou...  1.5 us
    pallas_call x1, Pallas kernels, cone_filter(): pl.pallas_call(functools.partial(filter_kernel, count, per_device, width)...  0.99 us
  transfers between devices with their start and end apart: 11, of which 5 were waited for; matrix products, arithmetic and copies ran while one was open for 0% of the time, Pallas kernels for 20%

profile of v4, /device:TPU:0, one launch (start us, length us, event | category | flops | bytes accessed | tf_op | source)
XLA Modules:
  0.0 41.0 jit_solution(9203373328275852085)
XLA Ops:
  0.6 1.5 %shard_map.112 = f32[3,8,512]{2,1,0:T(8,128)} custom-call(f32[3,24,8,512]{3,2,1,0:T(8,128)} %refs_0_.2, f32[3,24,8,512]{3,2,1,0:T(8,128)} %refs_1_.1), custom_call_target="tpu_custom_call" | custom-call | tf_op jit(solution)/shard_map/pallas_call | solution.py:104
  2.1 3.0 %collective-permute-start = (f32[3,8,512]{2,1,0:T(8,128)}, f32[3,8,512]{2,1,0:T(8,128)S(1)}, u32[]{:S(2)}, u32[]{:S(2)}) collective-permute-start(f32[3,8,512]{2,1,0:T(8,128)} %shard_map.112), channel_id=1, source_target_pairs={{0,1},{1,0},{2,3},{3,2},{4,5},{5,4},{6,7},{7,6},{8,9},{9,8},{10,11... | collective-permute-start | bytes 147464 | tf_op jit(solution)/shard_map/ppermute | solution.py:36
  5.2 3.1 %shard_map.111 = (f32[3,24,8,512]{3,2,1,0:T(8,128)S(1)}, f32[3,24,8,512]{3,2,1,0:T(8,128)S(1)}, f32[3,24,8,512]{3,2,1,0:T(8,128)S(1)}, f32[16,8,512]{2,1,0:T(8,1...) custom-call(f32[4]{0:T(128)} %permit_ref.1, ...), custom_call_target="tpu_custom_call" | custom-call | tf_op jit(solution)/shard_map/pallas_call | solution.py:247
  8.3 0.0 collective-permute-done.refs_2_.refs_6_.refs_4_.refs_3_
  8.3 0.1 shard_map.113
  8.5 1.6 %collective-permute-start.1 = (f32[72,512]{1,0:T(8,128)S(1)}, f32[72,512]{1,0:T(8,128)S(1)}, u32[]{:S(2)}, u32[]{:S(2)}) collective-permute-start(f32[72,512]{1,0:T(8,128)S(1)} %get-tuple-element.33), channel_id=1, source_target_pairs={{0,8},{16,24},{8,0},{24,16},{1,9},{17,25},{9,1},{25,17},{2,10},{18... | collective-permute-start | bytes 442376 | tf_op jit(solution)/shard_map/ppermute | solution.py:36
  10.1 0.7 %collective-permute-start.2 = (f32[72,512]{1,0:T(8,128)S(1)}, f32[72,512]{1,0:T(8,128)S(1)}, u32[]{:S(2)}, u32[]{:S(2)}) collective-permute-start(f32[72,512]{1,0:T(8,128)S(1)} %get-tuple-element.34), channel_id=1, source_target_pairs={{8,16},{16,8},{9,17},{17,9},{10,18},{18,10},{11,19},{19,11},{12,20... | collective-permute-start | bytes 442376 | tf_op jit(solution)/shard_map/ppermute | solution.py:36
  10.8 3.1 %collective-permute-done.1.refs_3_.refs_7_.refs_5_.refs_4_ = f32[72,512]{1,0:T(8,128)S(1)} collective-permute-done((f32[72,512]{1,0:T(8,128)S(1)}, f32[72,512]{1,0:T(8,128)S(1)}, u32[]{:S(2)}, u32[]{:S(2)}) %collective-permute-start.1) | collective-permute-done | bytes 147488 | tf_op jit(solution)/shard_map/ppermute | solution.py:36
  13.8 0.0 collective-permute-done.2.refs_4_.refs_8_.refs_6_.refs_5_
  13.8 0.1 shard_map.114
  14.0 0.1 collective-permute-start.3
  14.1 1.6 %collective-permute-start.4 = (f32[17,8,128]{2,1,0:T(8,128)S(1)}, f32[17,8,128]{2,1,0:T(8,128)S(1)}, u32[]{:S(2)}, u32[]{:S(2)}) collective-permute-start(f32[17,8,128]{2,1,0:T(8,128)S(1)} %get-tuple-element.38), channel_id=1, source_target_pairs={{2,4},{0,6},{4,2},{6,0},{3,5},{1,7},{5,3},{7,1},{10,12},{8,14},{12... | collective-permute-start | bytes 208904 | tf_op jit(solution)/shard_map/ppermute | solution.py:36
  15.7 0.5 %shard_map.116 = (f32[24,6,8,128]{3,2,1,0:T(8,128)S(1)}, f32[16,5,8,128]{3,2,1,0:T(8,128)S(1)}, f32[8,128]{1,0:T(8,128)S(1)}) custom-call(f32[3,24,8,512]{3,2,1,0:T(8,128)S(1)} %get-tuple-element.30.refs_0_.e_ref, f32[3,24,8,512]{3,2,1,0:T(8,128)S(1)} %get-tuple-element.31.refs_1_.h_ref, f32[3,24,8,512]{3,2,1,0:T(8,128)S(1)} %get-tuple-element.39.refs_2_.f_ref, ...), custom_call_target="tpu_custom_call" | custom-call | tf_op jit(solution)/shard_map/pallas_call | solution.py:294
  16.2 0.8 %shard_map.115.refs_0_ = f32[16,8,512]{2,1,0:T(8,128)S(1)} custom-call(f32[3,24,8,512]{3,2,1,0:T(8,128)S(1)} %get-tuple-element.30.refs_0_.e_ref, f32[3,24,8,512]{3,2,1,0:T(8,128)S(1)} %get-tuple-element.31.refs_1_.h_ref, f32[3,24,8,512]{3,2,1,0:T(8,128)S(1)} %get-tuple-element.39.refs_2_.f_ref, f32[24,8,512]{2,1,0:T(8,128)S(1)} %get-tuple-element.32.refs_3_.inv_ref.refs_2_, ...), custom_call_target="tpu_custom_call" | custom-call | tf_op jit(solution)/shard_map/pallas_call | solution.py:552
  17.0 0.0 copy-start
  17.0 0.0 collective-permute-done.3.refs_7_.refs_6_
  17.0 1.0 %collective-permute-done.4.refs_8_.refs_7_ = f32[17,8,128]{2,1,0:T(8,128)S(1)} collective-permute-done((f32[17,8,128]{2,1,0:T(8,128)S(1)}, f32[17,8,128]{2,1,0:T(8,128)S(1)}, u32[]{:S(2)}, u32[]{:S(2)}) %collective-permute-start.4) | collective-permute-done | bytes 69664 | tf_op jit(solution)/shard_map/ppermute | solution.py:36
  18.0 0.9 %shard_map.117 = (f32[8,2176]{1,0:T(8,128)S(1)}, f32[8,2176]{1,0:T(8,128)S(1)}, f32[8,2176]{1,0:T(8,128)S(1)}, f32[8,2176]{1,0:T(8,128)S(1)}) custom-call(f32[16,8,512]{2,1,0:T(8,128)S(1)} %shard_map.115.refs_0_, f32[24,6,8,128]{3,2,1,0:T(8,128)S(1)} %get-tuple-element.42.refs_1_, f32[16,5,8,128]{3,2,1,0:T(8,128)S(1)} %get-tuple-element.43.refs_2_, ...), custom_call_target="tpu_custom_call" | custom-call | tf_op jit(solution)/shard_map/pallas_call | solution.py:600
  18.9 3.7 %collective-permute-start.5 = (f32[8,2176]{1,0:T(8,128)S(1)}, f32[8,2176]{1,0:T(8,128)S(1)}, u32[]{:S(2)}, u32[]{:S(2)}) collective-permute-start(f32[8,2176]{1,0:T(8,128)S(1)} %get-tuple-element.45.refs_8_), channel_id=1, source_target_pairs={{0,24},{8,16},{16,8},{24,0},{1,25},{9,17},{17,9},{25,1},{2,26},{10... | collective-permute-start | bytes 208904 | tf_op jit(solution)/shard_map/ppermute | solution.py:774
  22.6 2.5 %collective-permute-start.6 = (f32[8,2176]{1,0:T(8,128)S(1)}, f32[8,2176]{1,0:T(8,128)S(1)}, u32[]{:S(2)}, u32[]{:S(2)}) collective-permute-start(f32[8,2176]{1,0:T(8,128)S(1)} %get-tuple-element.46.refs_9_), channel_id=1, source_target_pairs={{0,16},{8,24},{16,0},{24,8},{1,17},{9,25},{17,1},{25,9},{2,18},{10... | collective-permute-start | bytes 208904 | tf_op jit(solution)/shard_map/ppermute | solution.py:774
  25.1 0.4 collective-permute-start.7
  25.4 0.0 collective-permute-done.5.refs_1_
  25.5 4.9 %collective-permute-done.6.refs_2_ = f32[8,2176]{1,0:T(8,128)S(1)} collective-permute-done((f32[8,2176]{1,0:T(8,128)S(1)}, f32[8,2176]{1,0:T(8,128)S(1)}, u32[]{:S(2)}, u32[]{:S(2)}) %collective-permute-start.6) | collective-permute-done | bytes 69664 | tf_op jit(solution)/shard_map/ppermute | solution.py:774
  30.3 0.1 collective-permute-done.7.refs_3_
  30.4 0.0 copy-done
  30.4 1.0 %shard_map.119 = (f32[4,8,512]{2,1,0:T(8,128)S(1)}, f32[4,8,512]{2,1,0:T(8,128)S(1)}, f32[4,8,512]{2,1,0:T(8,128)S(1)}, f32[4,8,512]{2,1,0:T(8,128)S(1)}) custom-call(bf16[112,48]{1,0:T(8,128)(2,1)S(1)} %copy-done, f32[8,2176]{1,0:T(8,128)S(1)} %collective-permute-done.5.refs_1_, f32[8,2176]{1,0:T(8,128)S(1)} %collective-permute-done.6.refs_2_, ...), custom_call_target="tpu_custom_call" | custom-call | tf_op jit(solution)/shard_map/pallas_call | solution.py:730
  31.4 3.2 %collective-permute-start.8 = (f32[4,8,512]{2,1,0:T(8,128)S(1)}, f32[4,8,512]{2,1,0:T(8,128)S(1)}, u32[]{:S(2)}, u32[]{:S(2)}) collective-permute-start(f32[4,8,512]{2,1,0:T(8,128)S(1)} %get-tuple-element.52), channel_id=1, source_target_pairs={{0,24},{8,16},{16,8},{24,0},{1,25},{9,17},{17,9},{25,1},{2,26},{10... | collective-permute-start | bytes 196616 | tf_op jit(solution)/shard_map/ppermute | solution.py:774
  34.6 0.0 collective-permute-start.9
  34.6 1.3 %collective-permute-start.10 = (f32[4,8,512]{2,1,0:T(8,128)S(1)}, f32[4,8,512]{2,1,0:T(8,128)S(1)}, u32[]{:S(2)}, u32[]{:S(2)}) collective-permute-start(f32[4,8,512]{2,1,0:T(8,128)S(1)} %get-tuple-element.54), channel_id=1, source_target_pairs={{0,8},{8,0},{16,24},{24,16},{1,9},{9,1},{17,25},{25,17},{2,10},{10... | collective-permute-start | bytes 196616 | tf_op jit(solution)/shard_map/ppermute | solution.py:774
  35.8 3.6 %shard_map.118 = (f32[3,24,8,512]{3,2,1,0:T(8,128)}, f32[3,24,8,512]{3,2,1,0:T(8,128)}, f32[16,8,512]{2,1,0:T(8,128)}) custom-call(f32[3,24,8,512]{3,2,1,0:T(8,128)S(1)} %get-tuple-element.30.refs_0_.e_ref, f32[3,24,8,512]{3,2,1,0:T(8,128)S(1)} %get-tuple-element.31.refs_1_.h_ref, f32[24,8,512]{2,1,0:T(8,128)S(1)} %get-tuple-element.32.refs_3_.inv_ref.refs_2_, ...), custom_call_target="tpu_custom_call" | custom-call | tf_op jit(solution)/shard_map/pallas_call | solution.py:649
  39.4 0.0 collective-permute-done.8.refs_0_
  39.4 0.8 %collective-permute-done.9.refs_1_ = f32[4,8,512]{2,1,0:T(8,128)S(1)} collective-permute-done((f32[4,8,512]{2,1,0:T(8,128)S(1)}, f32[4,8,512]{2,1,0:T(8,128)S(1)}, u32[]{:S(2)}, u32[]{:S(2)}) %collective-permute-start.9) | collective-permute-done | bytes 65568 | tf_op jit(solution)/shard_map/ppermute | solution.py:774
  40.3 0.0 collective-permute-done.10.refs_2_
  40.3 0.7 %shard_map.120 = f32[16,8,512]{2,1,0:T(8,128)} custom-call(f32[4,8,512]{2,1,0:T(8,128)S(1)} %collective-permute-done.8.refs_0_, f32[4,8,512]{2,1,0:T(8,128)S(1)} %collective-permute-done.9.refs_1_, f32[4,8,512]{2,1,0:T(8,128)S(1)} %collective-permute-done.10.refs_2_, f32[4,8,512]{2,1,0:T(8,128)S(1)} %get-tuple-element.55.refs_3_), custom_call_target="tpu_custom_call" | custom-call | tf_op jit(solution)/shard_map/pallas_call | solution.py:760
Async XLA Ops:
  2.1 6.2 %collective-permute-start = (f32[3,8,512]{2,1,0:T(8,128)}, f32[3,8,512]{2,1,0:T(8,128)S(1)}, u32[]{:S(2)}, u32[]{:S(2)}) collective-permute-start(f32[3,8,512]{2,1,0:T(8,128)} %shard_map.112), channel_id=1, source_target_pairs={{0,1},{1,0},{2,3},{3,2},{4,5},{5,4},{6,7},{7,6},{8,9},{9,8},{10,11... | collective-permute-start | bytes 147464 | tf_op jit(solution)/shard_map/ppermute | solution.py:36
  8.5 5.4 %collective-permute-start.1 = (f32[72,512]{1,0:T(8,128)S(1)}, f32[72,512]{1,0:T(8,128)S(1)}, u32[]{:S(2)}, u32[]{:S(2)}) collective-permute-start(f32[72,512]{1,0:T(8,128)S(1)} %get-tuple-element.33), channel_id=1, source_target_pairs={{0,8},{16,24},{8,0},{24,16},{1,9},{17,25},{9,1},{25,17},{2,10},{18... | collective-permute-start | bytes 442376 | tf_op jit(solution)/shard_map/ppermute | solution.py:36
  10.1 3.7 %collective-permute-start.2 = (f32[72,512]{1,0:T(8,128)S(1)}, f32[72,512]{1,0:T(8,128)S(1)}, u32[]{:S(2)}, u32[]{:S(2)}) collective-permute-start(f32[72,512]{1,0:T(8,128)S(1)} %get-tuple-element.34), channel_id=1, source_target_pairs={{8,16},{16,8},{9,17},{17,9},{10,18},{18,10},{11,19},{19,11},{12,20... | collective-permute-start | bytes 442376 | tf_op jit(solution)/shard_map/ppermute | solution.py:36
  14.0 3.1 %collective-permute-start.3 = (f32[17,8,128]{2,1,0:T(8,128)S(1)}, f32[17,8,128]{2,1,0:T(8,128)S(1)}, u32[]{:S(2)}, u32[]{:S(2)}) collective-permute-start(f32[17,8,128]{2,1,0:T(8,128)S(1)} %get-tuple-element.37), channel_id=1, source_target_pairs={{0,2},{4,6},{2,0},{6,4},{1,3},{5,7},{3,1},{7,5},{8,10},{12,14},{10... | collective-permute-start | bytes 208904 | tf_op jit(solution)/shard_map/ppermute | solution.py:36
  14.1 4.0 %collective-permute-start.4 = (f32[17,8,128]{2,1,0:T(8,128)S(1)}, f32[17,8,128]{2,1,0:T(8,128)S(1)}, u32[]{:S(2)}, u32[]{:S(2)}) collective-permute-start(f32[17,8,128]{2,1,0:T(8,128)S(1)} %get-tuple-element.38), channel_id=1, source_target_pairs={{2,4},{0,6},{4,2},{6,0},{3,5},{1,7},{5,3},{7,1},{10,12},{8,14},{12... | collective-permute-start | bytes 208904 | tf_op jit(solution)/shard_map/ppermute | solution.py:36
  17.0 13.4 %copy-start = (bf16[112,48]{1,0:T(8,128)(2,1)S(1)}, bf16[112,48]{1,0:T(8,128)(2,1)}, u32[]{:S(2)}) copy-start(bf16[112,48]{1,0:T(8,128)(2,1)} %constant.2.clone.refs_0_) | copy-start | bytes 32260
  18.9 6.5 %collective-permute-start.5 = (f32[8,2176]{1,0:T(8,128)S(1)}, f32[8,2176]{1,0:T(8,128)S(1)}, u32[]{:S(2)}, u32[]{:S(2)}) collective-permute-start(f32[8,2176]{1,0:T(8,128)S(1)} %get-tuple-element.45.refs_8_), channel_id=1, source_target_pairs={{0,24},{8,16},{16,8},{24,0},{1,25},{9,17},{17,9},{25,1},{2,26},{10... | collective-permute-start | bytes 208904 | tf_op jit(solution)/shard_map/ppermute | solution.py:774
  22.6 7.7 %collective-permute-start.6 = (f32[8,2176]{1,0:T(8,128)S(1)}, f32[8,2176]{1,0:T(8,128)S(1)}, u32[]{:S(2)}, u32[]{:S(2)}) collective-permute-start(f32[8,2176]{1,0:T(8,128)S(1)} %get-tuple-element.46.refs_9_), channel_id=1, source_target_pairs={{0,16},{8,24},{16,0},{24,8},{1,17},{9,25},{17,1},{25,9},{2,18},{10... | collective-permute-start | bytes 208904 | tf_op jit(solution)/shard_map/ppermute | solution.py:774
  25.1 5.3 %collective-permute-start.7 = (f32[8,2176]{1,0:T(8,128)S(1)}, f32[8,2176]{1,0:T(8,128)S(1)}, u32[]{:S(2)}, u32[]{:S(2)}) collective-permute-start(f32[8,2176]{1,0:T(8,128)S(1)} %get-tuple-element.47.refs_10_), channel_id=1, source_target_pairs={{0,8},{8,0},{16,24},{24,16},{1,9},{9,1},{17,25},{25,17},{2,10},{10... | collective-permute-start | bytes 208904 | tf_op jit(solution)/shard_map/ppermute | solution.py:774
  31.4 8.0 %collective-permute-start.8 = (f32[4,8,512]{2,1,0:T(8,128)S(1)}, f32[4,8,512]{2,1,0:T(8,128)S(1)}, u32[]{:S(2)}, u32[]{:S(2)}) collective-permute-start(f32[4,8,512]{2,1,0:T(8,128)S(1)} %get-tuple-element.52), channel_id=1, source_target_pairs={{0,24},{8,16},{16,8},{24,0},{1,25},{9,17},{17,9},{25,1},{2,26},{10... | collective-permute-start | bytes 196616 | tf_op jit(solution)/shard_map/ppermute | solution.py:774
  34.6 5.7 %collective-permute-start.9 = (f32[4,8,512]{2,1,0:T(8,128)S(1)}, f32[4,8,512]{2,1,0:T(8,128)S(1)}, u32[]{:S(2)}, u32[]{:S(2)}) collective-permute-start(f32[4,8,512]{2,1,0:T(8,128)S(1)} %get-tuple-element.53), channel_id=1, source_target_pairs={{0,16},{8,24},{16,0},{24,8},{1,17},{9,25},{17,1},{25,9},{2,18},{10... | collective-permute-start | bytes 196616 | tf_op jit(solution)/shard_map/ppermute | solution.py:774
  34.6 5.7 %collective-permute-start.10 = (f32[4,8,512]{2,1,0:T(8,128)S(1)}, f32[4,8,512]{2,1,0:T(8,128)S(1)}, u32[]{:S(2)}, u32[]{:S(2)}) collective-permute-start(f32[4,8,512]{2,1,0:T(8,128)S(1)} %get-tuple-element.54), channel_id=1, source_target_pairs={{0,8},{8,0},{16,24},{24,16},{1,9},{9,1},{17,25},{25,17},{2,10},{10... | collective-permute-start | bytes 196616 | tf_op jit(solution)/shard_map/ppermute | solution.py:774

commit v5 on v4

--- a/solution.py
+++ b/solution.py
@@ -32,24 +32,37 @@
     return jax.ShapeDtypeStruct(shape, jnp.float32)
 
 
-def swap_pairs(value, axis, pairs):
-    return lax.ppermute(value, axis, pairs + [(b, a) for a, b in pairs])
+def fast(*shape):
+    return pltpu.VMEM(shape, jnp.float32)
 
 
 def rounds(axis):
     return 2 if lax.axis_size(axis) > 2 else 1
 
 
-def exchange(sends, axis, wrap=False):
+def exchange(sends, axis, mate):
     count = lax.axis_size(axis)
+    beside = lax.axis_size(mate)
     if count == 1:
         return sends
-    got = [swap_pairs(sends[0], axis, [(i, i + 1) for i in range(0, count - 1, 2)])]
-    if len(sends) > 1:
-        odd_pairs = [(i, i + 1) for i in range(1, count - 1, 2)]
-        if wrap and count % 2 == 0:
-            odd_pairs.append((0, count - 1))
-        got.append(swap_pairs(sends[1], axis, odd_pairs))
+    got = []
+    for start, value in enumerate(sends):
+        partner = list(range(count))
+        for low in range(start, count - 1, 2):
+            partner[low], partner[low + 1] = low + 1, low
+        axes = sorted((axis, mate))
+        steps = (beside, 1) if axes[0] == axis else (1, count)
+        pairs = []
+        for i in range(count):
+            for m in range(beside):
+                if partner[i] != i:
+                    to = (partner[i], m)
+                elif beside % 2 == 0:
+                    to = (i, m ^ 1)
+                else:
+                    continue
+                pairs.append((i * steps[0] + m * steps[1], to[0] * steps[0] + to[1] * steps[1]))
+        got.append(lax.ppermute(value, tuple(axes), pairs))
     return got
 
 
@@ -82,31 +95,31 @@
     e_ref, h_ref = refs[:2]
     sends, (e_low, e_high, h_high, sems) = refs[2:-4], refs[-4:]
     top = e_ref.shape[1] - 1
-    copies = [
-        pltpu.make_async_copy(e_ref.at[:, 0], e_low, sems.at[0]),
-        pltpu.make_async_copy(e_ref.at[:, top], e_high, sems.at[1]),
-        pltpu.make_async_copy(h_ref.at[:, top], h_high, sems.at[2]),
-    ]
+    planes = [(e_ref.at[c, 0], e_low.at[c]) for c in range(2)]
+    planes += [(e_ref.at[c, top], e_high.at[c]) for c in range(3)]
+    planes += [(h_ref.at[c, top], h_high.at[c]) for c in range(2)]
+    copies = [pltpu.make_async_copy(*plane, sems.at[n]) for n, plane in enumerate(planes)]
     for copy in copies:
         copy.start()
     for copy in copies:
         copy.wait()
     side = Side("gz")
     ex, ey, ez = (e_high[c] for c in range(3))
+    low = (e_low[0], e_low[1], jnp.zeros_like(ez))
     high = (h_high[0] + HALF * ez - HALF * ey, h_high[1] + HALF * ex - HALF * ez, ez)
     for c in range(3):
-        for ref, value in zip(sends, side.sends(e_low[c], high[c])):
+        for ref, value in zip(sends, side.sends(low[c], high[c])):
             ref[c] = value
 
 
 def z_faces(efield, hfield):
-    face = f32(*efield.shape[:1], *efield.shape[2:])
+    face = fast(*efield.shape[:1], *efield.shape[2:])
     return pl.pallas_call(
         z_faces_kernel,
         in_specs=[ANY] * 2,
         out_specs=[VMEM] * rounds("gz"),
         out_shape=[face] * rounds("gz"),
-        scratch_shapes=[pltpu.VMEM(face.shape, jnp.float32)] * 3 + [pltpu.SemaphoreType.DMA((3,))],
+        scratch_shapes=[pltpu.VMEM(face.shape, jnp.float32)] * 3 + [pltpu.SemaphoreType.DMA((7,))],
         compiler_params=params(60),
     )(efield, hfield)
 
@@ -145,7 +158,7 @@
 
 def x_faces(efield, hfield, zfaces):
     cells_z, cells_y = efield.shape[1], efield.shape[3]
-    face = f32(3 * cells_z, cells_y)
+    face = fast(3 * cells_z, cells_y)
     return pl.pallas_call(
         functools.partial(x_faces_kernel, len(zfaces)),
         in_specs=[VMEM] * (2 + len(zfaces)),
@@ -183,44 +196,52 @@
         high_ref[first + start // SLOTS] = high
 
 
-def load_kernel(
-    permit_ref, e_in, h_in, f_in, mat_in, grad_in, mask_ref,
-    e_ref, h_ref, f_ref, grad_ref, low_ref, high_ref, wide_ref, inv_ref, mat_ref, sems,
+def load_kernel(e_in, h_in, mat_in, grad_in, e_ref, h_ref, mat_ref, grad_ref, sems):
+    parts = [(source.at[c], target.at[c]) for source, target in ((e_in, e_ref), (h_in, h_ref)) for c in range(3)]
+    parts += [(mat_in, mat_ref), (grad_in, grad_ref)]
+    copies = [pltpu.make_async_copy(*part, sems.at[n]) for n, part in enumerate(parts)]
+    for copy in copies:
+        copy.start()
+    for copy in copies:
+        copy.wait()
+
+
+def load(*arrays):
+    return pl.pallas_call(
+        load_kernel,
+        in_specs=[ANY] * 4,
+        out_specs=[VMEM] * 4,
+        out_shape=[pltpu.VMEM(one.shape, one.dtype) for one in arrays],
+        scratch_shapes=[pltpu.SemaphoreType.DMA((8,))],
+        compiler_params=params(56),
+    )(*arrays)
+
+
+def strips_kernel(
+    permit_ref, e_ref, h_ref, f_in, mat_ref, grad_ref, mask_ref, f_ref, low_ref, high_ref, wide_ref, inv_ref, sems
 ):
     cells_z, width = e_ref.shape[1], e_ref.shape[3]
     layers = grad_ref.shape[0]
     blocks = mask_ref.shape[1]
-    pairs = [(e_in, e_ref), (h_in, h_ref), (f_in, f_ref)]
-    copies = [[pltpu.make_async_copy(mat_in, mat_ref, sems.at[0])]]
-    copies.append([pltpu.make_async_copy(grad_in, grad_ref, sems.at[1])])
-    for n, (source, target) in enumerate(pairs):
-        copies.append(
-            [pltpu.make_async_copy(source.at[c], target.at[c], sems.at[2 + 3 * n + c]) for c in range(3)]
-        )
-    for group in copies:
-        for copy in group:
-            copy.start()
-
+    copies = [pltpu.make_async_copy(f_in.at[c], f_ref.at[c], sems.at[c]) for c in range(3)]
+    for copy in copies:
+        copy.start()
+
+    inverse = [
+        jnp.broadcast_to(HALF * (1.0 / permit_ref[0:1, m : m + 1]), (ROWS, width))
+        for m in range(permit_ref.shape[1])
+    ]
+    for z in range(cells_z):
+        inv = inverse[0]
+        for m in range(1, len(inverse)):
+            inv = jnp.where(mat_ref[z] == m, inverse[m], inv)
+        inv_ref[z] = inv
     spread = (
         lax.broadcasted_iota(jnp.int32, (blocks, width), 0)
         == lax.broadcasted_iota(jnp.int32, (blocks, width), 1) // BLOCK
     ).astype(jnp.float32)
     mask = jnp.broadcast_to(mask_ref[...].astype(jnp.float32), (ROWS, blocks))
     wide_ref[...] = jnp.dot(mask, spread, preferred_element_type=jnp.float32)
-
-    def arrived(*groups):
-        for n in groups:
-            for copy in copies[n]:
-                copy.wait()
-
-    arrived(0)
-    inverse = [HALF * (1.0 / permit_ref[m]) for m in range(permit_ref.shape[0])]
-    for z in range(cells_z):
-        inv = jnp.full((ROWS, width), inverse[0])
-        for m in range(1, len(inverse)):
-            inv = jnp.where(mat_ref[z] == m, inverse[m], inv)
-        inv_ref[z] = inv
-    arrived(1, 2, 3)
     first = first_layer(cells_z, layers)
     tiles = []
     for z in range(cells_z):
@@ -228,7 +249,9 @@
             for c in range(3):
                 tiles.append((lambda s, r=ref, c=c, z=z: r[c, z, :, s], width))
     pack_strips(tiles, low_ref, high_ref, 0)
-    arrived(4)
+
+    for copy in copies:
+        copy.wait()
     done = len(tiles) // SLOTS
     tiles = []
     for layer in range(layers):
@@ -240,30 +263,19 @@
     pack_strips(tiles, low_ref, high_ref, done)
 
 
-def load(permit, efield, hfield, forward, material, grad_sum, mask):
+def strips(permit, efield, hfield, forward, material, grad_sum, mask):
     cells_z, width = efield.shape[1], efield.shape[3]
     count = (cells_z * 6 + grad_sum.shape[0] * 6) // SLOTS
     packed = (count, ROWS, LANES)
-    return pl.pallas_call(
-        load_kernel,
-        in_specs=[SMEM] + [ANY] * 5 + [VMEM],
-        out_specs=[VMEM] * 8,
-        out_shape=[
-            pltpu.VMEM(shape, jnp.float32)
-            for shape in (
-                efield.shape,
-                hfield.shape,
-                forward.shape,
-                grad_sum.shape,
-                packed,
-                packed,
-                (ROWS, width),
-                material.shape,
-            )
-        ],
-        scratch_shapes=[pltpu.VMEM(material.shape, jnp.int32), pltpu.SemaphoreType.DMA((11,))],
-        compiler_params=params(56),
-    )(permit, efield, hfield, forward, material, grad_sum, mask)
+    shapes = (forward.shape, packed, packed, (ROWS, width), material.shape)
+    return pl.pallas_call(
+        strips_kernel,
+        in_specs=[VMEM] * 3 + [ANY] + [VMEM] * 3,
+        out_specs=[VMEM] * 5,
+        out_shape=[fast(*shape) for shape in shapes],
+        scratch_shapes=[pltpu.SemaphoreType.DMA((3,))],
+        compiler_params=params(40),
+    )(permit.reshape(1, -1), efield, hfield, forward, material, grad_sum, mask)
 
 
 def edge_tile(load, width):
@@ -295,7 +307,7 @@
         edges_kernel,
         in_specs=[VMEM] * 6,
         out_specs=[VMEM] * 3,
-        out_shape=[f32(cells_z, 6, ROWS, LANES), f32(layers, 5, ROWS, LANES), f32(ROWS, LANES)],
+        out_shape=[fast(cells_z, 6, ROWS, LANES), fast(layers, 5, ROWS, LANES), fast(ROWS, LANES)],
         compiler_params=params(),
     )(*arrays)
 
@@ -333,7 +345,7 @@
 
 def y_faces(own_low, own_high, zfaces, xfaces):
     extra = math.ceil(face_count(xfaces[0]) / SLOTS)
-    packed = f32(own_low.shape[0] + extra, ROWS, LANES)
+    packed = fast(own_low.shape[0] + extra, ROWS, LANES)
     return pl.pallas_call(
         functools.partial(y_faces_kernel, (len(zfaces), len(xfaces))),
         in_specs=[VMEM] * (2 + len(zfaces) + len(xfaces)),
@@ -553,7 +565,7 @@
         functools.partial(own_gradient_kernel, (len(zfaces), len(xfaces))),
         in_specs=[VMEM] * (6 + len(zfaces) + len(xfaces)),
         out_specs=VMEM,
-        out_shape=f32(*grad_sum.shape),
+        out_shape=fast(*grad_sum.shape),
         scratch_shapes=fields_scratch(OWN, xfaces[0], None, grad_sum.shape[2]),
         compiler_params=params(),
     )(*arrays, *zfaces, *xfaces)
@@ -601,7 +613,7 @@
         functools.partial(edge_gradient_kernel, (len(zfaces), len(xfaces), len(yfaces)), per_device),
         in_specs=[VMEM] * (4 + len(faces)),
         out_specs=[VMEM] * count,
-        out_shape=[f32(ROWS, per_device * width + LANES)] * count,
+        out_shape=[fast(ROWS, per_device * width + LANES)] * count,
         scratch_shapes=fields_scratch(EDGE, xfaces[0], yfaces[0], width)
         + [pltpu.VMEM((layers, ROWS, LANES), jnp.float32)],
         compiler_params=params(),
@@ -731,7 +743,7 @@
         functools.partial(filter_kernel, count, per_device, width),
         in_specs=[VMEM] * (1 + count),
         out_specs=[VMEM] * count,
-        out_shape=[f32(per_device, ROWS, width)] * count,
+        out_shape=[fast(per_device, ROWS, width)] * count,
         scratch_shapes=[
             pltpu.VMEM((count, ROWS, per_device * width + LANES), jnp.float32),
             pltpu.VMEM((3 * rows, width + LANES), jnp.bfloat16),
@@ -777,14 +789,15 @@
 
 def on_device(efield, hfield, forward, material, permit, design_mask, grad_sum):
     layers, _, width = grad_sum.shape
-    zfaces = exchange(z_faces(efield, hfield), "gz")
-    efield, hfield, forward, grad_sum, own_low, own_high, mask, inv = load(
+    zfaces = exchange(z_faces(efield, hfield), "gz", "gy")
+    efield, hfield, material, grad_sum = load(efield, hfield, material, grad_sum)
+    xfaces = exchange(x_faces(efield, hfield, zfaces), "gx", "gy")
+    forward, own_low, own_high, mask, inv = strips(
         permit, efield, hfield, forward, material, grad_sum, design_mask
     )
     arrays = (efield, hfield, forward, inv, grad_sum, mask)
-    xfaces = exchange(x_faces(efield, hfield, zfaces), "gx")
     edges = own_edges(arrays)
-    yfaces = exchange(y_faces(own_low, own_high, zfaces, xfaces), "gy", wrap=True)
+    yfaces = exchange(y_faces(own_low, own_high, zfaces, xfaces), "gy", "gz")
     own = own_gradient(arrays, zfaces, xfaces)
     shares = edge_gradient(own, edges, zfaces, xfaces, yfaces)
     got = spread(shares)

time: 41.2 us -> 39.5 us (0.959)
  starting transfers between devices: 18 us -> 17 us
  Pallas kernels: 12.4 us -> 11.7 us
    ppermute x6, starting transfers between devices: 11 us -> 9.69 us  [spread(): got[k] = lax.ppermute(parts[k], 'gx', [(i, i ^ k) for i in range(count)])]
    ppermute x5, waiting for transfers between devices: 4.05 us -> 3.08 us  [exchange(): got.append(lax.ppermute(value, tuple(axes), pairs))]
    ppermute x6, waiting for transfers between devices: 5.75 us -> 6.65 us  [spread(): got[k] = lax.ppermute(parts[k], 'gx', [(i, i ^ k) for i in range(count)])]
    pallas_call x1, Pallas kernels: 1.5 us -> 0.89 us  [z_faces(): pl.pallas_call(z_faces_kernel, in_specs=[ANY] * 2, out_specs=[VMEM] * rou...]
    pallas_call x1 -> x2, Pallas kernels: 3.13 us -> 3.08 us  [the longest x1 1.85 us: load(): pl.pallas_call(load_kernel, in_specs=[ANY] * 4, out_specs=[VMEM] * 4, out...]
  transfers between devices with their start and end apart: 11 -> 11, of which waited for: 5 -> 7; matrix products, arithmetic and copies ran while one was open for 0% -> 0% of each run, Pallas kernels for 20% -> 20%
where the time goes in v5:
time: 39.5 us; the launch traced here: 39.2 us
  starting transfers between devices  17 us (43%)
  Pallas kernels  11.7 us (30%)
  waiting for transfers between devices  9.72 us (25%)
  between operations  0.74 us (2%)
    ppermute x6, starting transfers between devices, spread(): got[k] = lax.ppermute(parts[k], 'gx', [(i, i ^ k) for i in range(count)])  9.69 us
    ppermute x5, starting transfers between devices, exchange(): got.append(lax.ppermute(value, tuple(axes), pairs))  7.28 us
    ppermute x6, waiting for transfers between devices, spread(): got[k] = lax.ppermute(parts[k], 'gx', [(i, i ^ k) for i in range(count)])  6.65 us
    pallas_call x1, Pallas kernels, step(): pl.pallas_call(functools.partial(step_kernel, counts, layers), grid=(cell...  3.59 us
    ppermute x5, waiting for transfers between devices, exchange(): got.append(lax.ppermute(value, tuple(axes), pairs))  3.08 us
    pallas_call x1, Pallas kernels, load(): pl.pallas_call(load_kernel, in_specs=[ANY] * 4, out_specs=[VMEM] * 4, out...  1.85 us
    pallas_call x1, Pallas kernels, strips(): pl.pallas_call(strips_kernel, in_specs=[VMEM] * 3 + [ANY] + [VMEM] * 3, o...  1.24 us
    pallas_call x1, Pallas kernels, cone_filter(): pl.pallas_call(functools.partial(filter_kernel, count, per_device, width)...  1 us
  transfers between devices with their start and end apart: 11, of which 7 were waited for; matrix products, arithmetic and copies ran while one was open for 0% of the time, Pallas kernels for 20%

profile of v5, /device:TPU:0, one launch (start us, length us, event | category | flops | bytes accessed | tf_op | source)
XLA Modules:
  0.0 39.2 jit_solution(8877288094471031663)
XLA Ops:
  0.6 0.9 %shard_map.113 = f32[3,8,512]{2,1,0:T(8,128)S(1)} custom-call(f32[3,24,8,512]{3,2,1,0:T(8,128)} %refs_0_.2, f32[3,24,8,512]{3,2,1,0:T(8,128)} %refs_1_.1), custom_call_target="tpu_custom_call" | custom-call | tf_op jit(solution)/shard_map/pallas_call | solution.py:117
  1.5 3.0 %collective-permute-start = (f32[3,8,512]{2,1,0:T(8,128)S(1)}, f32[3,8,512]{2,1,0:T(8,128)S(1)}, u32[]{:S(2)}, u32[]{:S(2)}) collective-permute-start(f32[3,8,512]{2,1,0:T(8,128)S(1)} %shard_map.113), channel_id=1, source_target_pairs={{0,1},{2,3},{4,5},{6,7},{1,0},{3,2},{5,4},{7,6},{8,9},{10,11},{12,... | collective-permute-start | bytes 147464 | tf_op jit(solution)/shard_map/ppermute | solution.py:65
  4.6 1.8 %shard_map.111 = (f32[3,24,8,512]{3,2,1,0:T(8,128)S(1)}, f32[3,24,8,512]{3,2,1,0:T(8,128)S(1)}, s32[24,8,512]{2,1,0:T(8,128)S(1)}, f32[16,8,512]{2,1,0:T(8,128)S(1)}) custom-call(f32[3,24,8,512]{3,2,1,0:T(8,128)} %refs_0_.2, f32[3,24,8,512]{3,2,1,0:T(8,128)} %refs_1_.1, s32[24,8,512]{2,1,0:T(8,128)} %mat_in.1, f32[16,8,512]{2,1,0:T(8,128)} %grad_in.1), custom_call_target="tpu_custom_call" | custom-call | tf_op jit(solution)/shard_map/pallas_call | solution.py:210
  6.4 0.2 collective-permute-done.refs_2_.refs_6_.refs_4_.refs_3_
  6.6 0.0 copy-start
  6.6 0.0 copy-start.2
  6.6 0.0 copy-start.3
  6.6 0.1 shard_map.114
  6.8 2.1 %collective-permute-start.1 = (f32[72,512]{1,0:T(8,128)S(1)}, f32[72,512]{1,0:T(8,128)S(1)}, u32[]{:S(2)}, u32[]{:S(2)}) collective-permute-start(f32[72,512]{1,0:T(8,128)S(1)} %get-tuple-element.36), channel_id=1, source_target_pairs={{0,8},{2,10},{4,12},{6,14},{8,0},{10,2},{12,4},{14,6},{16,24},{18,... | collective-permute-start | bytes 442376 | tf_op jit(solution)/shard_map/ppermute | solution.py:65
  8.9 0.0 collective-permute-start.2
  8.9 0.0 copy-done
  8.9 0.0 copy-done.2
  8.9 0.0 copy-done.3
  8.9 1.2 %shard_map.112 = (f32[3,24,8,512]{3,2,1,0:T(8,128)S(1)}, f32[15,8,128]{2,1,0:T(8,128)S(1)}, f32[15,8,128]{2,1,0:T(8,128)S(1)}, f32[8,512]{1,0:T(8,128)S(1)}, f32[24,8,512]{2,1,0:T(8,128)S(1)}) custom-call(f32[1,4]{1,0:T(1,128)S(1)} %bitcast.1, f32[3,24,8,512]{3,2,1,0:T(8,128)S(1)} %get-tuple-element.31.e_ref.refs_0_, ...), custom_call_target="tpu_custom_call" | custom-call | tf_op jit(solution)/shard_map/pallas_call | solution.py:271
  10.2 1.9 %collective-permute-done.1.refs_3_.refs_7_.refs_5_.refs_4_ = f32[72,512]{1,0:T(8,128)S(1)} collective-permute-done((f32[72,512]{1,0:T(8,128)S(1)}, f32[72,512]{1,0:T(8,128)S(1)}, u32[]{:S(2)}, u32[]{:S(2)}) %collective-permute-start.1) | collective-permute-done | bytes 147488 | tf_op jit(solution)/shard_map/ppermute | solution.py:65
  12.0 0.0 collective-permute-done.2.refs_4_.refs_8_.refs_6_.refs_5_
  12.1 0.1 shard_map.115
  12.2 0.1 collective-permute-start.3
  12.3 2.0 %collective-permute-start.4 = (f32[17,8,128]{2,1,0:T(8,128)S(1)}, f32[17,8,128]{2,1,0:T(8,128)S(1)}, u32[]{:S(2)}, u32[]{:S(2)}) collective-permute-start(f32[17,8,128]{2,1,0:T(8,128)S(1)} %get-tuple-element.41), channel_id=1, source_target_pairs={{0,1},{1,0},{2,4},{3,5},{4,2},{5,3},{6,7},{7,6},{8,9},{9,8},{10,12... | collective-permute-start | bytes 208904 | tf_op jit(solution)/shard_map/ppermute | solution.py:65
  14.3 0.5 %shard_map.117 = (f32[24,6,8,128]{3,2,1,0:T(8,128)S(1)}, f32[16,5,8,128]{3,2,1,0:T(8,128)S(1)}, f32[8,128]{1,0:T(8,128)S(1)}) custom-call(f32[3,24,8,512]{3,2,1,0:T(8,128)S(1)} %get-tuple-element.31.e_ref.refs_0_, f32[3,24,8,512]{3,2,1,0:T(8,128)S(1)} %get-tuple-element.32.h_ref.refs_1_, f32[3,24,8,512]{3,2,1,0:T(8,128)S(1)} %get-tuple-element.42.refs_2_.f_ref, ...), custom_call_target="tpu_custom_call" | custom-call | tf_op jit(solution)/shard_map/pallas_call | solution.py:306
  14.8 0.8 %shard_map.116.refs_0_ = f32[16,8,512]{2,1,0:T(8,128)S(1)} custom-call(f32[3,24,8,512]{3,2,1,0:T(8,128)S(1)} %get-tuple-element.31.e_ref.refs_0_, f32[3,24,8,512]{3,2,1,0:T(8,128)S(1)} %get-tuple-element.32.h_ref.refs_1_, f32[3,24,8,512]{3,2,1,0:T(8,128)S(1)} %get-tuple-element.42.refs_2_.f_ref, f32[24,8,512]{2,1,0:T(8,128)S(1)} %get-tuple-element.35.refs_3_.inv_ref.refs_2_, ...), custom_call_target="tpu_custom_call" | custom-call | tf_op jit(solution)/shard_map/pallas_call | solution.py:564
  15.6 0.0 copy-start.1
  15.6 0.0 collective-permute-done.3.refs_7_.refs_6_
  15.6 1.0 %collective-permute-done.4.refs_8_.refs_7_ = f32[17,8,128]{2,1,0:T(8,128)S(1)} collective-permute-done((f32[17,8,128]{2,1,0:T(8,128)S(1)}, f32[17,8,128]{2,1,0:T(8,128)S(1)}, u32[]{:S(2)}, u32[]{:S(2)}) %collective-permute-start.4) | collective-permute-done | bytes 69664 | tf_op jit(solution)/shard_map/ppermute | solution.py:65
  16.6 0.9 %shard_map.118 = (f32[8,2176]{1,0:T(8,128)S(1)}, f32[8,2176]{1,0:T(8,128)S(1)}, f32[8,2176]{1,0:T(8,128)S(1)}, f32[8,2176]{1,0:T(8,128)S(1)}) custom-call(f32[16,8,512]{2,1,0:T(8,128)S(1)} %shard_map.116.refs_0_, f32[24,6,8,128]{3,2,1,0:T(8,128)S(1)} %get-tuple-element.44.refs_1_, f32[16,5,8,128]{3,2,1,0:T(8,128)S(1)} %get-tuple-element.45.refs_2_, ...), custom_call_target="tpu_custom_call" | custom-call | tf_op jit(solution)/shard_map/pallas_call | solution.py:612
  17.5 4.1 %collective-permute-start.5 = (f32[8,2176]{1,0:T(8,128)S(1)}, f32[8,2176]{1,0:T(8,128)S(1)}, u32[]{:S(2)}, u32[]{:S(2)}) collective-permute-start(f32[8,2176]{1,0:T(8,128)S(1)} %get-tuple-element.47.refs_8_), channel_id=1, source_target_pairs={{0,24},{8,16},{16,8},{24,0},{1,25},{9,17},{17,9},{25,1},{2,26},{10... | collective-permute-start | bytes 208904 | tf_op jit(solution)/shard_map/ppermute | solution.py:786
  21.6 0.6 %collective-permute-start.6 = (f32[8,2176]{1,0:T(8,128)S(1)}, f32[8,2176]{1,0:T(8,128)S(1)}, u32[]{:S(2)}, u32[]{:S(2)}) collective-permute-start(f32[8,2176]{1,0:T(8,128)S(1)} %get-tuple-element.48.refs_9_), channel_id=1, source_target_pairs={{0,16},{8,24},{16,0},{24,8},{1,17},{9,25},{17,1},{25,9},{2,18},{10... | collective-permute-start | bytes 208904 | tf_op jit(solution)/shard_map/ppermute | solution.py:786
  22.3 0.5 %collective-permute-start.7 = (f32[8,2176]{1,0:T(8,128)S(1)}, f32[8,2176]{1,0:T(8,128)S(1)}, u32[]{:S(2)}, u32[]{:S(2)}) collective-permute-start(f32[8,2176]{1,0:T(8,128)S(1)} %get-tuple-element.49.refs_10_), channel_id=1, source_target_pairs={{0,8},{8,0},{16,24},{24,16},{1,9},{9,1},{17,25},{25,17},{2,10},{10... | collective-permute-start | bytes 208904 | tf_op jit(solution)/shard_map/ppermute | solution.py:786
  22.7 1.5 %collective-permute-done.5.refs_1_ = f32[8,2176]{1,0:T(8,128)S(1)} collective-permute-done((f32[8,2176]{1,0:T(8,128)S(1)}, f32[8,2176]{1,0:T(8,128)S(1)}, u32[]{:S(2)}, u32[]{:S(2)}) %collective-permute-start.5) | collective-permute-done | bytes 69664 | tf_op jit(solution)/shard_map/ppermute | solution.py:786
  24.2 4.3 %collective-permute-done.6.refs_2_ = f32[8,2176]{1,0:T(8,128)S(1)} collective-permute-done((f32[8,2176]{1,0:T(8,128)S(1)}, f32[8,2176]{1,0:T(8,128)S(1)}, u32[]{:S(2)}, u32[]{:S(2)}) %collective-permute-start.6) | collective-permute-done | bytes 69664 | tf_op jit(solution)/shard_map/ppermute | solution.py:786
  28.6 0.0 collective-permute-done.7.refs_3_
  28.6 0.0 copy-done.1
  28.6 1.0 %shard_map.120 = (f32[4,8,512]{2,1,0:T(8,128)S(1)}, f32[4,8,512]{2,1,0:T(8,128)S(1)}, f32[4,8,512]{2,1,0:T(8,128)S(1)}, f32[4,8,512]{2,1,0:T(8,128)S(1)}) custom-call(bf16[112,48]{1,0:T(8,128)(2,1)S(1)} %copy-done.1, f32[8,2176]{1,0:T(8,128)S(1)} %collective-permute-done.5.refs_1_, f32[8,2176]{1,0:T(8,128)S(1)} %collective-permute-done.6.refs_2_, ...), custom_call_target="tpu_custom_call" | custom-call | tf_op jit(solution)/shard_map/pallas_call | solution.py:742
  29.6 3.3 %collective-permute-start.8 = (f32[4,8,512]{2,1,0:T(8,128)S(1)}, f32[4,8,512]{2,1,0:T(8,128)S(1)}, u32[]{:S(2)}, u32[]{:S(2)}) collective-permute-start(f32[4,8,512]{2,1,0:T(8,128)S(1)} %get-tuple-element.54), channel_id=1, source_target_pairs={{0,24},{8,16},{16,8},{24,0},{1,25},{9,17},{17,9},{25,1},{2,26},{10... | collective-permute-start | bytes 196616 | tf_op jit(solution)/shard_map/ppermute | solution.py:786
  32.8 0.0 collective-permute-start.9
  32.8 1.2 %collective-permute-start.10 = (f32[4,8,512]{2,1,0:T(8,128)S(1)}, f32[4,8,512]{2,1,0:T(8,128)S(1)}, u32[]{:S(2)}, u32[]{:S(2)}) collective-permute-start(f32[4,8,512]{2,1,0:T(8,128)S(1)} %get-tuple-element.56), channel_id=1, source_target_pairs={{0,8},{8,0},{16,24},{24,16},{1,9},{9,1},{17,25},{25,17},{2,10},{10... | collective-permute-start | bytes 196616 | tf_op jit(solution)/shard_map/ppermute | solution.py:786
  34.0 3.6 %shard_map.119 = (f32[3,24,8,512]{3,2,1,0:T(8,128)}, f32[3,24,8,512]{3,2,1,0:T(8,128)}, f32[16,8,512]{2,1,0:T(8,128)}) custom-call(f32[3,24,8,512]{3,2,1,0:T(8,128)S(1)} %get-tuple-element.31.e_ref.refs_0_, f32[3,24,8,512]{3,2,1,0:T(8,128)S(1)} %get-tuple-element.32.h_ref.refs_1_, f32[24,8,512]{2,1,0:T(8,128)S(1)} %get-tuple-element.35.refs_3_.inv_ref.refs_2_, ...), custom_call_target="tpu_custom_call" | custom-call | tf_op jit(solution)/shard_map/pallas_call | solution.py:661
  37.6 0.0 collective-permute-done.8.refs_0_
  37.6 0.7 %collective-permute-done.9.refs_1_ = f32[4,8,512]{2,1,0:T(8,128)S(1)} collective-permute-done((f32[4,8,512]{2,1,0:T(8,128)S(1)}, f32[4,8,512]{2,1,0:T(8,128)S(1)}, u32[]{:S(2)}, u32[]{:S(2)}) %collective-permute-start.9) | collective-permute-done | bytes 65568 | tf_op jit(solution)/shard_map/ppermute | solution.py:786
  38.4 0.1 collective-permute-done.10.refs_2_
  38.4 0.7 %shard_map.121 = f32[16,8,512]{2,1,0:T(8,128)} custom-call(f32[4,8,512]{2,1,0:T(8,128)S(1)} %collective-permute-done.8.refs_0_, f32[4,8,512]{2,1,0:T(8,128)S(1)} %collective-permute-done.9.refs_1_, f32[4,8,512]{2,1,0:T(8,128)S(1)} %collective-permute-done.10.refs_2_, f32[4,8,512]{2,1,0:T(8,128)S(1)} %get-tuple-element.57.refs_3_), custom_call_target="tpu_custom_call" | custom-call | tf_op jit(solution)/shard_map/pallas_call | solution.py:772
Async XLA Ops:
  1.5 5.1 %collective-permute-start = (f32[3,8,512]{2,1,0:T(8,128)S(1)}, f32[3,8,512]{2,1,0:T(8,128)S(1)}, u32[]{:S(2)}, u32[]{:S(2)}) collective-permute-start(f32[3,8,512]{2,1,0:T(8,128)S(1)} %shard_map.113), channel_id=1, source_target_pairs={{0,1},{2,3},{4,5},{6,7},{1,0},{3,2},{5,4},{7,6},{8,9},{10,11},{12,... | collective-permute-start | bytes 147464 | tf_op jit(solution)/shard_map/ppermute | solution.py:65
  6.6 2.3 %copy-start = (f32[3,24,8,512]{3,2,1,0:T(8,128)S(1)}, f32[3,24,8,512]{3,2,1,0:T(8,128)}, u32[]{:S(2)}) copy-start(f32[3,24,8,512]{3,2,1,0:T(8,128)} %f_in.1) | copy-start | bytes 3538948
  6.6 2.3 %copy-start.2 = (f32[4]{0:T(128)S(1)}, f32[4]{0:T(128)}, u32[]{:S(2)}) copy-start(f32[4]{0:T(128)} %param.12) | copy-start | bytes 52
  6.6 2.3 %copy-start.3 = (s32[1,64]{1,0:T(1,128)S(1)}, s32[1,64]{1,0:T(1,128)}, u32[]{:S(2)}) copy-start(s32[1,64]{1,0:T(1,128)} %mask_ref.1) | copy-start | bytes 772
  6.8 5.3 %collective-permute-start.1 = (f32[72,512]{1,0:T(8,128)S(1)}, f32[72,512]{1,0:T(8,128)S(1)}, u32[]{:S(2)}, u32[]{:S(2)}) collective-permute-start(f32[72,512]{1,0:T(8,128)S(1)} %get-tuple-element.36), channel_id=1, source_target_pairs={{0,8},{2,10},{4,12},{6,14},{8,0},{10,2},{12,4},{14,6},{16,24},{18,... | collective-permute-start | bytes 442376 | tf_op jit(solution)/shard_map/ppermute | solution.py:65
  8.9 3.1 %collective-permute-start.2 = (f32[72,512]{1,0:T(8,128)S(1)}, f32[72,512]{1,0:T(8,128)S(1)}, u32[]{:S(2)}, u32[]{:S(2)}) collective-permute-start(f32[72,512]{1,0:T(8,128)S(1)} %get-tuple-element.37), channel_id=1, source_target_pairs={{0,2},{2,0},{4,6},{6,4},{8,16},{10,18},{12,20},{14,22},{16,8},{18,... | collective-permute-start | bytes 442376 | tf_op jit(solution)/shard_map/ppermute | solution.py:65
  12.2 3.4 %collective-permute-start.3 = (f32[17,8,128]{2,1,0:T(8,128)S(1)}, f32[17,8,128]{2,1,0:T(8,128)S(1)}, u32[]{:S(2)}, u32[]{:S(2)}) collective-permute-start(f32[17,8,128]{2,1,0:T(8,128)S(1)} %get-tuple-element.40), channel_id=1, source_target_pairs={{0,2},{1,3},{2,0},{3,1},{4,6},{5,7},{6,4},{7,5},{8,10},{9,11},{10,... | collective-permute-start | bytes 208904 | tf_op jit(solution)/shard_map/ppermute | solution.py:65
  12.3 4.4 %collective-permute-start.4 = (f32[17,8,128]{2,1,0:T(8,128)S(1)}, f32[17,8,128]{2,1,0:T(8,128)S(1)}, u32[]{:S(2)}, u32[]{:S(2)}) collective-permute-start(f32[17,8,128]{2,1,0:T(8,128)S(1)} %get-tuple-element.41), channel_id=1, source_target_pairs={{0,1},{1,0},{2,4},{3,5},{4,2},{5,3},{6,7},{7,6},{8,9},{9,8},{10,12... | collective-permute-start | bytes 208904 | tf_op jit(solution)/shard_map/ppermute | solution.py:65
  15.6 13.0 %copy-start.1 = (bf16[112,48]{1,0:T(8,128)(2,1)S(1)}, bf16[112,48]{1,0:T(8,128)(2,1)}, u32[]{:S(2)}) copy-start(bf16[112,48]{1,0:T(8,128)(2,1)} %constant.2.clone.refs_0_) | copy-start | bytes 32260
  17.5 6.7 %collective-permute-start.5 = (f32[8,2176]{1,0:T(8,128)S(1)}, f32[8,2176]{1,0:T(8,128)S(1)}, u32[]{:S(2)}, u32[]{:S(2)}) collective-permute-start(f32[8,2176]{1,0:T(8,128)S(1)} %get-tuple-element.47.refs_8_), channel_id=1, source_target_pairs={{0,24},{8,16},{16,8},{24,0},{1,25},{9,17},{17,9},{25,1},{2,26},{10... | collective-permute-start | bytes 208904 | tf_op jit(solution)/shard_map/ppermute | solution.py:786
  21.6 6.9 %collective-permute-start.6 = (f32[8,2176]{1,0:T(8,128)S(1)}, f32[8,2176]{1,0:T(8,128)S(1)}, u32[]{:S(2)}, u32[]{:S(2)}) collective-permute-start(f32[8,2176]{1,0:T(8,128)S(1)} %get-tuple-element.48.refs_9_), channel_id=1, source_target_pairs={{0,16},{8,24},{16,0},{24,8},{1,17},{9,25},{17,1},{25,9},{2,18},{10... | collective-permute-start | bytes 208904 | tf_op jit(solution)/shard_map/ppermute | solution.py:786
  22.3 6.3 %collective-permute-start.7 = (f32[8,2176]{1,0:T(8,128)S(1)}, f32[8,2176]{1,0:T(8,128)S(1)}, u32[]{:S(2)}, u32[]{:S(2)}) collective-permute-start(f32[8,2176]{1,0:T(8,128)S(1)} %get-tuple-element.49.refs_10_), channel_id=1, source_target_pairs={{0,8},{8,0},{16,24},{24,16},{1,9},{9,1},{17,25},{25,17},{2,10},{10... | collective-permute-start | bytes 208904 | tf_op jit(solution)/shard_map/ppermute | solution.py:786
  29.6 8.0 %collective-permute-start.8 = (f32[4,8,512]{2,1,0:T(8,128)S(1)}, f32[4,8,512]{2,1,0:T(8,128)S(1)}, u32[]{:S(2)}, u32[]{:S(2)}) collective-permute-start(f32[4,8,512]{2,1,0:T(8,128)S(1)} %get-tuple-element.54), channel_id=1, source_target_pairs={{0,24},{8,16},{16,8},{24,0},{1,25},{9,17},{17,9},{25,1},{2,26},{10... | collective-permute-start | bytes 196616 | tf_op jit(solution)/shard_map/ppermute | solution.py:786
  32.8 5.5 %collective-permute-start.9 = (f32[4,8,512]{2,1,0:T(8,128)S(1)}, f32[4,8,512]{2,1,0:T(8,128)S(1)}, u32[]{:S(2)}, u32[]{:S(2)}) collective-permute-start(f32[4,8,512]{2,1,0:T(8,128)S(1)} %get-tuple-element.55), channel_id=1, source_target_pairs={{0,16},{8,24},{16,0},{24,8},{1,17},{9,25},{17,1},{25,9},{2,18},{10... | collective-permute-start | bytes 196616 | tf_op jit(solution)/shard_map/ppermute | solution.py:786
  32.8 5.6 %collective-permute-start.10 = (f32[4,8,512]{2,1,0:T(8,128)S(1)}, f32[4,8,512]{2,1,0:T(8,128)S(1)}, u32[]{:S(2)}, u32[]{:S(2)}) collective-permute-start(f32[4,8,512]{2,1,0:T(8,128)S(1)} %get-tuple-element.56), channel_id=1, source_target_pairs={{0,8},{8,0},{16,24},{24,16},{1,9},{9,1},{17,25},{25,17},{2,10},{10... | collective-permute-start | bytes 196616 | tf_op jit(solution)/shard_map/ppermute | solution.py:786

commit v6 on v5

--- a/solution.py
+++ b/solution.py
@@ -333,7 +333,7 @@
 def y_faces_kernel(counts, *refs):
     own_low, own_high = refs[:2]
     zfaces, xfaces = refs[2 : 2 + counts[0]], refs[2 + counts[0] : 2 + sum(counts)]
-    sends, (low_ref, high_ref) = refs[2 + sum(counts) : -2], refs[-2:]
+    sends, (low_ref, high_ref) = refs[3 + sum(counts) : -2], refs[-2:]
     own = own_low.shape[0]
     pack_strips(face_tiles(zfaces, xfaces), low_ref, high_ref, 0)
     side = Side("gy")
@@ -343,17 +343,17 @@
         ref[own:] = value
 
 
-def y_faces(own_low, own_high, zfaces, xfaces):
+def y_faces(own_low, own_high, zfaces, xfaces, after):
     extra = math.ceil(face_count(xfaces[0]) / SLOTS)
     packed = fast(own_low.shape[0] + extra, ROWS, LANES)
     return pl.pallas_call(
         functools.partial(y_faces_kernel, (len(zfaces), len(xfaces))),
-        in_specs=[VMEM] * (2 + len(zfaces) + len(xfaces)),
+        in_specs=[VMEM] * (2 + len(zfaces) + len(xfaces)) + [ANY],
         out_specs=[VMEM] * rounds("gy"),
         out_shape=[packed] * rounds("gy"),
         scratch_shapes=[pltpu.VMEM((extra, ROWS, LANES), jnp.float32)] * 2,
         compiler_params=params(),
-    )(own_low, own_high, *zfaces, *xfaces)
+    )(own_low, own_high, *zfaces, *xfaces, after)
 
 
 OWN, CIRCLE, EDGE = range(3)
@@ -546,39 +546,51 @@
     return out
 
 
-def own_gradient_kernel(counts, *refs):
+def own_gradient_kernel(counts, per_device, *refs):
     e_ref, h_ref, f_ref, inv_ref, grad_ref, mask_ref = refs[:6]
     zfaces, xfaces = refs[6 : 6 + counts[0]], refs[6 + counts[0] : 6 + sum(counts)]
-    grad_out, scratch = refs[6 + sum(counts)], refs[7 + sum(counts) :]
-    layers = grad_ref.shape[0]
+    shares, (own_ref, *scratch) = refs[6 + sum(counts) : -3][::-1], refs[-3:]
+    layers, _, width = grad_ref.shape
     fields = Fields(OWN, layers, (e_ref, h_ref), zfaces, xfaces, None, scratch)
 
     def store(layer, value):
-        grad_out[layer] = value
+        own_ref[layer] = value
 
     fields.gradient(layers, (f_ref, inv_ref, grad_ref, mask_ref), store)
 
+    me = lax.axis_index("gx")
+    for k, share in enumerate(shares):
+        chunk = lax.bitwise_xor(me, k)
+        for i in range(per_device):
+            share[:, i * width : (i + 1) * width] = own_ref[chunk * per_device + i]
+
 
 def own_gradient(arrays, zfaces, xfaces):
-    grad_sum = arrays[4]
-    return pl.pallas_call(
-        functools.partial(own_gradient_kernel, (len(zfaces), len(xfaces))),
+    layers, _, width = arrays[4].shape
+    count = lax.axis_size("gx")
+    per_device = layers // count
+    *shares, own = pl.pallas_call(
+        functools.partial(own_gradient_kernel, (len(zfaces), len(xfaces)), per_device),
         in_specs=[VMEM] * (6 + len(zfaces) + len(xfaces)),
-        out_specs=VMEM,
-        out_shape=fast(*grad_sum.shape),
-        scratch_shapes=fields_scratch(OWN, xfaces[0], None, grad_sum.shape[2]),
+        out_specs=[VMEM] * (count + 1),
+        out_shape=[fast(ROWS, per_device * width)] * count + [fast(layers, ROWS, width)],
+        scratch_shapes=fields_scratch(OWN, xfaces[0], None, width),
         compiler_params=params(),
     )(*arrays, *zfaces, *xfaces)
-
-
-def edge_gradient_kernel(counts, per_device, *refs):
+    return shares[::-1], own
+
+
+PART = 2 * STRIP
+
+
+def edge_gradient_kernel(counts, *refs):
     own_ref, eh_ref, grad_ref, mask_ref = refs[:4]
     ends = np.cumsum((4,) + counts)
     zfaces, xfaces, yfaces = (refs[i:j] for i, j in zip(ends[:-1], ends[1:]))
-    sends, scratch, edge_ref = refs[ends[-1] : -4], refs[-4:-1], refs[-1]
+    (message, edge_ref), scratch = refs[ends[-1] : -3], refs[-3:]
     layers, _, width = own_ref.shape
     lane = lax.broadcasted_iota(jnp.int32, (ROWS, LANES), 1)
-    me = lax.axis_index("gx")
+    first, last = STRIP, LANES - STRIP - 1
     fields = Fields(EDGE, layers, eh_ref, zfaces, xfaces, yfaces, scratch)
 
     def store(layer, value):
@@ -586,88 +598,98 @@
 
     fields.gradient(layers, (grad_ref, mask_ref), store)
 
-    for k, send_ref in enumerate(sends[::-1]):
-        chunk = lax.bitwise_xor(me, k)
+    per_tile = LANES // PART
+    for start in range(0, layers, per_tile):
         packed = jnp.zeros((ROWS, LANES), jnp.float32)
-        for i in range(per_device):
-            layer = chunk * per_device + i
+        for j in range(min(per_tile, layers - start)):
+            layer = start + j
             edge = edge_ref[layer]
-            at = i * width
-            head, tail = own_ref[layer, :, 0:LANES], own_ref[layer, :, width - LANES :]
-            send_ref[:, at : at + LANES] = jnp.where(lane == 0, pltpu.roll(edge, LANES - STRIP, 1), head)
-            send_ref[:, at + LANES : at + width - LANES] = own_ref[layer, :, LANES : width - LANES]
-            send_ref[:, at + width - LANES : at + width] = jnp.where(
-                lane == LANES - 1, pltpu.roll(edge, STRIP, 1), tail
-            )
-            side = pltpu.roll(edge, (2 * STRIP * i + STRIP) % LANES, 1)
-            packed = jnp.where(lane // (2 * STRIP) == i, side, packed)
-        send_ref[:, per_device * width :] = packed
+            own = edge_tile(lambda s: own_ref[layer, :, s], width)
+            more = jnp.where(jnp.logical_or(lane == first, lane == last), edge - own, edge)
+            left = pltpu.roll(more, (PART * j - 1) % LANES, 1)
+            right = pltpu.roll(more, (PART * j + STRIP - last) % LANES, 1)
+            packed = jnp.where(lane // STRIP == 2 * j, left, packed)
+            packed = jnp.where(lane // STRIP == 2 * j + 1, right, packed)
+        message[:, start // per_tile * LANES : (start // per_tile + 1) * LANES] = packed
 
 
 def edge_gradient(own, edges, zfaces, xfaces, yfaces):
     layers, _, width = own.shape
-    count = lax.axis_size("gx")
-    per_device = layers // count
     faces = (*zfaces, *xfaces, *yfaces)
-    shares = pl.pallas_call(
-        functools.partial(edge_gradient_kernel, (len(zfaces), len(xfaces), len(yfaces)), per_device),
+    tiles = math.ceil(layers * PART / LANES)
+    return pl.pallas_call(
+        functools.partial(edge_gradient_kernel, (len(zfaces), len(xfaces), len(yfaces))),
         in_specs=[VMEM] * (4 + len(faces)),
-        out_specs=[VMEM] * count,
-        out_shape=[fast(ROWS, per_device * width + LANES)] * count,
-        scratch_shapes=fields_scratch(EDGE, xfaces[0], yfaces[0], width)
-        + [pltpu.VMEM((layers, ROWS, LANES), jnp.float32)],
+        out_specs=[VMEM] * 2,
+        out_shape=[fast(ROWS, tiles * LANES), fast(layers, ROWS, LANES)],
+        scratch_shapes=fields_scratch(EDGE, xfaces[0], yfaces[0], width),
         compiler_params=params(),
     )(own, *edges, *faces)
-    return shares[::-1]
-
-
-def step_kernel(counts, layers, *refs):
-    e_ref, h_ref, inv_ref = refs[:3]
-    ends = np.cumsum((3,) + counts)
-    zfaces, xfaces, yfaces, shares = (refs[i:j] for i, j in zip(ends[:-1], ends[1:]))
-    shares = shares[::-1]
-    (e_out, h_out, grad_out), scratch, carry_ref = refs[ends[-1] : -4], refs[-4:-1], refs[-1]
-    width = e_ref.shape[3]
-    fields = Fields(CIRCLE, layers, (e_ref, h_ref), zfaces, xfaces, yfaces, scratch)
-    a = pl.program_id(0)
+
+
+def step_kernel(counts, *refs):
+    e_ref, h_ref, inv_ref, own_ref, edge_ref = refs[:5]
+    ends = np.cumsum((5,) + counts)
+    zfaces, xfaces, yfaces = (refs[i:j] for i, j in zip(ends[:-1], ends[1:]))
+    e_out, h_out, grad_out = refs[ends[-1] + 1 : ends[-1] + 4]
+    left_wide, right_wide, ybuf, e_new, h_new, grad_new, sems = refs[ends[-1] + 4 :]
+    layers, _, width = own_ref.shape
+    lane = lax.broadcasted_iota(jnp.int32, (ROWS, LANES), 1)
+
+    for layer in range(layers):
+        edge = edge_ref[layer]
+        head, tail = own_ref[layer, :, 0:LANES], own_ref[layer, :, width - LANES :]
+        grad_new[layer] = own_ref[layer]
+        grad_new[layer, :, 0:LANES] = jnp.where(lane == 0, pltpu.roll(edge, LANES - STRIP, 1), head)
+        grad_new[layer, :, width - LANES :] = jnp.where(lane == LANES - 1, pltpu.roll(edge, STRIP, 1), tail)
+    grad_copy = pltpu.make_async_copy(grad_new, grad_out, sems.at[0, 0])
+    grad_copy.start()
+
+    fields = Fields(CIRCLE, layers, (e_ref, h_ref), zfaces, xfaces, yfaces, (left_wide, right_wide, ybuf))
 
     def emit(a, b, efield, hfield, curl):
-        half_inv = inv_ref[ROWS * a + b]
+        z = ROWS * a + b
+        half_inv = inv_ref[z]
         for c in range(3):
-            e_out[c, b] = efield[c][:, :width] + half_inv * curl[c][:, :width]
-            h_out[c, b] = hfield[c][:, :width]
-
-    @pl.when(a == 0)
-    def _():
-        for i, v in enumerate(fields.start(0)):
-            carry_ref[i] = v
-        per_device = layers // len(shares)
-        me = lax.axis_index("gx")
-        for k, share in enumerate(shares):
-            chunk = lax.bitwise_xor(me, k)
-            for i in range(per_device):
-                grad_out[chunk * per_device + i] = share[:, i * width : (i + 1) * width]
-
-    carry = tuple(carry_ref[i] for i in range(4))
-    for i, v in enumerate(fields.group(a, carry, emit)):
-        carry_ref[i] = v
-
-
-def step(efield, hfield, inv, zfaces, xfaces, yfaces, shares, layers):
+            e_new[c, z] = efield[c][:, :width] + half_inv * curl[c][:, :width]
+            h_new[c, z] = hfield[c][:, :width]
+
+    def copies(a):
+        here = pl.ds(a * ROWS, ROWS)
+        return [
+            pltpu.make_async_copy(new.at[c, here], out.at[c, here], sems.at[1 + a, 3 * n + c])
+            for n, (new, out) in enumerate(((e_new, e_out), (h_new, h_out)))
+            for c in range(3)
+        ]
+
+    def body(a, carry):
+        carry = fields.group(a, carry, emit)
+        for copy in copies(a):
+            copy.start()
+        return carry
+
+    lax.fori_loop(0, fields.groups, body, fields.start(0))
+    for a in range(fields.groups):
+        for copy in copies(a):
+            copy.wait()
+    grad_copy.wait()
+
+
+def step(efield, hfield, inv, own, edge, zfaces, xfaces, yfaces, after):
     _, cells_z, _, width = efield.shape
-    block = pl.BlockSpec((3, ROWS, ROWS, width), lambda a: (0, a, 0, 0))
-    groups = (zfaces, xfaces, yfaces, shares[::-1])
+    groups = (zfaces, xfaces, yfaces)
     counts = tuple(len(group) for group in groups)
-    return pl.pallas_call(
-        functools.partial(step_kernel, counts, layers),
-        grid=(cells_z // ROWS,),
-        in_specs=[VMEM] * (3 + sum(counts)),
-        out_specs=[block, block, VMEM],
-        out_shape=[f32(*efield.shape)] * 2 + [f32(layers, ROWS, width)],
+    shapes = (efield.shape, hfield.shape, own.shape)
+    return pl.pallas_call(
+        functools.partial(step_kernel, counts),
+        in_specs=[VMEM] * (5 + sum(counts)) + [ANY],
+        out_specs=[ANY] * 3,
+        out_shape=[f32(*shape) for shape in shapes],
         scratch_shapes=fields_scratch(CIRCLE, xfaces[0], yfaces[0], width)
-        + [pltpu.VMEM((4, ROWS, width + LANES), jnp.float32)],
+        + [pltpu.VMEM(shape, jnp.float32) for shape in shapes]
+        + [pltpu.SemaphoreType.DMA((1 + cells_z // ROWS, 6))],
         compiler_params=params(),
-    )(efield, hfield, inv, *(one for group in groups for one in group))
+    )(efield, hfield, inv, own, edge, *(one for group in groups for one in group), after)
 
 
 def cone_matrix(rows):
@@ -693,90 +715,148 @@
     return jnp.where(row % 2 < 1, pltpu.roll(v, ROWS - 1, 0), pltpu.roll(v, 1, 0))
 
 
+def split_rows(symmetric, parts):
+    rows = symmetric.shape[0]
+    high = symmetric.astype(jnp.bfloat16)
+    low = (symmetric - high.astype(jnp.float32)).astype(jnp.bfloat16)
+    parts[0:rows, :] = high
+    parts[rows : 2 * rows, :] = high
+    parts[2 * rows : 3 * rows, :] = low
+
+
+def cone(taps_ref, parts, rows):
+    wide = parts.shape[1]
+    mixed = jnp.dot(taps_ref[...], parts[...], preferred_element_type=jnp.float32)
+    total = mixed[0:rows]
+    for b in range(1, RADIUS + 1):
+        part = mixed[b * rows : (b + 1) * rows]
+        total = total + (pltpu.roll(part, b, 1) + pltpu.roll(part, wide - b, 1))
+    return total
+
+
 def filter_kernel(count, per_device, width, *refs):
+    taps_ref, edges_ref = refs[:2]
+    got = refs[count + 1 : 1 : -1]
+    outs = refs[2 + count : 2 + 2 * count]
+    slabs, parts, done = refs[2 + 2 * count :]
+    me = lax.axis_index("gx")
+    half = count // 2
+    rows = half * ROWS
+    for k in range(count):
+        slabs[lax.bitwise_xor(me, k)] = got[k][...]
+
+    side = jnp.zeros((rows, LANES), jnp.float32)
+    for i in range(per_device):
+        here = slice(i * width, (i + 1) * width)
+        halves = [slabs[s, :, here] + flip_rows(slabs[count - 1 - s, :, here]) for s in range(half)]
+        split_rows(jnp.concatenate([jnp.concatenate(halves, axis=0), side], axis=1), parts)
+        total = cone(taps_ref, parts, rows)
+        for s in range(half):
+            own = total[s * ROWS : (s + 1) * ROWS, :width]
+            done[s, :, here] = own
+            done[count - 1 - s, :, here] = flip_rows(own)
+    for k in range(count):
+        outs[k][:, : per_device * width] = done[lax.bitwise_xor(me, k)]
+        outs[k][:, per_device * width :] = edges_ref[...]
+
+
+def cone_filter(taps, edges, got, per_device, width):
+    count = len(got)
+    rows = count // 2 * ROWS
+    return pl.pallas_call(
+        functools.partial(filter_kernel, count, per_device, width),
+        in_specs=[VMEM] * (2 + count),
+        out_specs=[VMEM] * count,
+        out_shape=[fast(ROWS, per_device * width + edges.shape[1])] * count,
+        scratch_shapes=[
+            pltpu.VMEM((count, ROWS, per_device * width), jnp.float32),
+            pltpu.VMEM((3 * rows, width + LANES), jnp.bfloat16),
+            pltpu.VMEM((count, ROWS, per_device * width), jnp.float32),
+        ],
+        compiler_params=params(),
+    )(taps, edges, *got[::-1])
+
+
+SPAN = 2 * PART
+
+
+def finish_kernel(count, per_device, width, *refs):
     taps_ref = refs[0]
     got = refs[count:0:-1]
-    outs = refs[1 + count : 1 + 2 * count]
-    slabs, parts, done = refs[1 + 2 * count :]
+    out, (slabs, parts, mine, left, right, done, sems) = refs[count + 1], refs[count + 2 :]
     me = lax.axis_index("gx")
-    wide = width + LANES
+    layers = count * per_device
     half = count // 2
     rows = half * ROWS
-    lane = lax.broadcasted_iota(jnp.int32, (ROWS, LANES), 1)
+    lane = lax.broadcasted_iota(jnp.int32, (rows, LANES), 1)
+    lane_out = lax.broadcasted_iota(jnp.int32, (ROWS, LANES), 1)
     for k in range(count):
-        slabs[lax.bitwise_xor(me, k)] = got[k][...]
-
-    def layer_of(slab, i):
-        edge = slabs[slab, :, per_device * width :]
-        at = 2 * STRIP * i
-        upper = pltpu.roll(edge, (LANES - at) % LANES, 1) if at else edge
-        lower = pltpu.roll(edge, (LANES - 2 * STRIP - at) % LANES, 1)
-        side = jnp.where(lane < STRIP, upper, lower)
-        return jnp.concatenate([slabs[slab, :, i * width : (i + 1) * width], side], axis=1)
-
-    for i in range(per_device):
-        halves = [layer_of(s, i) + flip_rows(layer_of(count - 1 - s, i)) for s in range(half)]
-        symmetric = jnp.concatenate(halves, axis=0)
-        high = symmetric.astype(jnp.bfloat16)
-        low = (symmetric - high.astype(jnp.float32)).astype(jnp.bfloat16)
-        parts[0:rows, :] = high
-        parts[rows : 2 * rows, :] = high
-        parts[2 * rows : 3 * rows, :] = low
-        mixed = jnp.dot(taps_ref[...], parts[...], preferred_element_type=jnp.float32)
-        total = mixed[0:rows]
-        for b in range(1, RADIUS + 1):
-            part = mixed[b * rows : (b + 1) * rows]
-            total = total + (pltpu.roll(part, b, 1) + pltpu.roll(part, wide - b, 1))
-        for s in range(half):
-            own = total[s * ROWS : (s + 1) * ROWS, :width]
-            done[s, i] = own
-            done[count - 1 - s, i] = flip_rows(own)
+        slabs[lax.bitwise_xor(me, k)] = got[k][:, per_device * width :]
+    symmetric = jnp.concatenate([slabs[s] + flip_rows(slabs[count - 1 - s]) for s in range(half)], axis=0)
+    per_tile = LANES // SPAN
+    tiles = []
+    for start in range(0, layers, per_tile):
+        tile = jnp.zeros((rows, LANES), jnp.float32)
+        for j in range(min(per_tile, layers - start)):
+            at = PART * (start + j)
+            source = symmetric[:, at // LANES * LANES : (at // LANES + 1) * LANES]
+            low, high = SPAN * j + 1, SPAN * j + PART + STRIP - 1
+            here = jnp.logical_and(lane >= low, lane < low + STRIP)
+            tile = jnp.where(here, pltpu.roll(source, (low - at) % LANES, 1), tile)
+            here = jnp.logical_and(lane >= high, lane < high + STRIP)
+            tile = jnp.where(here, pltpu.roll(source, (high - at - STRIP) % LANES, 1), tile)
+        tiles.append(tile)
+    split_rows(jnp.concatenate(tiles, axis=1), parts)
+    total = cone(taps_ref, parts, rows)
+    for s in range(half):
+        own = total[s * ROWS : (s + 1) * ROWS]
+        mine[s] = own
+        mine[count - 1 - s] = flip_rows(own)
+    mine_now = mine[me]
+    for layer in range(layers):
+        tile = mine_now[:, layer // per_tile * LANES : (layer // per_tile + 1) * LANES]
+        at = SPAN * (layer % per_tile)
+        head = pltpu.roll(tile, (-at - STRIP) % LANES, 1)
+        left[layer] = jnp.where(lane_out < STRIP - 1, head, 0.0)
+        tail = pltpu.roll(tile, (LANES - STRIP - at - PART) % LANES, 1)
+        right[layer] = jnp.where(lane_out > LANES - STRIP, tail, 0.0)
+
+    copies = []
     for k in range(count):
-        outs[k][...] = done[lax.bitwise_xor(me, k)]
-
-
-def cone_filter(got, per_device, width):
-    count = len(got)
+        first = lax.bitwise_xor(me, k) * per_device
+        for i in range(per_device):
+            at = i * width
+            done[k, i] = got[k][:, at : at + width]
+            done[k, i, :, :LANES] += left[first + i]
+            done[k, i, :, width - LANES :] += right[first + i]
+        copies.append(pltpu.make_async_copy(done.at[k], out.at[pl.ds(first, per_device)], sems.at[k]))
+        copies[-1].start()
+    for copy in copies:
+        copy.wait()
+
+
+def finish(taps, parts, layers, width):
+    count = len(parts)
+    per_device = layers // count
     rows = count // 2 * ROWS
-    taps = jnp.asarray(cone_matrix(rows))
-    return pl.pallas_call(
-        functools.partial(filter_kernel, count, per_device, width),
+    edges = parts[0].shape[1] - per_device * width
+    spread = math.ceil(layers * SPAN / LANES) * LANES
+    return pl.pallas_call(
+        functools.partial(finish_kernel, count, per_device, width),
         in_specs=[VMEM] * (1 + count),
-        out_specs=[VMEM] * count,
-        out_shape=[fast(per_device, ROWS, width)] * count,
+        out_specs=ANY,
+        out_shape=f32(layers, ROWS, width),
         scratch_shapes=[
-            pltpu.VMEM((count, ROWS, per_device * width + LANES), jnp.float32),
-            pltpu.VMEM((3 * rows, width + LANES), jnp.bfloat16),
+            pltpu.VMEM((count, ROWS, edges), jnp.float32),
+            pltpu.VMEM((3 * rows, spread), jnp.bfloat16),
+            pltpu.VMEM((count, ROWS, spread), jnp.float32),
+            pltpu.VMEM((layers, ROWS, LANES), jnp.float32),
+            pltpu.VMEM((layers, ROWS, LANES), jnp.float32),
             pltpu.VMEM((count, per_device, ROWS, width), jnp.float32),
+            pltpu.SemaphoreType.DMA((count,)),
         ],
         compiler_params=params(),
-    )(taps, *got[::-1])
-
-
-def place_kernel(count, per_device, *refs):
-    out, sems = refs[count], refs[count + 1]
-    parts = refs[count - 1 :: -1]
-    copies = []
-    for k in range(count):
-        at = lax.bitwise_xor(lax.axis_index("gx"), k) * per_device
-        copies.append(pltpu.make_async_copy(parts[k], out.at[pl.ds(at, per_device)], sems.at[k]))
-    for copy in copies:
-        copy.start()
-    for copy in copies:
-        copy.wait()
-
-
-def place_layers(parts):
-    count = len(parts)
-    per_device, rows, width = parts[0].shape
-    return pl.pallas_call(
-        functools.partial(place_kernel, count, per_device),
-        in_specs=[ANY] * count,
-        out_specs=ANY,
-        out_shape=f32(count * per_device, rows, width),
-        scratch_shapes=[pltpu.SemaphoreType.DMA((count,))],
-        compiler_params=params(),
-    )(*parts[::-1])
+    )(taps, *parts[::-1])
 
 
 def spread(parts):
@@ -797,13 +877,14 @@
     )
     arrays = (efield, hfield, forward, inv, grad_sum, mask)
     edges = own_edges(arrays)
-    yfaces = exchange(y_faces(own_low, own_high, zfaces, xfaces), "gy", "gz")
-    own = own_gradient(arrays, zfaces, xfaces)
-    shares = edge_gradient(own, edges, zfaces, xfaces, yfaces)
+    shares, own = own_gradient(arrays, zfaces, xfaces)
     got = spread(shares)
-    e_next, h_next, grad_total = step(efield, hfield, inv, zfaces, xfaces, yfaces, shares, layers)
-    filtered = spread(cone_filter(got, layers // len(got), width))
-    return e_next, h_next, grad_total, place_layers(filtered)
+    yfaces = exchange(y_faces(own_low, own_high, zfaces, xfaces, own), "gy", "gz")
+    message, edge = edge_gradient(own, edges, zfaces, xfaces, yfaces)
+    taps = jnp.asarray(cone_matrix(len(got) // 2 * ROWS))
+    parts = cone_filter(taps, message, got, layers // len(got), width)
+    e_next, h_next, grad_total = step(efield, hfield, inv, own, edge, zfaces, xfaces, yfaces, parts[0])
+    return e_next, h_next, grad_total, finish(taps, spread(parts), layers, width)
 
 
 def solution(mesh):

time: 39.5 us -> 36.9 us (0.934)
  waiting for transfers between devices: 9.72 us -> 7.51 us
  starting transfers between devices: 17 us -> 16.5 us
    ppermute x6, waiting for transfers between devices: 6.65 us -> 5.43 us  [spread(): got[k] = lax.ppermute(parts[k], 'gx', [(i, i ^ k) for i in range(count)])]
    ppermute x5, waiting for transfers between devices: 3.08 us -> 2.08 us  [exchange(): got.append(lax.ppermute(value, tuple(axes), pairs))]
    ppermute x6, starting transfers between devices: 9.69 us -> 9.18 us  [spread(): got[k] = lax.ppermute(parts[k], 'gx', [(i, i ^ k) for i in range(count)])]
  transfers between devices with their start and end apart: 11 -> 11, of which waited for: 7 -> 5; matrix products, arithmetic and copies ran while one was open for 0% -> 0% of each run, Pallas kernels for 20% -> 21%
where the time goes in v6:
time: 36.9 us; the launch traced here: 36.6 us
  starting transfers between devices  16.5 us (45%)
  Pallas kernels  11.8 us (32%)
  waiting for transfers between devices  7.51 us (20%)
  between operations  0.77 us (2%)
    ppermute x6, starting transfers between devices, spread(): got[k] = lax.ppermute(parts[k], 'gx', [(i, i ^ k) for i in range(count)])  9.18 us
    ppermute x5, starting transfers between devices, exchange(): got.append(lax.ppermute(value, tuple(axes), pairs))  7.28 us
    ppermute x6, waiting for transfers between devices, spread(): got[k] = lax.ppermute(parts[k], 'gx', [(i, i ^ k) for i in range(count)])  5.43 us
    pallas_call x1, Pallas kernels, step(): pl.pallas_call(functools.partial(step_kernel, counts), in_specs=[VMEM] *...  3.25 us
    ppermute x5, waiting for transfers between devices, exchange(): got.append(lax.ppermute(value, tuple(axes), pairs))  2.08 us
    pallas_call x1, Pallas kernels, load(): pl.pallas_call(load_kernel, in_specs=[ANY] * 4, out_specs=[VMEM] * 4, out...  1.85 us
    pallas_call x1, Pallas kernels, finish(): pl.pallas_call(functools.partial(finish_kernel, count, per_device, width)...  1.3 us
    pallas_call x1, Pallas kernels, strips(): pl.pallas_call(strips_kernel, in_specs=[VMEM] * 3 + [ANY] + [VMEM] * 3, o...  1.24 us
  transfers between devices with their start and end apart: 11, of which 5 were waited for; matrix products, arithmetic and copies ran while one was open for 0% of the time, Pallas kernels for 21%

profile of v6, /device:TPU:0, one launch (start us, length us, event | category | flops | bytes accessed | tf_op | source)
XLA Modules:
  0.0 36.6 jit_solution(14721980481194024610)
XLA Ops:
  0.6 0.9 %shard_map.113 = f32[3,8,512]{2,1,0:T(8,128)S(1)} custom-call(f32[3,24,8,512]{3,2,1,0:T(8,128)} %refs_0_.3, f32[3,24,8,512]{3,2,1,0:T(8,128)} %refs_1_.1), custom_call_target="tpu_custom_call" | custom-call | tf_op jit(solution)/shard_map/pallas_call | solution.py:117
  1.5 3.0 %collective-permute-start = (f32[3,8,512]{2,1,0:T(8,128)S(1)}, f32[3,8,512]{2,1,0:T(8,128)S(1)}, u32[]{:S(2)}, u32[]{:S(2)}) collective-permute-start(f32[3,8,512]{2,1,0:T(8,128)S(1)} %shard_map.113), channel_id=1, source_target_pairs={{0,1},{2,3},{4,5},{6,7},{1,0},{3,2},{5,4},{7,6},{8,9},{10,11},{12,... | collective-permute-start | bytes 147464 | tf_op jit(solution)/shard_map/ppermute | solution.py:65
  4.6 1.8 %shard_map.111 = (f32[3,24,8,512]{3,2,1,0:T(8,128)S(1)}, f32[3,24,8,512]{3,2,1,0:T(8,128)S(1)}, s32[24,8,512]{2,1,0:T(8,128)S(1)}, f32[16,8,512]{2,1,0:T(8,128)S(1)}) custom-call(f32[3,24,8,512]{3,2,1,0:T(8,128)} %refs_0_.3, f32[3,24,8,512]{3,2,1,0:T(8,128)} %refs_1_.1, s32[24,8,512]{2,1,0:T(8,128)} %mat_in.1, f32[16,8,512]{2,1,0:T(8,128)} %grad_in.1), custom_call_target="tpu_custom_call" | custom-call | tf_op jit(solution)/shard_map/pallas_call | solution.py:210
  6.4 0.2 collective-permute-done.refs_2_.refs_6_.refs_4_.refs_5_
  6.6 0.0 copy-start
  6.6 0.0 copy-start.2
  6.6 0.0 copy-start.3
  6.6 0.1 shard_map.114
  6.8 2.1 %collective-permute-start.1 = (f32[72,512]{1,0:T(8,128)S(1)}, f32[72,512]{1,0:T(8,128)S(1)}, u32[]{:S(2)}, u32[]{:S(2)}) collective-permute-start(f32[72,512]{1,0:T(8,128)S(1)} %get-tuple-element.41), channel_id=1, source_target_pairs={{0,8},{2,10},{4,12},{6,14},{8,0},{10,2},{12,4},{14,6},{16,24},{18,... | collective-permute-start | bytes 442376 | tf_op jit(solution)/shard_map/ppermute | solution.py:65
  8.9 0.0 collective-permute-start.2
  8.9 0.0 copy-done
  8.9 0.0 copy-done.2
  8.9 0.0 copy-done.3
  8.9 1.2 %shard_map.112 = (f32[3,24,8,512]{3,2,1,0:T(8,128)S(1)}, f32[15,8,128]{2,1,0:T(8,128)S(1)}, f32[15,8,128]{2,1,0:T(8,128)S(1)}, f32[8,512]{1,0:T(8,128)S(1)}, f32[24,8,512]{2,1,0:T(8,128)S(1)}) custom-call(f32[1,4]{1,0:T(1,128)S(1)} %bitcast.1, f32[3,24,8,512]{3,2,1,0:T(8,128)S(1)} %get-tuple-element.34.e_ref.refs_0_, ...), custom_call_target="tpu_custom_call" | custom-call | tf_op jit(solution)/shard_map/pallas_call | solution.py:271
  10.2 1.9 %collective-permute-done.1.refs_7_.refs_3_.refs_5_.refs_6_ = f32[72,512]{1,0:T(8,128)S(1)} collective-permute-done((f32[72,512]{1,0:T(8,128)S(1)}, f32[72,512]{1,0:T(8,128)S(1)}, u32[]{:S(2)}, u32[]{:S(2)}) %collective-permute-start.1) | collective-permute-done | bytes 147488 | tf_op jit(solution)/shard_map/ppermute | solution.py:65
  12.0 0.0 collective-permute-done.2.refs_8_.refs_4_.refs_6_.refs_7_
  12.1 0.8 %shard_map.115 = (f32[8,2048]{1,0:T(8,128)S(1)}, f32[8,2048]{1,0:T(8,128)S(1)}, f32[8,2048]{1,0:T(8,128)S(1)}, f32[8,2048]{1,0:T(8,128)S(1)}, f32[16,8,512]{2,1,0:T(8,128)S(1)}) custom-call(f32[3,24,8,512]{3,2,1,0:T(8,128)S(1)} %get-tuple-element.34.e_ref.refs_0_, f32[3,24,8,512]{3,2,1,0:T(8,128)S(1)} %get-tuple-element.35.h_ref.refs_1_, ...), custom_call_target="tpu_custom_call" | custom-call | tf_op jit(solution)/shard_map/pallas_call | solution.py:572
  12.8 0.1 shard_map.117
  13.0 0.1 collective-permute-start.3
  13.0 2.0 %collective-permute-start.4 = (f32[17,8,128]{2,1,0:T(8,128)S(1)}, f32[17,8,128]{2,1,0:T(8,128)S(1)}, u32[]{:S(2)}, u32[]{:S(2)}) collective-permute-start(f32[17,8,128]{2,1,0:T(8,128)S(1)} %get-tuple-element.50), channel_id=1, source_target_pairs={{0,1},{1,0},{2,4},{3,5},{4,2},{5,3},{6,7},{7,6},{8,9},{9,8},{10,12... | collective-permute-start | bytes 208904 | tf_op jit(solution)/shard_map/ppermute | solution.py:65
  15.1 3.6 %collective-permute-start.5 = (f32[8,2048]{1,0:T(8,128)S(1)}, f32[8,2048]{1,0:T(8,128)S(1)}, u32[]{:S(2)}, u32[]{:S(2)}) collective-permute-start(f32[8,2048]{1,0:T(8,128)S(1)} %get-tuple-element.53), channel_id=1, source_target_pairs={{0,24},{8,16},{16,8},{24,0},{1,25},{9,17},{17,9},{25,1},{2,26},{10... | collective-permute-start | bytes 196616 | tf_op jit(solution)/shard_map/ppermute | solution.py:866
  18.7 0.6 %collective-permute-start.6 = (f32[8,2048]{1,0:T(8,128)S(1)}, f32[8,2048]{1,0:T(8,128)S(1)}, u32[]{:S(2)}, u32[]{:S(2)}) collective-permute-start(f32[8,2048]{1,0:T(8,128)S(1)} %get-tuple-element.54), channel_id=1, source_target_pairs={{0,16},{8,24},{16,0},{24,8},{1,17},{9,25},{17,1},{25,9},{2,18},{10... | collective-permute-start | bytes 196616 | tf_op jit(solution)/shard_map/ppermute | solution.py:866
  19.2 0.6 %collective-permute-start.7 = (f32[8,2048]{1,0:T(8,128)S(1)}, f32[8,2048]{1,0:T(8,128)S(1)}, u32[]{:S(2)}, u32[]{:S(2)}) collective-permute-start(f32[8,2048]{1,0:T(8,128)S(1)} %get-tuple-element.55), channel_id=1, source_target_pairs={{0,8},{8,0},{16,24},{24,16},{1,9},{9,1},{17,25},{25,17},{2,10},{10... | collective-permute-start | bytes 196616 | tf_op jit(solution)/shard_map/ppermute | solution.py:866
  19.8 0.5 %shard_map.116 = (f32[24,6,8,128]{3,2,1,0:T(8,128)S(1)}, f32[16,5,8,128]{3,2,1,0:T(8,128)S(1)}, f32[8,128]{1,0:T(8,128)S(1)}) custom-call(f32[3,24,8,512]{3,2,1,0:T(8,128)S(1)} %get-tuple-element.34.e_ref.refs_0_, f32[3,24,8,512]{3,2,1,0:T(8,128)S(1)} %get-tuple-element.35.h_ref.refs_1_, f32[3,24,8,512]{3,2,1,0:T(8,128)S(1)} %get-tuple-element.39.refs_2_.f_ref, ...), custom_call_target="tpu_custom_call" | custom-call | tf_op jit(solution)/shard_map/pallas_call | solution.py:306
  20.4 0.0 copy-start.1
  20.4 0.0 collective-permute-done.3.refs_7_.refs_8_
  20.4 0.0 collective-permute-done.4.refs_8_.refs_9_
  20.4 0.9 %shard_map.118 = (f32[8,256]{1,0:T(8,128)S(1)}, f32[16,8,128]{2,1,0:T(8,128)S(1)}) custom-call(f32[16,8,512]{2,1,0:T(8,128)S(1)} %get-tuple-element.43.refs_5_.refs_0_.refs_3_, f32[24,6,8,128]{3,2,1,0:T(8,128)S(1)} %get-tuple-element.44.refs_1_, f32[16,5,8,128]{3,2,1,0:T(8,128)S(1)} %get-tuple-element.45.refs_2_, f32[8,128]{1,0:T(8,128)S(1)} %get-tuple-element.46.refs_3_, ...), custom_call_target="tpu_custom_call" | custom-call | tf_op jit(solution)/shard_map/pallas_call | solution.py:620
  21.3 0.0 collective-permute-done.5.refs_2_
  21.3 3.9 %collective-permute-done.6.refs_3_ = f32[8,2048]{1,0:T(8,128)S(1)} collective-permute-done((f32[8,2048]{1,0:T(8,128)S(1)}, f32[8,2048]{1,0:T(8,128)S(1)}, u32[]{:S(2)}, u32[]{:S(2)}) %collective-permute-start.6) | collective-permute-done | bytes 65568 | tf_op jit(solution)/shard_map/ppermute | solution.py:866
  25.2 0.0 collective-permute-done.7.refs_4_
  25.2 0.0 copy-done.1
  25.2 0.8 %shard_map.119 = (f32[8,2304]{1,0:T(8,128)S(1)}, f32[8,2304]{1,0:T(8,128)S(1)}, f32[8,2304]{1,0:T(8,128)S(1)}, f32[8,2304]{1,0:T(8,128)S(1)}) custom-call(bf16[112,48]{1,0:T(8,128)(2,1)S(1)} %copy-done.1, f32[8,256]{1,0:T(8,128)S(1)} %get-tuple-element.52.refs_1_, f32[8,2048]{1,0:T(8,128)S(1)} %collective-permute-done.5.refs_2_, ...), custom_call_target="tpu_custom_call" | custom-call | tf_op jit(solution)/shard_map/pallas_call | solution.py:766
  26.1 3.3 %collective-permute-start.8 = (f32[8,2304]{1,0:T(8,128)S(1)}, f32[8,2304]{1,0:T(8,128)S(1)}, u32[]{:S(2)}, u32[]{:S(2)}) collective-permute-start(f32[8,2304]{1,0:T(8,128)S(1)} %get-tuple-element.61), channel_id=1, source_target_pairs={{0,24},{8,16},{16,8},{24,0},{1,25},{9,17},{17,9},{25,1},{2,26},{10... | collective-permute-start | bytes 221192 | tf_op jit(solution)/shard_map/ppermute | solution.py:866
  29.3 0.0 collective-permute-start.9
  29.3 1.2 %collective-permute-start.10 = (f32[8,2304]{1,0:T(8,128)S(1)}, f32[8,2304]{1,0:T(8,128)S(1)}, u32[]{:S(2)}, u32[]{:S(2)}) collective-permute-start(f32[8,2304]{1,0:T(8,128)S(1)} %get-tuple-element.63), channel_id=1, source_target_pairs={{0,8},{8,0},{16,24},{24,16},{1,9},{9,1},{17,25},{25,17},{2,10},{10... | collective-permute-start | bytes 221192 | tf_op jit(solution)/shard_map/ppermute | solution.py:866
  30.5 3.2 %shard_map.120 = (f32[3,24,8,512]{3,2,1,0:T(8,128)}, f32[3,24,8,512]{3,2,1,0:T(8,128)}, f32[16,8,512]{2,1,0:T(8,128)}) custom-call(f32[3,24,8,512]{3,2,1,0:T(8,128)S(1)} %get-tuple-element.34.e_ref.refs_0_, f32[3,24,8,512]{3,2,1,0:T(8,128)S(1)} %get-tuple-element.35.h_ref.refs_1_, f32[24,8,512]{2,1,0:T(8,128)S(1)} %get-tuple-element.38.refs_3_.inv_ref.refs_2_, ...), custom_call_target="tpu_custom_call" | custom-call | tf_op jit(solution)/shard_map/pallas_call | solution.py:683
  33.8 0.0 collective-permute-done.8.refs_1_
  33.8 1.4 %collective-permute-done.9.refs_2_ = f32[8,2304]{1,0:T(8,128)S(1)} collective-permute-done((f32[8,2304]{1,0:T(8,128)S(1)}, f32[8,2304]{1,0:T(8,128)S(1)}, u32[]{:S(2)}, u32[]{:S(2)}) %collective-permute-start.9) | collective-permute-done | bytes 73760 | tf_op jit(solution)/shard_map/ppermute | solution.py:866
  35.1 0.1 collective-permute-done.10.refs_3_
  35.3 1.3 %shard_map.121 = f32[16,8,512]{2,1,0:T(8,128)} custom-call(bf16[112,48]{1,0:T(8,128)(2,1)S(1)} %copy-done.1, f32[8,2304]{1,0:T(8,128)S(1)} %collective-permute-done.8.refs_1_, f32[8,2304]{1,0:T(8,128)S(1)} %collective-permute-done.9.refs_2_, f32[8,2304]{1,0:T(8,128)S(1)} %collective-permute-done.10.refs_3_, f32[8,2304]{1,0:T(8,128)S(1)} %get-tuple-element.57.refs_10_.refs_4_), custom_call_target="tpu_custom_call" | custom-call | tf_op jit(solution)/shard_map/pallas_call | solution.py:844
Async XLA Ops:
  1.5 5.1 %collective-permute-start = (f32[3,8,512]{2,1,0:T(8,128)S(1)}, f32[3,8,512]{2,1,0:T(8,128)S(1)}, u32[]{:S(2)}, u32[]{:S(2)}) collective-permute-start(f32[3,8,512]{2,1,0:T(8,128)S(1)} %shard_map.113), channel_id=1, source_target_pairs={{0,1},{2,3},{4,5},{6,7},{1,0},{3,2},{5,4},{7,6},{8,9},{10,11},{12,... | collective-permute-start | bytes 147464 | tf_op jit(solution)/shard_map/ppermute | solution.py:65
  6.6 2.3 %copy-start = (f32[3,24,8,512]{3,2,1,0:T(8,128)S(1)}, f32[3,24,8,512]{3,2,1,0:T(8,128)}, u32[]{:S(2)}) copy-start(f32[3,24,8,512]{3,2,1,0:T(8,128)} %f_in.1) | copy-start | bytes 3538948
  6.6 2.3 %copy-start.2 = (f32[4]{0:T(128)S(1)}, f32[4]{0:T(128)}, u32[]{:S(2)}) copy-start(f32[4]{0:T(128)} %param.12) | copy-start | bytes 52
  6.6 2.3 %copy-start.3 = (s32[1,64]{1,0:T(1,128)S(1)}, s32[1,64]{1,0:T(1,128)}, u32[]{:S(2)}) copy-start(s32[1,64]{1,0:T(1,128)} %mask_ref.1) | copy-start | bytes 772
  6.8 5.3 %collective-permute-start.1 = (f32[72,512]{1,0:T(8,128)S(1)}, f32[72,512]{1,0:T(8,128)S(1)}, u32[]{:S(2)}, u32[]{:S(2)}) collective-permute-start(f32[72,512]{1,0:T(8,128)S(1)} %get-tuple-element.41), channel_id=1, source_target_pairs={{0,8},{2,10},{4,12},{6,14},{8,0},{10,2},{12,4},{14,6},{16,24},{18,... | collective-permute-start | bytes 442376 | tf_op jit(solution)/shard_map/ppermute | solution.py:65
  8.9 3.1 %collective-permute-start.2 = (f32[72,512]{1,0:T(8,128)S(1)}, f32[72,512]{1,0:T(8,128)S(1)}, u32[]{:S(2)}, u32[]{:S(2)}) collective-permute-start(f32[72,512]{1,0:T(8,128)S(1)} %get-tuple-element.42), channel_id=1, source_target_pairs={{0,2},{2,0},{4,6},{6,4},{8,16},{10,18},{12,20},{14,22},{16,8},{18,... | collective-permute-start | bytes 442376 | tf_op jit(solution)/shard_map/ppermute | solution.py:65
  13.0 7.4 %collective-permute-start.3 = (f32[17,8,128]{2,1,0:T(8,128)S(1)}, f32[17,8,128]{2,1,0:T(8,128)S(1)}, u32[]{:S(2)}, u32[]{:S(2)}) collective-permute-start(f32[17,8,128]{2,1,0:T(8,128)S(1)} %get-tuple-element.49), channel_id=1, source_target_pairs={{0,2},{1,3},{2,0},{3,1},{4,6},{5,7},{6,4},{7,5},{8,10},{9,11},{10,... | collective-permute-start | bytes 208904 | tf_op jit(solution)/shard_map/ppermute | solution.py:65
  13.0 7.3 %collective-permute-start.4 = (f32[17,8,128]{2,1,0:T(8,128)S(1)}, f32[17,8,128]{2,1,0:T(8,128)S(1)}, u32[]{:S(2)}, u32[]{:S(2)}) collective-permute-start(f32[17,8,128]{2,1,0:T(8,128)S(1)} %get-tuple-element.50), channel_id=1, source_target_pairs={{0,1},{1,0},{2,4},{3,5},{4,2},{5,3},{6,7},{7,6},{8,9},{9,8},{10,12... | collective-permute-start | bytes 208904 | tf_op jit(solution)/shard_map/ppermute | solution.py:65
  15.1 6.2 %collective-permute-start.5 = (f32[8,2048]{1,0:T(8,128)S(1)}, f32[8,2048]{1,0:T(8,128)S(1)}, u32[]{:S(2)}, u32[]{:S(2)}) collective-permute-start(f32[8,2048]{1,0:T(8,128)S(1)} %get-tuple-element.53), channel_id=1, source_target_pairs={{0,24},{8,16},{16,8},{24,0},{1,25},{9,17},{17,9},{25,1},{2,26},{10... | collective-permute-start | bytes 196616 | tf_op jit(solution)/shard_map/ppermute | solution.py:866
  18.7 6.6 %collective-permute-start.6 = (f32[8,2048]{1,0:T(8,128)S(1)}, f32[8,2048]{1,0:T(8,128)S(1)}, u32[]{:S(2)}, u32[]{:S(2)}) collective-permute-start(f32[8,2048]{1,0:T(8,128)S(1)} %get-tuple-element.54), channel_id=1, source_target_pairs={{0,16},{8,24},{16,0},{24,8},{1,17},{9,25},{17,1},{25,9},{2,18},{10... | collective-permute-start | bytes 196616 | tf_op jit(solution)/shard_map/ppermute | solution.py:866
  19.2 6.0 %collective-permute-start.7 = (f32[8,2048]{1,0:T(8,128)S(1)}, f32[8,2048]{1,0:T(8,128)S(1)}, u32[]{:S(2)}, u32[]{:S(2)}) collective-permute-start(f32[8,2048]{1,0:T(8,128)S(1)} %get-tuple-element.55), channel_id=1, source_target_pairs={{0,8},{8,0},{16,24},{24,16},{1,9},{9,1},{17,25},{25,17},{2,10},{10... | collective-permute-start | bytes 196616 | tf_op jit(solution)/shard_map/ppermute | solution.py:866
  20.4 4.9 %copy-start.1 = (bf16[112,48]{1,0:T(8,128)(2,1)S(1)}, bf16[112,48]{1,0:T(8,128)(2,1)}, u32[]{:S(2)}) copy-start(bf16[112,48]{1,0:T(8,128)(2,1)} %constant.2.clone.refs_0_) | copy-start | bytes 32260
  26.1 7.7 %collective-permute-start.8 = (f32[8,2304]{1,0:T(8,128)S(1)}, f32[8,2304]{1,0:T(8,128)S(1)}, u32[]{:S(2)}, u32[]{:S(2)}) collective-permute-start(f32[8,2304]{1,0:T(8,128)S(1)} %get-tuple-element.61), channel_id=1, source_target_pairs={{0,24},{8,16},{16,8},{24,0},{1,25},{9,17},{17,9},{25,1},{2,26},{10... | collective-permute-start | bytes 221192 | tf_op jit(solution)/shard_map/ppermute | solution.py:866
  29.3 5.8 %collective-permute-start.9 = (f32[8,2304]{1,0:T(8,128)S(1)}, f32[8,2304]{1,0:T(8,128)S(1)}, u32[]{:S(2)}, u32[]{:S(2)}) collective-permute-start(f32[8,2304]{1,0:T(8,128)S(1)} %get-tuple-element.62), channel_id=1, source_target_pairs={{0,16},{8,24},{16,0},{24,8},{1,17},{9,25},{17,1},{25,9},{2,18},{10... | collective-permute-start | bytes 221192 | tf_op jit(solution)/shard_map/ppermute | solution.py:866
  29.3 6.0 %collective-permute-start.10 = (f32[8,2304]{1,0:T(8,128)S(1)}, f32[8,2304]{1,0:T(8,128)S(1)}, u32[]{:S(2)}, u32[]{:S(2)}) collective-permute-start(f32[8,2304]{1,0:T(8,128)S(1)} %get-tuple-element.63), channel_id=1, source_target_pairs={{0,8},{8,0},{16,24},{24,16},{1,9},{9,1},{17,25},{25,17},{2,10},{10... | collective-permute-start | bytes 221192 | tf_op jit(solution)/shard_map/ppermute | solution.py:866

commit v7 on v6

--- a/solution.py
+++ b/solution.py
@@ -66,6 +66,35 @@
     return got
 
 
+def exchange_diagonal(sends):
+    along_x, along_y, along_z = (lax.axis_size(axis) for axis in AXES)
+
+    def flat(x, y, z):
+        return (x * along_y + y) * along_z + z
+
+    got = []
+    for start, value in enumerate(sends):
+        partner = {}
+        for low in range(start, along_z - 1, 2):
+            for x in range(1, along_x):
+                partner[x, low] = (x - 1, low + 1)
+                partner[x - 1, low + 1] = (x, low)
+        pairs = []
+        for x in range(along_x):
+            for z in range(along_z):
+                for y in range(along_y):
+                    if (x, z) in partner:
+                        to = partner[x, z]
+                        pairs.append((flat(x, y, z), flat(to[0], y, to[1])))
+                    elif along_y % 2 == 0:
+                        pairs.append((flat(x, y, z), flat(x, y ^ 1, z)))
+        got.append(lax.ppermute(value, AXES, pairs))
+    return got
+
+
+AXES = ("gx", "gy", "gz")
+
+
 class Side:
     def __init__(self, axis):
         index = lax.axis_index(axis)
@@ -91,47 +120,15 @@
     return (cells_z - layers) * (1 - lax.axis_index("gz"))
 
 
-def z_faces_kernel(*refs):
-    e_ref, h_ref = refs[:2]
-    sends, (e_low, e_high, h_high, sems) = refs[2:-4], refs[-4:]
-    top = e_ref.shape[1] - 1
-    planes = [(e_ref.at[c, 0], e_low.at[c]) for c in range(2)]
-    planes += [(e_ref.at[c, top], e_high.at[c]) for c in range(3)]
-    planes += [(h_ref.at[c, top], h_high.at[c]) for c in range(2)]
-    copies = [pltpu.make_async_copy(*plane, sems.at[n]) for n, plane in enumerate(planes)]
-    for copy in copies:
-        copy.start()
-    for copy in copies:
-        copy.wait()
-    side = Side("gz")
-    ex, ey, ez = (e_high[c] for c in range(3))
-    low = (e_low[0], e_low[1], jnp.zeros_like(ez))
-    high = (h_high[0] + HALF * ez - HALF * ey, h_high[1] + HALF * ex - HALF * ez, ez)
-    for c in range(3):
-        for ref, value in zip(sends, side.sends(low[c], high[c])):
-            ref[c] = value
-
-
-def z_faces(efield, hfield):
-    face = fast(*efield.shape[:1], *efield.shape[2:])
-    return pl.pallas_call(
-        z_faces_kernel,
-        in_specs=[ANY] * 2,
-        out_specs=[VMEM] * rounds("gz"),
-        out_shape=[face] * rounds("gz"),
-        scratch_shapes=[pltpu.VMEM(face.shape, jnp.float32)] * 3 + [pltpu.SemaphoreType.DMA((7,))],
-        compiler_params=params(60),
-    )(efield, hfield)
-
-
-def x_faces_kernel(z_rounds, *refs):
-    e_ref, h_ref = refs[:2]
-    zfaces = refs[2 : 2 + z_rounds]
-    sends, (low_ref, rows_ref) = refs[2 + z_rounds : -2], refs[-2:]
+def faces_kernel(x_rounds, e_ref, h_ref, *refs):
+    x_sends, (low_ref, rows_ref) = refs[:x_rounds], refs[-2:]
+    others = refs[x_rounds:-2]
+    z_sends, d_sends = others[: len(others) // 2], others[len(others) // 2 :]
     cells_z = e_ref.shape[1]
-    last = ROWS - 1
-    z_side = Side("gz")
-    low_ref[...] = jnp.zeros_like(low_ref)
+    last, top = ROWS - 1, cells_z - 1
+
+    low_ref[2 * cells_z :, :] = jnp.zeros_like(low_ref[2 * cells_z :, :])
+    rows_ref[5, top : top + 1, :] = jnp.zeros_like(rows_ref[5, top : top + 1, :])
     for z in range(cells_z):
         low_ref[z : z + 1, :] = e_ref[1, z, 0:1, :]
         low_ref[cells_z + z : cells_z + z + 1, :] = e_ref[2, z, 0:1, :]
@@ -141,8 +138,6 @@
             rows_ref[3 + c, z : z + 1, :] = h_ref[1 + c, z, last : last + 1, :]
         if z > 0:
             rows_ref[5, z - 1 : z, :] = e_ref[0, z, last : last + 1, :]
-    rows_ref[5, cells_z - 1 : cells_z, :] = z_side.upper([f[0, last : last + 1, :] for f in zfaces])
-    low_ref[2 * cells_z : 2 * cells_z + 1, :] = z_side.lower([f[2, 0:1, :] for f in zfaces])
     ex = rows_ref[0]
     high = (
         rows_ref[3] - HALF * (rows_ref[5] - ex + rows_ref[2]),
@@ -152,24 +147,43 @@
     side = Side("gx")
     for c in range(3):
         here = slice(c * cells_z, (c + 1) * cells_z)
-        for ref, value in zip(sends, side.sends(low_ref[here, :], high[c])):
+        for ref, value in zip(x_sends, side.sends(low_ref[here, :], high[c])):
             ref[here, :] = value
 
-
-def x_faces(efield, hfield, zfaces):
-    cells_z, cells_y = efield.shape[1], efield.shape[3]
-    face = fast(3 * cells_z, cells_y)
-    return pl.pallas_call(
-        functools.partial(x_faces_kernel, len(zfaces)),
-        in_specs=[VMEM] * (2 + len(zfaces)),
-        out_specs=[VMEM] * rounds("gx"),
-        out_shape=[face] * rounds("gx"),
+    side = Side("gz")
+    ex, ey, ez = (e_ref[c, top] for c in range(3))
+    low = (e_ref[0, 0], e_ref[1, 0], jnp.zeros_like(ez))
+    high = (h_ref[0, top] + HALF * ez - HALF * ey, h_ref[1, top] + HALF * ex - HALF * ez, ez)
+    for c in range(3):
+        for ref, value in zip(z_sends, side.sends(low[c], high[c])):
+            ref[c] = value
+
+    down, up = (
+        jnp.broadcast_to(line, (ROWS, line.shape[1]))
+        for line in (e_ref[0, 0, last : last + 1, :], e_ref[2, top, 0:1, :])
+    )
+    for ref, value in zip(d_sends, side.sends(down, up)):
+        ref[...] = value
+
+
+def halos(efield, hfield):
+    _, cells_z, cells_x, cells_y = efield.shape
+    x_rounds, z_rounds = rounds("gx"), rounds("gz")
+    x_face, z_face, line = fast(3 * cells_z, cells_y), fast(3, cells_x, cells_y), fast(ROWS, cells_y)
+    sends = pl.pallas_call(
+        functools.partial(faces_kernel, x_rounds),
+        in_specs=[VMEM] * 2,
+        out_specs=[VMEM] * (x_rounds + 2 * z_rounds),
+        out_shape=[x_face] * x_rounds + [z_face] * z_rounds + [line] * z_rounds,
         scratch_shapes=[
-            pltpu.VMEM(face.shape, jnp.float32),
+            pltpu.VMEM(x_face.shape, jnp.float32),
             pltpu.VMEM((6, cells_z, cells_y), jnp.float32),
         ],
         compiler_params=params(),
-    )(efield, hfield, *zfaces)
+    )(efield, hfield)
+    xfaces = exchange(sends[:x_rounds], "gx", "gy")
+    zfaces = exchange(sends[x_rounds : x_rounds + z_rounds], "gz", "gy")
+    return zfaces + exchange_diagonal(sends[x_rounds + z_rounds :]), xfaces
 
 
 def lane_group():
@@ -196,9 +210,8 @@
         high_ref[first + start // SLOTS] = high
 
 
-def load_kernel(e_in, h_in, mat_in, grad_in, e_ref, h_ref, mat_ref, grad_ref, sems):
+def load_kernel(e_in, h_in, e_ref, h_ref, sems):
     parts = [(source.at[c], target.at[c]) for source, target in ((e_in, e_ref), (h_in, h_ref)) for c in range(3)]
-    parts += [(mat_in, mat_ref), (grad_in, grad_ref)]
     copies = [pltpu.make_async_copy(*part, sems.at[n]) for n, part in enumerate(parts)]
     for copy in copies:
         copy.start()
@@ -206,15 +219,15 @@
         copy.wait()
 
 
-def load(*arrays):
+def load(*fields):
     return pl.pallas_call(
         load_kernel,
-        in_specs=[ANY] * 4,
-        out_specs=[VMEM] * 4,
-        out_shape=[pltpu.VMEM(one.shape, one.dtype) for one in arrays],
-        scratch_shapes=[pltpu.SemaphoreType.DMA((8,))],
+        in_specs=[ANY] * 2,
+        out_specs=[VMEM] * 2,
+        out_shape=[fast(*one.shape) for one in fields],
+        scratch_shapes=[pltpu.SemaphoreType.DMA((6,))],
         compiler_params=params(56),
-    )(*arrays)
+    )(*fields)
 
 
 def strips_kernel(
@@ -314,15 +327,35 @@
 
 def face_tiles(zfaces, xfaces):
     width = xfaces[0].shape[1]
+    rows = xfaces[0].shape[0]
+    cells_z = rows // 3
     z_side, x_side = Side("gz"), Side("gx")
+    zfaces, lines = zfaces[: len(zfaces) // 2], zfaces[len(zfaces) // 2 :]
+
+    def corner(s):
+        row = lax.broadcasted_iota(jnp.int32, (ROWS, s.stop - s.start), 0)
+        line = jnp.where(x_side.bottom, 0.0, z_side.upper([f[:, s] for f in lines]))
+        return jnp.where(row == ROWS - 1, -HALF * line, 0.0)
+
+    def beyond(s):
+        return jnp.where(x_side.top, 0.0, z_side.lower([f[:, s] for f in lines]))
+
+    def x_tile(pick, t, s):
+        value = pick([f[t : t + ROWS, s] for f in xfaces])
+        return value + corner(s) if t == cells_z - ROWS and pick == x_side.lower else value
+
     tiles = []
     for c in range(3):
         tiles.append((lambda s, c=c: z_side.lower([f[c, :, s] for f in zfaces]), width))
     for c in range(2):
         tiles.append((lambda s, c=c: z_side.upper([f[c, :, s] for f in zfaces]), width))
-    for pick in (x_side.lower, x_side.upper):
-        for t in range(0, xfaces[0].shape[0], ROWS):
-            tiles.append((lambda s, p=pick, t=t: p([f[t : t + ROWS, s] for f in xfaces]), width))
+    for t in range(0, rows, ROWS):
+        tiles.append((lambda s, t=t: x_tile(x_side.lower, t, s), width))
+    for t in range(0, rows, ROWS):
+        if t == 2 * cells_z:
+            tiles.append((beyond, width))
+        else:
+            tiles.append((lambda s, t=t: x_tile(x_side.upper, t, s), width))
     return tiles
 
 
@@ -869,9 +902,8 @@
 
 def on_device(efield, hfield, forward, material, permit, design_mask, grad_sum):
     layers, _, width = grad_sum.shape
-    zfaces = exchange(z_faces(efield, hfield), "gz", "gy")
-    efield, hfield, material, grad_sum = load(efield, hfield, material, grad_sum)
-    xfaces = exchange(x_faces(efield, hfield, zfaces), "gx", "gy")
+    efield, hfield = load(efield, hfield)
+    zfaces, xfaces = halos(efield, hfield)
     forward, own_low, own_high, mask, inv = strips(
         permit, efield, hfield, forward, material, grad_sum, design_mask
     )

time: 36.9 us -> 35.8 us (0.970)
  Pallas kernels: 11.8 us -> 10.8 us
  starting transfers between devices: 16.5 us -> 17.5 us
  waiting for transfers between devices: 7.51 us -> 6.58 us
    ppermute x5, starting transfers between devices: 7.28 us -> 8.46 us  [exchange(): got.append(lax.ppermute(value, tuple(axes), pairs))]
    pallas_call x3 -> x2, Pallas kernels: 2.88 us -> 1.78 us  [the longest x1 1.64 us: load(): pl.pallas_call(load_kernel, in_specs=[ANY] * 2, out_specs=[VMEM] * 2, out...]
    ppermute x5, waiting for transfers between devices: 2.08 us -> 1.13 us  [exchange(): got.append(lax.ppermute(value, tuple(axes), pairs))]
  transfers between devices with their start and end apart: 11 -> 12, of which waited for: 5 -> 4; matrix products, arithmetic and copies ran while one was open for 0% -> 0% of each run, Pallas kernels for 21% -> 17%
where the time goes in v7:
time: 35.8 us; the launch traced here: 35.7 us
  starting transfers between devices  17.5 us (49%)
  Pallas kernels  10.8 us (30%)
  waiting for transfers between devices  6.58 us (18%)
  between operations  0.81 us (2%)
    ppermute x6, starting transfers between devices, spread(): got[k] = lax.ppermute(parts[k], 'gx', [(i, i ^ k) for i in range(count)])  8.84 us
    ppermute x5, starting transfers between devices, exchange(): got.append(lax.ppermute(value, tuple(axes), pairs))  8.46 us
    ppermute x6, waiting for transfers between devices, spread(): got[k] = lax.ppermute(parts[k], 'gx', [(i, i ^ k) for i in range(count)])  5.44 us
    pallas_call x1, Pallas kernels, step(): pl.pallas_call(functools.partial(step_kernel, counts), in_specs=[VMEM] *...  3.25 us
    pallas_call x1, Pallas kernels, load(): pl.pallas_call(load_kernel, in_specs=[ANY] * 2, out_specs=[VMEM] * 2, out...  1.64 us
    pallas_call x1, Pallas kernels, finish(): pl.pallas_call(functools.partial(finish_kernel, count, per_device, width)...  1.3 us
    pallas_call x1, Pallas kernels, strips(): pl.pallas_call(strips_kernel, in_specs=[VMEM] * 3 + [ANY] + [VMEM] * 3, o...  1.24 us
    ppermute x5, waiting for transfers between devices, exchange(): got.append(lax.ppermute(value, tuple(axes), pairs))  1.13 us
  transfers between devices with their start and end apart: 12, of which 4 were waited for; matrix products, arithmetic and copies ran while one was open for 0% of the time, Pallas kernels for 17%

profile of v7, /device:TPU:0, one launch (start us, length us, event | category | flops | bytes accessed | tf_op | source)
XLA Modules:
  0.0 35.7 jit_solution(16189184217857114694)
XLA Ops:
  0.6 1.6 %shard_map.111 = (f32[3,24,8,512]{3,2,1,0:T(8,128)S(1)}, f32[3,24,8,512]{3,2,1,0:T(8,128)S(1)}) custom-call(f32[3,24,8,512]{3,2,1,0:T(8,128)} %e_in.1, f32[3,24,8,512]{3,2,1,0:T(8,128)} %h_in.1), custom_call_target="tpu_custom_call" | custom-call | tf_op jit(solution)/shard_map/pallas_call | solution.py:223
  2.3 0.0 copy-start
  2.3 0.0 copy-start.1
  2.3 0.0 copy-start.2
  2.3 0.0 copy-start.4
  2.3 0.0 copy-start.5
  2.3 0.1 shard_map.113
  2.5 3.1 %collective-permute-start.2 = (f32[72,512]{1,0:T(8,128)S(1)}, f32[72,512]{1,0:T(8,128)S(1)}, u32[]{:S(2)}, u32[]{:S(2)}) collective-permute-start(f32[72,512]{1,0:T(8,128)S(1)} %get-tuple-element.41), channel_id=1, source_target_pairs={{0,8},{2,10},{4,12},{6,14},{8,0},{10,2},{12,4},{14,6},{16,24},{18,... | collective-permute-start | bytes 442376 | tf_op jit(solution)/shard_map/ppermute | solution.py:65
  5.6 0.0 collective-permute-start.3
  5.6 1.5 %collective-permute-start = (f32[3,8,512]{2,1,0:T(8,128)S(1)}, f32[3,8,512]{2,1,0:T(8,128)S(1)}, u32[]{:S(2)}, u32[]{:S(2)}) collective-permute-start(f32[3,8,512]{2,1,0:T(8,128)S(1)} %get-tuple-element.39), channel_id=1, source_target_pairs={{0,1},{2,3},{4,5},{6,7},{1,0},{3,2},{5,4},{7,6},{8,9},{10,11},{12,... | collective-permute-start | bytes 147464 | tf_op jit(solution)/shard_map/ppermute | solution.py:65
  7.1 0.2 collective-permute-start.1
  7.3 0.0 copy-done
  7.3 0.0 copy-done.1
  7.3 0.0 copy-done.2
  7.3 0.0 copy-done.4
  7.3 0.0 copy-done.5
  7.3 1.2 %shard_map.112 = (f32[3,24,8,512]{3,2,1,0:T(8,128)S(1)}, f32[15,8,128]{2,1,0:T(8,128)S(1)}, f32[15,8,128]{2,1,0:T(8,128)S(1)}, f32[8,512]{1,0:T(8,128)S(1)}, f32[24,8,512]{2,1,0:T(8,128)S(1)}) custom-call(f32[1,4]{1,0:T(1,128)S(1)} %bitcast.1, f32[3,24,8,512]{3,2,1,0:T(8,128)S(1)} %get-tuple-element.34.e_ref.refs_0_, ...), custom_call_target="tpu_custom_call" | custom-call | tf_op jit(solution)/shard_map/pallas_call | solution.py:284
  8.6 0.0 collective-permute-done.1.refs_7_.refs_3_.refs_5_.refs_6_
  8.6 1.1 %collective-permute-done.refs_6_.refs_2_.refs_4_.refs_5_ = f32[3,8,512]{2,1,0:T(8,128)S(1)} collective-permute-done((f32[3,8,512]{2,1,0:T(8,128)S(1)}, f32[3,8,512]{2,1,0:T(8,128)S(1)}, u32[]{:S(2)}, u32[]{:S(2)}) %collective-permute-start) | collective-permute-done | bytes 49184 | tf_op jit(solution)/shard_map/ppermute | solution.py:65
  9.7 0.0 collective-permute-done.2.refs_8_.refs_4_.refs_6_.refs_7_
  9.7 0.0 collective-permute-done.3.refs_9_.refs_5_.refs_7_.refs_8_
  9.7 0.8 %shard_map.114 = (f32[8,2048]{1,0:T(8,128)S(1)}, f32[8,2048]{1,0:T(8,128)S(1)}, f32[8,2048]{1,0:T(8,128)S(1)}, f32[8,2048]{1,0:T(8,128)S(1)}, f32[16,8,512]{2,1,0:T(8,128)S(1)}) custom-call(f32[3,24,8,512]{3,2,1,0:T(8,128)S(1)} %get-tuple-element.34.e_ref.refs_0_, f32[3,24,8,512]{3,2,1,0:T(8,128)S(1)} %get-tuple-element.35.h_ref.refs_1_, ...), custom_call_target="tpu_custom_call" | custom-call | tf_op jit(solution)/shard_map/pallas_call | solution.py:605
  10.5 0.1 shard_map.116
  10.7 0.1 collective-permute-start.4
  10.7 3.8 %collective-permute-start.5 = (f32[17,8,128]{2,1,0:T(8,128)S(1)}, f32[17,8,128]{2,1,0:T(8,128)S(1)}, u32[]{:S(2)}, u32[]{:S(2)}) collective-permute-start(f32[17,8,128]{2,1,0:T(8,128)S(1)} %get-tuple-element.50), channel_id=1, source_target_pairs={{0,1},{1,0},{2,4},{3,5},{4,2},{5,3},{6,7},{7,6},{8,9},{9,8},{10,12... | collective-permute-start | bytes 208904 | tf_op jit(solution)/shard_map/ppermute | solution.py:65
  14.5 1.4 %collective-permute-start.6 = (f32[8,2048]{1,0:T(8,128)S(1)}, f32[8,2048]{1,0:T(8,128)S(1)}, u32[]{:S(2)}, u32[]{:S(2)}) collective-permute-start(f32[8,2048]{1,0:T(8,128)S(1)} %get-tuple-element.53), channel_id=1, source_target_pairs={{0,24},{8,16},{16,8},{24,0},{1,25},{9,17},{17,9},{25,1},{2,26},{10... | collective-permute-start | bytes 196616 | tf_op jit(solution)/shard_map/ppermute | solution.py:899
  16.0 2.0 %collective-permute-start.7 = (f32[8,2048]{1,0:T(8,128)S(1)}, f32[8,2048]{1,0:T(8,128)S(1)}, u32[]{:S(2)}, u32[]{:S(2)}) collective-permute-start(f32[8,2048]{1,0:T(8,128)S(1)} %get-tuple-element.54), channel_id=1, source_target_pairs={{0,16},{8,24},{16,0},{24,8},{1,17},{9,25},{17,1},{25,9},{2,18},{10... | collective-permute-start | bytes 196616 | tf_op jit(solution)/shard_map/ppermute | solution.py:899
  17.9 1.0 %collective-permute-start.8 = (f32[8,2048]{1,0:T(8,128)S(1)}, f32[8,2048]{1,0:T(8,128)S(1)}, u32[]{:S(2)}, u32[]{:S(2)}) collective-permute-start(f32[8,2048]{1,0:T(8,128)S(1)} %get-tuple-element.55), channel_id=1, source_target_pairs={{0,8},{8,0},{16,24},{24,16},{1,9},{9,1},{17,25},{25,17},{2,10},{10... | collective-permute-start | bytes 196616 | tf_op jit(solution)/shard_map/ppermute | solution.py:899
  18.9 0.5 %shard_map.115 = (f32[24,6,8,128]{3,2,1,0:T(8,128)S(1)}, f32[16,5,8,128]{3,2,1,0:T(8,128)S(1)}, f32[8,128]{1,0:T(8,128)S(1)}) custom-call(f32[3,24,8,512]{3,2,1,0:T(8,128)S(1)} %get-tuple-element.34.e_ref.refs_0_, f32[3,24,8,512]{3,2,1,0:T(8,128)S(1)} %get-tuple-element.35.h_ref.refs_1_, f32[3,24,8,512]{3,2,1,0:T(8,128)S(1)} %get-tuple-element.37.refs_2_.f_ref, ...), custom_call_target="tpu_custom_call" | custom-call | tf_op jit(solution)/shard_map/pallas_call | solution.py:319
  19.4 0.0 copy-start.3
  19.5 0.0 collective-permute-done.4.refs_8_.refs_9_
  19.5 0.0 collective-permute-done.5.refs_9_.refs_10_
  19.5 0.9 %shard_map.117 = (f32[8,256]{1,0:T(8,128)S(1)}, f32[16,8,128]{2,1,0:T(8,128)S(1)}) custom-call(f32[16,8,512]{2,1,0:T(8,128)S(1)} %get-tuple-element.43.refs_6_.refs_0_.refs_3_, f32[24,6,8,128]{3,2,1,0:T(8,128)S(1)} %get-tuple-element.44.refs_1_, f32[16,5,8,128]{3,2,1,0:T(8,128)S(1)} %get-tuple-element.45.refs_2_, f32[8,128]{1,0:T(8,128)S(1)} %get-tuple-element.46.refs_3_, ...), custom_call_target="tpu_custom_call" | custom-call | tf_op jit(solution)/shard_map/pallas_call | solution.py:653
  20.4 0.3 collective-permute-done.6.refs_2_
  20.7 3.6 %collective-permute-done.7.refs_3_ = f32[8,2048]{1,0:T(8,128)S(1)} collective-permute-done((f32[8,2048]{1,0:T(8,128)S(1)}, f32[8,2048]{1,0:T(8,128)S(1)}, u32[]{:S(2)}, u32[]{:S(2)}) %collective-permute-start.7) | collective-permute-done | bytes 65568 | tf_op jit(solution)/shard_map/ppermute | solution.py:899
  24.3 0.0 collective-permute-done.8.refs_4_
  24.3 0.0 copy-done.3
  24.3 0.8 %shard_map.118 = (f32[8,2304]{1,0:T(8,128)S(1)}, f32[8,2304]{1,0:T(8,128)S(1)}, f32[8,2304]{1,0:T(8,128)S(1)}, f32[8,2304]{1,0:T(8,128)S(1)}) custom-call(bf16[112,48]{1,0:T(8,128)(2,1)S(1)} %copy-done.3, f32[8,256]{1,0:T(8,128)S(1)} %get-tuple-element.52.refs_1_, f32[8,2048]{1,0:T(8,128)S(1)} %collective-permute-done.6.refs_2_, ...), custom_call_target="tpu_custom_call" | custom-call | tf_op jit(solution)/shard_map/pallas_call | solution.py:799
  25.1 1.9 %collective-permute-start.9 = (f32[8,2304]{1,0:T(8,128)S(1)}, f32[8,2304]{1,0:T(8,128)S(1)}, u32[]{:S(2)}, u32[]{:S(2)}) collective-permute-start(f32[8,2304]{1,0:T(8,128)S(1)} %get-tuple-element.61), channel_id=1, source_target_pairs={{0,24},{8,16},{16,8},{24,0},{1,25},{9,17},{17,9},{25,1},{2,26},{10... | collective-permute-start | bytes 221192 | tf_op jit(solution)/shard_map/ppermute | solution.py:899
  26.9 0.0 collective-permute-start.10
  26.9 2.6 %collective-permute-start.11 = (f32[8,2304]{1,0:T(8,128)S(1)}, f32[8,2304]{1,0:T(8,128)S(1)}, u32[]{:S(2)}, u32[]{:S(2)}) collective-permute-start(f32[8,2304]{1,0:T(8,128)S(1)} %get-tuple-element.63), channel_id=1, source_target_pairs={{0,8},{8,0},{16,24},{24,16},{1,9},{9,1},{17,25},{25,17},{2,10},{10... | collective-permute-start | bytes 221192 | tf_op jit(solution)/shard_map/ppermute | solution.py:899
  29.5 3.2 %shard_map.119 = (f32[3,24,8,512]{3,2,1,0:T(8,128)}, f32[3,24,8,512]{3,2,1,0:T(8,128)}, f32[16,8,512]{2,1,0:T(8,128)}) custom-call(f32[3,24,8,512]{3,2,1,0:T(8,128)S(1)} %get-tuple-element.34.e_ref.refs_0_, f32[3,24,8,512]{3,2,1,0:T(8,128)S(1)} %get-tuple-element.35.h_ref.refs_1_, f32[24,8,512]{2,1,0:T(8,128)S(1)} %get-tuple-element.36.refs_3_.inv_ref.refs_2_, ...), custom_call_target="tpu_custom_call" | custom-call | tf_op jit(solution)/shard_map/pallas_call | solution.py:716
  32.8 0.0 collective-permute-done.9.refs_1_
  32.8 1.6 %collective-permute-done.10.refs_2_ = f32[8,2304]{1,0:T(8,128)S(1)} collective-permute-done((f32[8,2304]{1,0:T(8,128)S(1)}, f32[8,2304]{1,0:T(8,128)S(1)}, u32[]{:S(2)}, u32[]{:S(2)}) %collective-permute-start.10) | collective-permute-done | bytes 73760 | tf_op jit(solution)/shard_map/ppermute | solution.py:899
  34.4 0.0 collective-permute-done.11.refs_3_
  34.4 1.3 %shard_map.120 = f32[16,8,512]{2,1,0:T(8,128)} custom-call(bf16[112,48]{1,0:T(8,128)(2,1)S(1)} %copy-done.3, f32[8,2304]{1,0:T(8,128)S(1)} %collective-permute-done.9.refs_1_, f32[8,2304]{1,0:T(8,128)S(1)} %collective-permute-done.10.refs_2_, f32[8,2304]{1,0:T(8,128)S(1)} %collective-permute-done.11.refs_3_, f32[8,2304]{1,0:T(8,128)S(1)} %get-tuple-element.57.refs_11_.refs_4_), custom_call_target="tpu_custom_call" | custom-call | tf_op jit(solution)/shard_map/pallas_call | solution.py:877
Async XLA Ops:
  2.3 5.0 %copy-start = (f32[16,8,512]{2,1,0:T(8,128)S(1)}, f32[16,8,512]{2,1,0:T(8,128)}, u32[]{:S(2)}) copy-start(f32[16,8,512]{2,1,0:T(8,128)} %grad_ref.3) | copy-start | bytes 786436
  2.3 5.0 %copy-start.1 = (f32[3,24,8,512]{3,2,1,0:T(8,128)S(1)}, f32[3,24,8,512]{3,2,1,0:T(8,128)}, u32[]{:S(2)}) copy-start(f32[3,24,8,512]{3,2,1,0:T(8,128)} %f_in.1) | copy-start | bytes 3538948
  2.3 5.0 %copy-start.2 = (s32[24,8,512]{2,1,0:T(8,128)S(1)}, s32[24,8,512]{2,1,0:T(8,128)}, u32[]{:S(2)}) copy-start(s32[24,8,512]{2,1,0:T(8,128)} %mat_ref.1) | copy-start | bytes 1179652
  2.3 5.0 %copy-start.4 = (f32[4]{0:T(128)S(1)}, f32[4]{0:T(128)}, u32[]{:S(2)}) copy-start(f32[4]{0:T(128)} %param.12) | copy-start | bytes 52
  2.3 5.0 %copy-start.5 = (s32[1,64]{1,0:T(1,128)S(1)}, s32[1,64]{1,0:T(1,128)}, u32[]{:S(2)}) copy-start(s32[1,64]{1,0:T(1,128)} %mask_ref.1) | copy-start | bytes 772
  2.5 7.2 %collective-permute-start.2 = (f32[72,512]{1,0:T(8,128)S(1)}, f32[72,512]{1,0:T(8,128)S(1)}, u32[]{:S(2)}, u32[]{:S(2)}) collective-permute-start(f32[72,512]{1,0:T(8,128)S(1)} %get-tuple-element.41), channel_id=1, source_target_pairs={{0,8},{2,10},{4,12},{6,14},{8,0},{10,2},{12,4},{14,6},{16,24},{18,... | collective-permute-start | bytes 442376 | tf_op jit(solution)/shard_map/ppermute | solution.py:65
  5.6 4.2 %collective-permute-start.3 = (f32[72,512]{1,0:T(8,128)S(1)}, f32[72,512]{1,0:T(8,128)S(1)}, u32[]{:S(2)}, u32[]{:S(2)}) collective-permute-start(f32[72,512]{1,0:T(8,128)S(1)} %get-tuple-element.42), channel_id=1, source_target_pairs={{0,2},{2,0},{4,6},{6,4},{8,16},{10,18},{12,20},{14,22},{16,8},{18,... | collective-permute-start | bytes 442376 | tf_op jit(solution)/shard_map/ppermute | solution.py:65
  5.6 4.2 %collective-permute-start = (f32[3,8,512]{2,1,0:T(8,128)S(1)}, f32[3,8,512]{2,1,0:T(8,128)S(1)}, u32[]{:S(2)}, u32[]{:S(2)}) collective-permute-start(f32[3,8,512]{2,1,0:T(8,128)S(1)} %get-tuple-element.39), channel_id=1, source_target_pairs={{0,1},{2,3},{4,5},{6,7},{1,0},{3,2},{5,4},{7,6},{8,9},{10,11},{12,... | collective-permute-start | bytes 147464 | tf_op jit(solution)/shard_map/ppermute | solution.py:65
  7.1 1.5 %collective-permute-start.1 = (f32[8,512]{1,0:T(8,128)S(1)}, f32[8,512]{1,0:T(8,128)S(1)}, u32[]{:S(2)}, u32[]{:S(2)}) collective-permute-start(f32[8,512]{1,0:T(8,128)S(1)} %get-tuple-element.40), channel_id=1, source_target_pairs={{0,2},{2,0},{4,6},{6,4},{1,8},{3,10},{5,12},{7,14},{8,1},{10,3},{1... | collective-permute-start | bytes 49160 | tf_op jit(solution)/shard_map/ppermute | solution.py:91
  10.7 8.8 %collective-permute-start.4 = (f32[17,8,128]{2,1,0:T(8,128)S(1)}, f32[17,8,128]{2,1,0:T(8,128)S(1)}, u32[]{:S(2)}, u32[]{:S(2)}) collective-permute-start(f32[17,8,128]{2,1,0:T(8,128)S(1)} %get-tuple-element.49), channel_id=1, source_target_pairs={{0,2},{1,3},{2,0},{3,1},{4,6},{5,7},{6,4},{7,5},{8,10},{9,11},{10,... | collective-permute-start | bytes 208904 | tf_op jit(solution)/shard_map/ppermute | solution.py:65
  10.7 8.7 %collective-permute-start.5 = (f32[17,8,128]{2,1,0:T(8,128)S(1)}, f32[17,8,128]{2,1,0:T(8,128)S(1)}, u32[]{:S(2)}, u32[]{:S(2)}) collective-permute-start(f32[17,8,128]{2,1,0:T(8,128)S(1)} %get-tuple-element.50), channel_id=1, source_target_pairs={{0,1},{1,0},{2,4},{3,5},{4,2},{5,3},{6,7},{7,6},{8,9},{9,8},{10,12... | collective-permute-start | bytes 208904 | tf_op jit(solution)/shard_map/ppermute | solution.py:65
  14.5 6.2 %collective-permute-start.6 = (f32[8,2048]{1,0:T(8,128)S(1)}, f32[8,2048]{1,0:T(8,128)S(1)}, u32[]{:S(2)}, u32[]{:S(2)}) collective-permute-start(f32[8,2048]{1,0:T(8,128)S(1)} %get-tuple-element.53), channel_id=1, source_target_pairs={{0,24},{8,16},{16,8},{24,0},{1,25},{9,17},{17,9},{25,1},{2,26},{10... | collective-permute-start | bytes 196616 | tf_op jit(solution)/shard_map/ppermute | solution.py:899
  16.0 8.3 %collective-permute-start.7 = (f32[8,2048]{1,0:T(8,128)S(1)}, f32[8,2048]{1,0:T(8,128)S(1)}, u32[]{:S(2)}, u32[]{:S(2)}) collective-permute-start(f32[8,2048]{1,0:T(8,128)S(1)} %get-tuple-element.54), channel_id=1, source_target_pairs={{0,16},{8,24},{16,0},{24,8},{1,17},{9,25},{17,1},{25,9},{2,18},{10... | collective-permute-start | bytes 196616 | tf_op jit(solution)/shard_map/ppermute | solution.py:899
  17.9 6.3 %collective-permute-start.8 = (f32[8,2048]{1,0:T(8,128)S(1)}, f32[8,2048]{1,0:T(8,128)S(1)}, u32[]{:S(2)}, u32[]{:S(2)}) collective-permute-start(f32[8,2048]{1,0:T(8,128)S(1)} %get-tuple-element.55), channel_id=1, source_target_pairs={{0,8},{8,0},{16,24},{24,16},{1,9},{9,1},{17,25},{25,17},{2,10},{10... | collective-permute-start | bytes 196616 | tf_op jit(solution)/shard_map/ppermute | solution.py:899
  19.4 4.8 %copy-start.3 = (bf16[112,48]{1,0:T(8,128)(2,1)S(1)}, bf16[112,48]{1,0:T(8,128)(2,1)}, u32[]{:S(2)}) copy-start(bf16[112,48]{1,0:T(8,128)(2,1)} %constant.2.clone.refs_0_) | copy-start | bytes 32260
  25.1 7.7 %collective-permute-start.9 = (f32[8,2304]{1,0:T(8,128)S(1)}, f32[8,2304]{1,0:T(8,128)S(1)}, u32[]{:S(2)}, u32[]{:S(2)}) collective-permute-start(f32[8,2304]{1,0:T(8,128)S(1)} %get-tuple-element.61), channel_id=1, source_target_pairs={{0,24},{8,16},{16,8},{24,0},{1,25},{9,17},{17,9},{25,1},{2,26},{10... | collective-permute-start | bytes 221192 | tf_op jit(solution)/shard_map/ppermute | solution.py:899
  26.9 7.5 %collective-permute-start.10 = (f32[8,2304]{1,0:T(8,128)S(1)}, f32[8,2304]{1,0:T(8,128)S(1)}, u32[]{:S(2)}, u32[]{:S(2)}) collective-permute-start(f32[8,2304]{1,0:T(8,128)S(1)} %get-tuple-element.62), channel_id=1, source_target_pairs={{0,16},{8,24},{16,0},{24,8},{1,17},{9,25},{17,1},{25,9},{2,18},{10... | collective-permute-start | bytes 221192 | tf_op jit(solution)/shard_map/ppermute | solution.py:899
  26.9 7.5 %collective-permute-start.11 = (f32[8,2304]{1,0:T(8,128)S(1)}, f32[8,2304]{1,0:T(8,128)S(1)}, u32[]{:S(2)}, u32[]{:S(2)}) collective-permute-start(f32[8,2304]{1,0:T(8,128)S(1)} %get-tuple-element.63), channel_id=1, source_target_pairs={{0,8},{8,0},{16,24},{24,16},{1,9},{9,1},{17,25},{25,17},{2,10},{10... | collective-permute-start | bytes 221192 | tf_op jit(solution)/shard_map/ppermute | solution.py:899

commit v8 on v7

--- a/solution.py
+++ b/solution.py
@@ -183,7 +183,7 @@
     )(efield, hfield)
     xfaces = exchange(sends[:x_rounds], "gx", "gy")
     zfaces = exchange(sends[x_rounds : x_rounds + z_rounds], "gz", "gy")
-    return zfaces + exchange_diagonal(sends[x_rounds + z_rounds :]), xfaces
+    return zfaces, xfaces, exchange_diagonal(sends[x_rounds + z_rounds :])
 
 
 def lane_group():
@@ -325,24 +325,26 @@
     )(*arrays)
 
 
-def face_tiles(zfaces, xfaces):
+def corner_lines(lines, s):
+    z_side, x_side = Side("gz"), Side("gx")
+    above = jnp.where(x_side.bottom, 0.0, z_side.upper([f[:, s] for f in lines]))
+    beyond = jnp.where(x_side.top, 0.0, z_side.lower([f[:, s] for f in lines]))
+    return above, beyond
+
+
+def face_tiles(zfaces, xfaces, lines):
     width = xfaces[0].shape[1]
     rows = xfaces[0].shape[0]
     cells_z = rows // 3
     z_side, x_side = Side("gz"), Side("gx")
-    zfaces, lines = zfaces[: len(zfaces) // 2], zfaces[len(zfaces) // 2 :]
 
     def corner(s):
         row = lax.broadcasted_iota(jnp.int32, (ROWS, s.stop - s.start), 0)
-        line = jnp.where(x_side.bottom, 0.0, z_side.upper([f[:, s] for f in lines]))
-        return jnp.where(row == ROWS - 1, -HALF * line, 0.0)
-
-    def beyond(s):
-        return jnp.where(x_side.top, 0.0, z_side.lower([f[:, s] for f in lines]))
+        return jnp.where(row == ROWS - 1, -HALF * corner_lines(lines, s)[0], 0.0)
 
     def x_tile(pick, t, s):
         value = pick([f[t : t + ROWS, s] for f in xfaces])
-        return value + corner(s) if t == cells_z - ROWS and pick == x_side.lower else value
+        return value + corner(s) if lines and t == cells_z - ROWS and pick == x_side.lower else value
 
     tiles = []
     for c in range(3):
@@ -352,8 +354,8 @@
     for t in range(0, rows, ROWS):
         tiles.append((lambda s, t=t: x_tile(x_side.lower, t, s), width))
     for t in range(0, rows, ROWS):
-        if t == 2 * cells_z:
-            tiles.append((beyond, width))
+        if lines and t == 2 * cells_z:
+            tiles.append((lambda s: corner_lines(lines, s)[1], width))
         else:
             tiles.append((lambda s, t=t: x_tile(x_side.upper, t, s), width))
     return tiles
@@ -365,10 +367,11 @@
 
 def y_faces_kernel(counts, *refs):
     own_low, own_high = refs[:2]
-    zfaces, xfaces = refs[2 : 2 + counts[0]], refs[2 + counts[0] : 2 + sum(counts)]
+    ends = np.cumsum((2,) + counts)
+    zfaces, xfaces, lines = (refs[i:j] for i, j in zip(ends[:-1], ends[1:]))
     sends, (low_ref, high_ref) = refs[3 + sum(counts) : -2], refs[-2:]
     own = own_low.shape[0]
-    pack_strips(face_tiles(zfaces, xfaces), low_ref, high_ref, 0)
+    pack_strips(face_tiles(zfaces, xfaces, lines), low_ref, high_ref, 0)
     side = Side("gy")
     for ref, value in zip(sends, side.sends(own_low[...], own_high[...])):
         ref[0:own] = value
@@ -376,17 +379,17 @@
         ref[own:] = value
 
 
-def y_faces(own_low, own_high, zfaces, xfaces, after):
+def y_faces(own_low, own_high, zfaces, xfaces, lines, after):
     extra = math.ceil(face_count(xfaces[0]) / SLOTS)
     packed = fast(own_low.shape[0] + extra, ROWS, LANES)
     return pl.pallas_call(
-        functools.partial(y_faces_kernel, (len(zfaces), len(xfaces))),
-        in_specs=[VMEM] * (2 + len(zfaces) + len(xfaces)) + [ANY],
+        functools.partial(y_faces_kernel, (len(zfaces), len(xfaces), len(lines))),
+        in_specs=[VMEM] * (2 + len(zfaces) + len(xfaces) + len(lines)) + [ANY],
         out_specs=[VMEM] * rounds("gy"),
         out_shape=[packed] * rounds("gy"),
         scratch_shapes=[pltpu.VMEM((extra, ROWS, LANES), jnp.float32)] * 2,
         compiler_params=params(),
-    )(own_low, own_high, *zfaces, *xfaces, after)
+    )(own_low, own_high, *zfaces, *xfaces, *lines, after)
 
 
 OWN, CIRCLE, EDGE = range(3)
@@ -397,7 +400,7 @@
 
 
 class Fields:
-    def __init__(self, mode, layers, fields, zfaces, xfaces, yfaces, scratch):
+    def __init__(self, mode, layers, fields, zfaces, xfaces, lines, yfaces, scratch):
         self.mode = mode
         self.fields = fields
         if mode == EDGE:
@@ -433,7 +436,7 @@
                 return self.edge(own, halo_base + slot // SLOTS, slot % SLOTS)
             return self.wider(load, halo_base + slot // SLOTS, slot % SLOTS)
 
-        full = [face(load, slot) for slot, (load, _) in enumerate(face_tiles(zfaces, xfaces))]
+        full = [face(load, slot) for slot, (load, _) in enumerate(face_tiles(zfaces, xfaces, lines))]
         self.below, self.above = full[:3], full[3:5]
         per_face = xfaces[0].shape[0] // ROWS
         for t in range(per_face):
@@ -584,7 +587,7 @@
     zfaces, xfaces = refs[6 : 6 + counts[0]], refs[6 + counts[0] : 6 + sum(counts)]
     shares, (own_ref, *scratch) = refs[6 + sum(counts) : -3][::-1], refs[-3:]
     layers, _, width = grad_ref.shape
-    fields = Fields(OWN, layers, (e_ref, h_ref), zfaces, xfaces, None, scratch)
+    fields = Fields(OWN, layers, (e_ref, h_ref), zfaces, xfaces, (), None, scratch)
 
     def store(layer, value):
         own_ref[layer] = value
@@ -617,14 +620,14 @@
 
 
 def edge_gradient_kernel(counts, *refs):
-    own_ref, eh_ref, grad_ref, mask_ref = refs[:4]
-    ends = np.cumsum((4,) + counts)
-    zfaces, xfaces, yfaces = (refs[i:j] for i, j in zip(ends[:-1], ends[1:]))
+    own_ref, f_ref, inv_ref, wide_ref, eh_ref, grad_ref, mask_ref = refs[:7]
+    ends = np.cumsum((7,) + counts)
+    zfaces, xfaces, lines, yfaces = (refs[i:j] for i, j in zip(ends[:-1], ends[1:]))
     (message, edge_ref), scratch = refs[ends[-1] : -3], refs[-3:]
     layers, _, width = own_ref.shape
     lane = lax.broadcasted_iota(jnp.int32, (ROWS, LANES), 1)
     first, last = STRIP, LANES - STRIP - 1
-    fields = Fields(EDGE, layers, eh_ref, zfaces, xfaces, yfaces, scratch)
+    fields = Fields(EDGE, layers, eh_ref, zfaces, xfaces, lines, yfaces, scratch)
 
     def store(layer, value):
         edge_ref[layer] = value
@@ -645,25 +648,50 @@
             packed = jnp.where(lane // STRIP == 2 * j + 1, right, packed)
         message[:, start // per_tile * LANES : (start // per_tile + 1) * LANES] = packed
 
-
-def edge_gradient(own, edges, zfaces, xfaces, yfaces):
+    tail = math.ceil(layers / per_tile) * LANES
+    message[:, tail:] = jnp.zeros_like(message[:, tail:])
+    top, last = fields.cells_z - 1, ROWS - 1
+    above, beyond = (line[0:1] for line in corner_lines(lines, slice(0, width)))
+    added = wide_ref[0:1, :] * f_ref[2, top, 0:1, :] * inv_ref[top, 0:1, :] * (HALF * above)
+    added += wide_ref[last:, :] * f_ref[0, 0, last:, :] * inv_ref[0, last:, :] * (HALF * beyond)
+    column = lax.broadcasted_iota(jnp.int32, (1, width), 1)
+    added = jnp.where(jnp.logical_or(column == 0, column == width - 1), 0.0, added)
+    for at, n in line_places(width):
+        message[n : n + 1, tail + at : tail + at + LANES] = added[:, (at // LANES * ROWS + n) * LANES :][:, :LANES]
+
+
+def line_places(width):
+    return [(t // ROWS * LANES, t % ROWS) for t in range(width // LANES)]
+
+
+def line_of(message, width):
+    tail = message.shape[1] - math.ceil(width / LANES / ROWS) * LANES
+    return jnp.concatenate([message[n : n + 1, tail + at : tail + at + LANES] for at, n in line_places(width)], axis=1)
+
+
+def line_spot(layers):
+    bottom = lax.axis_index("gz") == 0
+    return jnp.where(bottom, layers - 1, 0), jnp.where(bottom, 0, ROWS - 1)
+
+
+def edge_gradient(own, arrays, edges, zfaces, xfaces, lines, yfaces):
     layers, _, width = own.shape
-    faces = (*zfaces, *xfaces, *yfaces)
-    tiles = math.ceil(layers * PART / LANES)
+    faces = (*zfaces, *xfaces, *lines, *yfaces)
+    tiles = math.ceil(layers * PART / LANES) + math.ceil(width / LANES / ROWS)
     return pl.pallas_call(
-        functools.partial(edge_gradient_kernel, (len(zfaces), len(xfaces), len(yfaces))),
-        in_specs=[VMEM] * (4 + len(faces)),
+        functools.partial(edge_gradient_kernel, (len(zfaces), len(xfaces), len(lines), len(yfaces))),
+        in_specs=[VMEM] * (7 + len(faces)),
         out_specs=[VMEM] * 2,
         out_shape=[fast(ROWS, tiles * LANES), fast(layers, ROWS, LANES)],
         scratch_shapes=fields_scratch(EDGE, xfaces[0], yfaces[0], width),
         compiler_params=params(),
-    )(own, *edges, *faces)
+    )(own, arrays[2], arrays[3], arrays[5], *edges, *faces)
 
 
 def step_kernel(counts, *refs):
-    e_ref, h_ref, inv_ref, own_ref, edge_ref = refs[:5]
-    ends = np.cumsum((5,) + counts)
-    zfaces, xfaces, yfaces = (refs[i:j] for i, j in zip(ends[:-1], ends[1:]))
+    e_ref, h_ref, inv_ref, own_ref, edge_ref, message = refs[:6]
+    ends = np.cumsum((6,) + counts)
+    zfaces, xfaces, lines, yfaces = (refs[i:j] for i, j in zip(ends[:-1], ends[1:]))
     e_out, h_out, grad_out = refs[ends[-1] + 1 : ends[-1] + 4]
     left_wide, right_wide, ybuf, e_new, h_new, grad_new, sems = refs[ends[-1] + 4 :]
     layers, _, width = own_ref.shape
@@ -675,10 +703,13 @@
         grad_new[layer] = own_ref[layer]
         grad_new[layer, :, 0:LANES] = jnp.where(lane == 0, pltpu.roll(edge, LANES - STRIP, 1), head)
         grad_new[layer, :, width - LANES :] = jnp.where(lane == LANES - 1, pltpu.roll(edge, STRIP, 1), tail)
+    layer, spot = line_spot(layers)
+    row = lax.broadcasted_iota(jnp.int32, (ROWS, width), 0)
+    grad_new[layer] += jnp.where(row == spot, line_of(message, width), 0.0)
     grad_copy = pltpu.make_async_copy(grad_new, grad_out, sems.at[0, 0])
     grad_copy.start()
 
-    fields = Fields(CIRCLE, layers, (e_ref, h_ref), zfaces, xfaces, yfaces, (left_wide, right_wide, ybuf))
+    fields = Fields(CIRCLE, layers, (e_ref, h_ref), zfaces, xfaces, lines, yfaces, (left_wide, right_wide, ybuf))
 
     def emit(a, b, efield, hfield, curl):
         z = ROWS * a + b
@@ -708,21 +739,21 @@
     grad_copy.wait()
 
 
-def step(efield, hfield, inv, own, edge, zfaces, xfaces, yfaces, after):
+def step(efield, hfield, inv, own, edge, message, zfaces, xfaces, lines, yfaces, after):
     _, cells_z, _, width = efield.shape
-    groups = (zfaces, xfaces, yfaces)
+    groups = (zfaces, xfaces, lines, yfaces)
     counts = tuple(len(group) for group in groups)
     shapes = (efield.shape, hfield.shape, own.shape)
     return pl.pallas_call(
         functools.partial(step_kernel, counts),
-        in_specs=[VMEM] * (5 + sum(counts)) + [ANY],
+        in_specs=[VMEM] * (6 + sum(counts)) + [ANY],
         out_specs=[ANY] * 3,
         out_shape=[f32(*shape) for shape in shapes],
         scratch_shapes=fields_scratch(CIRCLE, xfaces[0], yfaces[0], width)
         + [pltpu.VMEM(shape, jnp.float32) for shape in shapes]
         + [pltpu.SemaphoreType.DMA((1 + cells_z // ROWS, 6))],
         compiler_params=params(),
-    )(efield, hfield, inv, own, edge, *(one for group in groups for one in group), after)
+    )(efield, hfield, inv, own, edge, message, *(one for group in groups for one in group), after)
 
 
 def cone_matrix(rows):
@@ -816,7 +847,7 @@
 def finish_kernel(count, per_device, width, *refs):
     taps_ref = refs[0]
     got = refs[count:0:-1]
-    out, (slabs, parts, mine, left, right, done, sems) = refs[count + 1], refs[count + 2 :]
+    out, (slabs, parts, mine, line_parts, line_mine, left, right, done, sems) = refs[count + 1], refs[count + 2 :]
     me = lax.axis_index("gx")
     layers = count * per_device
     half = count // 2
@@ -827,6 +858,21 @@
         slabs[lax.bitwise_xor(me, k)] = got[k][:, per_device * width :]
     symmetric = jnp.concatenate([slabs[s] + flip_rows(slabs[count - 1 - s]) for s in range(half)], axis=0)
     per_tile = LANES // SPAN
+
+    line_layer, spot = line_spot(layers)
+    row = lax.broadcasted_iota(jnp.int32, (ROWS, width), 0)
+    folded = [
+        jnp.where(row == spot, line_of(slabs[s], width), 0.0)
+        + jnp.where(row == ROWS - 1 - spot, line_of(slabs[count - 1 - s], width), 0.0)
+        for s in range(half)
+    ]
+    side = jnp.zeros((rows, LANES), jnp.float32)
+    split_rows(jnp.concatenate([jnp.concatenate(folded, axis=0), side], axis=1), line_parts)
+    total = cone(taps_ref, line_parts, rows)
+    for s in range(half):
+        own = total[s * ROWS : (s + 1) * ROWS, :width]
+        line_mine[s] = own
+        line_mine[count - 1 - s] = flip_rows(own)
     tiles = []
     for start in range(0, layers, per_tile):
         tile = jnp.zeros((rows, LANES), jnp.float32)
@@ -859,7 +905,8 @@
         first = lax.bitwise_xor(me, k) * per_device
         for i in range(per_device):
             at = i * width
-            done[k, i] = got[k][:, at : at + width]
+            line = jnp.where(first + i == line_layer, line_mine[me], 0.0)
+            done[k, i] = got[k][:, at : at + width] + line
             done[k, i, :, :LANES] += left[first + i]
             done[k, i, :, width - LANES :] += right[first + i]
         copies.append(pltpu.make_async_copy(done.at[k], out.at[pl.ds(first, per_device)], sems.at[k]))
@@ -883,6 +930,8 @@
             pltpu.VMEM((count, ROWS, edges), jnp.float32),
             pltpu.VMEM((3 * rows, spread), jnp.bfloat16),
             pltpu.VMEM((count, ROWS, spread), jnp.float32),
+            pltpu.VMEM((3 * rows, width + LANES), jnp.bfloat16),
+            pltpu.VMEM((count, ROWS, width), jnp.float32),
             pltpu.VMEM((layers, ROWS, LANES), jnp.float32),
             pltpu.VMEM((layers, ROWS, LANES), jnp.float32),
             pltpu.VMEM((count, per_device, ROWS, width), jnp.float32),
@@ -903,7 +952,7 @@
 def on_device(efield, hfield, forward, material, permit, design_mask, grad_sum):
     layers, _, width = grad_sum.shape
     efield, hfield = load(efield, hfield)
-    zfaces, xfaces = halos(efield, hfield)
+    zfaces, xfaces, lines = halos(efield, hfield)
     forward, own_low, own_high, mask, inv = strips(
         permit, efield, hfield, forward, material, grad_sum, design_mask
     )
@@ -911,11 +960,13 @@
     edges = own_edges(arrays)
     shares, own = own_gradient(arrays, zfaces, xfaces)
     got = spread(shares)
-    yfaces = exchange(y_faces(own_low, own_high, zfaces, xfaces, own), "gy", "gz")
-    message, edge = edge_gradient(own, edges, zfaces, xfaces, yfaces)
+    yfaces = exchange(y_faces(own_low, own_high, zfaces, xfaces, lines, own), "gy", "gz")
+    message, edge = edge_gradient(own, arrays, edges, zfaces, xfaces, lines, yfaces)
     taps = jnp.asarray(cone_matrix(len(got) // 2 * ROWS))
     parts = cone_filter(taps, message, got, layers // len(got), width)
-    e_next, h_next, grad_total = step(efield, hfield, inv, own, edge, zfaces, xfaces, yfaces, parts[0])
+    e_next, h_next, grad_total = step(
+        efield, hfield, inv, own, edge, message, zfaces, xfaces, lines, yfaces, parts[0]
+    )
     return e_next, h_next, grad_total, finish(taps, spread(parts), layers, width)
 
 

time: 35.8 us -> 35.3 us (0.986)
  starting transfers between devices: 17.5 us -> 17.1 us
    ppermute x5, starting transfers between devices: 8.46 us -> 8.03 us  [exchange(): got.append(lax.ppermute(value, tuple(axes), pairs))]
  transfers between devices with their start and end apart: 12 -> 12, of which waited for: 4 -> 4; matrix products, arithmetic and copies ran while one was open for 0% -> 0% of each run, Pallas kernels for 17% -> 19%
where the time goes in v8:
time: 35.3 us; the launch traced here: 35.2 us
  starting transfers between devices  17.1 us (48%)
  Pallas kernels  10.8 us (31%)
  waiting for transfers between devices  6.44 us (18%)
  between operations  0.81 us (2%)
    ppermute x6, starting transfers between devices, spread(): got[k] = lax.ppermute(parts[k], 'gx', [(i, i ^ k) for i in range(count)])  8.84 us
    ppermute x5, starting transfers between devices, exchange(): got.append(lax.ppermute(value, tuple(axes), pairs))  8.03 us
    ppermute x6, waiting for transfers between devices, spread(): got[k] = lax.ppermute(parts[k], 'gx', [(i, i ^ k) for i in range(count)])  5.3 us
    pallas_call x1, Pallas kernels, step(): pl.pallas_call(functools.partial(step_kernel, counts), in_specs=[VMEM] *...  3.24 us
    pallas_call x1, Pallas kernels, load(): pl.pallas_call(load_kernel, in_specs=[ANY] * 2, out_specs=[VMEM] * 2, out...  1.64 us
    pallas_call x1, Pallas kernels, finish(): pl.pallas_call(functools.partial(finish_kernel, count, per_device, width)...  1.34 us
    pallas_call x1, Pallas kernels, strips(): pl.pallas_call(strips_kernel, in_specs=[VMEM] * 3 + [ANY] + [VMEM] * 3, o...  1.24 us
    ppermute x5, waiting for transfers between devices, exchange(): got.append(lax.ppermute(value, tuple(axes), pairs))  1.14 us
  transfers between devices with their start and end apart: 12, of which 4 were waited for; matrix products, arithmetic and copies ran while one was open for 0% of the time, Pallas kernels for 19%

profile of v8, /device:TPU:0, one launch (start us, length us, event | category | flops | bytes accessed | tf_op | source)
XLA Modules:
  0.0 35.2 jit_solution(13128805461503322156)
XLA Ops:
  0.6 1.6 %shard_map.111 = (f32[3,24,8,512]{3,2,1,0:T(8,128)S(1)}, f32[3,24,8,512]{3,2,1,0:T(8,128)S(1)}) custom-call(f32[3,24,8,512]{3,2,1,0:T(8,128)} %e_in.1, f32[3,24,8,512]{3,2,1,0:T(8,128)} %h_in.1), custom_call_target="tpu_custom_call" | custom-call | tf_op jit(solution)/shard_map/pallas_call | solution.py:223
  2.3 0.0 copy-start
  2.3 0.0 copy-start.1
  2.3 0.0 copy-start.2
  2.3 0.0 copy-start.4
  2.3 0.0 copy-start.5
  2.3 0.1 shard_map.113
  2.5 3.1 %collective-permute-start.1 = (f32[72,512]{1,0:T(8,128)S(1)}, f32[72,512]{1,0:T(8,128)S(1)}, u32[]{:S(2)}, u32[]{:S(2)}) collective-permute-start(f32[72,512]{1,0:T(8,128)S(1)} %get-tuple-element.40), channel_id=1, source_target_pairs={{0,8},{2,10},{4,12},{6,14},{8,0},{10,2},{12,4},{14,6},{16,24},{18,... | collective-permute-start | bytes 442376 | tf_op jit(solution)/shard_map/ppermute | solution.py:65
  5.6 0.0 collective-permute-start.2
  5.6 1.5 %collective-permute-start = (f32[3,8,512]{2,1,0:T(8,128)S(1)}, f32[3,8,512]{2,1,0:T(8,128)S(1)}, u32[]{:S(2)}, u32[]{:S(2)}) collective-permute-start(f32[3,8,512]{2,1,0:T(8,128)S(1)} %get-tuple-element.39), channel_id=1, source_target_pairs={{0,1},{2,3},{4,5},{6,7},{1,0},{3,2},{5,4},{7,6},{8,9},{10,11},{12,... | collective-permute-start | bytes 147464 | tf_op jit(solution)/shard_map/ppermute | solution.py:65
  7.1 0.2 collective-permute-start.3
  7.3 0.0 copy-done
  7.3 0.0 copy-done.1
  7.3 0.0 copy-done.2
  7.3 0.0 copy-done.4
  7.3 0.0 copy-done.5
  7.3 1.2 %shard_map.112 = (f32[3,24,8,512]{3,2,1,0:T(8,128)S(1)}, f32[15,8,128]{2,1,0:T(8,128)S(1)}, f32[15,8,128]{2,1,0:T(8,128)S(1)}, f32[8,512]{1,0:T(8,128)S(1)}, f32[24,8,512]{2,1,0:T(8,128)S(1)}) custom-call(f32[1,4]{1,0:T(1,128)S(1)} %bitcast.1, f32[3,24,8,512]{3,2,1,0:T(8,128)S(1)} %get-tuple-element.34.e_ref.refs_0_, ...), custom_call_target="tpu_custom_call" | custom-call | tf_op jit(solution)/shard_map/pallas_call | solution.py:284
  8.6 1.1 %collective-permute-done.refs_6_.refs_2_.refs_7_ = f32[3,8,512]{2,1,0:T(8,128)S(1)} collective-permute-done((f32[3,8,512]{2,1,0:T(8,128)S(1)}, f32[3,8,512]{2,1,0:T(8,128)S(1)}, u32[]{:S(2)}, u32[]{:S(2)}) %collective-permute-start) | collective-permute-done | bytes 49184 | tf_op jit(solution)/shard_map/ppermute | solution.py:65
  9.7 0.0 collective-permute-done.1.refs_7_.refs_3_.refs_8_
  9.7 0.0 collective-permute-done.2.refs_8_.refs_4_.refs_9_
  9.7 0.8 %shard_map.114 = (f32[8,2048]{1,0:T(8,128)S(1)}, f32[8,2048]{1,0:T(8,128)S(1)}, f32[8,2048]{1,0:T(8,128)S(1)}, f32[8,2048]{1,0:T(8,128)S(1)}, f32[16,8,512]{2,1,0:T(8,128)S(1)}) custom-call(f32[3,24,8,512]{3,2,1,0:T(8,128)S(1)} %get-tuple-element.34.e_ref.refs_0_, f32[3,24,8,512]{3,2,1,0:T(8,128)S(1)} %get-tuple-element.35.h_ref.refs_1_, ...), custom_call_target="tpu_custom_call" | custom-call | tf_op jit(solution)/shard_map/pallas_call | solution.py:608
  10.5 0.0 collective-permute-done.3.refs_5_.refs_10_.refs_9_
  10.5 0.1 shard_map.116
  10.7 0.1 collective-permute-start.4
  10.8 3.3 %collective-permute-start.5 = (f32[17,8,128]{2,1,0:T(8,128)S(1)}, f32[17,8,128]{2,1,0:T(8,128)S(1)}, u32[]{:S(2)}, u32[]{:S(2)}) collective-permute-start(f32[17,8,128]{2,1,0:T(8,128)S(1)} %get-tuple-element.50), channel_id=1, source_target_pairs={{0,1},{1,0},{2,4},{3,5},{4,2},{5,3},{6,7},{7,6},{8,9},{9,8},{10,12... | collective-permute-start | bytes 208904 | tf_op jit(solution)/shard_map/ppermute | solution.py:65
  14.1 1.9 %collective-permute-start.6 = (f32[8,2048]{1,0:T(8,128)S(1)}, f32[8,2048]{1,0:T(8,128)S(1)}, u32[]{:S(2)}, u32[]{:S(2)}) collective-permute-start(f32[8,2048]{1,0:T(8,128)S(1)} %get-tuple-element.53), channel_id=1, source_target_pairs={{0,24},{8,16},{16,8},{24,0},{1,25},{9,17},{17,9},{25,1},{2,26},{10... | collective-permute-start | bytes 196616 | tf_op jit(solution)/shard_map/ppermute | solution.py:948
  16.0 1.2 %collective-permute-start.7 = (f32[8,2048]{1,0:T(8,128)S(1)}, f32[8,2048]{1,0:T(8,128)S(1)}, u32[]{:S(2)}, u32[]{:S(2)}) collective-permute-start(f32[8,2048]{1,0:T(8,128)S(1)} %get-tuple-element.54), channel_id=1, source_target_pairs={{0,16},{8,24},{16,0},{24,8},{1,17},{9,25},{17,1},{25,9},{2,18},{10... | collective-permute-start | bytes 196616 | tf_op jit(solution)/shard_map/ppermute | solution.py:948
  17.1 1.4 %collective-permute-start.8 = (f32[8,2048]{1,0:T(8,128)S(1)}, f32[8,2048]{1,0:T(8,128)S(1)}, u32[]{:S(2)}, u32[]{:S(2)}) collective-permute-start(f32[8,2048]{1,0:T(8,128)S(1)} %get-tuple-element.55), channel_id=1, source_target_pairs={{0,8},{8,0},{16,24},{24,16},{1,9},{9,1},{17,25},{25,17},{2,10},{10... | collective-permute-start | bytes 196616 | tf_op jit(solution)/shard_map/ppermute | solution.py:948
  18.5 0.5 %shard_map.115 = (f32[24,6,8,128]{3,2,1,0:T(8,128)S(1)}, f32[16,5,8,128]{3,2,1,0:T(8,128)S(1)}, f32[8,128]{1,0:T(8,128)S(1)}) custom-call(f32[3,24,8,512]{3,2,1,0:T(8,128)S(1)} %get-tuple-element.34.e_ref.refs_0_, f32[3,24,8,512]{3,2,1,0:T(8,128)S(1)} %get-tuple-element.35.h_ref.refs_1_, f32[3,24,8,512]{3,2,1,0:T(8,128)S(1)} %get-tuple-element.37.refs_2_.f_ref.refs_1_, ...), custom_call_target="tpu_custom_call" | custom-call | tf_op jit(solution)/shard_map/pallas_call | solution.py:319
  19.0 0.0 collective-permute-done.4.refs_11_.refs_10_
  19.1 0.0 collective-permute-done.5.refs_12_.refs_11_
  19.1 0.0 copy-start.3
  19.1 0.9 %shard_map.117 = (f32[8,384]{1,0:T(8,128)S(1)}, f32[16,8,128]{2,1,0:T(8,128)S(1)}) custom-call(f32[16,8,512]{2,1,0:T(8,128)S(1)} %get-tuple-element.42.refs_6_.refs_0_.refs_3_, f32[3,24,8,512]{3,2,1,0:T(8,128)S(1)} %get-tuple-element.37.refs_2_.f_ref.refs_1_, f32[24,8,512]{2,1,0:T(8,128)S(1)} %get-tuple-element.36.refs_3_.inv_ref.refs_2_, ...), custom_call_target="tpu_custom_call" | custom-call | tf_op jit(solution)/shard_map/pallas_call | solution.py:681
  20.0 0.6 %collective-permute-done.6.refs_2_ = f32[8,2048]{1,0:T(8,128)S(1)} collective-permute-done((f32[8,2048]{1,0:T(8,128)S(1)}, f32[8,2048]{1,0:T(8,128)S(1)}, u32[]{:S(2)}, u32[]{:S(2)}) %collective-permute-start.6) | collective-permute-done | bytes 65568 | tf_op jit(solution)/shard_map/ppermute | solution.py:948
  20.6 2.8 %collective-permute-done.7.refs_3_ = f32[8,2048]{1,0:T(8,128)S(1)} collective-permute-done((f32[8,2048]{1,0:T(8,128)S(1)}, f32[8,2048]{1,0:T(8,128)S(1)}, u32[]{:S(2)}, u32[]{:S(2)}) %collective-permute-start.7) | collective-permute-done | bytes 65568 | tf_op jit(solution)/shard_map/ppermute | solution.py:948
  23.4 0.0 collective-permute-done.8.refs_4_
  23.4 0.0 copy-done.3
  23.5 0.8 %shard_map.118 = (f32[8,2432]{1,0:T(8,128)S(1)}, f32[8,2432]{1,0:T(8,128)S(1)}, f32[8,2432]{1,0:T(8,128)S(1)}, f32[8,2432]{1,0:T(8,128)S(1)}) custom-call(bf16[112,48]{1,0:T(8,128)(2,1)S(1)} %copy-done.3, f32[8,384]{1,0:T(8,128)S(1)} %get-tuple-element.52.refs_1_.refs_5_, f32[8,2048]{1,0:T(8,128)S(1)} %collective-permute-done.6.refs_2_, ...), custom_call_target="tpu_custom_call" | custom-call | tf_op jit(solution)/shard_map/pallas_call | solution.py:830
  24.3 2.4 %collective-permute-start.9 = (f32[8,2432]{1,0:T(8,128)S(1)}, f32[8,2432]{1,0:T(8,128)S(1)}, u32[]{:S(2)}, u32[]{:S(2)}) collective-permute-start(f32[8,2432]{1,0:T(8,128)S(1)} %get-tuple-element.61), channel_id=1, source_target_pairs={{0,24},{8,16},{16,8},{24,0},{1,25},{9,17},{17,9},{25,1},{2,26},{10... | collective-permute-start | bytes 233480 | tf_op jit(solution)/shard_map/ppermute | solution.py:948
  26.7 0.0 collective-permute-start.10
  26.7 2.0 %collective-permute-start.11 = (f32[8,2432]{1,0:T(8,128)S(1)}, f32[8,2432]{1,0:T(8,128)S(1)}, u32[]{:S(2)}, u32[]{:S(2)}) collective-permute-start(f32[8,2432]{1,0:T(8,128)S(1)} %get-tuple-element.63), channel_id=1, source_target_pairs={{0,8},{8,0},{16,24},{24,16},{1,9},{9,1},{17,25},{25,17},{2,10},{10... | collective-permute-start | bytes 233480 | tf_op jit(solution)/shard_map/ppermute | solution.py:948
  28.7 3.2 %shard_map.119 = (f32[3,24,8,512]{3,2,1,0:T(8,128)}, f32[3,24,8,512]{3,2,1,0:T(8,128)}, f32[16,8,512]{2,1,0:T(8,128)}) custom-call(f32[3,24,8,512]{3,2,1,0:T(8,128)S(1)} %get-tuple-element.34.e_ref.refs_0_, f32[3,24,8,512]{3,2,1,0:T(8,128)S(1)} %get-tuple-element.35.h_ref.refs_1_, f32[24,8,512]{2,1,0:T(8,128)S(1)} %get-tuple-element.36.refs_3_.inv_ref.refs_2_, ...), custom_call_target="tpu_custom_call" | custom-call | tf_op jit(solution)/shard_map/pallas_call | solution.py:747
  32.0 0.0 collective-permute-done.9.refs_1_
  32.0 1.9 %collective-permute-done.10.refs_2_ = f32[8,2432]{1,0:T(8,128)S(1)} collective-permute-done((f32[8,2432]{1,0:T(8,128)S(1)}, f32[8,2432]{1,0:T(8,128)S(1)}, u32[]{:S(2)}, u32[]{:S(2)}) %collective-permute-start.10) | collective-permute-done | bytes 77856 | tf_op jit(solution)/shard_map/ppermute | solution.py:948
  33.8 0.0 collective-permute-done.11.refs_3_
  33.8 1.3 %shard_map.120 = f32[16,8,512]{2,1,0:T(8,128)} custom-call(bf16[112,48]{1,0:T(8,128)(2,1)S(1)} %copy-done.3, f32[8,2432]{1,0:T(8,128)S(1)} %collective-permute-done.9.refs_1_, f32[8,2432]{1,0:T(8,128)S(1)} %collective-permute-done.10.refs_2_, f32[8,2432]{1,0:T(8,128)S(1)} %collective-permute-done.11.refs_3_, f32[8,2432]{1,0:T(8,128)S(1)} %get-tuple-element.57.refs_12_.refs_4_), custom_call_target="tpu_custom_call" | custom-call | tf_op jit(solution)/shard_map/pallas_call | solution.py:924
Async XLA Ops:
  2.3 5.0 %copy-start = (f32[16,8,512]{2,1,0:T(8,128)S(1)}, f32[16,8,512]{2,1,0:T(8,128)}, u32[]{:S(2)}) copy-start(f32[16,8,512]{2,1,0:T(8,128)} %grad_ref.3) | copy-start | bytes 786436
  2.3 5.0 %copy-start.1 = (f32[3,24,8,512]{3,2,1,0:T(8,128)S(1)}, f32[3,24,8,512]{3,2,1,0:T(8,128)}, u32[]{:S(2)}) copy-start(f32[3,24,8,512]{3,2,1,0:T(8,128)} %f_in.1) | copy-start | bytes 3538948
  2.3 5.0 %copy-start.2 = (s32[24,8,512]{2,1,0:T(8,128)S(1)}, s32[24,8,512]{2,1,0:T(8,128)}, u32[]{:S(2)}) copy-start(s32[24,8,512]{2,1,0:T(8,128)} %mat_ref.1) | copy-start | bytes 1179652
  2.3 5.0 %copy-start.4 = (f32[4]{0:T(128)S(1)}, f32[4]{0:T(128)}, u32[]{:S(2)}) copy-start(f32[4]{0:T(128)} %param.12) | copy-start | bytes 52
  2.3 5.0 %copy-start.5 = (s32[1,64]{1,0:T(1,128)S(1)}, s32[1,64]{1,0:T(1,128)}, u32[]{:S(2)}) copy-start(s32[1,64]{1,0:T(1,128)} %mask_ref.1) | copy-start | bytes 772
  2.5 7.2 %collective-permute-start.1 = (f32[72,512]{1,0:T(8,128)S(1)}, f32[72,512]{1,0:T(8,128)S(1)}, u32[]{:S(2)}, u32[]{:S(2)}) collective-permute-start(f32[72,512]{1,0:T(8,128)S(1)} %get-tuple-element.40), channel_id=1, source_target_pairs={{0,8},{2,10},{4,12},{6,14},{8,0},{10,2},{12,4},{14,6},{16,24},{18,... | collective-permute-start | bytes 442376 | tf_op jit(solution)/shard_map/ppermute | solution.py:65
  5.6 4.2 %collective-permute-start.2 = (f32[72,512]{1,0:T(8,128)S(1)}, f32[72,512]{1,0:T(8,128)S(1)}, u32[]{:S(2)}, u32[]{:S(2)}) collective-permute-start(f32[72,512]{1,0:T(8,128)S(1)} %get-tuple-element.41), channel_id=1, source_target_pairs={{0,2},{2,0},{4,6},{6,4},{8,16},{10,18},{12,20},{14,22},{16,8},{18,... | collective-permute-start | bytes 442376 | tf_op jit(solution)/shard_map/ppermute | solution.py:65
  5.6 4.2 %collective-permute-start = (f32[3,8,512]{2,1,0:T(8,128)S(1)}, f32[3,8,512]{2,1,0:T(8,128)S(1)}, u32[]{:S(2)}, u32[]{:S(2)}) collective-permute-start(f32[3,8,512]{2,1,0:T(8,128)S(1)} %get-tuple-element.39), channel_id=1, source_target_pairs={{0,1},{2,3},{4,5},{6,7},{1,0},{3,2},{5,4},{7,6},{8,9},{10,11},{12,... | collective-permute-start | bytes 147464 | tf_op jit(solution)/shard_map/ppermute | solution.py:65
  7.1 3.4 %collective-permute-start.3 = (f32[8,512]{1,0:T(8,128)S(1)}, f32[8,512]{1,0:T(8,128)S(1)}, u32[]{:S(2)}, u32[]{:S(2)}) collective-permute-start(f32[8,512]{1,0:T(8,128)S(1)} %get-tuple-element.46), channel_id=1, source_target_pairs={{0,2},{2,0},{4,6},{6,4},{1,8},{3,10},{5,12},{7,14},{8,1},{10,3},{1... | collective-permute-start | bytes 49160 | tf_op jit(solution)/shard_map/ppermute | solution.py:91
  10.7 8.4 %collective-permute-start.4 = (f32[17,8,128]{2,1,0:T(8,128)S(1)}, f32[17,8,128]{2,1,0:T(8,128)S(1)}, u32[]{:S(2)}, u32[]{:S(2)}) collective-permute-start(f32[17,8,128]{2,1,0:T(8,128)S(1)} %get-tuple-element.49), channel_id=1, source_target_pairs={{0,2},{1,3},{2,0},{3,1},{4,6},{5,7},{6,4},{7,5},{8,10},{9,11},{10,... | collective-permute-start | bytes 208904 | tf_op jit(solution)/shard_map/ppermute | solution.py:65
  10.8 8.3 %collective-permute-start.5 = (f32[17,8,128]{2,1,0:T(8,128)S(1)}, f32[17,8,128]{2,1,0:T(8,128)S(1)}, u32[]{:S(2)}, u32[]{:S(2)}) collective-permute-start(f32[17,8,128]{2,1,0:T(8,128)S(1)} %get-tuple-element.50), channel_id=1, source_target_pairs={{0,1},{1,0},{2,4},{3,5},{4,2},{5,3},{6,7},{7,6},{8,9},{9,8},{10,12... | collective-permute-start | bytes 208904 | tf_op jit(solution)/shard_map/ppermute | solution.py:65
  14.1 6.5 %collective-permute-start.6 = (f32[8,2048]{1,0:T(8,128)S(1)}, f32[8,2048]{1,0:T(8,128)S(1)}, u32[]{:S(2)}, u32[]{:S(2)}) collective-permute-start(f32[8,2048]{1,0:T(8,128)S(1)} %get-tuple-element.53), channel_id=1, source_target_pairs={{0,24},{8,16},{16,8},{24,0},{1,25},{9,17},{17,9},{25,1},{2,26},{10... | collective-permute-start | bytes 196616 | tf_op jit(solution)/shard_map/ppermute | solution.py:948
  16.0 7.5 %collective-permute-start.7 = (f32[8,2048]{1,0:T(8,128)S(1)}, f32[8,2048]{1,0:T(8,128)S(1)}, u32[]{:S(2)}, u32[]{:S(2)}) collective-permute-start(f32[8,2048]{1,0:T(8,128)S(1)} %get-tuple-element.54), channel_id=1, source_target_pairs={{0,16},{8,24},{16,0},{24,8},{1,17},{9,25},{17,1},{25,9},{2,18},{10... | collective-permute-start | bytes 196616 | tf_op jit(solution)/shard_map/ppermute | solution.py:948
  17.1 6.3 %collective-permute-start.8 = (f32[8,2048]{1,0:T(8,128)S(1)}, f32[8,2048]{1,0:T(8,128)S(1)}, u32[]{:S(2)}, u32[]{:S(2)}) collective-permute-start(f32[8,2048]{1,0:T(8,128)S(1)} %get-tuple-element.55), channel_id=1, source_target_pairs={{0,8},{8,0},{16,24},{24,16},{1,9},{9,1},{17,25},{25,17},{2,10},{10... | collective-permute-start | bytes 196616 | tf_op jit(solution)/shard_map/ppermute | solution.py:948
  19.1 4.4 %copy-start.3 = (bf16[112,48]{1,0:T(8,128)(2,1)S(1)}, bf16[112,48]{1,0:T(8,128)(2,1)}, u32[]{:S(2)}) copy-start(bf16[112,48]{1,0:T(8,128)(2,1)} %constant.2.clone.refs_0_) | copy-start | bytes 32260
  24.3 7.7 %collective-permute-start.9 = (f32[8,2432]{1,0:T(8,128)S(1)}, f32[8,2432]{1,0:T(8,128)S(1)}, u32[]{:S(2)}, u32[]{:S(2)}) collective-permute-start(f32[8,2432]{1,0:T(8,128)S(1)} %get-tuple-element.61), channel_id=1, source_target_pairs={{0,24},{8,16},{16,8},{24,0},{1,25},{9,17},{17,9},{25,1},{2,26},{10... | collective-permute-start | bytes 233480 | tf_op jit(solution)/shard_map/ppermute | solution.py:948
  26.7 7.2 %collective-permute-start.10 = (f32[8,2432]{1,0:T(8,128)S(1)}, f32[8,2432]{1,0:T(8,128)S(1)}, u32[]{:S(2)}, u32[]{:S(2)}) collective-permute-start(f32[8,2432]{1,0:T(8,128)S(1)} %get-tuple-element.62), channel_id=1, source_target_pairs={{0,16},{8,24},{16,0},{24,8},{1,17},{9,25},{17,1},{25,9},{2,18},{10... | collective-permute-start | bytes 233480 | tf_op jit(solution)/shard_map/ppermute | solution.py:948
  26.7 7.2 %collective-permute-start.11 = (f32[8,2432]{1,0:T(8,128)S(1)}, f32[8,2432]{1,0:T(8,128)S(1)}, u32[]{:S(2)}, u32[]{:S(2)}) collective-permute-start(f32[8,2432]{1,0:T(8,128)S(1)} %get-tuple-element.63), channel_id=1, source_target_pairs={{0,8},{8,0},{16,24},{24,16},{1,9},{9,1},{17,25},{25,17},{2,10},{10... | collective-permute-start | bytes 233480 | tf_op jit(solution)/shard_map/ppermute | solution.py:948

commit v9 on v8

--- a/solution.py
+++ b/solution.py
@@ -138,17 +138,25 @@
             rows_ref[3 + c, z : z + 1, :] = h_ref[1 + c, z, last : last + 1, :]
         if z > 0:
             rows_ref[5, z - 1 : z, :] = e_ref[0, z, last : last + 1, :]
-    ex = rows_ref[0]
+    width = e_ref.shape[3]
+    ex, ey, ez = (rows_ref[c] for c in range(3))
+    column = lax.broadcasted_iota(jnp.int32, ex.shape, 1)
+    ex_next = jnp.where(column == width - 1, 0.0, pltpu.roll(ex, width - 1, 1))
+    lane = lax.broadcasted_iota(jnp.int32, (ROWS, LANES), 1)
+    strip = jnp.zeros((ROWS, LANES), jnp.float32)
+    for j in range(cells_z // ROWS):
+        head = rows_ref[0, j * ROWS : (j + 1) * ROWS, 0:LANES]
+        strip = jnp.where(lane // STRIP == j, pltpu.roll(head, STRIP * j, 1) if j else head, strip)
     high = (
-        rows_ref[3] - HALF * (rows_ref[5] - ex + rows_ref[2]),
-        rows_ref[4] + HALF * rows_ref[1] - HALF * ex,
-        ex,
+        rows_ref[3] - HALF * (rows_ref[5] - ex + ez),
+        rows_ref[4] + HALF * ey - HALF * (ex - ex_next),
+        jnp.concatenate([strip, jnp.zeros((ROWS, width - LANES), jnp.float32)], axis=1),
     )
     side = Side("gx")
-    for c in range(3):
-        here = slice(c * cells_z, (c + 1) * cells_z)
-        for ref, value in zip(x_sends, side.sends(low_ref[here, :], high[c])):
-            ref[here, :] = value
+    for c, value in enumerate(high):
+        here = slice(c * cells_z, c * cells_z + value.shape[0])
+        for ref, one in zip(x_sends, side.sends(low_ref[here, :], value)):
+            ref[here, :] = one
 
     side = Side("gz")
     ex, ey, ez = (e_ref[c, top] for c in range(3))
@@ -169,7 +177,7 @@
 def halos(efield, hfield):
     _, cells_z, cells_x, cells_y = efield.shape
     x_rounds, z_rounds = rounds("gx"), rounds("gz")
-    x_face, z_face, line = fast(3 * cells_z, cells_y), fast(3, cells_x, cells_y), fast(ROWS, cells_y)
+    x_face, z_face, line = fast(2 * cells_z + ROWS, cells_y), fast(3, cells_x, cells_y), fast(ROWS, cells_y)
     sends = pl.pallas_call(
         functools.partial(faces_kernel, x_rounds),
         in_specs=[VMEM] * 2,
@@ -335,7 +343,7 @@
 def face_tiles(zfaces, xfaces, lines):
     width = xfaces[0].shape[1]
     rows = xfaces[0].shape[0]
-    cells_z = rows // 3
+    cells_z = (rows - ROWS) // 2
     z_side, x_side = Side("gz"), Side("gx")
 
     def corner(s):
@@ -345,14 +353,25 @@
     def x_tile(pick, t, s):
         value = pick([f[t : t + ROWS, s] for f in xfaces])
         return value + corner(s) if lines and t == cells_z - ROWS and pick == x_side.lower else value
+
+    def strip(j, s):
+        zeros = jnp.zeros((ROWS, s.stop - s.start), jnp.float32)
+        if s.start:
+            return zeros
+        lane = lax.broadcasted_iota(jnp.int32, (ROWS, LANES), 1)
+        packed = x_side.lower([f[2 * cells_z :, 0:LANES] for f in xfaces])
+        head = jnp.where(lane < STRIP, pltpu.roll(packed, LANES - STRIP * j, 1) if j else packed, 0.0)
+        return head if s.stop == LANES else jnp.concatenate([head, zeros[:, LANES:]], axis=1)
 
     tiles = []
     for c in range(3):
         tiles.append((lambda s, c=c: z_side.lower([f[c, :, s] for f in zfaces]), width))
     for c in range(2):
         tiles.append((lambda s, c=c: z_side.upper([f[c, :, s] for f in zfaces]), width))
-    for t in range(0, rows, ROWS):
+    for t in range(0, 2 * cells_z, ROWS):
         tiles.append((lambda s, t=t: x_tile(x_side.lower, t, s), width))
+    for j in range(cells_z // ROWS):
+        tiles.append((lambda s, j=j: strip(j, s), width))
     for t in range(0, rows, ROWS):
         if lines and t == 2 * cells_z:
             tiles.append((lambda s: corner_lines(lines, s)[1], width))
@@ -362,7 +381,8 @@
 
 
 def face_count(xface):
-    return 5 + 2 * (xface.shape[0] // ROWS)
+    per_field = (xface.shape[0] - ROWS) // ROWS // 2
+    return 5 + 3 * per_field + 2 * per_field + 1
 
 
 def y_faces_kernel(counts, *refs):
@@ -438,12 +458,19 @@
 
         full = [face(load, slot) for slot, (load, _) in enumerate(face_tiles(zfaces, xfaces, lines))]
         self.below, self.above = full[:3], full[3:5]
-        per_face = xfaces[0].shape[0] // ROWS
-        for t in range(per_face):
+        groups = self.groups
+        for t in range(2 * groups):
             left_wide[t * ROWS : (t + 1) * ROWS, :] = full[5 + t]
-            right_wide[t * ROWS : (t + 1) * ROWS, :] = full[5 + per_face + t]
-        cells_z = self.cells_z
-        left_wide[cells_z : 2 * cells_z, :] += HALF * self.y_up(left_wide[2 * cells_z : 3 * cells_z, :])
+        for t in range(2 * groups + 1):
+            right_wide[t * ROWS : (t + 1) * ROWS, :] = full[5 + 3 * groups + t]
+        if mode != OWN:
+            column = lax.broadcasted_iota(jnp.int32, (ROWS, self.wide), 1)
+            ends = {CIRCLE: (self.width - 1, self.wide - 1), EDGE: (STRIP - 1, LANES - STRIP - 1)}[mode]
+            here = jnp.logical_or(column == ends[0], column == ends[1])
+            for j in range(groups):
+                ex_next = self.y_up(full[5 + 2 * groups + j])
+                at = (groups + j) * ROWS
+                left_wide[at : at + ROWS, :] += jnp.where(here, HALF * ex_next, 0.0)
 
     def wider(self, load, tile, k):
         if self.mode == OWN:
@@ -599,6 +626,11 @@
         chunk = lax.bitwise_xor(me, k)
         for i in range(per_device):
             share[:, i * width : (i + 1) * width] = own_ref[chunk * per_device + i]
+        if share.shape[1] > per_device * width:
+            share[:, per_device * width :] = jnp.zeros((ROWS, SPARE), jnp.float32)
+
+
+SPARE = 2 * LANES
 
 
 def own_gradient(arrays, zfaces, xfaces):
@@ -609,7 +641,9 @@
         functools.partial(own_gradient_kernel, (len(zfaces), len(xfaces)), per_device),
         in_specs=[VMEM] * (6 + len(zfaces) + len(xfaces)),
         out_specs=[VMEM] * (count + 1),
-        out_shape=[fast(ROWS, per_device * width)] * count + [fast(layers, ROWS, width)],
+        out_shape=[fast(ROWS, per_device * width + SPARE)]
+        + [fast(ROWS, per_device * width)] * (count - 1)
+        + [fast(layers, ROWS, width)],
         scratch_shapes=fields_scratch(OWN, xfaces[0], None, width),
         compiler_params=params(),
     )(*arrays, *zfaces, *xfaces)
@@ -807,7 +841,7 @@
     half = count // 2
     rows = half * ROWS
     for k in range(count):
-        slabs[lax.bitwise_xor(me, k)] = got[k][...]
+        slabs[lax.bitwise_xor(me, k)] = got[k][:, : per_device * width]
 
     side = jnp.zeros((rows, LANES), jnp.float32)
     for i in range(per_device):

time: 35.3 us -> 33 us (0.935)
  waiting for transfers between devices: 6.44 us -> 4 us
    ppermute x6, waiting for transfers between devices: 5.3 us -> 2.86 us  [spread(): got[k] = lax.ppermute(parts[k], 'gx', [(i, i ^ k) for i in range(count)])]
    ppermute x6, starting transfers between devices: 8.84 us -> 10.5 us  [spread(): got[k] = lax.ppermute(parts[k], 'gx', [(i, i ^ k) for i in range(count)])]
    ppermute x5, starting transfers between devices: 8.03 us -> 6.36 us  [exchange(): got.append(lax.ppermute(value, tuple(axes), pairs))]
  transfers between devices with their start and end apart: 12 -> 12, of which waited for: 4 -> 3; matrix products, arithmetic and copies ran while one was open for 0% -> 0% of each run, Pallas kernels for 19% -> 21%
where the time goes in v9:
time: 33 us; the launch traced here: 32.8 us
  starting transfers between devices  17.1 us (52%)
  Pallas kernels  10.9 us (33%)
  waiting for transfers between devices  4 us (12%)
  between operations  0.8 us (2%)
    ppermute x6, starting transfers between devices, spread(): got[k] = lax.ppermute(parts[k], 'gx', [(i, i ^ k) for i in range(count)])  10.5 us
    ppermute x5, starting transfers between devices, exchange(): got.append(lax.ppermute(value, tuple(axes), pairs))  6.36 us
    pallas_call x1, Pallas kernels, step(): pl.pallas_call(functools.partial(step_kernel, counts), in_specs=[VMEM] *...  3.24 us
    ppermute x6, waiting for transfers between devices, spread(): got[k] = lax.ppermute(parts[k], 'gx', [(i, i ^ k) for i in range(count)])  2.86 us
    pallas_call x1, Pallas kernels, load(): pl.pallas_call(load_kernel, in_specs=[ANY] * 2, out_specs=[VMEM] * 2, out...  1.64 us
    pallas_call x1, Pallas kernels, finish(): pl.pallas_call(functools.partial(finish_kernel, count, per_device, width)...  1.34 us
    pallas_call x1, Pallas kernels, strips(): pl.pallas_call(strips_kernel, in_specs=[VMEM] * 3 + [ANY] + [VMEM] * 3, o...  1.24 us
    ppermute x5, waiting for transfers between devices, exchange(): got.append(lax.ppermute(value, tuple(axes), pairs))  1.14 us
  transfers between devices with their start and end apart: 12, of which 3 were waited for; matrix products, arithmetic and copies ran while one was open for 0% of the time, Pallas kernels for 21%

profile of v9, /device:TPU:0, one launch (start us, length us, event | category | flops | bytes accessed | tf_op | source)
XLA Modules:
  0.0 32.8 jit_solution(17221253176041525803)
XLA Ops:
  0.6 1.6 %shard_map.111 = (f32[3,24,8,512]{3,2,1,0:T(8,128)S(1)}, f32[3,24,8,512]{3,2,1,0:T(8,128)S(1)}) custom-call(f32[3,24,8,512]{3,2,1,0:T(8,128)} %e_in.1, f32[3,24,8,512]{3,2,1,0:T(8,128)} %h_in.1), custom_call_target="tpu_custom_call" | custom-call | tf_op jit(solution)/shard_map/pallas_call | solution.py:231
  2.3 0.0 copy-start
  2.3 0.0 copy-start.1
  2.3 0.0 copy-start.2
  2.3 0.0 copy-start.4
  2.3 0.0 copy-start.5
  2.3 0.2 shard_map.113
  2.5 3.1 %collective-permute-start.1 = (f32[56,512]{1,0:T(8,128)S(1)}, f32[56,512]{1,0:T(8,128)S(1)}, u32[]{:S(2)}, u32[]{:S(2)}) collective-permute-start(f32[56,512]{1,0:T(8,128)S(1)} %get-tuple-element.40), channel_id=1, source_target_pairs={{0,8},{2,10},{4,12},{6,14},{8,0},{10,2},{12,4},{14,6},{16,24},{18,... | collective-permute-start | bytes 344072 | tf_op jit(solution)/shard_map/ppermute | solution.py:65
  5.6 0.0 collective-permute-start.2
  5.6 1.5 %collective-permute-start = (f32[3,8,512]{2,1,0:T(8,128)S(1)}, f32[3,8,512]{2,1,0:T(8,128)S(1)}, u32[]{:S(2)}, u32[]{:S(2)}) collective-permute-start(f32[3,8,512]{2,1,0:T(8,128)S(1)} %get-tuple-element.39), channel_id=1, source_target_pairs={{0,1},{2,3},{4,5},{6,7},{1,0},{3,2},{5,4},{7,6},{8,9},{10,11},{12,... | collective-permute-start | bytes 147464 | tf_op jit(solution)/shard_map/ppermute | solution.py:65
  7.1 0.2 collective-permute-start.3
  7.4 0.0 copy-done
  7.4 0.0 copy-done.1
  7.4 0.0 copy-done.2
  7.4 0.0 copy-done.4
  7.4 0.0 copy-done.5
  7.4 1.2 %shard_map.112 = (f32[3,24,8,512]{3,2,1,0:T(8,128)S(1)}, f32[15,8,128]{2,1,0:T(8,128)S(1)}, f32[15,8,128]{2,1,0:T(8,128)S(1)}, f32[8,512]{1,0:T(8,128)S(1)}, f32[24,8,512]{2,1,0:T(8,128)S(1)}) custom-call(f32[1,4]{1,0:T(1,128)S(1)} %bitcast.1, f32[3,24,8,512]{3,2,1,0:T(8,128)S(1)} %get-tuple-element.34.e_ref.refs_0_, ...), custom_call_target="tpu_custom_call" | custom-call | tf_op jit(solution)/shard_map/pallas_call | solution.py:292
  8.6 1.1 %collective-permute-done.refs_6_.refs_2_.refs_7_ = f32[3,8,512]{2,1,0:T(8,128)S(1)} collective-permute-done((f32[3,8,512]{2,1,0:T(8,128)S(1)}, f32[3,8,512]{2,1,0:T(8,128)S(1)}, u32[]{:S(2)}, u32[]{:S(2)}) %collective-permute-start) | collective-permute-done | bytes 49184 | tf_op jit(solution)/shard_map/ppermute | solution.py:65
  9.8 0.0 collective-permute-done.1.refs_7_.refs_3_.refs_8_
  9.8 0.0 collective-permute-done.2.refs_8_.refs_4_.refs_9_
  9.8 0.8 %shard_map.114 = (f32[8,2304]{1,0:T(8,128)S(1)}, f32[8,2048]{1,0:T(8,128)S(1)}, f32[8,2048]{1,0:T(8,128)S(1)}, f32[8,2048]{1,0:T(8,128)S(1)}, f32[16,8,512]{2,1,0:T(8,128)S(1)}) custom-call(f32[3,24,8,512]{3,2,1,0:T(8,128)S(1)} %get-tuple-element.34.e_ref.refs_0_, f32[3,24,8,512]{3,2,1,0:T(8,128)S(1)} %get-tuple-element.35.h_ref.refs_1_, ...), custom_call_target="tpu_custom_call" | custom-call | tf_op jit(solution)/shard_map/pallas_call | solution.py:640
  10.6 2.8 %collective-permute-start.6 = (f32[8,2304]{1,0:T(8,128)S(1)}, f32[8,2304]{1,0:T(8,128)S(1)}, u32[]{:S(2)}, u32[]{:S(2)}) collective-permute-start(f32[8,2304]{1,0:T(8,128)S(1)} %get-tuple-element.53), channel_id=1, source_target_pairs={{0,24},{8,16},{16,8},{24,0},{1,25},{9,17},{17,9},{25,1},{2,26},{10... | collective-permute-start | bytes 221192 | tf_op jit(solution)/shard_map/ppermute | solution.py:982
  13.4 0.0 collective-permute-done.3.refs_5_.refs_10_.refs_9_
  13.4 0.2 shard_map.116
  13.5 0.0 collective-permute-start.4
  13.6 1.7 %collective-permute-start.5 = (f32[17,8,128]{2,1,0:T(8,128)S(1)}, f32[17,8,128]{2,1,0:T(8,128)S(1)}, u32[]{:S(2)}, u32[]{:S(2)}) collective-permute-start(f32[17,8,128]{2,1,0:T(8,128)S(1)} %get-tuple-element.50), channel_id=1, source_target_pairs={{0,1},{1,0},{2,4},{3,5},{4,2},{5,3},{6,7},{7,6},{8,9},{9,8},{10,12... | collective-permute-start | bytes 208904 | tf_op jit(solution)/shard_map/ppermute | solution.py:65
  15.3 1.7 %collective-permute-start.7 = (f32[8,2048]{1,0:T(8,128)S(1)}, f32[8,2048]{1,0:T(8,128)S(1)}, u32[]{:S(2)}, u32[]{:S(2)}) collective-permute-start(f32[8,2048]{1,0:T(8,128)S(1)} %get-tuple-element.54), channel_id=1, source_target_pairs={{0,16},{8,24},{16,0},{24,8},{1,17},{9,25},{17,1},{25,9},{2,18},{10... | collective-permute-start | bytes 196616 | tf_op jit(solution)/shard_map/ppermute | solution.py:982
  17.0 1.6 %collective-permute-start.8 = (f32[8,2048]{1,0:T(8,128)S(1)}, f32[8,2048]{1,0:T(8,128)S(1)}, u32[]{:S(2)}, u32[]{:S(2)}) collective-permute-start(f32[8,2048]{1,0:T(8,128)S(1)} %get-tuple-element.55), channel_id=1, source_target_pairs={{0,8},{8,0},{16,24},{24,16},{1,9},{9,1},{17,25},{25,17},{2,10},{10... | collective-permute-start | bytes 196616 | tf_op jit(solution)/shard_map/ppermute | solution.py:982
  18.6 0.5 %shard_map.115 = (f32[24,6,8,128]{3,2,1,0:T(8,128)S(1)}, f32[16,5,8,128]{3,2,1,0:T(8,128)S(1)}, f32[8,128]{1,0:T(8,128)S(1)}) custom-call(f32[3,24,8,512]{3,2,1,0:T(8,128)S(1)} %get-tuple-element.34.e_ref.refs_0_, f32[3,24,8,512]{3,2,1,0:T(8,128)S(1)} %get-tuple-element.35.h_ref.refs_1_, f32[3,24,8,512]{3,2,1,0:T(8,128)S(1)} %get-tuple-element.37.refs_2_.f_ref.refs_1_, ...), custom_call_target="tpu_custom_call" | custom-call | tf_op jit(solution)/shard_map/pallas_call | solution.py:327
  19.1 0.0 collective-permute-done.4.refs_11_.refs_10_
  19.1 0.0 collective-permute-done.5.refs_12_.refs_11_
  19.1 0.0 copy-start.3
  19.1 0.9 %shard_map.117 = (f32[8,384]{1,0:T(8,128)S(1)}, f32[16,8,128]{2,1,0:T(8,128)S(1)}) custom-call(f32[16,8,512]{2,1,0:T(8,128)S(1)} %get-tuple-element.42.refs_6_.refs_0_.refs_3_, f32[3,24,8,512]{3,2,1,0:T(8,128)S(1)} %get-tuple-element.37.refs_2_.f_ref.refs_1_, f32[24,8,512]{2,1,0:T(8,128)S(1)} %get-tuple-element.36.refs_3_.inv_ref.refs_2_, ...), custom_call_target="tpu_custom_call" | custom-call | tf_op jit(solution)/shard_map/pallas_call | solution.py:715
  20.1 1.8 %collective-permute-done.7.refs_3_ = f32[8,2048]{1,0:T(8,128)S(1)} collective-permute-done((f32[8,2048]{1,0:T(8,128)S(1)}, f32[8,2048]{1,0:T(8,128)S(1)}, u32[]{:S(2)}, u32[]{:S(2)}) %collective-permute-start.7) | collective-permute-done | bytes 65568 | tf_op jit(solution)/shard_map/ppermute | solution.py:982
  21.9 0.0 collective-permute-done.8.refs_4_
  21.9 0.0 collective-permute-done.6.refs_2_
  21.9 0.0 copy-done.3
  21.9 0.8 %shard_map.118 = (f32[8,2432]{1,0:T(8,128)S(1)}, f32[8,2432]{1,0:T(8,128)S(1)}, f32[8,2432]{1,0:T(8,128)S(1)}, f32[8,2432]{1,0:T(8,128)S(1)}) custom-call(bf16[112,48]{1,0:T(8,128)(2,1)S(1)} %copy-done.3, f32[8,384]{1,0:T(8,128)S(1)} %get-tuple-element.52.refs_1_.refs_5_, f32[8,2304]{1,0:T(8,128)S(1)} %collective-permute-done.6.refs_2_, ...), custom_call_target="tpu_custom_call" | custom-call | tf_op jit(solution)/shard_map/pallas_call | solution.py:864
  22.7 2.0 %collective-permute-start.9 = (f32[8,2432]{1,0:T(8,128)S(1)}, f32[8,2432]{1,0:T(8,128)S(1)}, u32[]{:S(2)}, u32[]{:S(2)}) collective-permute-start(f32[8,2432]{1,0:T(8,128)S(1)} %get-tuple-element.61), channel_id=1, source_target_pairs={{0,24},{8,16},{16,8},{24,0},{1,25},{9,17},{17,9},{25,1},{2,26},{10... | collective-permute-start | bytes 233480 | tf_op jit(solution)/shard_map/ppermute | solution.py:982
  24.7 0.5 %collective-permute-start.10 = (f32[8,2432]{1,0:T(8,128)S(1)}, f32[8,2432]{1,0:T(8,128)S(1)}, u32[]{:S(2)}, u32[]{:S(2)}) collective-permute-start(f32[8,2432]{1,0:T(8,128)S(1)} %get-tuple-element.62), channel_id=1, source_target_pairs={{0,16},{8,24},{16,0},{24,8},{1,17},{9,25},{17,1},{25,9},{2,18},{10... | collective-permute-start | bytes 233480 | tf_op jit(solution)/shard_map/ppermute | solution.py:982
  25.2 2.0 %collective-permute-start.11 = (f32[8,2432]{1,0:T(8,128)S(1)}, f32[8,2432]{1,0:T(8,128)S(1)}, u32[]{:S(2)}, u32[]{:S(2)}) collective-permute-start(f32[8,2432]{1,0:T(8,128)S(1)} %get-tuple-element.63), channel_id=1, source_target_pairs={{0,8},{8,0},{16,24},{24,16},{1,9},{9,1},{17,25},{25,17},{2,10},{10... | collective-permute-start | bytes 233480 | tf_op jit(solution)/shard_map/ppermute | solution.py:982
  27.1 3.2 %shard_map.119 = (f32[3,24,8,512]{3,2,1,0:T(8,128)}, f32[3,24,8,512]{3,2,1,0:T(8,128)}, f32[16,8,512]{2,1,0:T(8,128)}) custom-call(f32[3,24,8,512]{3,2,1,0:T(8,128)S(1)} %get-tuple-element.34.e_ref.refs_0_, f32[3,24,8,512]{3,2,1,0:T(8,128)S(1)} %get-tuple-element.35.h_ref.refs_1_, f32[24,8,512]{2,1,0:T(8,128)S(1)} %get-tuple-element.36.refs_3_.inv_ref.refs_2_, ...), custom_call_target="tpu_custom_call" | custom-call | tf_op jit(solution)/shard_map/pallas_call | solution.py:781
  30.4 0.0 collective-permute-done.9.refs_1_
  30.4 1.1 %collective-permute-done.10.refs_2_ = f32[8,2432]{1,0:T(8,128)S(1)} collective-permute-done((f32[8,2432]{1,0:T(8,128)S(1)}, f32[8,2432]{1,0:T(8,128)S(1)}, u32[]{:S(2)}, u32[]{:S(2)}) %collective-permute-start.10) | collective-permute-done | bytes 77856 | tf_op jit(solution)/shard_map/ppermute | solution.py:982
  31.5 0.0 collective-permute-done.11.refs_3_
  31.5 1.3 %shard_map.120 = f32[16,8,512]{2,1,0:T(8,128)} custom-call(bf16[112,48]{1,0:T(8,128)(2,1)S(1)} %copy-done.3, f32[8,2432]{1,0:T(8,128)S(1)} %collective-permute-done.9.refs_1_, f32[8,2432]{1,0:T(8,128)S(1)} %collective-permute-done.10.refs_2_, f32[8,2432]{1,0:T(8,128)S(1)} %collective-permute-done.11.refs_3_, f32[8,2432]{1,0:T(8,128)S(1)} %get-tuple-element.57.refs_12_.refs_4_), custom_call_target="tpu_custom_call" | custom-call | tf_op jit(solution)/shard_map/pallas_call | solution.py:958
Async XLA Ops:
  2.3 5.1 %copy-start = (f32[16,8,512]{2,1,0:T(8,128)S(1)}, f32[16,8,512]{2,1,0:T(8,128)}, u32[]{:S(2)}) copy-start(f32[16,8,512]{2,1,0:T(8,128)} %grad_ref.3) | copy-start | bytes 786436
  2.3 5.1 %copy-start.1 = (f32[3,24,8,512]{3,2,1,0:T(8,128)S(1)}, f32[3,24,8,512]{3,2,1,0:T(8,128)}, u32[]{:S(2)}) copy-start(f32[3,24,8,512]{3,2,1,0:T(8,128)} %f_in.1) | copy-start | bytes 3538948
  2.3 5.1 %copy-start.2 = (s32[24,8,512]{2,1,0:T(8,128)S(1)}, s32[24,8,512]{2,1,0:T(8,128)}, u32[]{:S(2)}) copy-start(s32[24,8,512]{2,1,0:T(8,128)} %mat_ref.1) | copy-start | bytes 1179652
  2.3 5.0 %copy-start.4 = (f32[4]{0:T(128)S(1)}, f32[4]{0:T(128)}, u32[]{:S(2)}) copy-start(f32[4]{0:T(128)} %param.12) | copy-start | bytes 52
  2.3 5.0 %copy-start.5 = (s32[1,64]{1,0:T(1,128)S(1)}, s32[1,64]{1,0:T(1,128)}, u32[]{:S(2)}) copy-start(s32[1,64]{1,0:T(1,128)} %mask_ref.1) | copy-start | bytes 772
  2.5 7.2 %collective-permute-start.1 = (f32[56,512]{1,0:T(8,128)S(1)}, f32[56,512]{1,0:T(8,128)S(1)}, u32[]{:S(2)}, u32[]{:S(2)}) collective-permute-start(f32[56,512]{1,0:T(8,128)S(1)} %get-tuple-element.40), channel_id=1, source_target_pairs={{0,8},{2,10},{4,12},{6,14},{8,0},{10,2},{12,4},{14,6},{16,24},{18,... | collective-permute-start | bytes 344072 | tf_op jit(solution)/shard_map/ppermute | solution.py:65
  5.6 4.2 %collective-permute-start.2 = (f32[56,512]{1,0:T(8,128)S(1)}, f32[56,512]{1,0:T(8,128)S(1)}, u32[]{:S(2)}, u32[]{:S(2)}) collective-permute-start(f32[56,512]{1,0:T(8,128)S(1)} %get-tuple-element.41), channel_id=1, source_target_pairs={{0,2},{2,0},{4,6},{6,4},{8,16},{10,18},{12,20},{14,22},{16,8},{18,... | collective-permute-start | bytes 344072 | tf_op jit(solution)/shard_map/ppermute | solution.py:65
  5.6 4.2 %collective-permute-start = (f32[3,8,512]{2,1,0:T(8,128)S(1)}, f32[3,8,512]{2,1,0:T(8,128)S(1)}, u32[]{:S(2)}, u32[]{:S(2)}) collective-permute-start(f32[3,8,512]{2,1,0:T(8,128)S(1)} %get-tuple-element.39), channel_id=1, source_target_pairs={{0,1},{2,3},{4,5},{6,7},{1,0},{3,2},{5,4},{7,6},{8,9},{10,11},{12,... | collective-permute-start | bytes 147464 | tf_op jit(solution)/shard_map/ppermute | solution.py:65
  7.1 6.3 %collective-permute-start.3 = (f32[8,512]{1,0:T(8,128)S(1)}, f32[8,512]{1,0:T(8,128)S(1)}, u32[]{:S(2)}, u32[]{:S(2)}) collective-permute-start(f32[8,512]{1,0:T(8,128)S(1)} %get-tuple-element.46), channel_id=1, source_target_pairs={{0,2},{2,0},{4,6},{6,4},{1,8},{3,10},{5,12},{7,14},{8,1},{10,3},{1... | collective-permute-start | bytes 49160 | tf_op jit(solution)/shard_map/ppermute | solution.py:91
  10.6 11.3 %collective-permute-start.6 = (f32[8,2304]{1,0:T(8,128)S(1)}, f32[8,2304]{1,0:T(8,128)S(1)}, u32[]{:S(2)}, u32[]{:S(2)}) collective-permute-start(f32[8,2304]{1,0:T(8,128)S(1)} %get-tuple-element.53), channel_id=1, source_target_pairs={{0,24},{8,16},{16,8},{24,0},{1,25},{9,17},{17,9},{25,1},{2,26},{10... | collective-permute-start | bytes 221192 | tf_op jit(solution)/shard_map/ppermute | solution.py:982
  13.5 5.6 %collective-permute-start.4 = (f32[17,8,128]{2,1,0:T(8,128)S(1)}, f32[17,8,128]{2,1,0:T(8,128)S(1)}, u32[]{:S(2)}, u32[]{:S(2)}) collective-permute-start(f32[17,8,128]{2,1,0:T(8,128)S(1)} %get-tuple-element.49), channel_id=1, source_target_pairs={{0,2},{1,3},{2,0},{3,1},{4,6},{5,7},{6,4},{7,5},{8,10},{9,11},{10,... | collective-permute-start | bytes 208904 | tf_op jit(solution)/shard_map/ppermute | solution.py:65
  13.6 5.5 %collective-permute-start.5 = (f32[17,8,128]{2,1,0:T(8,128)S(1)}, f32[17,8,128]{2,1,0:T(8,128)S(1)}, u32[]{:S(2)}, u32[]{:S(2)}) collective-permute-start(f32[17,8,128]{2,1,0:T(8,128)S(1)} %get-tuple-element.50), channel_id=1, source_target_pairs={{0,1},{1,0},{2,4},{3,5},{4,2},{5,3},{6,7},{7,6},{8,9},{9,8},{10,12... | collective-permute-start | bytes 208904 | tf_op jit(solution)/shard_map/ppermute | solution.py:65
  15.3 6.6 %collective-permute-start.7 = (f32[8,2048]{1,0:T(8,128)S(1)}, f32[8,2048]{1,0:T(8,128)S(1)}, u32[]{:S(2)}, u32[]{:S(2)}) collective-permute-start(f32[8,2048]{1,0:T(8,128)S(1)} %get-tuple-element.54), channel_id=1, source_target_pairs={{0,16},{8,24},{16,0},{24,8},{1,17},{9,25},{17,1},{25,9},{2,18},{10... | collective-permute-start | bytes 196616 | tf_op jit(solution)/shard_map/ppermute | solution.py:982
  17.0 4.9 %collective-permute-start.8 = (f32[8,2048]{1,0:T(8,128)S(1)}, f32[8,2048]{1,0:T(8,128)S(1)}, u32[]{:S(2)}, u32[]{:S(2)}) collective-permute-start(f32[8,2048]{1,0:T(8,128)S(1)} %get-tuple-element.55), channel_id=1, source_target_pairs={{0,8},{8,0},{16,24},{24,16},{1,9},{9,1},{17,25},{25,17},{2,10},{10... | collective-permute-start | bytes 196616 | tf_op jit(solution)/shard_map/ppermute | solution.py:982
  19.1 2.7 %copy-start.3 = (bf16[112,48]{1,0:T(8,128)(2,1)S(1)}, bf16[112,48]{1,0:T(8,128)(2,1)}, u32[]{:S(2)}) copy-start(bf16[112,48]{1,0:T(8,128)(2,1)} %constant.2.clone.refs_0_) | copy-start | bytes 32260
  22.7 7.7 %collective-permute-start.9 = (f32[8,2432]{1,0:T(8,128)S(1)}, f32[8,2432]{1,0:T(8,128)S(1)}, u32[]{:S(2)}, u32[]{:S(2)}) collective-permute-start(f32[8,2432]{1,0:T(8,128)S(1)} %get-tuple-element.61), channel_id=1, source_target_pairs={{0,24},{8,16},{16,8},{24,0},{1,25},{9,17},{17,9},{25,1},{2,26},{10... | collective-permute-start | bytes 233480 | tf_op jit(solution)/shard_map/ppermute | solution.py:982
  24.7 6.8 %collective-permute-start.10 = (f32[8,2432]{1,0:T(8,128)S(1)}, f32[8,2432]{1,0:T(8,128)S(1)}, u32[]{:S(2)}, u32[]{:S(2)}) collective-permute-start(f32[8,2432]{1,0:T(8,128)S(1)} %get-tuple-element.62), channel_id=1, source_target_pairs={{0,16},{8,24},{16,0},{24,8},{1,17},{9,25},{17,1},{25,9},{2,18},{10... | collective-permute-start | bytes 233480 | tf_op jit(solution)/shard_map/ppermute | solution.py:982
  25.2 6.3 %collective-permute-start.11 = (f32[8,2432]{1,0:T(8,128)S(1)}, f32[8,2432]{1,0:T(8,128)S(1)}, u32[]{:S(2)}, u32[]{:S(2)}) collective-permute-start(f32[8,2432]{1,0:T(8,128)S(1)} %get-tuple-element.63), channel_id=1, source_target_pairs={{0,8},{8,0},{16,24},{24,16},{1,9},{9,1},{17,25},{25,17},{2,10},{10... | collective-permute-start | bytes 233480 | tf_op jit(solution)/shard_map/ppermute | solution.py:982

commit v10 on v9

--- a/solution.py
+++ b/solution.py
@@ -120,24 +120,35 @@
     return (cells_z - layers) * (1 - lax.axis_index("gz"))
 
 
-def faces_kernel(x_rounds, e_ref, h_ref, *refs):
-    x_sends, (low_ref, rows_ref) = refs[:x_rounds], refs[-2:]
-    others = refs[x_rounds:-2]
+def faces_kernel(x_rounds, e_in, h_in, e_ref, h_ref, *refs):
+    x_sends, (low_ref, rows_ref, sems) = refs[:x_rounds], refs[-3:]
+    others = refs[x_rounds:-3]
     z_sends, d_sends = others[: len(others) // 2], others[len(others) // 2 :]
     cells_z = e_ref.shape[1]
     last, top = ROWS - 1, cells_z - 1
+    copies = [
+        [pltpu.make_async_copy(source.at[c], target.at[c], sems.at[n, c]) for c in range(3)]
+        for n, (source, target) in enumerate(((e_in, e_ref), (h_in, h_ref)))
+    ]
+    for copy in copies[0] + copies[1]:
+        copy.start()
 
     low_ref[2 * cells_z :, :] = jnp.zeros_like(low_ref[2 * cells_z :, :])
     rows_ref[5, top : top + 1, :] = jnp.zeros_like(rows_ref[5, top : top + 1, :])
+    for copy in copies[0]:
+        copy.wait()
     for z in range(cells_z):
         low_ref[z : z + 1, :] = e_ref[1, z, 0:1, :]
         low_ref[cells_z + z : cells_z + z + 1, :] = e_ref[2, z, 0:1, :]
         for c in range(3):
             rows_ref[c, z : z + 1, :] = e_ref[c, z, last : last + 1, :]
+        if z > 0:
+            rows_ref[5, z - 1 : z, :] = e_ref[0, z, last : last + 1, :]
+    for copy in copies[1]:
+        copy.wait()
+    for z in range(cells_z):
         for c in range(2):
             rows_ref[3 + c, z : z + 1, :] = h_ref[1 + c, z, last : last + 1, :]
-        if z > 0:
-            rows_ref[5, z - 1 : z, :] = e_ref[0, z, last : last + 1, :]
     width = e_ref.shape[3]
     ex, ey, ez = (rows_ref[c] for c in range(3))
     column = lax.broadcasted_iota(jnp.int32, ex.shape, 1)
@@ -178,20 +189,22 @@
     _, cells_z, cells_x, cells_y = efield.shape
     x_rounds, z_rounds = rounds("gx"), rounds("gz")
     x_face, z_face, line = fast(2 * cells_z + ROWS, cells_y), fast(3, cells_x, cells_y), fast(ROWS, cells_y)
-    sends = pl.pallas_call(
+    fields = [fast(*field.shape) for field in (efield, hfield)]
+    efield, hfield, *sends = pl.pallas_call(
         functools.partial(faces_kernel, x_rounds),
-        in_specs=[VMEM] * 2,
-        out_specs=[VMEM] * (x_rounds + 2 * z_rounds),
-        out_shape=[x_face] * x_rounds + [z_face] * z_rounds + [line] * z_rounds,
+        in_specs=[ANY] * 2,
+        out_specs=[VMEM] * (2 + x_rounds + 2 * z_rounds),
+        out_shape=fields + [x_face] * x_rounds + [z_face] * z_rounds + [line] * z_rounds,
         scratch_shapes=[
             pltpu.VMEM(x_face.shape, jnp.float32),
             pltpu.VMEM((6, cells_z, cells_y), jnp.float32),
+            pltpu.SemaphoreType.DMA((2, 3)),
         ],
-        compiler_params=params(),
+        compiler_params=params(54),
     )(efield, hfield)
     xfaces = exchange(sends[:x_rounds], "gx", "gy")
     zfaces = exchange(sends[x_rounds : x_rounds + z_rounds], "gz", "gy")
-    return zfaces, xfaces, exchange_diagonal(sends[x_rounds + z_rounds :])
+    return efield, hfield, zfaces, xfaces, exchange_diagonal(sends[x_rounds + z_rounds :])
 
 
 def lane_group():
@@ -216,26 +229,6 @@
             high = jnp.where(here, pltpu.roll(right, shift, 1) if shift else right, high)
         low_ref[first + start // SLOTS] = low
         high_ref[first + start // SLOTS] = high
-
-
-def load_kernel(e_in, h_in, e_ref, h_ref, sems):
-    parts = [(source.at[c], target.at[c]) for source, target in ((e_in, e_ref), (h_in, h_ref)) for c in range(3)]
-    copies = [pltpu.make_async_copy(*part, sems.at[n]) for n, part in enumerate(parts)]
-    for copy in copies:
-        copy.start()
-    for copy in copies:
-        copy.wait()
-
-
-def load(*fields):
-    return pl.pallas_call(
-        load_kernel,
-        in_specs=[ANY] * 2,
-        out_specs=[VMEM] * 2,
-        out_shape=[fast(*one.shape) for one in fields],
-        scratch_shapes=[pltpu.SemaphoreType.DMA((6,))],
-        compiler_params=params(56),
-    )(*fields)
 
 
 def strips_kernel(
@@ -651,13 +644,15 @@
 
 
 PART = 2 * STRIP
+SPAN = 2 * PART
 
 
 def edge_gradient_kernel(counts, *refs):
-    own_ref, f_ref, inv_ref, wide_ref, eh_ref, grad_ref, mask_ref = refs[:7]
-    ends = np.cumsum((7,) + counts)
+    own_ref, f_ref, inv_ref, wide_ref, eh_ref, grad_ref, mask_ref, taps_ref = refs[:8]
+    ends = np.cumsum((8,) + counts)
     zfaces, xfaces, lines, yfaces = (refs[i:j] for i, j in zip(ends[:-1], ends[1:]))
-    (message, edge_ref), scratch = refs[ends[-1] : -3], refs[-3:]
+    (shares, message, edge_ref), scratch = refs[ends[-1] : -6], refs[-6:-3]
+    folded, parts, slabs = refs[-3:]
     layers, _, width = own_ref.shape
     lane = lax.broadcasted_iota(jnp.int32, (ROWS, LANES), 1)
     first, last = STRIP, LANES - STRIP - 1
@@ -668,22 +663,48 @@
 
     fields.gradient(layers, (grad_ref, mask_ref), store)
 
-    per_tile = LANES // PART
+    count = shares.shape[0]
+    half = count // 2
+    rows = half * ROWS
+    me = lax.axis_index("gx")
+    folded[...] = jnp.zeros_like(folded)
+    fold = jnp.minimum(me, count - 1 - me)
+    per_tile = LANES // SPAN
     for start in range(0, layers, per_tile):
-        packed = jnp.zeros((ROWS, LANES), jnp.float32)
+        tile = jnp.zeros((ROWS, LANES), jnp.float32)
         for j in range(min(per_tile, layers - start)):
-            layer = start + j
-            edge = edge_ref[layer]
-            own = edge_tile(lambda s: own_ref[layer, :, s], width)
+            edge = edge_ref[start + j]
+            own = edge_tile(lambda s: own_ref[start + j, :, s], width)
             more = jnp.where(jnp.logical_or(lane == first, lane == last), edge - own, edge)
-            left = pltpu.roll(more, (PART * j - 1) % LANES, 1)
-            right = pltpu.roll(more, (PART * j + STRIP - last) % LANES, 1)
-            packed = jnp.where(lane // STRIP == 2 * j, left, packed)
-            packed = jnp.where(lane // STRIP == 2 * j + 1, right, packed)
-        message[:, start // per_tile * LANES : (start // per_tile + 1) * LANES] = packed
-
-    tail = math.ceil(layers / per_tile) * LANES
-    message[:, tail:] = jnp.zeros_like(message[:, tail:])
+            low, high = SPAN * j + 1, SPAN * j + PART + STRIP - 1
+            here = jnp.logical_and(lane >= low, lane < low + STRIP)
+            tile = jnp.where(here, pltpu.roll(more, (low - 1) % LANES, 1), tile)
+            here = jnp.logical_and(lane >= high, lane < high + STRIP)
+            tile = jnp.where(here, pltpu.roll(more, (high - last) % LANES, 1), tile)
+        tile = jnp.where(me < half, tile, flip_rows(tile))
+        folded[fold, :, start // per_tile * LANES : (start // per_tile + 1) * LANES] = tile
+    split_rows(jnp.concatenate([folded[s] for s in range(half)], axis=0), parts)
+    total = cone(taps_ref, parts, rows)
+    lanes = lax.broadcasted_iota(jnp.int32, (rows, LANES), 1)
+    per_share = LANES // PART
+    for start in range(0, layers, per_share):
+        packed = jnp.zeros((rows, LANES), jnp.float32)
+        for j in range(min(per_share, layers - start)):
+            at = SPAN * (start + j)
+            tile = total[:, at // LANES * LANES : (at // LANES + 1) * LANES]
+            left = pltpu.roll(tile, (PART * j - STRIP - at) % LANES, 1)
+            right = pltpu.roll(tile, (PART * j + STRIP - PART - 1 - at) % LANES, 1)
+            packed = jnp.where(lanes // STRIP == 2 * j, left, packed)
+            packed = jnp.where(lanes // STRIP == 2 * j + 1, right, packed)
+        here = slice(start // per_share * LANES, (start // per_share + 1) * LANES)
+        for s in range(half):
+            one = packed[s * ROWS : (s + 1) * ROWS]
+            slabs[s, :, here] = one
+            slabs[count - 1 - s, :, here] = flip_rows(one)
+    for k in range(count):
+        shares[k] = slabs[lax.bitwise_xor(me, k)]
+
+    message[...] = jnp.zeros_like(message)
     top, last = fields.cells_z - 1, ROWS - 1
     above, beyond = (line[0:1] for line in corner_lines(lines, slice(0, width)))
     added = wide_ref[0:1, :] * f_ref[2, top, 0:1, :] * inv_ref[top, 0:1, :] * (HALF * above)
@@ -691,7 +712,7 @@
     column = lax.broadcasted_iota(jnp.int32, (1, width), 1)
     added = jnp.where(jnp.logical_or(column == 0, column == width - 1), 0.0, added)
     for at, n in line_places(width):
-        message[n : n + 1, tail + at : tail + at + LANES] = added[:, (at // LANES * ROWS + n) * LANES :][:, :LANES]
+        message[n : n + 1, at : at + LANES] = added[:, (at // LANES * ROWS + n) * LANES :][:, :LANES]
 
 
 def line_places(width):
@@ -699,8 +720,7 @@
 
 
 def line_of(message, width):
-    tail = message.shape[1] - math.ceil(width / LANES / ROWS) * LANES
-    return jnp.concatenate([message[n : n + 1, tail + at : tail + at + LANES] for at, n in line_places(width)], axis=1)
+    return jnp.concatenate([message[n : n + 1, at : at + LANES] for at, n in line_places(width)], axis=1)
 
 
 def line_spot(layers):
@@ -708,18 +728,26 @@
     return jnp.where(bottom, layers - 1, 0), jnp.where(bottom, 0, ROWS - 1)
 
 
-def edge_gradient(own, arrays, edges, zfaces, xfaces, lines, yfaces):
+def edge_gradient(own, arrays, edges, taps, zfaces, xfaces, lines, yfaces):
     layers, _, width = own.shape
     faces = (*zfaces, *xfaces, *lines, *yfaces)
-    tiles = math.ceil(layers * PART / LANES) + math.ceil(width / LANES / ROWS)
+    count = lax.axis_size("gx")
+    share = (count, ROWS, math.ceil(layers * PART / LANES) * LANES)
+    spread = math.ceil(layers * SPAN / LANES) * LANES
+    line = math.ceil(width / LANES / ROWS) * LANES
     return pl.pallas_call(
         functools.partial(edge_gradient_kernel, (len(zfaces), len(xfaces), len(lines), len(yfaces))),
-        in_specs=[VMEM] * (7 + len(faces)),
-        out_specs=[VMEM] * 2,
-        out_shape=[fast(ROWS, tiles * LANES), fast(layers, ROWS, LANES)],
-        scratch_shapes=fields_scratch(EDGE, xfaces[0], yfaces[0], width),
+        in_specs=[VMEM] * (8 + len(faces)),
+        out_specs=[VMEM] * 3,
+        out_shape=[fast(*share), fast(ROWS, line), fast(layers, ROWS, LANES)],
+        scratch_shapes=fields_scratch(EDGE, xfaces[0], yfaces[0], width)
+        + [
+            pltpu.VMEM((count // 2, ROWS, spread), jnp.float32),
+            pltpu.VMEM((3 * count // 2 * ROWS, spread), jnp.bfloat16),
+            pltpu.VMEM(share, jnp.float32),
+        ],
         compiler_params=params(),
-    )(own, arrays[2], arrays[3], arrays[5], *edges, *faces)
+    )(own, arrays[2], arrays[3], arrays[5], *edges, taps, *faces)
 
 
 def step_kernel(counts, *refs):
@@ -790,10 +818,17 @@
     )(efield, hfield, inv, own, edge, message, *(one for group in groups for one in group), after)
 
 
+def cone_taps():
+    span = np.arange(-RADIUS, RADIUS + 1, dtype=np.float64)
+    return np.maximum(RADIUS - np.sqrt(span[:, None] ** 2 + span[None, :] ** 2), 0.0)
+
+
+def cone_sum():
+    return cone_taps().sum()
+
+
 def cone_matrix(rows):
-    span = np.arange(-RADIUS, RADIUS + 1, dtype=np.float64)
-    cone = np.maximum(RADIUS - np.sqrt(span[:, None] ** 2 + span[None, :] ** 2), 0.0)
-    weight = cone / cone.sum()
+    weight = cone_taps() / cone_sum()
     x = np.arange(rows)
     out = np.zeros((RADIUS + 1, rows, rows))
     for b in range(RADIUS + 1):
@@ -833,10 +868,10 @@
 
 
 def filter_kernel(count, per_device, width, *refs):
-    taps_ref, edges_ref = refs[:2]
-    got = refs[count + 1 : 1 : -1]
-    outs = refs[2 + count : 2 + 2 * count]
-    slabs, parts, done = refs[2 + 2 * count :]
+    taps_ref, edges_ref, line_ref = refs[:3]
+    got = refs[count + 2 : 2 : -1]
+    outs = refs[3 + count : 3 + 2 * count]
+    slabs, parts, done = refs[3 + 2 * count :]
     me = lax.axis_index("gx")
     half = count // 2
     rows = half * ROWS
@@ -855,92 +890,81 @@
             done[count - 1 - s, :, here] = flip_rows(own)
     for k in range(count):
         outs[k][:, : per_device * width] = done[lax.bitwise_xor(me, k)]
-        outs[k][:, per_device * width :] = edges_ref[...]
-
-
-def cone_filter(taps, edges, got, per_device, width):
+        tail = per_device * width + edges_ref.shape[2]
+        outs[k][:, per_device * width : tail] = edges_ref[k]
+        outs[k][:, tail:] = line_ref[...]
+
+
+def cone_filter(taps, edges, line, got, per_device, width):
     count = len(got)
     rows = count // 2 * ROWS
     return pl.pallas_call(
         functools.partial(filter_kernel, count, per_device, width),
-        in_specs=[VMEM] * (2 + count),
+        in_specs=[VMEM] * (3 + count),
         out_specs=[VMEM] * count,
-        out_shape=[fast(ROWS, per_device * width + edges.shape[1])] * count,
+        out_shape=[fast(ROWS, per_device * width + edges.shape[2] + line.shape[1])] * count,
         scratch_shapes=[
             pltpu.VMEM((count, ROWS, per_device * width), jnp.float32),
             pltpu.VMEM((3 * rows, width + LANES), jnp.bfloat16),
             pltpu.VMEM((count, ROWS, per_device * width), jnp.float32),
         ],
         compiler_params=params(),
-    )(taps, edges, *got[::-1])
-
-
-SPAN = 2 * PART
+    )(taps, edges, line, *got[::-1])
+
+
+def cone_weight(along_x, along_y):
+    near = jnp.maximum(RADIUS - jnp.sqrt(along_x * along_x + float(along_y * along_y)), 0.0)
+    return near * float(1.0 / cone_sum())
 
 
 def finish_kernel(count, per_device, width, *refs):
-    taps_ref = refs[0]
-    got = refs[count:0:-1]
-    out, (slabs, parts, mine, line_parts, line_mine, left, right, done, sems) = refs[count + 1], refs[count + 2 :]
+    got = refs[count - 1 :: -1]
+    out, (left, right, done, sems) = refs[count], refs[count + 1 :]
     me = lax.axis_index("gx")
     layers = count * per_device
-    half = count // 2
-    rows = half * ROWS
-    lane = lax.broadcasted_iota(jnp.int32, (rows, LANES), 1)
-    lane_out = lax.broadcasted_iota(jnp.int32, (ROWS, LANES), 1)
+    lane = lax.broadcasted_iota(jnp.int32, (ROWS, LANES), 1)
+    edges_at = per_device * width
+    line_at = edges_at + math.ceil(layers * PART / LANES) * LANES
+
+    per_tile = LANES // PART
+    for start in range(0, layers, per_tile):
+        at = edges_at + start * PART
+        tile = got[0][:, at : at + LANES]
+        for k in range(1, count):
+            tile = tile + got[k][:, at : at + LANES]
+        for j in range(min(per_tile, layers - start)):
+            head = pltpu.roll(tile, (-PART * j) % LANES, 1)
+            left[start + j] = jnp.where(lane < STRIP - 1, head, 0.0)
+            tail = pltpu.roll(tile, (LANES + 1 - 2 * STRIP - PART * j) % LANES, 1)
+            right[start + j] = jnp.where(lane > LANES - STRIP, tail, 0.0)
+
+    line_layer, spot = line_spot(layers)
+    end = count * ROWS - 1
+    row = lax.broadcasted_iota(jnp.int32, (ROWS, LANES), 0) + me * ROWS
+    lines, near, far = [], [], []
     for k in range(count):
-        slabs[lax.bitwise_xor(me, k)] = got[k][:, per_device * width :]
-    symmetric = jnp.concatenate([slabs[s] + flip_rows(slabs[count - 1 - s]) for s in range(half)], axis=0)
-    per_tile = LANES // SPAN
-
-    line_layer, spot = line_spot(layers)
-    row = lax.broadcasted_iota(jnp.int32, (ROWS, width), 0)
-    folded = [
-        jnp.where(row == spot, line_of(slabs[s], width), 0.0)
-        + jnp.where(row == ROWS - 1 - spot, line_of(slabs[count - 1 - s], width), 0.0)
-        for s in range(half)
-    ]
-    side = jnp.zeros((rows, LANES), jnp.float32)
-    split_rows(jnp.concatenate([jnp.concatenate(folded, axis=0), side], axis=1), line_parts)
-    total = cone(taps_ref, line_parts, rows)
-    for s in range(half):
-        own = total[s * ROWS : (s + 1) * ROWS, :width]
-        line_mine[s] = own
-        line_mine[count - 1 - s] = flip_rows(own)
-    tiles = []
-    for start in range(0, layers, per_tile):
-        tile = jnp.zeros((rows, LANES), jnp.float32)
-        for j in range(min(per_tile, layers - start)):
-            at = PART * (start + j)
-            source = symmetric[:, at // LANES * LANES : (at // LANES + 1) * LANES]
-            low, high = SPAN * j + 1, SPAN * j + PART + STRIP - 1
-            here = jnp.logical_and(lane >= low, lane < low + STRIP)
-            tile = jnp.where(here, pltpu.roll(source, (low - at) % LANES, 1), tile)
-            here = jnp.logical_and(lane >= high, lane < high + STRIP)
-            tile = jnp.where(here, pltpu.roll(source, (high - at - STRIP) % LANES, 1), tile)
-        tiles.append(tile)
-    split_rows(jnp.concatenate(tiles, axis=1), parts)
-    total = cone(taps_ref, parts, rows)
-    for s in range(half):
-        own = total[s * ROWS : (s + 1) * ROWS]
-        mine[s] = own
-        mine[count - 1 - s] = flip_rows(own)
-    mine_now = mine[me]
-    for layer in range(layers):
-        tile = mine_now[:, layer // per_tile * LANES : (layer // per_tile + 1) * LANES]
-        at = SPAN * (layer % per_tile)
-        head = pltpu.roll(tile, (-at - STRIP) % LANES, 1)
-        left[layer] = jnp.where(lane_out < STRIP - 1, head, 0.0)
-        tail = pltpu.roll(tile, (LANES - STRIP - at - PART) % LANES, 1)
-        right[layer] = jnp.where(lane_out > LANES - STRIP, tail, 0.0)
+        lines.append(line_of(got[k][:, line_at:], width))
+        where = lax.bitwise_xor(me, k) * ROWS + spot
+        near.append((row - where).astype(jnp.float32))
+        far.append((row - (end - where)).astype(jnp.float32))
+    total = None
+    for b in range(RADIUS + 1):
+        mixed = jnp.zeros((ROWS, width), jnp.float32)
+        for k in range(count):
+            weight = cone_weight(near[k], b) + cone_weight(far[k], b)
+            mixed = mixed + jnp.concatenate([weight] * (width // LANES), axis=1) * lines[k]
+        mixed = jnp.concatenate([mixed, jnp.zeros((ROWS, LANES), jnp.float32)], axis=1)
+        if b:
+            mixed = pltpu.roll(mixed, b, 1) + pltpu.roll(mixed, width + LANES - b, 1)
+        total = mixed if total is None else total + mixed
+    line = total[:, :width]
 
     copies = []
     for k in range(count):
         first = lax.bitwise_xor(me, k) * per_device
         for i in range(per_device):
             at = i * width
-            line = jnp.where(first + i == line_layer, line_mine[me], 0.0)
-            done[k, i] = got[k][:, at : at + width] + line
+            done[k, i] = got[k][:, at : at + width] + jnp.where(first + i == line_layer, line, 0.0)
             done[k, i, :, :LANES] += left[first + i]
             done[k, i, :, width - LANES :] += right[first + i]
         copies.append(pltpu.make_async_copy(done.at[k], out.at[pl.ds(first, per_device)], sems.at[k]))
@@ -949,30 +973,22 @@
         copy.wait()
 
 
-def finish(taps, parts, layers, width):
+def finish(parts, layers, width):
     count = len(parts)
     per_device = layers // count
-    rows = count // 2 * ROWS
-    edges = parts[0].shape[1] - per_device * width
-    spread = math.ceil(layers * SPAN / LANES) * LANES
     return pl.pallas_call(
         functools.partial(finish_kernel, count, per_device, width),
-        in_specs=[VMEM] * (1 + count),
+        in_specs=[VMEM] * count,
         out_specs=ANY,
         out_shape=f32(layers, ROWS, width),
         scratch_shapes=[
-            pltpu.VMEM((count, ROWS, edges), jnp.float32),
-            pltpu.VMEM((3 * rows, spread), jnp.bfloat16),
-            pltpu.VMEM((count, ROWS, spread), jnp.float32),
-            pltpu.VMEM((3 * rows, width + LANES), jnp.bfloat16),
-            pltpu.VMEM((count, ROWS, width), jnp.float32),
             pltpu.VMEM((layers, ROWS, LANES), jnp.float32),
             pltpu.VMEM((layers, ROWS, LANES), jnp.float32),
             pltpu.VMEM((count, per_device, ROWS, width), jnp.float32),
             pltpu.SemaphoreType.DMA((count,)),
         ],
         compiler_params=params(),
-    )(taps, *parts[::-1])
+    )(*parts[::-1])
 
 
 def spread(parts):
@@ -985,8 +1001,7 @@
 
 def on_device(efield, hfield, forward, material, permit, design_mask, grad_sum):
     layers, _, width = grad_sum.shape
-    efield, hfield = load(efield, hfield)
-    zfaces, xfaces, lines = halos(efield, hfield)
+    efield, hfield, zfaces, xfaces, lines = halos(efield, hfield)
     forward, own_low, own_high, mask, inv = strips(
         permit, efield, hfield, forward, material, grad_sum, design_mask
     )
@@ -995,13 +1010,13 @@
     shares, own = own_gradient(arrays, zfaces, xfaces)
     got = spread(shares)
     yfaces = exchange(y_faces(own_low, own_high, zfaces, xfaces, lines, own), "gy", "gz")
-    message, edge = edge_gradient(own, arrays, edges, zfaces, xfaces, lines, yfaces)
     taps = jnp.asarray(cone_matrix(len(got) // 2 * ROWS))
-    parts = cone_filter(taps, message, got, layers // len(got), width)
+    added, line, edge = edge_gradient(own, arrays, edges, taps, zfaces, xfaces, lines, yfaces)
+    parts = cone_filter(taps, added, line, got, layers // len(got), width)
     e_next, h_next, grad_total = step(
-        efield, hfield, inv, own, edge, message, zfaces, xfaces, lines, yfaces, parts[0]
+        efield, hfield, inv, own, edge, line, zfaces, xfaces, lines, yfaces, parts[0]
     )
-    return e_next, h_next, grad_total, finish(taps, spread(parts), layers, width)
+    return e_next, h_next, grad_total, finish(spread(parts), layers, width)
 
 
 def solution(mesh):

time: 33 us -> 32.7 us (level)
  waiting for transfers between devices: 4 us -> 3.59 us
    pallas_call x1, Pallas kernels: 0.94 us -> 1.4 us  [edge_gradient(): pl.pallas_call(functools.partial(edge_gradient_kernel, (len(zfaces), len(...]
    ppermute x6, waiting for transfers between devices: 2.86 us -> 2.44 us  [spread(): got[k] = lax.ppermute(parts[k], 'gx', [(i, i ^ k) for i in range(count)])]
    pallas_call x1, Pallas kernels: 1.34 us -> 0.97 us  [finish(): pl.pallas_call(functools.partial(finish_kernel, count, per_device, width)...]
    pallas_call x2 -> x1, Pallas kernels: 1.81 us -> 1.87 us  [halos(): pl.pallas_call(functools.partial(faces_kernel, x_rounds), in_specs=[ANY]...]
  transfers between devices with their start and end apart: 12 -> 12, of which waited for: 3 -> 3; matrix products, arithmetic and copies ran while one was open for 0% -> 0% of each run, Pallas kernels for 21% -> 23%
where the time goes in v10:
time: 32.7 us; the launch traced here: 32.5 us
  starting transfers between devices  17.1 us (52%)
  Pallas kernels  11 us (34%)
  waiting for transfers between devices  3.59 us (11%)
  between operations  0.79 us (2%)
    ppermute x6, starting transfers between devices, spread(): got[k] = lax.ppermute(parts[k], 'gx', [(i, i ^ k) for i in range(count)])  10.5 us
    ppermute x5, starting transfers between devices, exchange(): got.append(lax.ppermute(value, tuple(axes), pairs))  6.36 us
    pallas_call x1, Pallas kernels, step(): pl.pallas_call(functools.partial(step_kernel, counts), in_specs=[VMEM] *...  3.24 us
    ppermute x6, waiting for transfers between devices, spread(): got[k] = lax.ppermute(parts[k], 'gx', [(i, i ^ k) for i in range(count)])  2.44 us
    pallas_call x1, Pallas kernels, halos(): pl.pallas_call(functools.partial(faces_kernel, x_rounds), in_specs=[ANY]...  1.87 us
    pallas_call x1, Pallas kernels, edge_gradient(): pl.pallas_call(functools.partial(edge_gradient_kernel, (len(zfaces), len(...  1.4 us
    pallas_call x1, Pallas kernels, strips(): pl.pallas_call(strips_kernel, in_specs=[VMEM] * 3 + [ANY] + [VMEM] * 3, o...  1.24 us
    ppermute x5, waiting for transfers between devices, exchange(): got.append(lax.ppermute(value, tuple(axes), pairs))  1.15 us
  transfers between devices with their start and end apart: 12, of which 3 were waited for; matrix products, arithmetic and copies ran while one was open for 0% of the time, Pallas kernels for 23%

profile of v10, /device:TPU:0, one launch (start us, length us, event | category | flops | bytes accessed | tf_op | source)
XLA Modules:
  0.0 32.5 jit_solution(10401380875478264772)
XLA Ops:
  0.6 0.0 copy-start
  0.6 0.0 copy-start.5
  0.7 0.0 copy-start.4
  0.7 0.0 copy-start.2
  0.7 0.0 copy-start.1
  0.7 1.9 %shard_map.111 = (f32[3,24,8,512]{3,2,1,0:T(8,128)S(1)}, f32[3,24,8,512]{3,2,1,0:T(8,128)S(1)}, f32[56,512]{1,0:T(8,128)S(1)}, f32[56,512]{1,0:T(8,128)S(1)}, f3...) custom-call(f32[3,24,8,512]{3,2,1,0:T(8,128)} %e_in.1, f32[3,24,8,512]{3,2,1,0:T(8,128)} %h_in.1), custom_call_target="tpu_custom_call" | custom-call | tf_op jit(solution)/shard_map/pallas_call | solution.py:193
  2.6 3.1 %collective-permute-start.1 = (f32[56,512]{1,0:T(8,128)S(1)}, f32[56,512]{1,0:T(8,128)S(1)}, u32[]{:S(2)}, u32[]{:S(2)}) collective-permute-start(f32[56,512]{1,0:T(8,128)S(1)} %get-tuple-element.41), channel_id=1, source_target_pairs={{0,8},{2,10},{4,12},{6,14},{8,0},{10,2},{12,4},{14,6},{16,24},{18,... | collective-permute-start | bytes 344072 | tf_op jit(solution)/shard_map/ppermute | solution.py:65
  5.7 0.0 collective-permute-start.2
  5.7 1.5 %collective-permute-start = (f32[3,8,512]{2,1,0:T(8,128)S(1)}, f32[3,8,512]{2,1,0:T(8,128)S(1)}, u32[]{:S(2)}, u32[]{:S(2)}) collective-permute-start(f32[3,8,512]{2,1,0:T(8,128)S(1)} %get-tuple-element.40), channel_id=1, source_target_pairs={{0,1},{2,3},{4,5},{6,7},{1,0},{3,2},{5,4},{7,6},{8,9},{10,11},{12,... | collective-permute-start | bytes 147464 | tf_op jit(solution)/shard_map/ppermute | solution.py:65
  7.2 0.2 collective-permute-start.3
  7.4 0.0 copy-done
  7.4 0.0 copy-done.5
  7.4 0.0 copy-done.4
  7.4 0.0 copy-done.2
  7.4 0.0 copy-done.1
  7.4 1.2 %shard_map.112 = (f32[3,24,8,512]{3,2,1,0:T(8,128)S(1)}, f32[15,8,128]{2,1,0:T(8,128)S(1)}, f32[15,8,128]{2,1,0:T(8,128)S(1)}, f32[8,512]{1,0:T(8,128)S(1)}, f32[24,8,512]{2,1,0:T(8,128)S(1)}) custom-call(f32[1,4]{1,0:T(1,128)S(1)} %bitcast.1, f32[3,24,8,512]{3,2,1,0:T(8,128)S(1)} %get-tuple-element.35.e_ref.refs_0_, ...), custom_call_target="tpu_custom_call" | custom-call | tf_op jit(solution)/shard_map/pallas_call | solution.py:285
  8.7 1.1 %collective-permute-done.refs_6_.refs_2_.refs_8_ = f32[3,8,512]{2,1,0:T(8,128)S(1)} collective-permute-done((f32[3,8,512]{2,1,0:T(8,128)S(1)}, f32[3,8,512]{2,1,0:T(8,128)S(1)}, u32[]{:S(2)}, u32[]{:S(2)}) %collective-permute-start) | collective-permute-done | bytes 49184 | tf_op jit(solution)/shard_map/ppermute | solution.py:65
  9.8 0.0 collective-permute-done.1.refs_7_.refs_3_.refs_9_
  9.8 0.0 collective-permute-done.2.refs_8_.refs_4_.refs_10_
  9.8 0.8 %shard_map.113 = (f32[8,2304]{1,0:T(8,128)S(1)}, f32[8,2048]{1,0:T(8,128)S(1)}, f32[8,2048]{1,0:T(8,128)S(1)}, f32[8,2048]{1,0:T(8,128)S(1)}, f32[16,8,512]{2,1,0:T(8,128)S(1)}) custom-call(f32[3,24,8,512]{3,2,1,0:T(8,128)S(1)} %get-tuple-element.35.e_ref.refs_0_, f32[3,24,8,512]{3,2,1,0:T(8,128)S(1)} %get-tuple-element.36.h_ref.refs_1_, ...), custom_call_target="tpu_custom_call" | custom-call | tf_op jit(solution)/shard_map/pallas_call | solution.py:633
  10.6 2.8 %collective-permute-start.6 = (f32[8,2304]{1,0:T(8,128)S(1)}, f32[8,2304]{1,0:T(8,128)S(1)}, u32[]{:S(2)}, u32[]{:S(2)}) collective-permute-start(f32[8,2304]{1,0:T(8,128)S(1)} %get-tuple-element.55), channel_id=1, source_target_pairs={{0,24},{8,16},{16,8},{24,0},{1,25},{9,17},{17,9},{25,1},{2,26},{10... | collective-permute-start | bytes 221192 | tf_op jit(solution)/shard_map/ppermute | solution.py:998
  13.4 0.0 collective-permute-done.3.refs_5_.refs_11_.refs_9_
  13.4 0.2 shard_map.115
  13.6 0.0 collective-permute-start.4
  13.6 1.7 %collective-permute-start.5 = (f32[17,8,128]{2,1,0:T(8,128)S(1)}, f32[17,8,128]{2,1,0:T(8,128)S(1)}, u32[]{:S(2)}, u32[]{:S(2)}) collective-permute-start(f32[17,8,128]{2,1,0:T(8,128)S(1)} %get-tuple-element.51), channel_id=1, source_target_pairs={{0,1},{1,0},{2,4},{3,5},{4,2},{5,3},{6,7},{7,6},{8,9},{9,8},{10,12... | collective-permute-start | bytes 208904 | tf_op jit(solution)/shard_map/ppermute | solution.py:65
  15.3 1.7 %collective-permute-start.7 = (f32[8,2048]{1,0:T(8,128)S(1)}, f32[8,2048]{1,0:T(8,128)S(1)}, u32[]{:S(2)}, u32[]{:S(2)}) collective-permute-start(f32[8,2048]{1,0:T(8,128)S(1)} %get-tuple-element.56), channel_id=1, source_target_pairs={{0,16},{8,24},{16,0},{24,8},{1,17},{9,25},{17,1},{25,9},{2,18},{10... | collective-permute-start | bytes 196616 | tf_op jit(solution)/shard_map/ppermute | solution.py:998
  17.0 0.0 copy-start.3
  17.0 1.6 %collective-permute-start.8 = (f32[8,2048]{1,0:T(8,128)S(1)}, f32[8,2048]{1,0:T(8,128)S(1)}, u32[]{:S(2)}, u32[]{:S(2)}) collective-permute-start(f32[8,2048]{1,0:T(8,128)S(1)} %get-tuple-element.57), channel_id=1, source_target_pairs={{0,8},{8,0},{16,24},{24,16},{1,9},{9,1},{17,25},{25,17},{2,10},{10... | collective-permute-start | bytes 196616 | tf_op jit(solution)/shard_map/ppermute | solution.py:998
  18.6 0.5 %shard_map.114 = (f32[24,6,8,128]{3,2,1,0:T(8,128)S(1)}, f32[16,5,8,128]{3,2,1,0:T(8,128)S(1)}, f32[8,128]{1,0:T(8,128)S(1)}) custom-call(f32[3,24,8,512]{3,2,1,0:T(8,128)S(1)} %get-tuple-element.35.e_ref.refs_0_, f32[3,24,8,512]{3,2,1,0:T(8,128)S(1)} %get-tuple-element.36.h_ref.refs_1_, f32[3,24,8,512]{3,2,1,0:T(8,128)S(1)} %get-tuple-element.38.refs_2_.f_ref.refs_1_, ...), custom_call_target="tpu_custom_call" | custom-call | tf_op jit(solution)/shard_map/pallas_call | solution.py:320
  19.2 0.0 collective-permute-done.4.refs_12_.refs_10_
  19.2 0.0 collective-permute-done.5.refs_13_.refs_11_
  19.2 0.0 copy-done.3
  19.2 1.4 %shard_map.116 = (f32[4,8,256]{2,1,0:T(8,128)S(1)}, f32[8,128]{1,0:T(8,128)S(1)}, f32[16,8,128]{2,1,0:T(8,128)S(1)}) custom-call(f32[16,8,512]{2,1,0:T(8,128)S(1)} %get-tuple-element.43.refs_6_.refs_0_.refs_3_, f32[3,24,8,512]{3,2,1,0:T(8,128)S(1)} %get-tuple-element.38.refs_2_.f_ref.refs_1_, f32[24,8,512]{2,1,0:T(8,128)S(1)} %get-tuple-element.37.refs_3_.inv_ref.refs_2_, ...), custom_call_target="tpu_custom_call" | custom-call | tf_op jit(solution)/shard_map/pallas_call | solution.py:738
  20.6 1.3 %collective-permute-done.7.refs_4_ = f32[8,2048]{1,0:T(8,128)S(1)} collective-permute-done((f32[8,2048]{1,0:T(8,128)S(1)}, f32[8,2048]{1,0:T(8,128)S(1)}, u32[]{:S(2)}, u32[]{:S(2)}) %collective-permute-start.7) | collective-permute-done | bytes 65568 | tf_op jit(solution)/shard_map/ppermute | solution.py:998
  21.9 0.0 collective-permute-done.8.refs_5_
  21.9 0.0 collective-permute-done.6.refs_3_
  21.9 0.8 %shard_map.117 = (f32[8,2432]{1,0:T(8,128)S(1)}, f32[8,2432]{1,0:T(8,128)S(1)}, f32[8,2432]{1,0:T(8,128)S(1)}, f32[8,2432]{1,0:T(8,128)S(1)}) custom-call(bf16[112,48]{1,0:T(8,128)(2,1)S(1)} %copy-done.3, f32[4,8,256]{2,1,0:T(8,128)S(1)} %get-tuple-element.54.refs_1_, f32[8,128]{1,0:T(8,128)S(1)} %get-tuple-element.53.refs_2_.refs_5_, ...), custom_call_target="tpu_custom_call" | custom-call | tf_op jit(solution)/shard_map/pallas_call | solution.py:901
  22.7 2.0 %collective-permute-start.9 = (f32[8,2432]{1,0:T(8,128)S(1)}, f32[8,2432]{1,0:T(8,128)S(1)}, u32[]{:S(2)}, u32[]{:S(2)}) collective-permute-start(f32[8,2432]{1,0:T(8,128)S(1)} %get-tuple-element.63), channel_id=1, source_target_pairs={{0,24},{8,16},{16,8},{24,0},{1,25},{9,17},{17,9},{25,1},{2,26},{10... | collective-permute-start | bytes 233480 | tf_op jit(solution)/shard_map/ppermute | solution.py:998
  24.7 0.5 %collective-permute-start.10 = (f32[8,2432]{1,0:T(8,128)S(1)}, f32[8,2432]{1,0:T(8,128)S(1)}, u32[]{:S(2)}, u32[]{:S(2)}) collective-permute-start(f32[8,2432]{1,0:T(8,128)S(1)} %get-tuple-element.64), channel_id=1, source_target_pairs={{0,16},{8,24},{16,0},{24,8},{1,17},{9,25},{17,1},{25,9},{2,18},{10... | collective-permute-start | bytes 233480 | tf_op jit(solution)/shard_map/ppermute | solution.py:998
  25.2 2.0 %collective-permute-start.11 = (f32[8,2432]{1,0:T(8,128)S(1)}, f32[8,2432]{1,0:T(8,128)S(1)}, u32[]{:S(2)}, u32[]{:S(2)}) collective-permute-start(f32[8,2432]{1,0:T(8,128)S(1)} %get-tuple-element.65), channel_id=1, source_target_pairs={{0,8},{8,0},{16,24},{24,16},{1,9},{9,1},{17,25},{25,17},{2,10},{10... | collective-permute-start | bytes 233480 | tf_op jit(solution)/shard_map/ppermute | solution.py:998
  27.2 3.2 %shard_map.118 = (f32[3,24,8,512]{3,2,1,0:T(8,128)}, f32[3,24,8,512]{3,2,1,0:T(8,128)}, f32[16,8,512]{2,1,0:T(8,128)}) custom-call(f32[3,24,8,512]{3,2,1,0:T(8,128)S(1)} %get-tuple-element.35.e_ref.refs_0_, f32[3,24,8,512]{3,2,1,0:T(8,128)S(1)} %get-tuple-element.36.h_ref.refs_1_, f32[24,8,512]{2,1,0:T(8,128)S(1)} %get-tuple-element.37.refs_3_.inv_ref.refs_2_, ...), custom_call_target="tpu_custom_call" | custom-call | tf_op jit(solution)/shard_map/pallas_call | solution.py:809
  30.4 0.0 collective-permute-done.9.refs_0_
  30.4 1.1 %collective-permute-done.10.refs_1_ = f32[8,2432]{1,0:T(8,128)S(1)} collective-permute-done((f32[8,2432]{1,0:T(8,128)S(1)}, f32[8,2432]{1,0:T(8,128)S(1)}, u32[]{:S(2)}, u32[]{:S(2)}) %collective-permute-start.10) | collective-permute-done | bytes 77856 | tf_op jit(solution)/shard_map/ppermute | solution.py:998
  31.6 0.0 collective-permute-done.11.refs_2_
  31.6 1.0 %shard_map.119 = f32[16,8,512]{2,1,0:T(8,128)} custom-call(f32[8,2432]{1,0:T(8,128)S(1)} %collective-permute-done.9.refs_0_, f32[8,2432]{1,0:T(8,128)S(1)} %collective-permute-done.10.refs_1_, f32[8,2432]{1,0:T(8,128)S(1)} %collective-permute-done.11.refs_2_, f32[8,2432]{1,0:T(8,128)S(1)} %get-tuple-element.59.refs_12_.refs_3_), custom_call_target="tpu_custom_call" | custom-call | tf_op jit(solution)/shard_map/pallas_call | solution.py:979
Async XLA Ops:
  0.6 6.8 %copy-start = (f32[16,8,512]{2,1,0:T(8,128)S(1)}, f32[16,8,512]{2,1,0:T(8,128)}, u32[]{:S(2)}) copy-start(f32[16,8,512]{2,1,0:T(8,128)} %grad_ref.3) | copy-start | bytes 786436
  0.6 6.8 %copy-start.5 = (s32[1,64]{1,0:T(1,128)S(1)}, s32[1,64]{1,0:T(1,128)}, u32[]{:S(2)}) copy-start(s32[1,64]{1,0:T(1,128)} %mask_ref.1) | copy-start | bytes 772
  0.7 6.8 %copy-start.4 = (f32[4]{0:T(128)S(1)}, f32[4]{0:T(128)}, u32[]{:S(2)}) copy-start(f32[4]{0:T(128)} %param.12) | copy-start | bytes 52
  0.7 6.8 %copy-start.2 = (s32[24,8,512]{2,1,0:T(8,128)S(1)}, s32[24,8,512]{2,1,0:T(8,128)}, u32[]{:S(2)}) copy-start(s32[24,8,512]{2,1,0:T(8,128)} %mat_ref.1) | copy-start | bytes 1179652
  0.7 6.7 %copy-start.1 = (f32[3,24,8,512]{3,2,1,0:T(8,128)S(1)}, f32[3,24,8,512]{3,2,1,0:T(8,128)}, u32[]{:S(2)}) copy-start(f32[3,24,8,512]{3,2,1,0:T(8,128)} %f_in.1) | copy-start | bytes 3538948
  2.6 7.2 %collective-permute-start.1 = (f32[56,512]{1,0:T(8,128)S(1)}, f32[56,512]{1,0:T(8,128)S(1)}, u32[]{:S(2)}, u32[]{:S(2)}) collective-permute-start(f32[56,512]{1,0:T(8,128)S(1)} %get-tuple-element.41), channel_id=1, source_target_pairs={{0,8},{2,10},{4,12},{6,14},{8,0},{10,2},{12,4},{14,6},{16,24},{18,... | collective-permute-start | bytes 344072 | tf_op jit(solution)/shard_map/ppermute | solution.py:65
  5.7 4.2 %collective-permute-start.2 = (f32[56,512]{1,0:T(8,128)S(1)}, f32[56,512]{1,0:T(8,128)S(1)}, u32[]{:S(2)}, u32[]{:S(2)}) collective-permute-start(f32[56,512]{1,0:T(8,128)S(1)} %get-tuple-element.42), channel_id=1, source_target_pairs={{0,2},{2,0},{4,6},{6,4},{8,16},{10,18},{12,20},{14,22},{16,8},{18,... | collective-permute-start | bytes 344072 | tf_op jit(solution)/shard_map/ppermute | solution.py:65
  5.7 4.2 %collective-permute-start = (f32[3,8,512]{2,1,0:T(8,128)S(1)}, f32[3,8,512]{2,1,0:T(8,128)S(1)}, u32[]{:S(2)}, u32[]{:S(2)}) collective-permute-start(f32[3,8,512]{2,1,0:T(8,128)S(1)} %get-tuple-element.40), channel_id=1, source_target_pairs={{0,1},{2,3},{4,5},{6,7},{1,0},{3,2},{5,4},{7,6},{8,9},{10,11},{12,... | collective-permute-start | bytes 147464 | tf_op jit(solution)/shard_map/ppermute | solution.py:65
  7.2 6.2 %collective-permute-start.3 = (f32[8,512]{1,0:T(8,128)S(1)}, f32[8,512]{1,0:T(8,128)S(1)}, u32[]{:S(2)}, u32[]{:S(2)}) collective-permute-start(f32[8,512]{1,0:T(8,128)S(1)} %get-tuple-element.47), channel_id=1, source_target_pairs={{0,2},{2,0},{4,6},{6,4},{1,8},{3,10},{5,12},{7,14},{8,1},{10,3},{1... | collective-permute-start | bytes 49160 | tf_op jit(solution)/shard_map/ppermute | solution.py:91
  10.6 11.3 %collective-permute-start.6 = (f32[8,2304]{1,0:T(8,128)S(1)}, f32[8,2304]{1,0:T(8,128)S(1)}, u32[]{:S(2)}, u32[]{:S(2)}) collective-permute-start(f32[8,2304]{1,0:T(8,128)S(1)} %get-tuple-element.55), channel_id=1, source_target_pairs={{0,24},{8,16},{16,8},{24,0},{1,25},{9,17},{17,9},{25,1},{2,26},{10... | collective-permute-start | bytes 221192 | tf_op jit(solution)/shard_map/ppermute | solution.py:998
  13.6 5.6 %collective-permute-start.4 = (f32[17,8,128]{2,1,0:T(8,128)S(1)}, f32[17,8,128]{2,1,0:T(8,128)S(1)}, u32[]{:S(2)}, u32[]{:S(2)}) collective-permute-start(f32[17,8,128]{2,1,0:T(8,128)S(1)} %get-tuple-element.50), channel_id=1, source_target_pairs={{0,2},{1,3},{2,0},{3,1},{4,6},{5,7},{6,4},{7,5},{8,10},{9,11},{10,... | collective-permute-start | bytes 208904 | tf_op jit(solution)/shard_map/ppermute | solution.py:65
  13.6 5.5 %collective-permute-start.5 = (f32[17,8,128]{2,1,0:T(8,128)S(1)}, f32[17,8,128]{2,1,0:T(8,128)S(1)}, u32[]{:S(2)}, u32[]{:S(2)}) collective-permute-start(f32[17,8,128]{2,1,0:T(8,128)S(1)} %get-tuple-element.51), channel_id=1, source_target_pairs={{0,1},{1,0},{2,4},{3,5},{4,2},{5,3},{6,7},{7,6},{8,9},{9,8},{10,12... | collective-permute-start | bytes 208904 | tf_op jit(solution)/shard_map/ppermute | solution.py:65
  15.3 6.6 %collective-permute-start.7 = (f32[8,2048]{1,0:T(8,128)S(1)}, f32[8,2048]{1,0:T(8,128)S(1)}, u32[]{:S(2)}, u32[]{:S(2)}) collective-permute-start(f32[8,2048]{1,0:T(8,128)S(1)} %get-tuple-element.56), channel_id=1, source_target_pairs={{0,16},{8,24},{16,0},{24,8},{1,17},{9,25},{17,1},{25,9},{2,18},{10... | collective-permute-start | bytes 196616 | tf_op jit(solution)/shard_map/ppermute | solution.py:998
  17.0 2.2 %copy-start.3 = (bf16[112,48]{1,0:T(8,128)(2,1)S(1)}, bf16[112,48]{1,0:T(8,128)(2,1)}, u32[]{:S(2)}) copy-start(bf16[112,48]{1,0:T(8,128)(2,1)} %constant.2.clone.refs_7_.refs_0_) | copy-start | bytes 32260
  17.0 4.9 %collective-permute-start.8 = (f32[8,2048]{1,0:T(8,128)S(1)}, f32[8,2048]{1,0:T(8,128)S(1)}, u32[]{:S(2)}, u32[]{:S(2)}) collective-permute-start(f32[8,2048]{1,0:T(8,128)S(1)} %get-tuple-element.57), channel_id=1, source_target_pairs={{0,8},{8,0},{16,24},{24,16},{1,9},{9,1},{17,25},{25,17},{2,10},{10... | collective-permute-start | bytes 196616 | tf_op jit(solution)/shard_map/ppermute | solution.py:998
  22.7 7.7 %collective-permute-start.9 = (f32[8,2432]{1,0:T(8,128)S(1)}, f32[8,2432]{1,0:T(8,128)S(1)}, u32[]{:S(2)}, u32[]{:S(2)}) collective-permute-start(f32[8,2432]{1,0:T(8,128)S(1)} %get-tuple-element.63), channel_id=1, source_target_pairs={{0,24},{8,16},{16,8},{24,0},{1,25},{9,17},{17,9},{25,1},{2,26},{10... | collective-permute-start | bytes 233480 | tf_op jit(solution)/shard_map/ppermute | solution.py:998
  24.7 6.8 %collective-permute-start.10 = (f32[8,2432]{1,0:T(8,128)S(1)}, f32[8,2432]{1,0:T(8,128)S(1)}, u32[]{:S(2)}, u32[]{:S(2)}) collective-permute-start(f32[8,2432]{1,0:T(8,128)S(1)} %get-tuple-element.64), channel_id=1, source_target_pairs={{0,16},{8,24},{16,0},{24,8},{1,17},{9,25},{17,1},{25,9},{2,18},{10... | collective-permute-start | bytes 233480 | tf_op jit(solution)/shard_map/ppermute | solution.py:998
  25.2 6.3 %collective-permute-start.11 = (f32[8,2432]{1,0:T(8,128)S(1)}, f32[8,2432]{1,0:T(8,128)S(1)}, u32[]{:S(2)}, u32[]{:S(2)}) collective-permute-start(f32[8,2432]{1,0:T(8,128)S(1)} %get-tuple-element.65), channel_id=1, source_target_pairs={{0,8},{8,0},{16,24},{24,16},{1,9},{9,1},{17,25},{25,17},{2,10},{10... | collective-permute-start | bytes 233480 | tf_op jit(solution)/shard_map/ppermute | solution.py:998

commit v11 on v10

--- a/solution.py
+++ b/solution.py
@@ -232,15 +232,11 @@
 
 
 def strips_kernel(
-    permit_ref, e_ref, h_ref, f_in, mat_ref, grad_ref, mask_ref, f_ref, low_ref, high_ref, wide_ref, inv_ref, sems
+    permit_ref, e_ref, h_ref, f_ref, mat_ref, grad_ref, mask_ref, low_ref, high_ref, wide_ref, inv_ref
 ):
     cells_z, width = e_ref.shape[1], e_ref.shape[3]
     layers = grad_ref.shape[0]
     blocks = mask_ref.shape[1]
-    copies = [pltpu.make_async_copy(f_in.at[c], f_ref.at[c], sems.at[c]) for c in range(3)]
-    for copy in copies:
-        copy.start()
-
     inverse = [
         jnp.broadcast_to(HALF * (1.0 / permit_ref[0:1, m : m + 1]), (ROWS, width))
         for m in range(permit_ref.shape[1])
@@ -264,8 +260,6 @@
                 tiles.append((lambda s, r=ref, c=c, z=z: r[c, z, :, s], width))
     pack_strips(tiles, low_ref, high_ref, 0)
 
-    for copy in copies:
-        copy.wait()
     done = len(tiles) // SLOTS
     tiles = []
     for layer in range(layers):
@@ -281,14 +275,13 @@
     cells_z, width = efield.shape[1], efield.shape[3]
     count = (cells_z * 6 + grad_sum.shape[0] * 6) // SLOTS
     packed = (count, ROWS, LANES)
-    shapes = (forward.shape, packed, packed, (ROWS, width), material.shape)
+    shapes = (packed, packed, (ROWS, width), material.shape)
     return pl.pallas_call(
         strips_kernel,
-        in_specs=[VMEM] * 3 + [ANY] + [VMEM] * 3,
-        out_specs=[VMEM] * 5,
+        in_specs=[VMEM] * 7,
+        out_specs=[VMEM] * 4,
         out_shape=[fast(*shape) for shape in shapes],
-        scratch_shapes=[pltpu.SemaphoreType.DMA((3,))],
-        compiler_params=params(40),
+        compiler_params=params(),
     )(permit.reshape(1, -1), efield, hfield, forward, material, grad_sum, mask)
 
 
@@ -616,7 +609,7 @@
 
     me = lax.axis_index("gx")
     for k, share in enumerate(shares):
-        chunk = lax.bitwise_xor(me, k)
+        chunk = lax.bitwise_xor(me, way_there(len(shares))[k])
         for i in range(per_device):
             share[:, i * width : (i + 1) * width] = own_ref[chunk * per_device + i]
         if share.shape[1] > per_device * width:
@@ -876,7 +869,7 @@
     half = count // 2
     rows = half * ROWS
     for k in range(count):
-        slabs[lax.bitwise_xor(me, k)] = got[k][:, : per_device * width]
+        slabs[lax.bitwise_xor(me, way_there(count)[k])] = got[k][:, : per_device * width]
 
     side = jnp.zeros((rows, LANES), jnp.float32)
     for i in range(per_device):
@@ -888,10 +881,10 @@
             own = total[s * ROWS : (s + 1) * ROWS, :width]
             done[s, :, here] = own
             done[count - 1 - s, :, here] = flip_rows(own)
-    for k in range(count):
-        outs[k][:, : per_device * width] = done[lax.bitwise_xor(me, k)]
+    for k, apart in enumerate(way_back(count)):
+        outs[k][:, : per_device * width] = done[lax.bitwise_xor(me, apart)]
         tail = per_device * width + edges_ref.shape[2]
-        outs[k][:, per_device * width : tail] = edges_ref[k]
+        outs[k][:, per_device * width : tail] = edges_ref[apart]
         outs[k][:, tail:] = line_ref[...]
 
 
@@ -942,9 +935,9 @@
     end = count * ROWS - 1
     row = lax.broadcasted_iota(jnp.int32, (ROWS, LANES), 0) + me * ROWS
     lines, near, far = [], [], []
-    for k in range(count):
+    for k, apart in enumerate(way_back(count)):
         lines.append(line_of(got[k][:, line_at:], width))
-        where = lax.bitwise_xor(me, k) * ROWS + spot
+        where = lax.bitwise_xor(me, apart) * ROWS + spot
         near.append((row - where).astype(jnp.float32))
         far.append((row - (end - where)).astype(jnp.float32))
     total = None
@@ -960,8 +953,8 @@
     line = total[:, :width]
 
     copies = []
-    for k in range(count):
-        first = lax.bitwise_xor(me, k) * per_device
+    for k, apart in enumerate(way_back(count)):
+        first = lax.bitwise_xor(me, apart) * per_device
         for i in range(per_device):
             at = i * width
             done[k, i] = got[k][:, at : at + width] + jnp.where(first + i == line_layer, line, 0.0)
@@ -991,24 +984,34 @@
     )(*parts[::-1])
 
 
-def spread(parts):
+def spread(parts, order):
     count = len(parts)
     got = list(parts)
-    for k in range(count - 1, 0, -1):
-        got[k] = lax.ppermute(parts[k], "gx", [(i, i ^ k) for i in range(count)])
+    for j in range(count - 1, 0, -1):
+        got[j] = lax.ppermute(parts[j], "gx", [(i, i ^ order[j]) for i in range(count)])
     return got
+
+
+def way_there(count):
+    return list(range(count))
+
+
+def way_back(count):
+    if count < 4:
+        return list(range(count))
+    return [0] + list(range(2, count - 1)) + [1, count - 1]
 
 
 def on_device(efield, hfield, forward, material, permit, design_mask, grad_sum):
     layers, _, width = grad_sum.shape
     efield, hfield, zfaces, xfaces, lines = halos(efield, hfield)
-    forward, own_low, own_high, mask, inv = strips(
+    own_low, own_high, mask, inv = strips(
         permit, efield, hfield, forward, material, grad_sum, design_mask
     )
     arrays = (efield, hfield, forward, inv, grad_sum, mask)
     edges = own_edges(arrays)
     shares, own = own_gradient(arrays, zfaces, xfaces)
-    got = spread(shares)
+    got = spread(shares, way_there(len(shares)))
     yfaces = exchange(y_faces(own_low, own_high, zfaces, xfaces, lines, own), "gy", "gz")
     taps = jnp.asarray(cone_matrix(len(got) // 2 * ROWS))
     added, line, edge = edge_gradient(own, arrays, edges, taps, zfaces, xfaces, lines, yfaces)
@@ -1016,7 +1019,7 @@
     e_next, h_next, grad_total = step(
         efield, hfield, inv, own, edge, line, zfaces, xfaces, lines, yfaces, parts[0]
     )
-    return e_next, h_next, grad_total, finish(spread(parts), layers, width)
+    return e_next, h_next, grad_total, finish(spread(parts, way_back(len(parts))), layers, width)
 
 
 def solution(mesh):

time: 32.7 us -> 31.8 us (0.972)
  Pallas kernels: 11 us -> 10.3 us
  starting transfers between devices: 17.1 us -> 16.5 us
  waiting for transfers between devices: 3.59 us -> 4.05 us
    ppermute x5, waiting for transfers between devices: 1.15 us -> 1.83 us  [exchange(): got.append(lax.ppermute(value, tuple(axes), pairs))]
    ppermute x6, starting transfers between devices: 10.5 us -> 9.86 us  [spread(): lax.ppermute(parts[j], 'gx', [(i, i ^ order[j]) for i in range(count)])]
    pallas_call x1, Pallas kernels: 1.24 us -> 0.56 us  [strips(): pl.pallas_call(strips_kernel, in_specs=[VMEM] * 7, out_specs=[VMEM] * 4,...]
  transfers between devices with their start and end apart: 12 -> 12, of which waited for: 3 -> 3; matrix products, arithmetic and copies ran while one was open for 0% -> 0% of each run, Pallas kernels for 23% -> 21%
where the time goes in v11:
time: 31.8 us; the launch traced here: 31.6 us
  starting transfers between devices  16.5 us (52%)
  Pallas kernels  10.3 us (32%)
  waiting for transfers between devices  4.05 us (13%)
  between operations  0.79 us (2%)
    ppermute x6, starting transfers between devices, spread(): lax.ppermute(parts[j], 'gx', [(i, i ^ order[j]) for i in range(count)])  9.86 us
    ppermute x5, starting transfers between devices, exchange(): got.append(lax.ppermute(value, tuple(axes), pairs))  6.36 us
    pallas_call x1, Pallas kernels, step(): pl.pallas_call(functools.partial(step_kernel, counts), in_specs=[VMEM] *...  3.25 us
    ppermute x6, waiting for transfers between devices, spread(): lax.ppermute(parts[j], 'gx', [(i, i ^ order[j]) for i in range(count)])  2.22 us
    pallas_call x1, Pallas kernels, halos(): pl.pallas_call(functools.partial(faces_kernel, x_rounds), in_specs=[ANY]...  1.87 us
    ppermute x5, waiting for transfers between devices, exchange(): got.append(lax.ppermute(value, tuple(axes), pairs))  1.83 us
    pallas_call x1, Pallas kernels, edge_gradient(): pl.pallas_call(functools.partial(edge_gradient_kernel, (len(zfaces), len(...  1.4 us
    pallas_call x1, Pallas kernels, finish(): pl.pallas_call(functools.partial(finish_kernel, count, per_device, width)...  0.97 us
  transfers between devices with their start and end apart: 12, of which 3 were waited for; matrix products, arithmetic and copies ran while one was open for 0% of the time, Pallas kernels for 21%

profile of v11, /device:TPU:0, one launch (start us, length us, event | category | flops | bytes accessed | tf_op | source)
XLA Modules:
  0.0 31.6 jit_solution(17761853263704363634)
XLA Ops:
  0.6 0.0 copy-start
  0.6 0.0 copy-start.1
  0.7 0.0 copy-start.5
  0.7 0.0 copy-start.4
  0.7 0.0 copy-start.2
  0.7 1.9 %shard_map.111 = (f32[3,24,8,512]{3,2,1,0:T(8,128)S(1)}, f32[3,24,8,512]{3,2,1,0:T(8,128)S(1)}, f32[56,512]{1,0:T(8,128)S(1)}, f32[56,512]{1,0:T(8,128)S(1)}, f3...) custom-call(f32[3,24,8,512]{3,2,1,0:T(8,128)} %e_in.1, f32[3,24,8,512]{3,2,1,0:T(8,128)} %h_in.1), custom_call_target="tpu_custom_call" | custom-call | tf_op jit(solution)/shard_map/pallas_call | solution.py:193
  2.6 3.1 %collective-permute-start.1 = (f32[56,512]{1,0:T(8,128)S(1)}, f32[56,512]{1,0:T(8,128)S(1)}, u32[]{:S(2)}, u32[]{:S(2)}) collective-permute-start(f32[56,512]{1,0:T(8,128)S(1)} %get-tuple-element.39), channel_id=1, source_target_pairs={{0,8},{2,10},{4,12},{6,14},{8,0},{10,2},{12,4},{14,6},{16,24},{18,... | collective-permute-start | bytes 344072 | tf_op jit(solution)/shard_map/ppermute | solution.py:65
  5.7 0.0 collective-permute-start.2
  5.7 1.5 %collective-permute-start = (f32[3,8,512]{2,1,0:T(8,128)S(1)}, f32[3,8,512]{2,1,0:T(8,128)S(1)}, u32[]{:S(2)}, u32[]{:S(2)}) collective-permute-start(f32[3,8,512]{2,1,0:T(8,128)S(1)} %get-tuple-element.38), channel_id=1, source_target_pairs={{0,1},{2,3},{4,5},{6,7},{1,0},{3,2},{5,4},{7,6},{8,9},{10,11},{12,... | collective-permute-start | bytes 147464 | tf_op jit(solution)/shard_map/ppermute | solution.py:65
  7.2 0.2 collective-permute-start.3
  7.4 0.0 copy-done
  7.4 0.0 copy-done.1
  7.4 0.0 copy-done.5
  7.4 0.0 copy-done.4
  7.4 0.0 copy-done.2
  7.4 0.6 %shard_map.112 = (f32[15,8,128]{2,1,0:T(8,128)S(1)}, f32[15,8,128]{2,1,0:T(8,128)S(1)}, f32[8,512]{1,0:T(8,128)S(1)}, f32[24,8,512]{2,1,0:T(8,128)S(1)}) custom-call(f32[1,4]{1,0:T(1,128)S(1)} %bitcast.1, f32[3,24,8,512]{3,2,1,0:T(8,128)S(1)} %get-tuple-element.34.e_ref.refs_0_, f32[3,24,8,512]{3,2,1,0:T(8,128)S(1)} %get-tuple-element.35.h_ref.refs_1_, ...), custom_call_target="tpu_custom_call" | custom-call | tf_op jit(solution)/shard_map/pallas_call | solution.py:279
  8.0 1.8 %collective-permute-done.refs_6_.refs_2_.refs_8_ = f32[3,8,512]{2,1,0:T(8,128)S(1)} collective-permute-done((f32[3,8,512]{2,1,0:T(8,128)S(1)}, f32[3,8,512]{2,1,0:T(8,128)S(1)}, u32[]{:S(2)}, u32[]{:S(2)}) %collective-permute-start) | collective-permute-done | bytes 49184 | tf_op jit(solution)/shard_map/ppermute | solution.py:65
  9.8 0.0 collective-permute-done.1.refs_7_.refs_3_.refs_9_
  9.8 0.0 collective-permute-done.2.refs_8_.refs_4_.refs_10_
  9.8 0.8 %shard_map.113 = (f32[8,2304]{1,0:T(8,128)S(1)}, f32[8,2048]{1,0:T(8,128)S(1)}, f32[8,2048]{1,0:T(8,128)S(1)}, f32[8,2048]{1,0:T(8,128)S(1)}, f32[16,8,512]{2,1,0:T(8,128)S(1)}) custom-call(f32[3,24,8,512]{3,2,1,0:T(8,128)S(1)} %get-tuple-element.34.e_ref.refs_0_, f32[3,24,8,512]{3,2,1,0:T(8,128)S(1)} %get-tuple-element.35.h_ref.refs_1_, ...), custom_call_target="tpu_custom_call" | custom-call | tf_op jit(solution)/shard_map/pallas_call | solution.py:626
  10.6 2.8 %collective-permute-start.6 = (f32[8,2304]{1,0:T(8,128)S(1)}, f32[8,2304]{1,0:T(8,128)S(1)}, u32[]{:S(2)}, u32[]{:S(2)}) collective-permute-start(f32[8,2304]{1,0:T(8,128)S(1)} %get-tuple-element.53), channel_id=1, source_target_pairs={{0,24},{8,16},{16,8},{24,0},{1,25},{9,17},{17,9},{25,1},{2,26},{10... | collective-permute-start | bytes 221192 | tf_op jit(solution)/shard_map/ppermute | solution.py:991
  13.4 0.0 collective-permute-done.3.refs_5_.refs_11_.refs_9_
  13.4 0.2 shard_map.115
  13.6 0.0 collective-permute-start.4
  13.6 1.7 %collective-permute-start.5 = (f32[17,8,128]{2,1,0:T(8,128)S(1)}, f32[17,8,128]{2,1,0:T(8,128)S(1)}, u32[]{:S(2)}, u32[]{:S(2)}) collective-permute-start(f32[17,8,128]{2,1,0:T(8,128)S(1)} %get-tuple-element.49), channel_id=1, source_target_pairs={{0,1},{1,0},{2,4},{3,5},{4,2},{5,3},{6,7},{7,6},{8,9},{9,8},{10,12... | collective-permute-start | bytes 208904 | tf_op jit(solution)/shard_map/ppermute | solution.py:65
  15.3 1.7 %collective-permute-start.7 = (f32[8,2048]{1,0:T(8,128)S(1)}, f32[8,2048]{1,0:T(8,128)S(1)}, u32[]{:S(2)}, u32[]{:S(2)}) collective-permute-start(f32[8,2048]{1,0:T(8,128)S(1)} %get-tuple-element.54), channel_id=1, source_target_pairs={{0,16},{8,24},{16,0},{24,8},{1,17},{9,25},{17,1},{25,9},{2,18},{10... | collective-permute-start | bytes 196616 | tf_op jit(solution)/shard_map/ppermute | solution.py:991
  17.0 0.0 copy-start.3
  17.0 0.9 %collective-permute-start.8 = (f32[8,2048]{1,0:T(8,128)S(1)}, f32[8,2048]{1,0:T(8,128)S(1)}, u32[]{:S(2)}, u32[]{:S(2)}) collective-permute-start(f32[8,2048]{1,0:T(8,128)S(1)} %get-tuple-element.55), channel_id=1, source_target_pairs={{0,8},{8,0},{16,24},{24,16},{1,9},{9,1},{17,25},{25,17},{2,10},{10... | collective-permute-start | bytes 196616 | tf_op jit(solution)/shard_map/ppermute | solution.py:991
  17.9 0.5 %shard_map.114 = (f32[24,6,8,128]{3,2,1,0:T(8,128)S(1)}, f32[16,5,8,128]{3,2,1,0:T(8,128)S(1)}, f32[8,128]{1,0:T(8,128)S(1)}) custom-call(f32[3,24,8,512]{3,2,1,0:T(8,128)S(1)} %get-tuple-element.34.e_ref.refs_0_, f32[3,24,8,512]{3,2,1,0:T(8,128)S(1)} %get-tuple-element.35.h_ref.refs_1_, f32[3,24,8,512]{3,2,1,0:T(8,128)S(1)} %copy-done, ...), custom_call_target="tpu_custom_call" | custom-call | tf_op jit(solution)/shard_map/pallas_call | solution.py:313
  18.5 0.0 collective-permute-done.4.refs_12_.refs_10_
  18.5 0.0 collective-permute-done.5.refs_13_.refs_11_
  18.5 0.0 copy-done.3
  18.5 1.4 %shard_map.116 = (f32[4,8,256]{2,1,0:T(8,128)S(1)}, f32[8,128]{1,0:T(8,128)S(1)}, f32[16,8,128]{2,1,0:T(8,128)S(1)}) custom-call(f32[16,8,512]{2,1,0:T(8,128)S(1)} %get-tuple-element.41.refs_6_.refs_0_.refs_3_, f32[3,24,8,512]{3,2,1,0:T(8,128)S(1)} %copy-done, f32[24,8,512]{2,1,0:T(8,128)S(1)} %get-tuple-element.36.refs_3_.inv_ref.refs_2_, ...), custom_call_target="tpu_custom_call" | custom-call | tf_op jit(solution)/shard_map/pallas_call | solution.py:731
  19.9 2.0 %collective-permute-done.7.refs_4_ = f32[8,2048]{1,0:T(8,128)S(1)} collective-permute-done((f32[8,2048]{1,0:T(8,128)S(1)}, f32[8,2048]{1,0:T(8,128)S(1)}, u32[]{:S(2)}, u32[]{:S(2)}) %collective-permute-start.7) | collective-permute-done | bytes 65568 | tf_op jit(solution)/shard_map/ppermute | solution.py:991
  21.9 0.0 collective-permute-done.8.refs_5_
  21.9 0.0 collective-permute-done.6.refs_3_
  21.9 0.8 %shard_map.117 = (f32[8,2432]{1,0:T(8,128)S(1)}, f32[8,2432]{1,0:T(8,128)S(1)}, f32[8,2432]{1,0:T(8,128)S(1)}, f32[8,2432]{1,0:T(8,128)S(1)}) custom-call(bf16[112,48]{1,0:T(8,128)(2,1)S(1)} %copy-done.3, f32[4,8,256]{2,1,0:T(8,128)S(1)} %get-tuple-element.52.refs_1_, f32[8,128]{1,0:T(8,128)S(1)} %get-tuple-element.51.refs_2_.refs_5_, ...), custom_call_target="tpu_custom_call" | custom-call | tf_op jit(solution)/shard_map/pallas_call | solution.py:894
  22.7 1.8 %collective-permute-start.9 = (f32[8,2432]{1,0:T(8,128)S(1)}, f32[8,2432]{1,0:T(8,128)S(1)}, u32[]{:S(2)}, u32[]{:S(2)}) collective-permute-start(f32[8,2432]{1,0:T(8,128)S(1)} %get-tuple-element.61), channel_id=1, source_target_pairs={{0,24},{8,16},{16,8},{24,0},{1,25},{9,17},{17,9},{25,1},{2,26},{10... | collective-permute-start | bytes 233480 | tf_op jit(solution)/shard_map/ppermute | solution.py:991
  24.5 0.1 collective-permute-start.10
  24.6 2.6 %collective-permute-start.11 = (f32[8,2432]{1,0:T(8,128)S(1)}, f32[8,2432]{1,0:T(8,128)S(1)}, u32[]{:S(2)}, u32[]{:S(2)}) collective-permute-start(f32[8,2432]{1,0:T(8,128)S(1)} %get-tuple-element.63), channel_id=1, source_target_pairs={{0,16},{8,24},{16,0},{24,8},{1,17},{9,25},{17,1},{25,9},{2,18},{10... | collective-permute-start | bytes 233480 | tf_op jit(solution)/shard_map/ppermute | solution.py:991
  27.2 3.3 %shard_map.118 = (f32[3,24,8,512]{3,2,1,0:T(8,128)}, f32[3,24,8,512]{3,2,1,0:T(8,128)}, f32[16,8,512]{2,1,0:T(8,128)}) custom-call(f32[3,24,8,512]{3,2,1,0:T(8,128)S(1)} %get-tuple-element.34.e_ref.refs_0_, f32[3,24,8,512]{3,2,1,0:T(8,128)S(1)} %get-tuple-element.35.h_ref.refs_1_, f32[24,8,512]{2,1,0:T(8,128)S(1)} %get-tuple-element.36.refs_3_.inv_ref.refs_2_, ...), custom_call_target="tpu_custom_call" | custom-call | tf_op jit(solution)/shard_map/pallas_call | solution.py:802
  30.4 0.0 collective-permute-done.9.refs_0_
  30.4 0.0 collective-permute-done.10.refs_1_
  30.4 0.2 collective-permute-done.11.refs_2_
  30.7 1.0 %shard_map.119 = f32[16,8,512]{2,1,0:T(8,128)} custom-call(f32[8,2432]{1,0:T(8,128)S(1)} %collective-permute-done.9.refs_0_, f32[8,2432]{1,0:T(8,128)S(1)} %collective-permute-done.10.refs_1_, f32[8,2432]{1,0:T(8,128)S(1)} %collective-permute-done.11.refs_2_, f32[8,2432]{1,0:T(8,128)S(1)} %get-tuple-element.57.refs_12_.refs_3_), custom_call_target="tpu_custom_call" | custom-call | tf_op jit(solution)/shard_map/pallas_call | solution.py:972
Async XLA Ops:
  0.6 6.8 %copy-start = (f32[3,24,8,512]{3,2,1,0:T(8,128)S(1)}, f32[3,24,8,512]{3,2,1,0:T(8,128)}, u32[]{:S(2)}) copy-start(f32[3,24,8,512]{3,2,1,0:T(8,128)} %refs_1_.1) | copy-start | bytes 3538948
  0.6 6.8 %copy-start.1 = (f32[16,8,512]{2,1,0:T(8,128)S(1)}, f32[16,8,512]{2,1,0:T(8,128)}, u32[]{:S(2)}) copy-start(f32[16,8,512]{2,1,0:T(8,128)} %grad_ref.3) | copy-start | bytes 786436
  0.7 6.8 %copy-start.5 = (s32[1,64]{1,0:T(1,128)S(1)}, s32[1,64]{1,0:T(1,128)}, u32[]{:S(2)}) copy-start(s32[1,64]{1,0:T(1,128)} %mask_ref.1) | copy-start | bytes 772
  0.7 6.8 %copy-start.4 = (f32[4]{0:T(128)S(1)}, f32[4]{0:T(128)}, u32[]{:S(2)}) copy-start(f32[4]{0:T(128)} %param.12) | copy-start | bytes 52
  0.7 6.7 %copy-start.2 = (s32[24,8,512]{2,1,0:T(8,128)S(1)}, s32[24,8,512]{2,1,0:T(8,128)}, u32[]{:S(2)}) copy-start(s32[24,8,512]{2,1,0:T(8,128)} %mat_ref.1) | copy-start | bytes 1179652
  2.6 7.2 %collective-permute-start.1 = (f32[56,512]{1,0:T(8,128)S(1)}, f32[56,512]{1,0:T(8,128)S(1)}, u32[]{:S(2)}, u32[]{:S(2)}) collective-permute-start(f32[56,512]{1,0:T(8,128)S(1)} %get-tuple-element.39), channel_id=1, source_target_pairs={{0,8},{2,10},{4,12},{6,14},{8,0},{10,2},{12,4},{14,6},{16,24},{18,... | collective-permute-start | bytes 344072 | tf_op jit(solution)/shard_map/ppermute | solution.py:65
  5.7 4.2 %collective-permute-start.2 = (f32[56,512]{1,0:T(8,128)S(1)}, f32[56,512]{1,0:T(8,128)S(1)}, u32[]{:S(2)}, u32[]{:S(2)}) collective-permute-start(f32[56,512]{1,0:T(8,128)S(1)} %get-tuple-element.40), channel_id=1, source_target_pairs={{0,2},{2,0},{4,6},{6,4},{8,16},{10,18},{12,20},{14,22},{16,8},{18,... | collective-permute-start | bytes 344072 | tf_op jit(solution)/shard_map/ppermute | solution.py:65
  5.7 4.2 %collective-permute-start = (f32[3,8,512]{2,1,0:T(8,128)S(1)}, f32[3,8,512]{2,1,0:T(8,128)S(1)}, u32[]{:S(2)}, u32[]{:S(2)}) collective-permute-start(f32[3,8,512]{2,1,0:T(8,128)S(1)} %get-tuple-element.38), channel_id=1, source_target_pairs={{0,1},{2,3},{4,5},{6,7},{1,0},{3,2},{5,4},{7,6},{8,9},{10,11},{12,... | collective-permute-start | bytes 147464 | tf_op jit(solution)/shard_map/ppermute | solution.py:65
  7.2 6.2 %collective-permute-start.3 = (f32[8,512]{1,0:T(8,128)S(1)}, f32[8,512]{1,0:T(8,128)S(1)}, u32[]{:S(2)}, u32[]{:S(2)}) collective-permute-start(f32[8,512]{1,0:T(8,128)S(1)} %get-tuple-element.45), channel_id=1, source_target_pairs={{0,2},{2,0},{4,6},{6,4},{1,8},{3,10},{5,12},{7,14},{8,1},{10,3},{1... | collective-permute-start | bytes 49160 | tf_op jit(solution)/shard_map/ppermute | solution.py:91
  10.6 11.3 %collective-permute-start.6 = (f32[8,2304]{1,0:T(8,128)S(1)}, f32[8,2304]{1,0:T(8,128)S(1)}, u32[]{:S(2)}, u32[]{:S(2)}) collective-permute-start(f32[8,2304]{1,0:T(8,128)S(1)} %get-tuple-element.53), channel_id=1, source_target_pairs={{0,24},{8,16},{16,8},{24,0},{1,25},{9,17},{17,9},{25,1},{2,26},{10... | collective-permute-start | bytes 221192 | tf_op jit(solution)/shard_map/ppermute | solution.py:991
  13.6 4.9 %collective-permute-start.4 = (f32[17,8,128]{2,1,0:T(8,128)S(1)}, f32[17,8,128]{2,1,0:T(8,128)S(1)}, u32[]{:S(2)}, u32[]{:S(2)}) collective-permute-start(f32[17,8,128]{2,1,0:T(8,128)S(1)} %get-tuple-element.48), channel_id=1, source_target_pairs={{0,2},{1,3},{2,0},{3,1},{4,6},{5,7},{6,4},{7,5},{8,10},{9,11},{10,... | collective-permute-start | bytes 208904 | tf_op jit(solution)/shard_map/ppermute | solution.py:65
  13.6 4.9 %collective-permute-start.5 = (f32[17,8,128]{2,1,0:T(8,128)S(1)}, f32[17,8,128]{2,1,0:T(8,128)S(1)}, u32[]{:S(2)}, u32[]{:S(2)}) collective-permute-start(f32[17,8,128]{2,1,0:T(8,128)S(1)} %get-tuple-element.49), channel_id=1, source_target_pairs={{0,1},{1,0},{2,4},{3,5},{4,2},{5,3},{6,7},{7,6},{8,9},{9,8},{10,12... | collective-permute-start | bytes 208904 | tf_op jit(solution)/shard_map/ppermute | solution.py:65
  15.3 6.6 %collective-permute-start.7 = (f32[8,2048]{1,0:T(8,128)S(1)}, f32[8,2048]{1,0:T(8,128)S(1)}, u32[]{:S(2)}, u32[]{:S(2)}) collective-permute-start(f32[8,2048]{1,0:T(8,128)S(1)} %get-tuple-element.54), channel_id=1, source_target_pairs={{0,16},{8,24},{16,0},{24,8},{1,17},{9,25},{17,1},{25,9},{2,18},{10... | collective-permute-start | bytes 196616 | tf_op jit(solution)/shard_map/ppermute | solution.py:991
  17.0 1.5 %copy-start.3 = (bf16[112,48]{1,0:T(8,128)(2,1)S(1)}, bf16[112,48]{1,0:T(8,128)(2,1)}, u32[]{:S(2)}) copy-start(bf16[112,48]{1,0:T(8,128)(2,1)} %constant.2.clone.refs_7_.refs_0_) | copy-start | bytes 32260
  17.0 4.9 %collective-permute-start.8 = (f32[8,2048]{1,0:T(8,128)S(1)}, f32[8,2048]{1,0:T(8,128)S(1)}, u32[]{:S(2)}, u32[]{:S(2)}) collective-permute-start(f32[8,2048]{1,0:T(8,128)S(1)} %get-tuple-element.55), channel_id=1, source_target_pairs={{0,8},{8,0},{16,24},{24,16},{1,9},{9,1},{17,25},{25,17},{2,10},{10... | collective-permute-start | bytes 196616 | tf_op jit(solution)/shard_map/ppermute | solution.py:991
  22.7 7.7 %collective-permute-start.9 = (f32[8,2432]{1,0:T(8,128)S(1)}, f32[8,2432]{1,0:T(8,128)S(1)}, u32[]{:S(2)}, u32[]{:S(2)}) collective-permute-start(f32[8,2432]{1,0:T(8,128)S(1)} %get-tuple-element.61), channel_id=1, source_target_pairs={{0,24},{8,16},{16,8},{24,0},{1,25},{9,17},{17,9},{25,1},{2,26},{10... | collective-permute-start | bytes 233480 | tf_op jit(solution)/shard_map/ppermute | solution.py:991
  24.5 5.9 %collective-permute-start.10 = (f32[8,2432]{1,0:T(8,128)S(1)}, f32[8,2432]{1,0:T(8,128)S(1)}, u32[]{:S(2)}, u32[]{:S(2)}) collective-permute-start(f32[8,2432]{1,0:T(8,128)S(1)} %get-tuple-element.62), channel_id=1, source_target_pairs={{0,8},{8,0},{16,24},{24,16},{1,9},{9,1},{17,25},{25,17},{2,10},{10... | collective-permute-start | bytes 233480 | tf_op jit(solution)/shard_map/ppermute | solution.py:991
  24.6 6.0 %collective-permute-start.11 = (f32[8,2432]{1,0:T(8,128)S(1)}, f32[8,2432]{1,0:T(8,128)S(1)}, u32[]{:S(2)}, u32[]{:S(2)}) collective-permute-start(f32[8,2432]{1,0:T(8,128)S(1)} %get-tuple-element.63), channel_id=1, source_target_pairs={{0,16},{8,24},{16,0},{24,8},{1,17},{9,25},{17,1},{25,9},{2,18},{10... | collective-permute-start | bytes 233480 | tf_op jit(solution)/shard_map/ppermute | solution.py:991

commit v12 on v11

--- a/solution.py
+++ b/solution.py
@@ -366,6 +366,17 @@
     return tiles
 
 
+FREE = 5
+
+
+def face_slot(index, layers, cells_z):
+    grad_base = 6 * cells_z // SLOTS
+    if index < FREE:
+        slot = 6 * (index + 1) + 5
+        return grad_base + slot // SLOTS, slot % SLOTS
+    return grad_base + 6 * layers // SLOTS + (index - FREE) // SLOTS, (index - FREE) % SLOTS
+
+
 def face_count(xface):
     per_field = (xface.shape[0] - ROWS) // ROWS // 2
     return 5 + 3 * per_field + 2 * per_field + 1
@@ -377,16 +388,26 @@
     zfaces, xfaces, lines = (refs[i:j] for i, j in zip(ends[:-1], ends[1:]))
     sends, (low_ref, high_ref) = refs[3 + sum(counts) : -2], refs[-2:]
     own = own_low.shape[0]
-    pack_strips(face_tiles(zfaces, xfaces, lines), low_ref, high_ref, 0)
+    tiles = face_tiles(zfaces, xfaces, lines)
+    pack_strips(tiles[FREE:], low_ref, high_ref, 0)
     side = Side("gy")
     for ref, value in zip(sends, side.sends(own_low[...], own_high[...])):
         ref[0:own] = value
+    group = lane_group()
+    cells_z = (xfaces[0].shape[0] - ROWS) // 2
+    layers = own * SLOTS // 6 - cells_z
+    for index, (load, width) in enumerate(tiles[:FREE]):
+        tile, k = face_slot(index, layers, cells_z)
+        low = pltpu.roll(load(slice(0, LANES)), STRIP * k, 1)
+        high = pltpu.roll(load(slice(width - LANES, width)), (STRIP * k + STRIP) % LANES, 1)
+        for ref, value in zip(sends, side.sends(low, high)):
+            ref[tile] = jnp.where(group == k, value, ref[tile])
     for ref, value in zip(sends, side.sends(low_ref[...], high_ref[...])):
         ref[own:] = value
 
 
 def y_faces(own_low, own_high, zfaces, xfaces, lines, after):
-    extra = math.ceil(face_count(xfaces[0]) / SLOTS)
+    extra = math.ceil((face_count(xfaces[0]) - FREE) / SLOTS)
     packed = fast(own_low.shape[0] + extra, ROWS, LANES)
     return pl.pallas_call(
         functools.partial(y_faces_kernel, (len(zfaces), len(xfaces), len(lines))),
@@ -419,7 +440,6 @@
         self.per_group = 6 * ROWS // SLOTS
         self.groups = self.cells_z // ROWS
         self.grad_base = self.per_group * self.groups
-        halo_base = self.grad_base + self.per_group * (layers // ROWS)
         self.left_wide, self.right_wide = left_wide, right_wide = scratch[:2]
         if mode != OWN:
             self.ybuf = scratch[2]
@@ -439,8 +459,8 @@
         def face(load, slot):
             if mode == EDGE:
                 own = edge_tile(load, self.width)
-                return self.edge(own, halo_base + slot // SLOTS, slot % SLOTS)
-            return self.wider(load, halo_base + slot // SLOTS, slot % SLOTS)
+                return self.edge(own, *face_slot(slot, layers, self.cells_z))
+            return self.wider(load, *face_slot(slot, layers, self.cells_z))
 
         full = [face(load, slot) for slot, (load, _) in enumerate(face_tiles(zfaces, xfaces, lines))]
         self.below, self.above = full[:3], full[3:5]
@@ -616,7 +636,7 @@
             share[:, per_device * width :] = jnp.zeros((ROWS, SPARE), jnp.float32)
 
 
-SPARE = 2 * LANES
+SPARE = LANES
 
 
 def own_gradient(arrays, zfaces, xfaces):

time: 31.8 us -> 31.8 us (level)
  no operation moved by 1% of the time
where the time goes in v12:
time: 31.8 us; the launch traced here: 31.6 us
  starting transfers between devices  16.5 us (52%)
  Pallas kernels  10.3 us (32%)
  waiting for transfers between devices  4.04 us (13%)
  between operations  0.79 us (2%)
    ppermute x6, starting transfers between devices, spread(): lax.ppermute(parts[j], 'gx', [(i, i ^ order[j]) for i in range(count)])  9.86 us
    ppermute x5, starting transfers between devices, exchange(): got.append(lax.ppermute(value, tuple(axes), pairs))  6.37 us
    pallas_call x1, Pallas kernels, step(): pl.pallas_call(functools.partial(step_kernel, counts), in_specs=[VMEM] *...  3.26 us
    ppermute x6, waiting for transfers between devices, spread(): lax.ppermute(parts[j], 'gx', [(i, i ^ order[j]) for i in range(count)])  2.21 us
    pallas_call x1, Pallas kernels, halos(): pl.pallas_call(functools.partial(faces_kernel, x_rounds), in_specs=[ANY]...  1.87 us
    ppermute x5, waiting for transfers between devices, exchange(): got.append(lax.ppermute(value, tuple(axes), pairs))  1.83 us
    pallas_call x1, Pallas kernels, edge_gradient(): pl.pallas_call(functools.partial(edge_gradient_kernel, (len(zfaces), len(...  1.4 us
    pallas_call x1, Pallas kernels, finish(): pl.pallas_call(functools.partial(finish_kernel, count, per_device, width)...  0.97 us
  transfers between devices with their start and end apart: 12, of which 3 were waited for; matrix products, arithmetic and copies ran while one was open for 0% of the time, Pallas kernels for 21%

profile of v12, /device:TPU:0, one launch (start us, length us, event | category | flops | bytes accessed | tf_op | source)
XLA Modules:
  0.0 31.6 jit_solution(10194752695083413095)
XLA Ops:
  0.6 0.0 copy-start
  0.6 0.0 copy-start.1
  0.7 0.0 copy-start.5
  0.7 0.0 copy-start.4
  0.7 0.0 copy-start.2
  0.7 1.9 %shard_map.111 = (f32[3,24,8,512]{3,2,1,0:T(8,128)S(1)}, f32[3,24,8,512]{3,2,1,0:T(8,128)S(1)}, f32[56,512]{1,0:T(8,128)S(1)}, f32[56,512]{1,0:T(8,128)S(1)}, f3...) custom-call(f32[3,24,8,512]{3,2,1,0:T(8,128)} %e_in.1, f32[3,24,8,512]{3,2,1,0:T(8,128)} %h_in.1), custom_call_target="tpu_custom_call" | custom-call | tf_op jit(solution)/shard_map/pallas_call | solution.py:193
  2.6 3.1 %collective-permute-start.1 = (f32[56,512]{1,0:T(8,128)S(1)}, f32[56,512]{1,0:T(8,128)S(1)}, u32[]{:S(2)}, u32[]{:S(2)}) collective-permute-start(f32[56,512]{1,0:T(8,128)S(1)} %get-tuple-element.39), channel_id=1, source_target_pairs={{0,8},{2,10},{4,12},{6,14},{8,0},{10,2},{12,4},{14,6},{16,24},{18,... | collective-permute-start | bytes 344072 | tf_op jit(solution)/shard_map/ppermute | solution.py:65
  5.7 0.0 collective-permute-start.2
  5.7 1.5 %collective-permute-start = (f32[3,8,512]{2,1,0:T(8,128)S(1)}, f32[3,8,512]{2,1,0:T(8,128)S(1)}, u32[]{:S(2)}, u32[]{:S(2)}) collective-permute-start(f32[3,8,512]{2,1,0:T(8,128)S(1)} %get-tuple-element.38), channel_id=1, source_target_pairs={{0,1},{2,3},{4,5},{6,7},{1,0},{3,2},{5,4},{7,6},{8,9},{10,11},{12,... | collective-permute-start | bytes 147464 | tf_op jit(solution)/shard_map/ppermute | solution.py:65
  7.2 0.2 collective-permute-start.3
  7.4 0.0 copy-done
  7.4 0.0 copy-done.1
  7.4 0.0 copy-done.5
  7.4 0.0 copy-done.4
  7.4 0.0 copy-done.2
  7.4 0.6 %shard_map.112 = (f32[15,8,128]{2,1,0:T(8,128)S(1)}, f32[15,8,128]{2,1,0:T(8,128)S(1)}, f32[8,512]{1,0:T(8,128)S(1)}, f32[24,8,512]{2,1,0:T(8,128)S(1)}) custom-call(f32[1,4]{1,0:T(1,128)S(1)} %bitcast.1, f32[3,24,8,512]{3,2,1,0:T(8,128)S(1)} %get-tuple-element.34.e_ref.refs_0_, f32[3,24,8,512]{3,2,1,0:T(8,128)S(1)} %get-tuple-element.35.h_ref.refs_1_, ...), custom_call_target="tpu_custom_call" | custom-call | tf_op jit(solution)/shard_map/pallas_call | solution.py:279
  8.0 1.8 %collective-permute-done.refs_6_.refs_2_.refs_8_ = f32[3,8,512]{2,1,0:T(8,128)S(1)} collective-permute-done((f32[3,8,512]{2,1,0:T(8,128)S(1)}, f32[3,8,512]{2,1,0:T(8,128)S(1)}, u32[]{:S(2)}, u32[]{:S(2)}) %collective-permute-start) | collective-permute-done | bytes 49184 | tf_op jit(solution)/shard_map/ppermute | solution.py:65
  9.8 0.0 collective-permute-done.1.refs_7_.refs_3_.refs_9_
  9.8 0.0 collective-permute-done.2.refs_8_.refs_4_.refs_10_
  9.8 0.8 %shard_map.113 = (f32[8,2176]{1,0:T(8,128)S(1)}, f32[8,2048]{1,0:T(8,128)S(1)}, f32[8,2048]{1,0:T(8,128)S(1)}, f32[8,2048]{1,0:T(8,128)S(1)}, f32[16,8,512]{2,1,0:T(8,128)S(1)}) custom-call(f32[3,24,8,512]{3,2,1,0:T(8,128)S(1)} %get-tuple-element.34.e_ref.refs_0_, f32[3,24,8,512]{3,2,1,0:T(8,128)S(1)} %get-tuple-element.35.h_ref.refs_1_, ...), custom_call_target="tpu_custom_call" | custom-call | tf_op jit(solution)/shard_map/pallas_call | solution.py:646
  10.6 2.8 %collective-permute-start.6 = (f32[8,2176]{1,0:T(8,128)S(1)}, f32[8,2176]{1,0:T(8,128)S(1)}, u32[]{:S(2)}, u32[]{:S(2)}) collective-permute-start(f32[8,2176]{1,0:T(8,128)S(1)} %get-tuple-element.53), channel_id=1, source_target_pairs={{0,24},{8,16},{16,8},{24,0},{1,25},{9,17},{17,9},{25,1},{2,26},{10... | collective-permute-start | bytes 208904 | tf_op jit(solution)/shard_map/ppermute | solution.py:1011
  13.4 0.0 collective-permute-done.3.refs_5_.refs_11_.refs_9_
  13.4 0.2 shard_map.115
  13.5 0.1 collective-permute-start.4
  13.6 1.7 %collective-permute-start.5 = (f32[16,8,128]{2,1,0:T(8,128)S(1)}, f32[16,8,128]{2,1,0:T(8,128)S(1)}, u32[]{:S(2)}, u32[]{:S(2)}) collective-permute-start(f32[16,8,128]{2,1,0:T(8,128)S(1)} %get-tuple-element.49), channel_id=1, source_target_pairs={{0,1},{1,0},{2,4},{3,5},{4,2},{5,3},{6,7},{7,6},{8,9},{9,8},{10,12... | collective-permute-start | bytes 196616 | tf_op jit(solution)/shard_map/ppermute | solution.py:65
  15.3 1.7 %collective-permute-start.7 = (f32[8,2048]{1,0:T(8,128)S(1)}, f32[8,2048]{1,0:T(8,128)S(1)}, u32[]{:S(2)}, u32[]{:S(2)}) collective-permute-start(f32[8,2048]{1,0:T(8,128)S(1)} %get-tuple-element.54), channel_id=1, source_target_pairs={{0,16},{8,24},{16,0},{24,8},{1,17},{9,25},{17,1},{25,9},{2,18},{10... | collective-permute-start | bytes 196616 | tf_op jit(solution)/shard_map/ppermute | solution.py:1011
  17.0 0.0 copy-start.3
  17.0 0.9 %collective-permute-start.8 = (f32[8,2048]{1,0:T(8,128)S(1)}, f32[8,2048]{1,0:T(8,128)S(1)}, u32[]{:S(2)}, u32[]{:S(2)}) collective-permute-start(f32[8,2048]{1,0:T(8,128)S(1)} %get-tuple-element.55), channel_id=1, source_target_pairs={{0,8},{8,0},{16,24},{24,16},{1,9},{9,1},{17,25},{25,17},{2,10},{10... | collective-permute-start | bytes 196616 | tf_op jit(solution)/shard_map/ppermute | solution.py:1011
  17.9 0.5 %shard_map.114 = (f32[24,6,8,128]{3,2,1,0:T(8,128)S(1)}, f32[16,5,8,128]{3,2,1,0:T(8,128)S(1)}, f32[8,128]{1,0:T(8,128)S(1)}) custom-call(f32[3,24,8,512]{3,2,1,0:T(8,128)S(1)} %get-tuple-element.34.e_ref.refs_0_, f32[3,24,8,512]{3,2,1,0:T(8,128)S(1)} %get-tuple-element.35.h_ref.refs_1_, f32[3,24,8,512]{3,2,1,0:T(8,128)S(1)} %copy-done, ...), custom_call_target="tpu_custom_call" | custom-call | tf_op jit(solution)/shard_map/pallas_call | solution.py:313
  18.5 0.0 collective-permute-done.4.refs_12_.refs_10_
  18.5 0.0 collective-permute-done.5.refs_13_.refs_11_
  18.5 0.0 copy-done.3
  18.5 1.4 %shard_map.116 = (f32[4,8,256]{2,1,0:T(8,128)S(1)}, f32[8,128]{1,0:T(8,128)S(1)}, f32[16,8,128]{2,1,0:T(8,128)S(1)}) custom-call(f32[16,8,512]{2,1,0:T(8,128)S(1)} %get-tuple-element.41.refs_6_.refs_0_.refs_3_, f32[3,24,8,512]{3,2,1,0:T(8,128)S(1)} %copy-done, f32[24,8,512]{2,1,0:T(8,128)S(1)} %get-tuple-element.36.refs_3_.inv_ref.refs_2_, ...), custom_call_target="tpu_custom_call" | custom-call | tf_op jit(solution)/shard_map/pallas_call | solution.py:751
  19.9 2.0 %collective-permute-done.7.refs_4_ = f32[8,2048]{1,0:T(8,128)S(1)} collective-permute-done((f32[8,2048]{1,0:T(8,128)S(1)}, f32[8,2048]{1,0:T(8,128)S(1)}, u32[]{:S(2)}, u32[]{:S(2)}) %collective-permute-start.7) | collective-permute-done | bytes 65568 | tf_op jit(solution)/shard_map/ppermute | solution.py:1011
  21.9 0.0 collective-permute-done.8.refs_5_
  21.9 0.0 collective-permute-done.6.refs_3_
  21.9 0.8 %shard_map.117 = (f32[8,2432]{1,0:T(8,128)S(1)}, f32[8,2432]{1,0:T(8,128)S(1)}, f32[8,2432]{1,0:T(8,128)S(1)}, f32[8,2432]{1,0:T(8,128)S(1)}) custom-call(bf16[112,48]{1,0:T(8,128)(2,1)S(1)} %copy-done.3, f32[4,8,256]{2,1,0:T(8,128)S(1)} %get-tuple-element.52.refs_1_, f32[8,128]{1,0:T(8,128)S(1)} %get-tuple-element.51.refs_2_.refs_5_, ...), custom_call_target="tpu_custom_call" | custom-call | tf_op jit(solution)/shard_map/pallas_call | solution.py:914
  22.7 1.8 %collective-permute-start.9 = (f32[8,2432]{1,0:T(8,128)S(1)}, f32[8,2432]{1,0:T(8,128)S(1)}, u32[]{:S(2)}, u32[]{:S(2)}) collective-permute-start(f32[8,2432]{1,0:T(8,128)S(1)} %get-tuple-element.61), channel_id=1, source_target_pairs={{0,24},{8,16},{16,8},{24,0},{1,25},{9,17},{17,9},{25,1},{2,26},{10... | collective-permute-start | bytes 233480 | tf_op jit(solution)/shard_map/ppermute | solution.py:1011
  24.5 0.1 collective-permute-start.10
  24.6 2.5 %collective-permute-start.11 = (f32[8,2432]{1,0:T(8,128)S(1)}, f32[8,2432]{1,0:T(8,128)S(1)}, u32[]{:S(2)}, u32[]{:S(2)}) collective-permute-start(f32[8,2432]{1,0:T(8,128)S(1)} %get-tuple-element.63), channel_id=1, source_target_pairs={{0,16},{8,24},{16,0},{24,8},{1,17},{9,25},{17,1},{25,9},{2,18},{10... | collective-permute-start | bytes 233480 | tf_op jit(solution)/shard_map/ppermute | solution.py:1011
  27.2 3.3 %shard_map.118 = (f32[3,24,8,512]{3,2,1,0:T(8,128)}, f32[3,24,8,512]{3,2,1,0:T(8,128)}, f32[16,8,512]{2,1,0:T(8,128)}) custom-call(f32[3,24,8,512]{3,2,1,0:T(8,128)S(1)} %get-tuple-element.34.e_ref.refs_0_, f32[3,24,8,512]{3,2,1,0:T(8,128)S(1)} %get-tuple-element.35.h_ref.refs_1_, f32[24,8,512]{2,1,0:T(8,128)S(1)} %get-tuple-element.36.refs_3_.inv_ref.refs_2_, ...), custom_call_target="tpu_custom_call" | custom-call | tf_op jit(solution)/shard_map/pallas_call | solution.py:822
  30.4 0.0 collective-permute-done.9.refs_0_
  30.4 0.0 collective-permute-done.10.refs_1_
  30.5 0.2 collective-permute-done.11.refs_2_
  30.7 1.0 %shard_map.119 = f32[16,8,512]{2,1,0:T(8,128)} custom-call(f32[8,2432]{1,0:T(8,128)S(1)} %collective-permute-done.9.refs_0_, f32[8,2432]{1,0:T(8,128)S(1)} %collective-permute-done.10.refs_1_, f32[8,2432]{1,0:T(8,128)S(1)} %collective-permute-done.11.refs_2_, f32[8,2432]{1,0:T(8,128)S(1)} %get-tuple-element.57.refs_12_.refs_3_), custom_call_target="tpu_custom_call" | custom-call | tf_op jit(solution)/shard_map/pallas_call | solution.py:992
Async XLA Ops:
  0.6 6.8 %copy-start = (f32[3,24,8,512]{3,2,1,0:T(8,128)S(1)}, f32[3,24,8,512]{3,2,1,0:T(8,128)}, u32[]{:S(2)}) copy-start(f32[3,24,8,512]{3,2,1,0:T(8,128)} %refs_1_.1) | copy-start | bytes 3538948
  0.6 6.8 %copy-start.1 = (f32[16,8,512]{2,1,0:T(8,128)S(1)}, f32[16,8,512]{2,1,0:T(8,128)}, u32[]{:S(2)}) copy-start(f32[16,8,512]{2,1,0:T(8,128)} %grad_ref.3) | copy-start | bytes 786436
  0.7 6.8 %copy-start.5 = (s32[1,64]{1,0:T(1,128)S(1)}, s32[1,64]{1,0:T(1,128)}, u32[]{:S(2)}) copy-start(s32[1,64]{1,0:T(1,128)} %mask_ref.1) | copy-start | bytes 772
  0.7 6.8 %copy-start.4 = (f32[4]{0:T(128)S(1)}, f32[4]{0:T(128)}, u32[]{:S(2)}) copy-start(f32[4]{0:T(128)} %param.12) | copy-start | bytes 52
  0.7 6.7 %copy-start.2 = (s32[24,8,512]{2,1,0:T(8,128)S(1)}, s32[24,8,512]{2,1,0:T(8,128)}, u32[]{:S(2)}) copy-start(s32[24,8,512]{2,1,0:T(8,128)} %mat_ref.1) | copy-start | bytes 1179652
  2.6 7.2 %collective-permute-start.1 = (f32[56,512]{1,0:T(8,128)S(1)}, f32[56,512]{1,0:T(8,128)S(1)}, u32[]{:S(2)}, u32[]{:S(2)}) collective-permute-start(f32[56,512]{1,0:T(8,128)S(1)} %get-tuple-element.39), channel_id=1, source_target_pairs={{0,8},{2,10},{4,12},{6,14},{8,0},{10,2},{12,4},{14,6},{16,24},{18,... | collective-permute-start | bytes 344072 | tf_op jit(solution)/shard_map/ppermute | solution.py:65
  5.7 4.2 %collective-permute-start.2 = (f32[56,512]{1,0:T(8,128)S(1)}, f32[56,512]{1,0:T(8,128)S(1)}, u32[]{:S(2)}, u32[]{:S(2)}) collective-permute-start(f32[56,512]{1,0:T(8,128)S(1)} %get-tuple-element.40), channel_id=1, source_target_pairs={{0,2},{2,0},{4,6},{6,4},{8,16},{10,18},{12,20},{14,22},{16,8},{18,... | collective-permute-start | bytes 344072 | tf_op jit(solution)/shard_map/ppermute | solution.py:65
  5.7 4.2 %collective-permute-start = (f32[3,8,512]{2,1,0:T(8,128)S(1)}, f32[3,8,512]{2,1,0:T(8,128)S(1)}, u32[]{:S(2)}, u32[]{:S(2)}) collective-permute-start(f32[3,8,512]{2,1,0:T(8,128)S(1)} %get-tuple-element.38), channel_id=1, source_target_pairs={{0,1},{2,3},{4,5},{6,7},{1,0},{3,2},{5,4},{7,6},{8,9},{10,11},{12,... | collective-permute-start | bytes 147464 | tf_op jit(solution)/shard_map/ppermute | solution.py:65
  7.2 6.2 %collective-permute-start.3 = (f32[8,512]{1,0:T(8,128)S(1)}, f32[8,512]{1,0:T(8,128)S(1)}, u32[]{:S(2)}, u32[]{:S(2)}) collective-permute-start(f32[8,512]{1,0:T(8,128)S(1)} %get-tuple-element.45), channel_id=1, source_target_pairs={{0,2},{2,0},{4,6},{6,4},{1,8},{3,10},{5,12},{7,14},{8,1},{10,3},{1... | collective-permute-start | bytes 49160 | tf_op jit(solution)/shard_map/ppermute | solution.py:91
  10.6 11.3 %collective-permute-start.6 = (f32[8,2176]{1,0:T(8,128)S(1)}, f32[8,2176]{1,0:T(8,128)S(1)}, u32[]{:S(2)}, u32[]{:S(2)}) collective-permute-start(f32[8,2176]{1,0:T(8,128)S(1)} %get-tuple-element.53), channel_id=1, source_target_pairs={{0,24},{8,16},{16,8},{24,0},{1,25},{9,17},{17,9},{25,1},{2,26},{10... | collective-permute-start | bytes 208904 | tf_op jit(solution)/shard_map/ppermute | solution.py:1011
  13.5 4.9 %collective-permute-start.4 = (f32[16,8,128]{2,1,0:T(8,128)S(1)}, f32[16,8,128]{2,1,0:T(8,128)S(1)}, u32[]{:S(2)}, u32[]{:S(2)}) collective-permute-start(f32[16,8,128]{2,1,0:T(8,128)S(1)} %get-tuple-element.48), channel_id=1, source_target_pairs={{0,2},{1,3},{2,0},{3,1},{4,6},{5,7},{6,4},{7,5},{8,10},{9,11},{10,... | collective-permute-start | bytes 196616 | tf_op jit(solution)/shard_map/ppermute | solution.py:65
  13.6 4.9 %collective-permute-start.5 = (f32[16,8,128]{2,1,0:T(8,128)S(1)}, f32[16,8,128]{2,1,0:T(8,128)S(1)}, u32[]{:S(2)}, u32[]{:S(2)}) collective-permute-start(f32[16,8,128]{2,1,0:T(8,128)S(1)} %get-tuple-element.49), channel_id=1, source_target_pairs={{0,1},{1,0},{2,4},{3,5},{4,2},{5,3},{6,7},{7,6},{8,9},{9,8},{10,12... | collective-permute-start | bytes 196616 | tf_op jit(solution)/shard_map/ppermute | solution.py:65
  15.3 6.6 %collective-permute-start.7 = (f32[8,2048]{1,0:T(8,128)S(1)}, f32[8,2048]{1,0:T(8,128)S(1)}, u32[]{:S(2)}, u32[]{:S(2)}) collective-permute-start(f32[8,2048]{1,0:T(8,128)S(1)} %get-tuple-element.54), channel_id=1, source_target_pairs={{0,16},{8,24},{16,0},{24,8},{1,17},{9,25},{17,1},{25,9},{2,18},{10... | collective-permute-start | bytes 196616 | tf_op jit(solution)/shard_map/ppermute | solution.py:1011
  17.0 1.5 %copy-start.3 = (bf16[112,48]{1,0:T(8,128)(2,1)S(1)}, bf16[112,48]{1,0:T(8,128)(2,1)}, u32[]{:S(2)}) copy-start(bf16[112,48]{1,0:T(8,128)(2,1)} %constant.2.clone.refs_7_.refs_0_) | copy-start | bytes 32260
  17.0 4.9 %collective-permute-start.8 = (f32[8,2048]{1,0:T(8,128)S(1)}, f32[8,2048]{1,0:T(8,128)S(1)}, u32[]{:S(2)}, u32[]{:S(2)}) collective-permute-start(f32[8,2048]{1,0:T(8,128)S(1)} %get-tuple-element.55), channel_id=1, source_target_pairs={{0,8},{8,0},{16,24},{24,16},{1,9},{9,1},{17,25},{25,17},{2,10},{10... | collective-permute-start | bytes 196616 | tf_op jit(solution)/shard_map/ppermute | solution.py:1011
  22.7 7.7 %collective-permute-start.9 = (f32[8,2432]{1,0:T(8,128)S(1)}, f32[8,2432]{1,0:T(8,128)S(1)}, u32[]{:S(2)}, u32[]{:S(2)}) collective-permute-start(f32[8,2432]{1,0:T(8,128)S(1)} %get-tuple-element.61), channel_id=1, source_target_pairs={{0,24},{8,16},{16,8},{24,0},{1,25},{9,17},{17,9},{25,1},{2,26},{10... | collective-permute-start | bytes 233480 | tf_op jit(solution)/shard_map/ppermute | solution.py:1011
  24.5 5.9 %collective-permute-start.10 = (f32[8,2432]{1,0:T(8,128)S(1)}, f32[8,2432]{1,0:T(8,128)S(1)}, u32[]{:S(2)}, u32[]{:S(2)}) collective-permute-start(f32[8,2432]{1,0:T(8,128)S(1)} %get-tuple-element.62), channel_id=1, source_target_pairs={{0,8},{8,0},{16,24},{24,16},{1,9},{9,1},{17,25},{25,17},{2,10},{10... | collective-permute-start | bytes 233480 | tf_op jit(solution)/shard_map/ppermute | solution.py:1011
  24.6 6.0 %collective-permute-start.11 = (f32[8,2432]{1,0:T(8,128)S(1)}, f32[8,2432]{1,0:T(8,128)S(1)}, u32[]{:S(2)}, u32[]{:S(2)}) collective-permute-start(f32[8,2432]{1,0:T(8,128)S(1)} %get-tuple-element.63), channel_id=1, source_target_pairs={{0,16},{8,24},{16,0},{24,8},{1,17},{9,25},{17,1},{25,9},{2,18},{10... | collective-permute-start | bytes 233480 | tf_op jit(solution)/shard_map/ppermute | solution.py:1011

commit v13 on v12

--- a/solution.py
+++ b/solution.py
@@ -130,7 +130,7 @@
         [pltpu.make_async_copy(source.at[c], target.at[c], sems.at[n, c]) for c in range(3)]
         for n, (source, target) in enumerate(((e_in, e_ref), (h_in, h_ref)))
     ]
-    for copy in copies[0] + copies[1]:
+    for copy in copies[0] + copies[1][1:] + copies[1][:1]:
         copy.start()
 
     low_ref[2 * cells_z :, :] = jnp.zeros_like(low_ref[2 * cells_z :, :])
@@ -144,7 +144,7 @@
             rows_ref[c, z : z + 1, :] = e_ref[c, z, last : last + 1, :]
         if z > 0:
             rows_ref[5, z - 1 : z, :] = e_ref[0, z, last : last + 1, :]
-    for copy in copies[1]:
+    for copy in copies[1][1:]:
         copy.wait()
     for z in range(cells_z):
         for c in range(2):
@@ -169,6 +169,7 @@
         for ref, one in zip(x_sends, side.sends(low_ref[here, :], value)):
             ref[here, :] = one
 
+    copies[1][0].wait()
     side = Side("gz")
     ex, ey, ez = (e_ref[c, top] for c in range(3))
     low = (e_ref[0, 0], e_ref[1, 0], jnp.zeros_like(ez))

time: 31.8 us -> 31.7 us (level)
  no operation moved by 1% of the time
where the time goes in v13:
time: 31.7 us; the launch traced here: 31.5 us
  starting transfers between devices  16.5 us (52%)
  Pallas kernels  10.2 us (32%)
  waiting for transfers between devices  4.05 us (13%)
  between operations  0.79 us (2%)
    ppermute x6, starting transfers between devices, spread(): lax.ppermute(parts[j], 'gx', [(i, i ^ order[j]) for i in range(count)])  9.86 us
    ppermute x5, starting transfers between devices, exchange(): got.append(lax.ppermute(value, tuple(axes), pairs))  6.37 us
    pallas_call x1, Pallas kernels, step(): pl.pallas_call(functools.partial(step_kernel, counts), in_specs=[VMEM] *...  3.26 us
    ppermute x6, waiting for transfers between devices, spread(): lax.ppermute(parts[j], 'gx', [(i, i ^ order[j]) for i in range(count)])  2.22 us
    ppermute x5, waiting for transfers between devices, exchange(): got.append(lax.ppermute(value, tuple(axes), pairs))  1.83 us
    pallas_call x1, Pallas kernels, halos(): pl.pallas_call(functools.partial(faces_kernel, x_rounds), in_specs=[ANY]...  1.78 us
    pallas_call x1, Pallas kernels, edge_gradient(): pl.pallas_call(functools.partial(edge_gradient_kernel, (len(zfaces), len(...  1.4 us
    pallas_call x1, Pallas kernels, finish(): pl.pallas_call(functools.partial(finish_kernel, count, per_device, width)...  0.97 us
  transfers between devices with their start and end apart: 12, of which 3 were waited for; matrix products, arithmetic and copies ran while one was open for 0% of the time, Pallas kernels for 21%

profile of v13, /device:TPU:0, one launch (start us, length us, event | category | flops | bytes accessed | tf_op | source)
XLA Modules:
  0.0 31.5 jit_solution(4832768902160183904)
XLA Ops:
  0.6 0.0 copy-start
  0.6 0.0 copy-start.1
  0.7 0.0 copy-start.5
  0.7 0.0 copy-start.4
  0.7 0.0 copy-start.2
  0.7 1.8 %shard_map.111 = (f32[3,24,8,512]{3,2,1,0:T(8,128)S(1)}, f32[3,24,8,512]{3,2,1,0:T(8,128)S(1)}, f32[56,512]{1,0:T(8,128)S(1)}, f32[56,512]{1,0:T(8,128)S(1)}, f3...) custom-call(f32[3,24,8,512]{3,2,1,0:T(8,128)} %e_in.1, f32[3,24,8,512]{3,2,1,0:T(8,128)} %h_in.1), custom_call_target="tpu_custom_call" | custom-call | tf_op jit(solution)/shard_map/pallas_call | solution.py:194
  2.5 3.1 %collective-permute-start.1 = (f32[56,512]{1,0:T(8,128)S(1)}, f32[56,512]{1,0:T(8,128)S(1)}, u32[]{:S(2)}, u32[]{:S(2)}) collective-permute-start(f32[56,512]{1,0:T(8,128)S(1)} %get-tuple-element.39), channel_id=1, source_target_pairs={{0,8},{2,10},{4,12},{6,14},{8,0},{10,2},{12,4},{14,6},{16,24},{18,... | collective-permute-start | bytes 344072 | tf_op jit(solution)/shard_map/ppermute | solution.py:65
  5.6 0.0 collective-permute-start.2
  5.6 1.5 %collective-permute-start = (f32[3,8,512]{2,1,0:T(8,128)S(1)}, f32[3,8,512]{2,1,0:T(8,128)S(1)}, u32[]{:S(2)}, u32[]{:S(2)}) collective-permute-start(f32[3,8,512]{2,1,0:T(8,128)S(1)} %get-tuple-element.38), channel_id=1, source_target_pairs={{0,1},{2,3},{4,5},{6,7},{1,0},{3,2},{5,4},{7,6},{8,9},{10,11},{12,... | collective-permute-start | bytes 147464 | tf_op jit(solution)/shard_map/ppermute | solution.py:65
  7.1 0.2 collective-permute-start.3
  7.3 0.0 copy-done
  7.3 0.0 copy-done.1
  7.3 0.0 copy-done.5
  7.3 0.0 copy-done.4
  7.3 0.0 copy-done.2
  7.3 0.6 %shard_map.112 = (f32[15,8,128]{2,1,0:T(8,128)S(1)}, f32[15,8,128]{2,1,0:T(8,128)S(1)}, f32[8,512]{1,0:T(8,128)S(1)}, f32[24,8,512]{2,1,0:T(8,128)S(1)}) custom-call(f32[1,4]{1,0:T(1,128)S(1)} %bitcast.1, f32[3,24,8,512]{3,2,1,0:T(8,128)S(1)} %get-tuple-element.34.e_ref.refs_0_, f32[3,24,8,512]{3,2,1,0:T(8,128)S(1)} %get-tuple-element.35.h_ref.refs_1_, ...), custom_call_target="tpu_custom_call" | custom-call | tf_op jit(solution)/shard_map/pallas_call | solution.py:280
  7.9 1.8 %collective-permute-done.refs_6_.refs_2_.refs_8_ = f32[3,8,512]{2,1,0:T(8,128)S(1)} collective-permute-done((f32[3,8,512]{2,1,0:T(8,128)S(1)}, f32[3,8,512]{2,1,0:T(8,128)S(1)}, u32[]{:S(2)}, u32[]{:S(2)}) %collective-permute-start) | collective-permute-done | bytes 49184 | tf_op jit(solution)/shard_map/ppermute | solution.py:65
  9.7 0.0 collective-permute-done.1.refs_7_.refs_3_.refs_9_
  9.7 0.0 collective-permute-done.2.refs_8_.refs_4_.refs_10_
  9.7 0.8 %shard_map.113 = (f32[8,2176]{1,0:T(8,128)S(1)}, f32[8,2048]{1,0:T(8,128)S(1)}, f32[8,2048]{1,0:T(8,128)S(1)}, f32[8,2048]{1,0:T(8,128)S(1)}, f32[16,8,512]{2,1,0:T(8,128)S(1)}) custom-call(f32[3,24,8,512]{3,2,1,0:T(8,128)S(1)} %get-tuple-element.34.e_ref.refs_0_, f32[3,24,8,512]{3,2,1,0:T(8,128)S(1)} %get-tuple-element.35.h_ref.refs_1_, ...), custom_call_target="tpu_custom_call" | custom-call | tf_op jit(solution)/shard_map/pallas_call | solution.py:647
  10.5 2.8 %collective-permute-start.6 = (f32[8,2176]{1,0:T(8,128)S(1)}, f32[8,2176]{1,0:T(8,128)S(1)}, u32[]{:S(2)}, u32[]{:S(2)}) collective-permute-start(f32[8,2176]{1,0:T(8,128)S(1)} %get-tuple-element.53), channel_id=1, source_target_pairs={{0,24},{8,16},{16,8},{24,0},{1,25},{9,17},{17,9},{25,1},{2,26},{10... | collective-permute-start | bytes 208904 | tf_op jit(solution)/shard_map/ppermute | solution.py:1012
  13.3 0.0 collective-permute-done.3.refs_5_.refs_11_.refs_9_
  13.3 0.2 shard_map.115
  13.5 0.1 collective-permute-start.4
  13.5 1.7 %collective-permute-start.5 = (f32[16,8,128]{2,1,0:T(8,128)S(1)}, f32[16,8,128]{2,1,0:T(8,128)S(1)}, u32[]{:S(2)}, u32[]{:S(2)}) collective-permute-start(f32[16,8,128]{2,1,0:T(8,128)S(1)} %get-tuple-element.49), channel_id=1, source_target_pairs={{0,1},{1,0},{2,4},{3,5},{4,2},{5,3},{6,7},{7,6},{8,9},{9,8},{10,12... | collective-permute-start | bytes 196616 | tf_op jit(solution)/shard_map/ppermute | solution.py:65
  15.2 1.7 %collective-permute-start.7 = (f32[8,2048]{1,0:T(8,128)S(1)}, f32[8,2048]{1,0:T(8,128)S(1)}, u32[]{:S(2)}, u32[]{:S(2)}) collective-permute-start(f32[8,2048]{1,0:T(8,128)S(1)} %get-tuple-element.54), channel_id=1, source_target_pairs={{0,16},{8,24},{16,0},{24,8},{1,17},{9,25},{17,1},{25,9},{2,18},{10... | collective-permute-start | bytes 196616 | tf_op jit(solution)/shard_map/ppermute | solution.py:1012
  16.9 0.0 copy-start.3
  16.9 0.9 %collective-permute-start.8 = (f32[8,2048]{1,0:T(8,128)S(1)}, f32[8,2048]{1,0:T(8,128)S(1)}, u32[]{:S(2)}, u32[]{:S(2)}) collective-permute-start(f32[8,2048]{1,0:T(8,128)S(1)} %get-tuple-element.55), channel_id=1, source_target_pairs={{0,8},{8,0},{16,24},{24,16},{1,9},{9,1},{17,25},{25,17},{2,10},{10... | collective-permute-start | bytes 196616 | tf_op jit(solution)/shard_map/ppermute | solution.py:1012
  17.8 0.5 %shard_map.114 = (f32[24,6,8,128]{3,2,1,0:T(8,128)S(1)}, f32[16,5,8,128]{3,2,1,0:T(8,128)S(1)}, f32[8,128]{1,0:T(8,128)S(1)}) custom-call(f32[3,24,8,512]{3,2,1,0:T(8,128)S(1)} %get-tuple-element.34.e_ref.refs_0_, f32[3,24,8,512]{3,2,1,0:T(8,128)S(1)} %get-tuple-element.35.h_ref.refs_1_, f32[3,24,8,512]{3,2,1,0:T(8,128)S(1)} %copy-done, ...), custom_call_target="tpu_custom_call" | custom-call | tf_op jit(solution)/shard_map/pallas_call | solution.py:314
  18.4 0.0 collective-permute-done.4.refs_12_.refs_10_
  18.4 0.0 collective-permute-done.5.refs_13_.refs_11_
  18.4 0.0 copy-done.3
  18.4 1.4 %shard_map.116 = (f32[4,8,256]{2,1,0:T(8,128)S(1)}, f32[8,128]{1,0:T(8,128)S(1)}, f32[16,8,128]{2,1,0:T(8,128)S(1)}) custom-call(f32[16,8,512]{2,1,0:T(8,128)S(1)} %get-tuple-element.41.refs_6_.refs_0_.refs_3_, f32[3,24,8,512]{3,2,1,0:T(8,128)S(1)} %copy-done, f32[24,8,512]{2,1,0:T(8,128)S(1)} %get-tuple-element.36.refs_3_.inv_ref.refs_2_, ...), custom_call_target="tpu_custom_call" | custom-call | tf_op jit(solution)/shard_map/pallas_call | solution.py:752
  19.8 2.0 %collective-permute-done.7.refs_4_ = f32[8,2048]{1,0:T(8,128)S(1)} collective-permute-done((f32[8,2048]{1,0:T(8,128)S(1)}, f32[8,2048]{1,0:T(8,128)S(1)}, u32[]{:S(2)}, u32[]{:S(2)}) %collective-permute-start.7) | collective-permute-done | bytes 65568 | tf_op jit(solution)/shard_map/ppermute | solution.py:1012
  21.8 0.0 collective-permute-done.8.refs_5_
  21.8 0.0 collective-permute-done.6.refs_3_
  21.8 0.8 %shard_map.117 = (f32[8,2432]{1,0:T(8,128)S(1)}, f32[8,2432]{1,0:T(8,128)S(1)}, f32[8,2432]{1,0:T(8,128)S(1)}, f32[8,2432]{1,0:T(8,128)S(1)}) custom-call(bf16[112,48]{1,0:T(8,128)(2,1)S(1)} %copy-done.3, f32[4,8,256]{2,1,0:T(8,128)S(1)} %get-tuple-element.52.refs_1_, f32[8,128]{1,0:T(8,128)S(1)} %get-tuple-element.51.refs_2_.refs_5_, ...), custom_call_target="tpu_custom_call" | custom-call | tf_op jit(solution)/shard_map/pallas_call | solution.py:915
  22.6 1.8 %collective-permute-start.9 = (f32[8,2432]{1,0:T(8,128)S(1)}, f32[8,2432]{1,0:T(8,128)S(1)}, u32[]{:S(2)}, u32[]{:S(2)}) collective-permute-start(f32[8,2432]{1,0:T(8,128)S(1)} %get-tuple-element.61), channel_id=1, source_target_pairs={{0,24},{8,16},{16,8},{24,0},{1,25},{9,17},{17,9},{25,1},{2,26},{10... | collective-permute-start | bytes 233480 | tf_op jit(solution)/shard_map/ppermute | solution.py:1012
  24.4 0.1 collective-permute-start.10
  24.5 2.5 %collective-permute-start.11 = (f32[8,2432]{1,0:T(8,128)S(1)}, f32[8,2432]{1,0:T(8,128)S(1)}, u32[]{:S(2)}, u32[]{:S(2)}) collective-permute-start(f32[8,2432]{1,0:T(8,128)S(1)} %get-tuple-element.63), channel_id=1, source_target_pairs={{0,16},{8,24},{16,0},{24,8},{1,17},{9,25},{17,1},{25,9},{2,18},{10... | collective-permute-start | bytes 233480 | tf_op jit(solution)/shard_map/ppermute | solution.py:1012
  27.1 3.3 %shard_map.118 = (f32[3,24,8,512]{3,2,1,0:T(8,128)}, f32[3,24,8,512]{3,2,1,0:T(8,128)}, f32[16,8,512]{2,1,0:T(8,128)}) custom-call(f32[3,24,8,512]{3,2,1,0:T(8,128)S(1)} %get-tuple-element.34.e_ref.refs_0_, f32[3,24,8,512]{3,2,1,0:T(8,128)S(1)} %get-tuple-element.35.h_ref.refs_1_, f32[24,8,512]{2,1,0:T(8,128)S(1)} %get-tuple-element.36.refs_3_.inv_ref.refs_2_, ...), custom_call_target="tpu_custom_call" | custom-call | tf_op jit(solution)/shard_map/pallas_call | solution.py:823
  30.3 0.0 collective-permute-done.9.refs_0_
  30.3 0.0 collective-permute-done.10.refs_1_
  30.4 0.2 collective-permute-done.11.refs_2_
  30.6 1.0 %shard_map.119 = f32[16,8,512]{2,1,0:T(8,128)} custom-call(f32[8,2432]{1,0:T(8,128)S(1)} %collective-permute-done.9.refs_0_, f32[8,2432]{1,0:T(8,128)S(1)} %collective-permute-done.10.refs_1_, f32[8,2432]{1,0:T(8,128)S(1)} %collective-permute-done.11.refs_2_, f32[8,2432]{1,0:T(8,128)S(1)} %get-tuple-element.57.refs_12_.refs_3_), custom_call_target="tpu_custom_call" | custom-call | tf_op jit(solution)/shard_map/pallas_call | solution.py:993
Async XLA Ops:
  0.6 6.7 %copy-start = (f32[3,24,8,512]{3,2,1,0:T(8,128)S(1)}, f32[3,24,8,512]{3,2,1,0:T(8,128)}, u32[]{:S(2)}) copy-start(f32[3,24,8,512]{3,2,1,0:T(8,128)} %refs_1_.1) | copy-start | bytes 3538948
  0.6 6.7 %copy-start.1 = (f32[16,8,512]{2,1,0:T(8,128)S(1)}, f32[16,8,512]{2,1,0:T(8,128)}, u32[]{:S(2)}) copy-start(f32[16,8,512]{2,1,0:T(8,128)} %grad_ref.3) | copy-start | bytes 786436
  0.7 6.7 %copy-start.5 = (s32[1,64]{1,0:T(1,128)S(1)}, s32[1,64]{1,0:T(1,128)}, u32[]{:S(2)}) copy-start(s32[1,64]{1,0:T(1,128)} %mask_ref.1) | copy-start | bytes 772
  0.7 6.7 %copy-start.4 = (f32[4]{0:T(128)S(1)}, f32[4]{0:T(128)}, u32[]{:S(2)}) copy-start(f32[4]{0:T(128)} %param.12) | copy-start | bytes 52
  0.7 6.7 %copy-start.2 = (s32[24,8,512]{2,1,0:T(8,128)S(1)}, s32[24,8,512]{2,1,0:T(8,128)}, u32[]{:S(2)}) copy-start(s32[24,8,512]{2,1,0:T(8,128)} %mat_ref.1) | copy-start | bytes 1179652
  2.5 7.2 %collective-permute-start.1 = (f32[56,512]{1,0:T(8,128)S(1)}, f32[56,512]{1,0:T(8,128)S(1)}, u32[]{:S(2)}, u32[]{:S(2)}) collective-permute-start(f32[56,512]{1,0:T(8,128)S(1)} %get-tuple-element.39), channel_id=1, source_target_pairs={{0,8},{2,10},{4,12},{6,14},{8,0},{10,2},{12,4},{14,6},{16,24},{18,... | collective-permute-start | bytes 344072 | tf_op jit(solution)/shard_map/ppermute | solution.py:65
  5.6 4.2 %collective-permute-start.2 = (f32[56,512]{1,0:T(8,128)S(1)}, f32[56,512]{1,0:T(8,128)S(1)}, u32[]{:S(2)}, u32[]{:S(2)}) collective-permute-start(f32[56,512]{1,0:T(8,128)S(1)} %get-tuple-element.40), channel_id=1, source_target_pairs={{0,2},{2,0},{4,6},{6,4},{8,16},{10,18},{12,20},{14,22},{16,8},{18,... | collective-permute-start | bytes 344072 | tf_op jit(solution)/shard_map/ppermute | solution.py:65
  5.6 4.2 %collective-permute-start = (f32[3,8,512]{2,1,0:T(8,128)S(1)}, f32[3,8,512]{2,1,0:T(8,128)S(1)}, u32[]{:S(2)}, u32[]{:S(2)}) collective-permute-start(f32[3,8,512]{2,1,0:T(8,128)S(1)} %get-tuple-element.38), channel_id=1, source_target_pairs={{0,1},{2,3},{4,5},{6,7},{1,0},{3,2},{5,4},{7,6},{8,9},{10,11},{12,... | collective-permute-start | bytes 147464 | tf_op jit(solution)/shard_map/ppermute | solution.py:65
  7.1 6.2 %collective-permute-start.3 = (f32[8,512]{1,0:T(8,128)S(1)}, f32[8,512]{1,0:T(8,128)S(1)}, u32[]{:S(2)}, u32[]{:S(2)}) collective-permute-start(f32[8,512]{1,0:T(8,128)S(1)} %get-tuple-element.45), channel_id=1, source_target_pairs={{0,2},{2,0},{4,6},{6,4},{1,8},{3,10},{5,12},{7,14},{8,1},{10,3},{1... | collective-permute-start | bytes 49160 | tf_op jit(solution)/shard_map/ppermute | solution.py:91
  10.5 11.3 %collective-permute-start.6 = (f32[8,2176]{1,0:T(8,128)S(1)}, f32[8,2176]{1,0:T(8,128)S(1)}, u32[]{:S(2)}, u32[]{:S(2)}) collective-permute-start(f32[8,2176]{1,0:T(8,128)S(1)} %get-tuple-element.53), channel_id=1, source_target_pairs={{0,24},{8,16},{16,8},{24,0},{1,25},{9,17},{17,9},{25,1},{2,26},{10... | collective-permute-start | bytes 208904 | tf_op jit(solution)/shard_map/ppermute | solution.py:1012
  13.5 4.9 %collective-permute-start.4 = (f32[16,8,128]{2,1,0:T(8,128)S(1)}, f32[16,8,128]{2,1,0:T(8,128)S(1)}, u32[]{:S(2)}, u32[]{:S(2)}) collective-permute-start(f32[16,8,128]{2,1,0:T(8,128)S(1)} %get-tuple-element.48), channel_id=1, source_target_pairs={{0,2},{1,3},{2,0},{3,1},{4,6},{5,7},{6,4},{7,5},{8,10},{9,11},{10,... | collective-permute-start | bytes 196616 | tf_op jit(solution)/shard_map/ppermute | solution.py:65
  13.5 4.9 %collective-permute-start.5 = (f32[16,8,128]{2,1,0:T(8,128)S(1)}, f32[16,8,128]{2,1,0:T(8,128)S(1)}, u32[]{:S(2)}, u32[]{:S(2)}) collective-permute-start(f32[16,8,128]{2,1,0:T(8,128)S(1)} %get-tuple-element.49), channel_id=1, source_target_pairs={{0,1},{1,0},{2,4},{3,5},{4,2},{5,3},{6,7},{7,6},{8,9},{9,8},{10,12... | collective-permute-start | bytes 196616 | tf_op jit(solution)/shard_map/ppermute | solution.py:65
  15.2 6.6 %collective-permute-start.7 = (f32[8,2048]{1,0:T(8,128)S(1)}, f32[8,2048]{1,0:T(8,128)S(1)}, u32[]{:S(2)}, u32[]{:S(2)}) collective-permute-start(f32[8,2048]{1,0:T(8,128)S(1)} %get-tuple-element.54), channel_id=1, source_target_pairs={{0,16},{8,24},{16,0},{24,8},{1,17},{9,25},{17,1},{25,9},{2,18},{10... | collective-permute-start | bytes 196616 | tf_op jit(solution)/shard_map/ppermute | solution.py:1012
  16.9 1.5 %copy-start.3 = (bf16[112,48]{1,0:T(8,128)(2,1)S(1)}, bf16[112,48]{1,0:T(8,128)(2,1)}, u32[]{:S(2)}) copy-start(bf16[112,48]{1,0:T(8,128)(2,1)} %constant.2.clone.refs_7_.refs_0_) | copy-start | bytes 32260
  16.9 4.9 %collective-permute-start.8 = (f32[8,2048]{1,0:T(8,128)S(1)}, f32[8,2048]{1,0:T(8,128)S(1)}, u32[]{:S(2)}, u32[]{:S(2)}) collective-permute-start(f32[8,2048]{1,0:T(8,128)S(1)} %get-tuple-element.55), channel_id=1, source_target_pairs={{0,8},{8,0},{16,24},{24,16},{1,9},{9,1},{17,25},{25,17},{2,10},{10... | collective-permute-start | bytes 196616 | tf_op jit(solution)/shard_map/ppermute | solution.py:1012
  22.6 7.7 %collective-permute-start.9 = (f32[8,2432]{1,0:T(8,128)S(1)}, f32[8,2432]{1,0:T(8,128)S(1)}, u32[]{:S(2)}, u32[]{:S(2)}) collective-permute-start(f32[8,2432]{1,0:T(8,128)S(1)} %get-tuple-element.61), channel_id=1, source_target_pairs={{0,24},{8,16},{16,8},{24,0},{1,25},{9,17},{17,9},{25,1},{2,26},{10... | collective-permute-start | bytes 233480 | tf_op jit(solution)/shard_map/ppermute | solution.py:1012
  24.4 5.9 %collective-permute-start.10 = (f32[8,2432]{1,0:T(8,128)S(1)}, f32[8,2432]{1,0:T(8,128)S(1)}, u32[]{:S(2)}, u32[]{:S(2)}) collective-permute-start(f32[8,2432]{1,0:T(8,128)S(1)} %get-tuple-element.62), channel_id=1, source_target_pairs={{0,8},{8,0},{16,24},{24,16},{1,9},{9,1},{17,25},{25,17},{2,10},{10... | collective-permute-start | bytes 233480 | tf_op jit(solution)/shard_map/ppermute | solution.py:1012
  24.5 6.1 %collective-permute-start.11 = (f32[8,2432]{1,0:T(8,128)S(1)}, f32[8,2432]{1,0:T(8,128)S(1)}, u32[]{:S(2)}, u32[]{:S(2)}) collective-permute-start(f32[8,2432]{1,0:T(8,128)S(1)} %get-tuple-element.63), channel_id=1, source_target_pairs={{0,16},{8,24},{16,0},{24,8},{1,17},{9,25},{17,1},{25,9},{2,18},{10... | collective-permute-start | bytes 233480 | tf_op jit(solution)/shard_map/ppermute | solution.py:1012

commit v14 on v13

--- a/solution.py
+++ b/solution.py
@@ -130,18 +130,21 @@
         [pltpu.make_async_copy(source.at[c], target.at[c], sems.at[n, c]) for c in range(3)]
         for n, (source, target) in enumerate(((e_in, e_ref), (h_in, h_ref)))
     ]
-    for copy in copies[0] + copies[1][1:] + copies[1][:1]:
+    for copy in copies[0][1:] + copies[0][:1] + copies[1][1:] + copies[1][:1]:
         copy.start()
 
     low_ref[2 * cells_z :, :] = jnp.zeros_like(low_ref[2 * cells_z :, :])
     rows_ref[5, top : top + 1, :] = jnp.zeros_like(rows_ref[5, top : top + 1, :])
-    for copy in copies[0]:
+    for copy in copies[0][1:]:
         copy.wait()
     for z in range(cells_z):
         low_ref[z : z + 1, :] = e_ref[1, z, 0:1, :]
         low_ref[cells_z + z : cells_z + z + 1, :] = e_ref[2, z, 0:1, :]
-        for c in range(3):
+        for c in range(1, 3):
             rows_ref[c, z : z + 1, :] = e_ref[c, z, last : last + 1, :]
+    copies[0][0].wait()
+    for z in range(cells_z):
+        rows_ref[0, z : z + 1, :] = e_ref[0, z, last : last + 1, :]
         if z > 0:
             rows_ref[5, z - 1 : z, :] = e_ref[0, z, last : last + 1, :]
     for copy in copies[1][1:]:

time: 31.7 us -> 31.7 us (level)
  no operation moved by 1% of the time
where the time goes in v14:
time: 31.7 us; the launch traced here: 31.5 us
  starting transfers between devices  16.5 us (52%)
  Pallas kernels  10.2 us (32%)
  waiting for transfers between devices  4.05 us (13%)
  between operations  0.79 us (2%)
    ppermute x6, starting transfers between devices, spread(): lax.ppermute(parts[j], 'gx', [(i, i ^ order[j]) for i in range(count)])  9.86 us
    ppermute x5, starting transfers between devices, exchange(): got.append(lax.ppermute(value, tuple(axes), pairs))  6.37 us
    pallas_call x1, Pallas kernels, step(): pl.pallas_call(functools.partial(step_kernel, counts), in_specs=[VMEM] *...  3.26 us
    ppermute x6, waiting for transfers between devices, spread(): lax.ppermute(parts[j], 'gx', [(i, i ^ order[j]) for i in range(count)])  2.22 us
    ppermute x5, waiting for transfers between devices, exchange(): got.append(lax.ppermute(value, tuple(axes), pairs))  1.83 us
    pallas_call x1, Pallas kernels, halos(): pl.pallas_call(functools.partial(faces_kernel, x_rounds), in_specs=[ANY]...  1.78 us
    pallas_call x1, Pallas kernels, edge_gradient(): pl.pallas_call(functools.partial(edge_gradient_kernel, (len(zfaces), len(...  1.4 us
    pallas_call x1, Pallas kernels, finish(): pl.pallas_call(functools.partial(finish_kernel, count, per_device, width)...  0.97 us
  transfers between devices with their start and end apart: 12, of which 3 were waited for; matrix products, arithmetic and copies ran while one was open for 0% of the time, Pallas kernels for 21%

profile of v14, /device:TPU:0, one launch (start us, length us, event | category | flops | bytes accessed | tf_op | source)
XLA Modules:
  0.0 31.5 jit_solution(6916608180934931354)
XLA Ops:
  0.6 0.0 copy-start
  0.6 0.0 copy-start.1
  0.7 0.0 copy-start.5
  0.7 0.0 copy-start.4
  0.7 0.0 copy-start.2
  0.7 1.8 %shard_map.111 = (f32[3,24,8,512]{3,2,1,0:T(8,128)S(1)}, f32[3,24,8,512]{3,2,1,0:T(8,128)S(1)}, f32[56,512]{1,0:T(8,128)S(1)}, f32[56,512]{1,0:T(8,128)S(1)}, f3...) custom-call(f32[3,24,8,512]{3,2,1,0:T(8,128)} %e_in.1, f32[3,24,8,512]{3,2,1,0:T(8,128)} %h_in.1), custom_call_target="tpu_custom_call" | custom-call | tf_op jit(solution)/shard_map/pallas_call | solution.py:197
  2.5 3.1 %collective-permute-start.1 = (f32[56,512]{1,0:T(8,128)S(1)}, f32[56,512]{1,0:T(8,128)S(1)}, u32[]{:S(2)}, u32[]{:S(2)}) collective-permute-start(f32[56,512]{1,0:T(8,128)S(1)} %get-tuple-element.39), channel_id=1, source_target_pairs={{0,8},{2,10},{4,12},{6,14},{8,0},{10,2},{12,4},{14,6},{16,24},{18,... | collective-permute-start | bytes 344072 | tf_op jit(solution)/shard_map/ppermute | solution.py:65
  5.6 0.0 collective-permute-start.2
  5.6 1.5 %collective-permute-start = (f32[3,8,512]{2,1,0:T(8,128)S(1)}, f32[3,8,512]{2,1,0:T(8,128)S(1)}, u32[]{:S(2)}, u32[]{:S(2)}) collective-permute-start(f32[3,8,512]{2,1,0:T(8,128)S(1)} %get-tuple-element.38), channel_id=1, source_target_pairs={{0,1},{2,3},{4,5},{6,7},{1,0},{3,2},{5,4},{7,6},{8,9},{10,11},{12,... | collective-permute-start | bytes 147464 | tf_op jit(solution)/shard_map/ppermute | solution.py:65
  7.1 0.2 collective-permute-start.3
  7.3 0.0 copy-done
  7.3 0.0 copy-done.1
  7.3 0.0 copy-done.5
  7.3 0.0 copy-done.4
  7.3 0.0 copy-done.2
  7.3 0.6 %shard_map.112 = (f32[15,8,128]{2,1,0:T(8,128)S(1)}, f32[15,8,128]{2,1,0:T(8,128)S(1)}, f32[8,512]{1,0:T(8,128)S(1)}, f32[24,8,512]{2,1,0:T(8,128)S(1)}) custom-call(f32[1,4]{1,0:T(1,128)S(1)} %bitcast.1, f32[3,24,8,512]{3,2,1,0:T(8,128)S(1)} %get-tuple-element.34.e_ref.refs_0_, f32[3,24,8,512]{3,2,1,0:T(8,128)S(1)} %get-tuple-element.35.h_ref.refs_1_, ...), custom_call_target="tpu_custom_call" | custom-call | tf_op jit(solution)/shard_map/pallas_call | solution.py:283
  7.9 1.8 %collective-permute-done.refs_6_.refs_2_.refs_8_ = f32[3,8,512]{2,1,0:T(8,128)S(1)} collective-permute-done((f32[3,8,512]{2,1,0:T(8,128)S(1)}, f32[3,8,512]{2,1,0:T(8,128)S(1)}, u32[]{:S(2)}, u32[]{:S(2)}) %collective-permute-start) | collective-permute-done | bytes 49184 | tf_op jit(solution)/shard_map/ppermute | solution.py:65
  9.7 0.0 collective-permute-done.1.refs_7_.refs_3_.refs_9_
  9.7 0.0 collective-permute-done.2.refs_8_.refs_4_.refs_10_
  9.7 0.8 %shard_map.113 = (f32[8,2176]{1,0:T(8,128)S(1)}, f32[8,2048]{1,0:T(8,128)S(1)}, f32[8,2048]{1,0:T(8,128)S(1)}, f32[8,2048]{1,0:T(8,128)S(1)}, f32[16,8,512]{2,1,0:T(8,128)S(1)}) custom-call(f32[3,24,8,512]{3,2,1,0:T(8,128)S(1)} %get-tuple-element.34.e_ref.refs_0_, f32[3,24,8,512]{3,2,1,0:T(8,128)S(1)} %get-tuple-element.35.h_ref.refs_1_, ...), custom_call_target="tpu_custom_call" | custom-call | tf_op jit(solution)/shard_map/pallas_call | solution.py:650
  10.5 2.8 %collective-permute-start.6 = (f32[8,2176]{1,0:T(8,128)S(1)}, f32[8,2176]{1,0:T(8,128)S(1)}, u32[]{:S(2)}, u32[]{:S(2)}) collective-permute-start(f32[8,2176]{1,0:T(8,128)S(1)} %get-tuple-element.53), channel_id=1, source_target_pairs={{0,24},{8,16},{16,8},{24,0},{1,25},{9,17},{17,9},{25,1},{2,26},{10... | collective-permute-start | bytes 208904 | tf_op jit(solution)/shard_map/ppermute | solution.py:1015
  13.3 0.0 collective-permute-done.3.refs_5_.refs_11_.refs_9_
  13.3 0.2 shard_map.115
  13.5 0.1 collective-permute-start.4
  13.5 1.7 %collective-permute-start.5 = (f32[16,8,128]{2,1,0:T(8,128)S(1)}, f32[16,8,128]{2,1,0:T(8,128)S(1)}, u32[]{:S(2)}, u32[]{:S(2)}) collective-permute-start(f32[16,8,128]{2,1,0:T(8,128)S(1)} %get-tuple-element.49), channel_id=1, source_target_pairs={{0,1},{1,0},{2,4},{3,5},{4,2},{5,3},{6,7},{7,6},{8,9},{9,8},{10,12... | collective-permute-start | bytes 196616 | tf_op jit(solution)/shard_map/ppermute | solution.py:65
  15.2 1.7 %collective-permute-start.7 = (f32[8,2048]{1,0:T(8,128)S(1)}, f32[8,2048]{1,0:T(8,128)S(1)}, u32[]{:S(2)}, u32[]{:S(2)}) collective-permute-start(f32[8,2048]{1,0:T(8,128)S(1)} %get-tuple-element.54), channel_id=1, source_target_pairs={{0,16},{8,24},{16,0},{24,8},{1,17},{9,25},{17,1},{25,9},{2,18},{10... | collective-permute-start | bytes 196616 | tf_op jit(solution)/shard_map/ppermute | solution.py:1015
  16.9 0.0 copy-start.3
  16.9 0.9 %collective-permute-start.8 = (f32[8,2048]{1,0:T(8,128)S(1)}, f32[8,2048]{1,0:T(8,128)S(1)}, u32[]{:S(2)}, u32[]{:S(2)}) collective-permute-start(f32[8,2048]{1,0:T(8,128)S(1)} %get-tuple-element.55), channel_id=1, source_target_pairs={{0,8},{8,0},{16,24},{24,16},{1,9},{9,1},{17,25},{25,17},{2,10},{10... | collective-permute-start | bytes 196616 | tf_op jit(solution)/shard_map/ppermute | solution.py:1015
  17.8 0.5 %shard_map.114 = (f32[24,6,8,128]{3,2,1,0:T(8,128)S(1)}, f32[16,5,8,128]{3,2,1,0:T(8,128)S(1)}, f32[8,128]{1,0:T(8,128)S(1)}) custom-call(f32[3,24,8,512]{3,2,1,0:T(8,128)S(1)} %get-tuple-element.34.e_ref.refs_0_, f32[3,24,8,512]{3,2,1,0:T(8,128)S(1)} %get-tuple-element.35.h_ref.refs_1_, f32[3,24,8,512]{3,2,1,0:T(8,128)S(1)} %copy-done, ...), custom_call_target="tpu_custom_call" | custom-call | tf_op jit(solution)/shard_map/pallas_call | solution.py:317
  18.4 0.0 collective-permute-done.4.refs_12_.refs_10_
  18.4 0.0 collective-permute-done.5.refs_13_.refs_11_
  18.4 0.0 copy-done.3
  18.4 1.4 %shard_map.116 = (f32[4,8,256]{2,1,0:T(8,128)S(1)}, f32[8,128]{1,0:T(8,128)S(1)}, f32[16,8,128]{2,1,0:T(8,128)S(1)}) custom-call(f32[16,8,512]{2,1,0:T(8,128)S(1)} %get-tuple-element.41.refs_6_.refs_0_.refs_3_, f32[3,24,8,512]{3,2,1,0:T(8,128)S(1)} %copy-done, f32[24,8,512]{2,1,0:T(8,128)S(1)} %get-tuple-element.36.refs_3_.inv_ref.refs_2_, ...), custom_call_target="tpu_custom_call" | custom-call | tf_op jit(solution)/shard_map/pallas_call | solution.py:755
  19.8 2.0 %collective-permute-done.7.refs_4_ = f32[8,2048]{1,0:T(8,128)S(1)} collective-permute-done((f32[8,2048]{1,0:T(8,128)S(1)}, f32[8,2048]{1,0:T(8,128)S(1)}, u32[]{:S(2)}, u32[]{:S(2)}) %collective-permute-start.7) | collective-permute-done | bytes 65568 | tf_op jit(solution)/shard_map/ppermute | solution.py:1015
  21.8 0.0 collective-permute-done.8.refs_5_
  21.8 0.0 collective-permute-done.6.refs_3_
  21.8 0.8 %shard_map.117 = (f32[8,2432]{1,0:T(8,128)S(1)}, f32[8,2432]{1,0:T(8,128)S(1)}, f32[8,2432]{1,0:T(8,128)S(1)}, f32[8,2432]{1,0:T(8,128)S(1)}) custom-call(bf16[112,48]{1,0:T(8,128)(2,1)S(1)} %copy-done.3, f32[4,8,256]{2,1,0:T(8,128)S(1)} %get-tuple-element.52.refs_1_, f32[8,128]{1,0:T(8,128)S(1)} %get-tuple-element.51.refs_2_.refs_5_, ...), custom_call_target="tpu_custom_call" | custom-call | tf_op jit(solution)/shard_map/pallas_call | solution.py:918
  22.6 1.8 %collective-permute-start.9 = (f32[8,2432]{1,0:T(8,128)S(1)}, f32[8,2432]{1,0:T(8,128)S(1)}, u32[]{:S(2)}, u32[]{:S(2)}) collective-permute-start(f32[8,2432]{1,0:T(8,128)S(1)} %get-tuple-element.61), channel_id=1, source_target_pairs={{0,24},{8,16},{16,8},{24,0},{1,25},{9,17},{17,9},{25,1},{2,26},{10... | collective-permute-start | bytes 233480 | tf_op jit(solution)/shard_map/ppermute | solution.py:1015
  24.4 0.1 collective-permute-start.10
  24.5 2.5 %collective-permute-start.11 = (f32[8,2432]{1,0:T(8,128)S(1)}, f32[8,2432]{1,0:T(8,128)S(1)}, u32[]{:S(2)}, u32[]{:S(2)}) collective-permute-start(f32[8,2432]{1,0:T(8,128)S(1)} %get-tuple-element.63), channel_id=1, source_target_pairs={{0,16},{8,24},{16,0},{24,8},{1,17},{9,25},{17,1},{25,9},{2,18},{10... | collective-permute-start | bytes 233480 | tf_op jit(solution)/shard_map/ppermute | solution.py:1015
  27.1 3.3 %shard_map.118 = (f32[3,24,8,512]{3,2,1,0:T(8,128)}, f32[3,24,8,512]{3,2,1,0:T(8,128)}, f32[16,8,512]{2,1,0:T(8,128)}) custom-call(f32[3,24,8,512]{3,2,1,0:T(8,128)S(1)} %get-tuple-element.34.e_ref.refs_0_, f32[3,24,8,512]{3,2,1,0:T(8,128)S(1)} %get-tuple-element.35.h_ref.refs_1_, f32[24,8,512]{2,1,0:T(8,128)S(1)} %get-tuple-element.36.refs_3_.inv_ref.refs_2_, ...), custom_call_target="tpu_custom_call" | custom-call | tf_op jit(solution)/shard_map/pallas_call | solution.py:826
  30.3 0.0 collective-permute-done.9.refs_0_
  30.3 0.0 collective-permute-done.10.refs_1_
  30.4 0.2 collective-permute-done.11.refs_2_
  30.6 1.0 %shard_map.119 = f32[16,8,512]{2,1,0:T(8,128)} custom-call(f32[8,2432]{1,0:T(8,128)S(1)} %collective-permute-done.9.refs_0_, f32[8,2432]{1,0:T(8,128)S(1)} %collective-permute-done.10.refs_1_, f32[8,2432]{1,0:T(8,128)S(1)} %collective-permute-done.11.refs_2_, f32[8,2432]{1,0:T(8,128)S(1)} %get-tuple-element.57.refs_12_.refs_3_), custom_call_target="tpu_custom_call" | custom-call | tf_op jit(solution)/shard_map/pallas_call | solution.py:996
Async XLA Ops:
  0.6 6.7 %copy-start = (f32[3,24,8,512]{3,2,1,0:T(8,128)S(1)}, f32[3,24,8,512]{3,2,1,0:T(8,128)}, u32[]{:S(2)}) copy-start(f32[3,24,8,512]{3,2,1,0:T(8,128)} %refs_1_.1) | copy-start | bytes 3538948
  0.6 6.7 %copy-start.1 = (f32[16,8,512]{2,1,0:T(8,128)S(1)}, f32[16,8,512]{2,1,0:T(8,128)}, u32[]{:S(2)}) copy-start(f32[16,8,512]{2,1,0:T(8,128)} %grad_ref.3) | copy-start | bytes 786436
  0.7 6.7 %copy-start.5 = (s32[1,64]{1,0:T(1,128)S(1)}, s32[1,64]{1,0:T(1,128)}, u32[]{:S(2)}) copy-start(s32[1,64]{1,0:T(1,128)} %mask_ref.1) | copy-start | bytes 772
  0.7 6.7 %copy-start.4 = (f32[4]{0:T(128)S(1)}, f32[4]{0:T(128)}, u32[]{:S(2)}) copy-start(f32[4]{0:T(128)} %param.12) | copy-start | bytes 52
  0.7 6.7 %copy-start.2 = (s32[24,8,512]{2,1,0:T(8,128)S(1)}, s32[24,8,512]{2,1,0:T(8,128)}, u32[]{:S(2)}) copy-start(s32[24,8,512]{2,1,0:T(8,128)} %mat_ref.1) | copy-start | bytes 1179652
  2.5 7.2 %collective-permute-start.1 = (f32[56,512]{1,0:T(8,128)S(1)}, f32[56,512]{1,0:T(8,128)S(1)}, u32[]{:S(2)}, u32[]{:S(2)}) collective-permute-start(f32[56,512]{1,0:T(8,128)S(1)} %get-tuple-element.39), channel_id=1, source_target_pairs={{0,8},{2,10},{4,12},{6,14},{8,0},{10,2},{12,4},{14,6},{16,24},{18,... | collective-permute-start | bytes 344072 | tf_op jit(solution)/shard_map/ppermute | solution.py:65
  5.6 4.2 %collective-permute-start.2 = (f32[56,512]{1,0:T(8,128)S(1)}, f32[56,512]{1,0:T(8,128)S(1)}, u32[]{:S(2)}, u32[]{:S(2)}) collective-permute-start(f32[56,512]{1,0:T(8,128)S(1)} %get-tuple-element.40), channel_id=1, source_target_pairs={{0,2},{2,0},{4,6},{6,4},{8,16},{10,18},{12,20},{14,22},{16,8},{18,... | collective-permute-start | bytes 344072 | tf_op jit(solution)/shard_map/ppermute | solution.py:65
  5.6 4.2 %collective-permute-start = (f32[3,8,512]{2,1,0:T(8,128)S(1)}, f32[3,8,512]{2,1,0:T(8,128)S(1)}, u32[]{:S(2)}, u32[]{:S(2)}) collective-permute-start(f32[3,8,512]{2,1,0:T(8,128)S(1)} %get-tuple-element.38), channel_id=1, source_target_pairs={{0,1},{2,3},{4,5},{6,7},{1,0},{3,2},{5,4},{7,6},{8,9},{10,11},{12,... | collective-permute-start | bytes 147464 | tf_op jit(solution)/shard_map/ppermute | solution.py:65
  7.1 6.2 %collective-permute-start.3 = (f32[8,512]{1,0:T(8,128)S(1)}, f32[8,512]{1,0:T(8,128)S(1)}, u32[]{:S(2)}, u32[]{:S(2)}) collective-permute-start(f32[8,512]{1,0:T(8,128)S(1)} %get-tuple-element.45), channel_id=1, source_target_pairs={{0,2},{2,0},{4,6},{6,4},{1,8},{3,10},{5,12},{7,14},{8,1},{10,3},{1... | collective-permute-start | bytes 49160 | tf_op jit(solution)/shard_map/ppermute | solution.py:91
  10.5 11.3 %collective-permute-start.6 = (f32[8,2176]{1,0:T(8,128)S(1)}, f32[8,2176]{1,0:T(8,128)S(1)}, u32[]{:S(2)}, u32[]{:S(2)}) collective-permute-start(f32[8,2176]{1,0:T(8,128)S(1)} %get-tuple-element.53), channel_id=1, source_target_pairs={{0,24},{8,16},{16,8},{24,0},{1,25},{9,17},{17,9},{25,1},{2,26},{10... | collective-permute-start | bytes 208904 | tf_op jit(solution)/shard_map/ppermute | solution.py:1015
  13.5 4.9 %collective-permute-start.4 = (f32[16,8,128]{2,1,0:T(8,128)S(1)}, f32[16,8,128]{2,1,0:T(8,128)S(1)}, u32[]{:S(2)}, u32[]{:S(2)}) collective-permute-start(f32[16,8,128]{2,1,0:T(8,128)S(1)} %get-tuple-element.48), channel_id=1, source_target_pairs={{0,2},{1,3},{2,0},{3,1},{4,6},{5,7},{6,4},{7,5},{8,10},{9,11},{10,... | collective-permute-start | bytes 196616 | tf_op jit(solution)/shard_map/ppermute | solution.py:65
  13.5 4.9 %collective-permute-start.5 = (f32[16,8,128]{2,1,0:T(8,128)S(1)}, f32[16,8,128]{2,1,0:T(8,128)S(1)}, u32[]{:S(2)}, u32[]{:S(2)}) collective-permute-start(f32[16,8,128]{2,1,0:T(8,128)S(1)} %get-tuple-element.49), channel_id=1, source_target_pairs={{0,1},{1,0},{2,4},{3,5},{4,2},{5,3},{6,7},{7,6},{8,9},{9,8},{10,12... | collective-permute-start | bytes 196616 | tf_op jit(solution)/shard_map/ppermute | solution.py:65
  15.2 6.6 %collective-permute-start.7 = (f32[8,2048]{1,0:T(8,128)S(1)}, f32[8,2048]{1,0:T(8,128)S(1)}, u32[]{:S(2)}, u32[]{:S(2)}) collective-permute-start(f32[8,2048]{1,0:T(8,128)S(1)} %get-tuple-element.54), channel_id=1, source_target_pairs={{0,16},{8,24},{16,0},{24,8},{1,17},{9,25},{17,1},{25,9},{2,18},{10... | collective-permute-start | bytes 196616 | tf_op jit(solution)/shard_map/ppermute | solution.py:1015
  16.9 1.5 %copy-start.3 = (bf16[112,48]{1,0:T(8,128)(2,1)S(1)}, bf16[112,48]{1,0:T(8,128)(2,1)}, u32[]{:S(2)}) copy-start(bf16[112,48]{1,0:T(8,128)(2,1)} %constant.2.clone.refs_7_.refs_0_) | copy-start | bytes 32260
  16.9 4.9 %collective-permute-start.8 = (f32[8,2048]{1,0:T(8,128)S(1)}, f32[8,2048]{1,0:T(8,128)S(1)}, u32[]{:S(2)}, u32[]{:S(2)}) collective-permute-start(f32[8,2048]{1,0:T(8,128)S(1)} %get-tuple-element.55), channel_id=1, source_target_pairs={{0,8},{8,0},{16,24},{24,16},{1,9},{9,1},{17,25},{25,17},{2,10},{10... | collective-permute-start | bytes 196616 | tf_op jit(solution)/shard_map/ppermute | solution.py:1015
  22.6 7.7 %collective-permute-start.9 = (f32[8,2432]{1,0:T(8,128)S(1)}, f32[8,2432]{1,0:T(8,128)S(1)}, u32[]{:S(2)}, u32[]{:S(2)}) collective-permute-start(f32[8,2432]{1,0:T(8,128)S(1)} %get-tuple-element.61), channel_id=1, source_target_pairs={{0,24},{8,16},{16,8},{24,0},{1,25},{9,17},{17,9},{25,1},{2,26},{10... | collective-permute-start | bytes 233480 | tf_op jit(solution)/shard_map/ppermute | solution.py:1015
  24.4 5.9 %collective-permute-start.10 = (f32[8,2432]{1,0:T(8,128)S(1)}, f32[8,2432]{1,0:T(8,128)S(1)}, u32[]{:S(2)}, u32[]{:S(2)}) collective-permute-start(f32[8,2432]{1,0:T(8,128)S(1)} %get-tuple-element.62), channel_id=1, source_target_pairs={{0,8},{8,0},{16,24},{24,16},{1,9},{9,1},{17,25},{25,17},{2,10},{10... | collective-permute-start | bytes 233480 | tf_op jit(solution)/shard_map/ppermute | solution.py:1015
  24.5 6.0 %collective-permute-start.11 = (f32[8,2432]{1,0:T(8,128)S(1)}, f32[8,2432]{1,0:T(8,128)S(1)}, u32[]{:S(2)}, u32[]{:S(2)}) collective-permute-start(f32[8,2432]{1,0:T(8,128)S(1)} %get-tuple-element.63), channel_id=1, source_target_pairs={{0,16},{8,24},{16,0},{24,8},{1,17},{9,25},{17,1},{25,9},{2,18},{10... | collective-permute-start | bytes 233480 | tf_op jit(solution)/shard_map/ppermute | solution.py:1015
